TPU v7x, 32 devices: a whole 2x2x4 slice. The times are simulated.
32 devices in a mesh: groups: 2 (over x), blk: 16 (over z, y, core).
Axes of the slice: x: 2, y: 2, z: 4, core: 2. Of those that a mesh axis runs over, the one named last changes fastest.
Arguments:
- embed: bfloat16 [16384, 1024], P(('groups', 'blk')), parts along dimension 0, may hold values from -6 to 6
- owner: int32 [16384, 1], P(('groups', 'blk')), parts along dimension 0, may hold values from 0 to 15; in each aligned block of 512 rows (0 to 511, 512 to 1023, ...) at most 64 rows name the same one
- near: int32 [32], P('groups'), parts along dimension 0, may hold values from 0 to 1
Outputs:
- density: float32 [16384], P(('groups', 'blk')), parts along dimension 0
There are 2 independent parts, one for each index of `groups`. A program takes and returns all parts, laid end to end along the dimension named above; each array names one. Nothing has to cross between parts.
Inputs may be any that keep to these rules, and one draw needn't show every extreme that they name: Among the rows of one device no owner is named more than 64 times, a bound that some block reaches.
All inputs are finite; a program needn't handle non-finite values.
Results may differ from a plain program's by a relative error of at most 0.0003.
Values may be sent and summed in bfloat16 or wider, within the bound.
No kernel may reach another device: no remote copies, remote signals or barrier semaphores. Data moves between devices by JAX's collectives and lax.ppermute only.
A program may use at most 64 MiB of HBM per device.

v0:
```python
import jax
import jax.numpy as jnp
from jax import lax
from jax.sharding import PartitionSpec as P


def passed_along(block, axis, distance):
    devices = range(lax.axis_size(axis))
    route = [((i - distance) % len(devices), i) for i in devices]
    return lax.ppermute(block, axis, route)


def pair_terms(a_rows, a_used, b_rows, b_used, same, factor):
    sim = lax.dot_general(
        a_rows, b_rows, (((1,), (1,)), ((), ())), preferred_element_type=jnp.float32
    )
    weight = a_used[:, None] * b_used[None, :] * factor
    if same:
        count = a_rows.shape[0]
        weight = jnp.where(jnp.arange(count)[:, None] == jnp.arange(count)[None, :], 0.0, weight)
    return weight * jnp.exp(16.0 * sim)


def per_device(embed, owner, near):
    rows, width = embed.shape
    blocks = lax.axis_size("blk")
    mine = lax.axis_index("blk")
    cap = 2 * rows // blocks
    slots = blocks * cap
    values = embed.astype(jnp.float32)
    scale = lax.rsqrt(jnp.mean(values * values, axis=-1, keepdims=True) + 1e-06) / jnp.sqrt(
        jnp.float32(width)
    )
    unit = (values * scale).astype(jnp.bfloat16)
    owned = owner[:, 0]
    onehot = (owned[:, None] == jnp.arange(blocks, dtype=jnp.int32)[None, :]).astype(jnp.int32)
    rank = jnp.sum((jnp.cumsum(onehot, axis=0) - onehot) * onehot, axis=1)
    position = owned * cap + rank
    send_rows = jnp.zeros((slots, width), jnp.bfloat16).at[position].set(unit)
    send_used = jnp.zeros((slots,), jnp.bfloat16).at[position].set(jnp.ones((rows,), jnp.bfloat16))
    got_rows, got_used = (
        lax.all_to_all(
            send_rows.reshape(blocks, cap, width), "blk", split_axis=0, concat_axis=0, tiled=True
        ),
        lax.all_to_all(
            send_used.reshape(blocks, cap), "blk", split_axis=0, concat_axis=0, tiled=True
        ),
    )
    own_rows = got_rows.reshape(slots, width)
    own_used_b = got_used.reshape(slots)
    own_used = own_used_b.astype(jnp.float32)
    before = (mine + blocks - 1) % blocks
    to_prev = 0.5 * (near[mine] == 0).astype(jnp.float32) + 0.5 * (near[before] == 1).astype(
        jnp.float32
    )
    left_rows, left_used = passed_along((own_rows, own_used_b), "blk", 1)
    sums = jnp.sum(pair_terms(own_rows, own_used, own_rows, own_used, True, 1.0), axis=1)
    cross = pair_terms(own_rows, own_used, left_rows, left_used.astype(jnp.float32), False, to_prev)
    returned = passed_along(jnp.sum(cross, axis=0), "blk", -1)
    sums = sums + jnp.sum(cross, axis=1) + returned
    scores = jnp.log1p(sums)
    answer = lax.all_to_all(
        scores.reshape(blocks, cap), "blk", split_axis=0, concat_axis=0, tiled=True
    )
    return answer.reshape(slots)[position]


def solution(mesh):
    return jax.shard_map(
        per_device,
        mesh=mesh,
        in_specs=(P(("groups", "blk"), None), P(("groups", "blk"), None), P("groups")),
        out_specs=P(("groups", "blk")),
        check_vma=False,
    )
```

profile of v0, /device:TPU:0, one launch (start us, length us, event | category | flops | bytes accessed | tf_op | source)
XLA Modules:
  0.0 124.1 jit_solution(7833229362835722950)
XLA Ops:
  0.0 0.7 fusion.11
  0.7 1.1 reduce-window.6
  1.8 0.2 slice_reduce_fusion
  2.1 0.8 fusion.10
  2.9 0.7 compare_select_fusion
  3.5 1.5 %fusion.2 = f32[512]{0:T(512)S(1)} fusion(bf16[512,1024]{1,0:T(8,128)(2,1)} %param.3), kind=kLoop, calls=%fused_computation.10 | loop fusion | flops 1572352 | bytes 1050624 | tf_op jit(solution)/shard_map/reduce_sum | solution.py:31
  5.1 4.0 %scatter_custom_fusion.1 = bf16[1024,1024]{1,0:T(8,128)(2,1)S(1)} fusion(s32[512]{0:T(512)S(1)} %bitcast.33, bf16[512,1024]{1,0:T(8,128)(2,1)} %param.3, f32[512]{0:T(512)S(1)} %rsqrt_multiply_fusion, bf16[]{:T(256)} %constant.44.clone.1), kind=kCustom, calls=%fused_computation.12 | custom fusion | flops 1572864 | bytes 3147778 | tf_op jit(solution)/shard_map/scatter | solution.py:39
  9.0 0.0 copy-start
  9.0 54.6 %all_to_all.24 = bf16[16,64,1024]{2,1,0:T(8,128)(2,1)} all-to-all(bf16[16,64,1024]{2,1,0:T(8,128)(2,1)S(1)} %bitcast.30), channel_id=1, replica_groups=mesh['groups'=2,'blk'=16] {'blk'}, dimensions={0} | all-to-all | bytes 4194304 | tf_op jit(solution)/shard_map/all_to_all | solution.py:42
  63.7 0.8 collective-permute-start.1
  64.4 3.8 %scatter_custom_fusion = bf16[1024]{0:T(1024)(128)(2,1)S(1)} fusion(s32[512]{0:T(512)S(1)} %bitcast.34, bf16[512]{0:T(512)(128)(2,1)S(1)} %broadcast.52, bf16[]{:T(256)} %constant.44.clone.1), kind=kCustom, calls=%fused_computation.28 | custom fusion | bytes 2050 | tf_op jit(solution)/shard_map/scatter | solution.py:40
  68.2 0.1 all_to_all.20
  68.3 24.0 %all_to_all.25 = bf16[16,1,64]{2,1,0:T(2,128)(2,1)S(1)} all-to-all(bf16[16,1,64]{2,1,0:T(2,128)(2,1)S(1)} %all_to_all.20), channel_id=1, replica_groups=mesh['groups'=2,'blk'=16] {'blk'}, dimensions={0} | all-to-all | bytes 4096 | tf_op jit(solution)/shard_map/all_to_all | solution.py:45
  92.3 0.1 reshape.74
  92.4 0.1 collective-permute-start
  92.4 0.0 copy-done
  92.4 0.6 fusion.14
  94.3 3.8 %collective-permute-done = bf16[1024]{0:T(1024)(128)(2,1)S(1)} collective-permute-done((bf16[1024]{0:T(1024)(128)(2,1)S(1)}, bf16[1024]{0:T(1024)(128)(2,1)S(1)}, u32[]{:S(2)}, u32[]{:S(2)}) %collective-permute-start) | collective-permute-done | bytes 2080 | tf_op jit(solution)/shard_map/ppermute | solution.py:10
  98.1 0.0 collective-permute-done.1
  98.1 5.0 %fusion.1 = (f32[1024]{0:T(1024)S(1)}, f32[1024]{0:T(1024)S(1)}) fusion(f32[]{:T(128)} %bitcast.7, f32[1024]{0:T(1024)S(1)} %convert_element_type.34, f32[1024]{0:T(1024)S(1)} %convert_element_type.31, bf16[1024,1024]{1,0:T(8,128)(2,1)} %bitcast.6, bf16[1024,1024]{1,0:T(8,128)(2,1)} %collective-permute-done.1), kind=kOutput, calls=%fused_computation.7 | convolution fusion | flops 2153773056 | bytes 4210692 | tf_op jit(solution)/shard_map/dot_general | solution.py:14
  103.1 0.9 collective-permute-start.2
  104.0 4.9 %multiply_reduce_fusion = f32[1024]{0:T(1024)S(1)} fusion(bf16[1024,1024]{1,0:T(8,128)(2,1)} %bitcast.6, f32[1024]{0:T(1024)S(1)} %convert_element_type.31), kind=kOutput, calls=%fused_computation.4 | convolution fusion | flops 2153774080 | bytes 2105344 | tf_op jit(solution)/shard_map/dot_general | solution.py:14
  108.9 0.0 collective-permute-done.2
  108.9 0.7 all_to_all.18
  109.6 3.5 %all-to-all-start.2 = ((f32[16,1,64]{2,1,0:T(1,128)}), f32[16,1,64]{2,1,0:T(1,128)S(1)}, u32[]{:S(2)}, u32[]{:S(2)}) async-start(f32[16,1,64]{2,1,0:T(1,128)} %all_to_all.18), calls=%async_computation.2 | async-start | bytes 16384 | tf_op jit(solution)/shard_map/all_to_all | solution.py:62
  113.1 6.4 %all-to-all-done.2 = f32[16,1,64]{2,1,0:T(1,128)S(1)} async-done(((f32[16,1,64]{2,1,0:T(1,128)}), f32[16,1,64]{2,1,0:T(1,128)S(1)}, u32[]{:S(2)}, u32[]{:S(2)}) %all-to-all-start.2) | async-done | bytes 4128 | tf_op jit(solution)/shard_map/all_to_all | solution.py:62
  119.5 0.5 broadcast.69
  120.0 0.7 reduce.6
  120.6 0.1 reshape.77
  120.7 3.4 %gather_fusion = f32[512]{0:T(512)} fusion(f32[1024]{0:T(1024)S(1)} %reshape.77, s32[1024]{0:T(1024)S(1)} %pad_clamp_fusion), kind=kCustom, calls=%fused_computation | custom fusion | bytes 6144 | tf_op jit(solution)/shard_map/gather | solution.py:65
  (9 shorter events, 0.1 us)
Async XLA Ops:
  9.0 83.4 %copy-start = (s32[16]{0:T(128)S(1)}, s32[16]{0:T(128)}, u32[]{:S(2)}) copy-start(s32[16]{0:T(128)} %param.5) | copy-start | bytes 196
  63.7 34.4 %collective-permute-start.1 = (bf16[1024,1024]{1,0:T(8,128)(2,1)}, bf16[1024,1024]{1,0:T(8,128)(2,1)}, u32[]{:S(2)}, u32[]{:S(2)}) collective-permute-start(bf16[1024,1024]{1,0:T(8,128)(2,1)} %bitcast.6), channel_id=1, source_target_pairs={{15,0},{0,1},{1,2},{2,3},{3,4},{4,5},{5,6},{6,7},{7,8},{8,9},{9,10... | collective-permute-start | bytes 6291464 | tf_op jit(solution)/shard_map/ppermute | solution.py:10
  92.4 5.7 %collective-permute-start = (bf16[1024]{0:T(1024)(128)(2,1)S(1)}, bf16[1024]{0:T(1024)(128)(2,1)S(1)}, u32[]{:S(2)}, u32[]{:S(2)}) collective-permute-start(bf16[1024]{0:T(1024)(128)(2,1)S(1)} %reshape.74), channel_id=1, source_target_pairs={{15,0},{0,1},{1,2},{2,3},{3,4},{4,5},{5,6},{6,7},{7,8},{8,9},{9,10... | collective-permute-start | bytes 6152 | tf_op jit(solution)/shard_map/ppermute | solution.py:10
  103.1 5.8 %collective-permute-start.2 = (f32[1024]{0:T(1024)S(1)}, f32[1024]{0:T(1024)S(1)}, u32[]{:S(2)}, u32[]{:S(2)}) collective-permute-start(f32[1024]{0:T(1024)S(1)} %get-tuple-element.6), channel_id=1, source_target_pairs={{1,0},{2,1},{3,2},{4,3},{5,4},{6,5},{7,6},{8,7},{9,8},{10,9},{11,1... | collective-permute-start | bytes 12296 | tf_op jit(solution)/shard_map/ppermute | solution.py:10
  109.6 9.9 %all-to-all-start.2 = ((f32[16,1,64]{2,1,0:T(1,128)}), f32[16,1,64]{2,1,0:T(1,128)S(1)}, u32[]{:S(2)}, u32[]{:S(2)}) async-start(f32[16,1,64]{2,1,0:T(1,128)} %all_to_all.18), calls=%async_computation.2 | async-start | bytes 16384 | tf_op jit(solution)/shard_map/all_to_all | solution.py:62
where the time goes:
time: 125 us; the launch traced here: 124 us
  blocking collectives  78.6 us (63%)
  waiting for transfers between devices  10.1 us (8%)
  matrix products  9.9 us (8%)
  other arithmetic  9.53 us (8%)
  local copies, waits for them, and re-layouts  9.42 us (8%)
  starting transfers between devices  5.2 us (4%)
  between operations  1.37 us (1%)
    all_to_all x1, blocking collectives, per_device(): lax.all_to_all(send_rows.reshape(blocks, cap, width), 'blk', split_axis=0...  54.6 us
    all_to_all x1, blocking collectives, per_device(): lax.all_to_all(send_used.reshape(blocks, cap), 'blk', split_axis=0, conca...  24 us
    dot_general x2, matrix products, pair_terms(): lax.dot_general(a_rows, b_rows, (((1,), (1,)), ((), ())), preferred_eleme...  9.9 us
    all_to_all x1, waiting for transfers between devices, per_device(): lax.all_to_all(scores.reshape(blocks, cap), 'blk', split_axis=0, concat_a...  6.36 us
    scatter x1, other arithmetic, per_device(): send_rows = jnp.zeros((slots, width), jnp.bfloat16).at[position].set(unit)  3.97 us
    ppermute x3, waiting for transfers between devices, passed_along(): return lax.ppermute(block, axis, route)  3.77 us
    scatter x1, local copies, waits for them, and re-layouts, per_device(): jnp.zeros((slots,), jnp.bfloat16).at[position]  3.77 us
    all_to_all x1, starting transfers between devices, per_device(): lax.all_to_all(scores.reshape(blocks, cap), 'blk', split_axis=0, concat_a...  3.49 us
  transfers between devices with their start and end apart: 4, of which 2 were waited for; matrix products, arithmetic and copies ran while one was open for 8% of the time, Pallas kernels for 0%

commit v1 on v0

v1 whole, which is shorter than its diff:
```python
import functools

import jax
import jax.numpy as jnp
from jax import lax
from jax.experimental import pallas as pl
from jax.experimental.pallas import tpu as pltpu
from jax.sharding import PartitionSpec as P

STRIP = 256


def unit_rows(values):
    values = values.astype(jnp.float32)
    width = values.shape[-1]
    scale = lax.rsqrt(jnp.mean(values * values, axis=-1, keepdims=True) + 1e-06) / jnp.sqrt(
        jnp.float32(width)
    )
    return (values * scale).astype(jnp.bfloat16)


def decode(code, clusters):
    own = code // 2
    near = code - 2 * own
    nearest = own + 2 * near - 1
    nearest = jnp.where(nearest < 0, nearest + clusters, nearest)
    nearest = jnp.where(nearest >= clusters, nearest - clusters, nearest)
    return own, nearest


def as_column(row):
    return jnp.transpose(jnp.broadcast_to(row, (128, row.shape[1])))


def terms(a_unit, b_unit, a_own, a_near, b_own, b_near):
    sim = lax.dot_general(
        a_unit, b_unit, (((1,), (1,)), ((), ())), preferred_element_type=jnp.float32
    )
    value = jnp.exp(16.0 * sim)
    wide = value.shape[1] // 128
    a_own, a_near = jnp.tile(a_own, (1, wide)), jnp.tile(a_near, (1, wide))
    near = jnp.where(a_near == b_own, value, 0.0) + jnp.where(a_own == b_near, value, 0.0)
    return jnp.where(a_own == b_own, value, 0.0) + 0.5 * near


def lanes_added(x):
    out = x[:, :128]
    for at in range(128, x.shape[1], 128):
        out = out + x[:, at : at + 128]
    return out


def as_row(x):
    return jnp.sum(jnp.transpose(x), axis=0, keepdims=True)


def normalise(source, target):
    rows = source.shape[0]
    for at in range(0, rows, STRIP):
        target[at : at + STRIP, :] = unit_rows(source[at : at + STRIP, :])


def own_kernel(clusters, mine, other, mine_code, other_code, mine_unit, other_unit, sums):
    normalise(mine, mine_unit)
    normalise(other, other_unit)
    rows = mine.shape[0]
    a_own, a_near = [as_column(v) for v in decode(mine_code[...], clusters)]
    strips = []
    for at in range(0, rows, STRIP):
        total = jnp.zeros((STRIP, 128), jnp.float32)
        for same, unit, code in ((True, mine_unit, mine_code), (False, other_unit, other_code)):
            b_own, b_near = decode(code[...], clusters)
            value = terms(
                mine_unit[at : at + STRIP, :],
                unit[...],
                a_own[at : at + STRIP],
                a_near[at : at + STRIP],
                b_own,
                b_near,
            )
            if same:
                place = lax.broadcasted_iota(jnp.int32, value.shape, 0) + at
                value = jnp.where(
                    place == lax.broadcasted_iota(jnp.int32, value.shape, 1), 0.0, value
                )
            total = total + lanes_added(value)
        strips.append(as_row(total))
    sums[...] = jnp.concatenate(strips, axis=1)


def pair_kernel(clusters, ready, raw, *refs):
    blocks = ready + raw
    a_rows, refs = refs[:blocks], refs[blocks:]
    a_codes, refs = refs[:blocks], refs[blocks:]
    b_rows, b_code, refs = refs[0], refs[1], refs[2:]
    a_units, refs = refs[:raw], refs[raw:]
    a_sums, b_sums, b_unit = refs
    normalise(b_rows, b_unit)
    b_own, b_near = decode(b_code[...], clusters)
    rows = b_rows.shape[0]
    b_total = jnp.zeros((8, rows), jnp.float32)
    for block in range(blocks):
        a_own, a_near = [as_column(v) for v in decode(a_codes[block][...], clusters)]
        unit = a_rows[block]
        if block >= ready:
            unit = a_units[block - ready]
            normalise(a_rows[block], unit)
        for at in range(0, rows, STRIP):
            value = terms(
                unit[at : at + STRIP, :],
                b_unit[...],
                a_own[at : at + STRIP],
                a_near[at : at + STRIP],
                b_own,
                b_near,
            )
            a_sums[block : block + 1, at : at + STRIP] = as_row(lanes_added(value))
            b_total = b_total + jnp.sum(value.reshape(STRIP // 8, 8, rows), axis=0)
    b_sums[...] = jnp.sum(b_total, axis=0, keepdims=True)


def vmem(count):
    return [pl.BlockSpec(memory_space=pltpu.VMEM)] * count


def cost(tiles, rows, width):
    return pl.CostEstimate(
        flops=2 * tiles * rows * rows * width,
        bytes_accessed=4 * rows * width,
        transcendentals=tiles * rows * rows,
    )


def own_terms(clusters, mine, other, mine_code, other_code):
    rows, width = mine.shape
    unit = jax.ShapeDtypeStruct((rows, width), jnp.bfloat16)
    return pl.pallas_call(
        functools.partial(own_kernel, clusters),
        out_shape=(unit, unit, jax.ShapeDtypeStruct((1, rows), jnp.float32)),
        in_specs=vmem(4),
        out_specs=vmem(3),
        compiler_params=pltpu.CompilerParams(vmem_limit_bytes=40 << 20),
        cost_estimate=cost(2, rows, width),
        name="own_terms",
    )(mine, other, mine_code, other_code)


def pair_sums(clusters, ready, raw, a_codes, b_rows, b_code):
    rows, width = b_rows.shape
    blocks = len(ready) + len(raw)
    unit = jax.ShapeDtypeStruct((rows, width), jnp.bfloat16)
    outs = pl.pallas_call(
        functools.partial(pair_kernel, clusters, len(ready), len(raw)),
        out_shape=(unit,) * len(raw)
        + (
            jax.ShapeDtypeStruct((blocks, rows), jnp.float32),
            jax.ShapeDtypeStruct((1, rows), jnp.float32),
        ),
        in_specs=vmem(2 * blocks + 2),
        out_specs=vmem(len(raw) + 2),
        scratch_shapes=[pltpu.VMEM((rows, width), jnp.bfloat16)],
        compiler_params=pltpu.CompilerParams(vmem_limit_bytes=40 << 20),
        cost_estimate=cost(blocks, rows, width),
        name="pair_sums",
    )(*ready, *raw, *a_codes, b_rows, b_code)
    a_sums = outs[-2]
    return outs[: len(raw)], [a_sums[i : i + 1] for i in range(blocks)], outs[-1]


def per_device(embed, owner, near):
    rows = embed.shape[0]
    clusters = near.shape[0]
    chips = lax.axis_size("blk") // 2
    hops = chips // 4
    order = list(range(0, chips, 2)) + list(range(chips - 1, 0, -2))

    def along(block, distance, crossed=lambda place: 0):
        route = []
        for place in range(chips):
            there = (place + distance) % chips
            for core in range(2):
                route.append((2 * order[place] + core, 2 * order[there] + (core ^ crossed(there))))
        return lax.ppermute(block, "blk", route)

    def other_core(block):
        return lax.ppermute(block, "blk", [(i, i ^ 1) for i in range(2 * chips)])

    def late(place):
        return int(place >= chips // 2)

    owned = owner[:, 0]
    names = jnp.arange(clusters, dtype=jnp.int32)
    nearby = jnp.sum(
        jnp.where(owned[None, :] == names[:, None], near[:, None], 0), axis=0, keepdims=True
    )
    code = 2 * owned[None, :] + nearby

    behind, ahead = [embed], [embed]
    behind_code, ahead_code = [code], [code]
    for hop in range(1, hops + 1):
        crossed = late if hop == hops else lambda place: 0
        behind.append(along(behind[-1], 1))
        ahead.append(along(ahead[-1], -1, crossed))
        behind_code.append(along(behind_code[-1], 1))
        ahead_code.append(along(ahead_code[-1], -1, crossed))
    spare = [other_core(block) for block in behind[:hops]]
    spare_code = [other_core(block) for block in behind_code[:hops]]

    unit, spare_unit, total = own_terms(clusters, embed, spare[0], code, spare_code[0])
    units = [unit, spare_unit]
    codes = [code, spare_code[0]]
    sums = None
    for hop in range(1, hops + 1):
        last = hop == hops
        raw = [behind[hop]] if last else [behind[hop], spare[hop]]
        raw_codes = [behind_code[hop]] if last else [behind_code[hop], spare_code[hop]]
        raw_units, a_sums, b_sums = pair_sums(
            clusters, units, raw, codes + raw_codes, ahead[hop], ahead_code[hop]
        )
        if sums is not None:
            a_sums[0], a_sums[1] = a_sums[0] + sums[0], a_sums[1] + sums[1]
        done = a_sums[0] + other_core(a_sums[1])
        total = total + (done if hop == 1 else along(done, 1 - hop))
        if last:
            route = []
            for place in range(chips):
                there = (place + hop) % chips
                for core in range(2):
                    route.append(
                        (2 * order[place] + core, 2 * order[there] + (core ^ late(place)))
                    )
            total = total + lax.ppermute(b_sums, "blk", route)
            total = total + along(a_sums[2], -hop)
        else:
            total = total + along(b_sums, hop)
            sums = a_sums[2:]
            units, codes = list(raw_units), raw_codes
    return jnp.log1p(total)[0]


def solution(mesh):
    return jax.shard_map(
        per_device,
        mesh=mesh,
        in_specs=(P(("groups", "blk"), None), P(("groups", "blk"), None), P("groups")),
        out_specs=P(("groups", "blk")),
        check_vma=False,
    )
```

time: 125 us -> 75.6 us (0.60)
  blocking collectives: 78.6 us -> 0 us
  waiting for transfers between devices: 10.1 us -> 46 us
  starting transfers between devices: 5.2 us -> 16.2 us
  Pallas kernels: 0 us -> 10.4 us
  matrix products: 9.9 us -> 0 us
  local copies, waits for them, and re-layouts: 9.42 us -> 1.23 us
  other arithmetic: 9.53 us -> 1.46 us
  between operations: 1.37 us -> 0.07 us
    all_to_all x2 -> x0, blocking collectives: 78.6 us -> none  [the longest x1 54.6 us: per_device(): lax.all_to_all(send_rows.reshape(blocks, cap, width), 'blk', split_axis=0...]
    ppermute x3 -> x18, waiting for transfers between devices: 3.77 us -> 46 us  [the longest x11 43.7 us: along(): return lax.ppermute(block, 'blk', route)]
    ppermute x3 -> x18, starting transfers between devices: 1.71 us -> 16.2 us  [the longest x11 15.2 us: along(): return lax.ppermute(block, 'blk', route)]
    pallas_call x0 -> x3, Pallas kernels: none -> 10.4 us  [the longest x2 8.14 us: pair_sums(): pl.pallas_call(functools.partial(pair_kernel, clusters, len(ready), len(r...]
    dot_general x2 -> x0, matrix products: 9.9 us -> none  [pair_terms(): lax.dot_general(a_rows, b_rows, (((1,), (1,)), ((), ())), preferred_eleme...]
    all_to_all x1 -> x0, waiting for transfers between devices: 6.36 us -> none  [per_device(): lax.all_to_all(scores.reshape(blocks, cap), 'blk', split_axis=0, concat_a...]
    scatter x1 -> x0, other arithmetic: 3.97 us -> none  [per_device(): send_rows = jnp.zeros((slots, width), jnp.bfloat16).at[position].set(unit)]
    scatter x1 -> x0, local copies, waits for them, and re-layouts: 3.77 us -> none  [per_device(): jnp.zeros((slots,), jnp.bfloat16).at[position]]
  transfers between devices with their start and end apart: 4 -> 18, of which waited for: 2 -> 5; matrix products, arithmetic and copies ran while one was open for 8% -> 1% of each run, Pallas kernels for 0% -> 9%
where the time goes in v1:
time: 75.6 us; the launch traced here: 75.4 us
  waiting for transfers between devices  46 us (61%)
  starting transfers between devices  16.2 us (21%)
  Pallas kernels  10.4 us (14%)
  other arithmetic  1.46 us (2%)
  local copies, waits for them, and re-layouts  1.23 us (2%)
    ppermute x11, waiting for transfers between devices, along(): return lax.ppermute(block, 'blk', route)  43.7 us
    ppermute x11, starting transfers between devices, along(): return lax.ppermute(block, 'blk', route)  15.2 us
    pallas_call x2, Pallas kernels, pair_sums(): pl.pallas_call(functools.partial(pair_kernel, clusters, len(ready), len(r...  8.14 us
    pallas_call x1, Pallas kernels, own_terms(): pl.pallas_call(functools.partial(own_kernel, clusters), out_shape=(unit,...  2.27 us
  transfers between devices with their start and end apart: 18, of which 5 were waited for; matrix products, arithmetic and copies ran while one was open for 1% of the time, Pallas kernels for 9%

profile of v1, /device:TPU:0, one launch (start us, length us, event | category | flops | bytes accessed | tf_op | source)
XLA Modules:
  0.0 75.4 jit_solution(6560129629311975178)
XLA Ops:
  0.0 0.0 copy-start.2
  0.0 3.0 %collective-permute-start.2 = (bf16[512,1024]{1,0:T(8,128)(2,1)}, bf16[512,1024]{1,0:T(8,128)(2,1)S(1)}, u32[]{:S(2)}, u32[]{:S(2)}) collective-permute-start(bf16[512,1024]{1,0:T(8,128)(2,1)} %mine.1), channel_id=1, source_target_pairs={{0,4},{1,5},{4,8},{5,9},{8,12},{9,13},{12,14},{13,15},{14,10},{15,... | collective-permute-start | bytes 3145736 | tf_op jit(solution)/shard_map/ppermute | solution.py:183
  3.0 0.0 collective-permute-start.6
  3.0 0.0 collective-permute-start
  3.0 23.3 %collective-permute-done.2.refs_2_ = bf16[512,1024]{1,0:T(8,128)(2,1)S(1)} collective-permute-done((bf16[512,1024]{1,0:T(8,128)(2,1)}, bf16[512,1024]{1,0:T(8,128)(2,1)S(1)}, u32[]{:S(2)}, u32[]{:S(2)}) %collective-permute-start.2) | collective-permute-done | bytes 1048608 | tf_op jit(solution)/shard_map/ppermute | solution.py:183
  26.3 0.0 collective-permute-start.3
  26.3 1.8 %collective-permute-start.10 = (bf16[512,1024]{1,0:T(8,128)(2,1)S(1)}, bf16[512,1024]{1,0:T(8,128)(2,1)S(1)}, u32[]{:S(2)}, u32[]{:S(2)}) collective-permute-start(bf16[512,1024]{1,0:T(8,128)(2,1)S(1)} %collective-permute-done.2.refs_2_), channel_id=1, source_target_pairs={{0,4},{1,5},{4,8},{5,9},{8,12},{9,13},{12,14},{13,15},{14,10},{15,... | collective-permute-start | bytes 3145736 | tf_op jit(solution)/shard_map/ppermute | solution.py:183
  28.1 0.0 collective-permute-done.6.refs_8_
  28.1 0.1 collective-permute-start.12
  28.2 0.0 copy-done.2
  28.2 0.0 copy-start.1
  28.2 0.8 %select_reduce_fusion = s32[512]{0:T(512)S(1)} fusion(s32[16]{0:T(128)S(1)} %copy-done.2, s32[512]{0:T(512)} %bitcast.5), kind=kLoop, calls=%fused_computation | loop fusion | flops 24064 | bytes 4160 | tf_op jit(solution)/shard_map/reduce_sum | solution.py:193
  29.0 0.0 copy-done.1
  29.1 0.3 collective-permute-start.1
  29.4 0.9 %collective-permute-done.1.other_code.refs_5_ = s32[1,512]{1,0:T(1,128)S(1)} collective-permute-done((s32[1,512]{1,0:T(1,128)S(1)}, s32[1,512]{1,0:T(1,128)S(1)}, u32[]{:S(2)}, u32[]{:S(2)}) %collective-permute-start.1) | collective-permute-done | bytes 2080 | tf_op jit(solution)/shard_map/ppermute | solution.py:186
  30.3 2.0 %collective-permute-start.4 = (s32[1,512]{1,0:T(1,128)S(1)}, s32[1,512]{1,0:T(1,128)S(1)}, u32[]{:S(2)}, u32[]{:S(2)}) collective-permute-start(s32[1,512]{1,0:T(1,128)S(1)} %bitcast_add_fusion.mine_code.refs_4_), channel_id=1, source_target_pairs={{0,4},{1,5},{4,8},{5,9},{8,12},{9,13},{12,14},{13,15},{14,10},{15,... | collective-permute-start | bytes 6152 | tf_op jit(solution)/shard_map/ppermute | solution.py:183
  32.2 19.7 %collective-permute-done.4.refs_6_.refs_3_ = s32[1,512]{1,0:T(1,128)S(1)} collective-permute-done((s32[1,512]{1,0:T(1,128)S(1)}, s32[1,512]{1,0:T(1,128)S(1)}, u32[]{:S(2)}, u32[]{:S(2)}) %collective-permute-start.4) | collective-permute-done | bytes 2080 | tf_op jit(solution)/shard_map/ppermute | solution.py:183
  52.0 1.7 %collective-permute-start.7 = (s32[1,512]{1,0:T(1,128)S(1)}, s32[1,512]{1,0:T(1,128)S(1)}, u32[]{:S(2)}, u32[]{:S(2)}) collective-permute-start(s32[1,512]{1,0:T(1,128)S(1)} %bitcast_add_fusion.mine_code.refs_4_), channel_id=1, source_target_pairs={{0,2},{1,3},{4,0},{5,1},{8,4},{9,5},{12,8},{13,9},{14,12},{15,13},... | collective-permute-start | bytes 6152 | tf_op jit(solution)/shard_map/ppermute | solution.py:183
  53.7 0.0 collective-permute-done.other
  53.7 0.0 collective-permute-start.5
  53.7 0.0 copy-start
  53.7 1.2 %copy-done = bf16[512,1024]{1,0:T(8,128)(2,1)S(1)} copy-done((bf16[512,1024]{1,0:T(8,128)(2,1)S(1)}, bf16[512,1024]{1,0:T(8,128)(2,1)}, u32[]{:S(2)}) %copy-start) | copy-done | bytes 1048600
  54.9 2.3 %own_terms.1 = (bf16[512,1024]{1,0:T(8,128)(2,1)S(1)}, bf16[512,1024]{1,0:T(8,128)(2,1)S(1)}, f32[1,512]{1,0:T(1,128)S(1)}) custom-call(bf16[512,1024]{1,0:T(8,128)(2,1)S(1)} %copy-done, bf16[512,1024]{1,0:T(8,128)(2,1)S(1)} %collective-permute-done.other, s32[1,512]{1,0:T(1,128)S(1)} %bitcast_add_fusion.mine_code.refs_4_, ...), custom_call_target="tpu_custom_call" | custom-call | flops 1073741824 | bytes 2097152 | tf_op jit(solution)/shard_map/own_terms/pallas_call | solution.py:137
  57.2 0.0 collective-permute-done.7.refs_9_
  57.2 0.3 collective-permute-start.11
  57.5 0.0 collective-permute-done.5.refs_7_.refs_4_
  57.5 1.6 %collective-permute-start.13 = (s32[1,512]{1,0:T(1,128)S(1)}, s32[1,512]{1,0:T(1,128)S(1)}, u32[]{:S(2)}, u32[]{:S(2)}) collective-permute-start(s32[1,512]{1,0:T(1,128)S(1)} %collective-permute-done.7.refs_9_), channel_id=1, source_target_pairs={{0,3},{1,2},{4,0},{5,1},{8,4},{9,5},{12,8},{13,9},{14,12},{15,13},... | collective-permute-start | bytes 6152 | tf_op jit(solution)/shard_map/ppermute | solution.py:183
  59.1 0.0 collective-permute-done.3.refs_3_
  59.1 4.5 %pair_sums.2 = (bf16[512,1024]{1,0:T(8,128)(2,1)S(1)}, bf16[512,1024]{1,0:T(8,128)(2,1)S(1)}, f32[4,512]{1,0:T(4,128)S(1)}, f32[1,512]{1,0:T(1,128)S(1)}) custom-call(bf16[512,1024]{1,0:T(8,128)(2,1)S(1)} %get-tuple-element.15.refs_0_, bf16[512,1024]{1,0:T(8,128)(2,1)S(1)} %get-tuple-element.16.refs_1_, ...), custom_call_target="tpu_custom_call" | custom-call | flops 2147483648 | bytes 2097152 | tf_op jit(solution)/shard_map/pair_sums/pallas_call | solution.py:152
  63.6 0.0 collective-permute-done.11.refs_5_
  63.6 0.0 collective-permute-done.13.refs_7_
  63.6 0.0 collective-permute-done.10.refs_2_
  63.6 0.0 collective-permute-done.12.refs_6_
  63.6 3.7 %pair_sums.3 = (bf16[512,1024]{1,0:T(8,128)(2,1)}, f32[3,512]{1,0:T(4,128)S(1)}, f32[1,512]{1,0:T(1,128)S(1)}) custom-call(bf16[512,1024]{1,0:T(8,128)(2,1)S(1)} %get-tuple-element.19.refs_0_, bf16[512,1024]{1,0:T(8,128)(2,1)S(1)} %get-tuple-element.20.refs_1_, bf16[512,1024]{1,0:T(8,128)(2,1)S(1)} %collective-permute-done.10.refs_2_, ...), custom_call_target="tpu_custom_call" | custom-call | flops 1610612736 | bytes 2097152 | tf_op jit(solution)/shard_map/pair_sums/pallas_call | solution.py:152
  67.3 0.4 collective-permute-start.14
  67.7 2.6 %collective-permute-start.17 = (f32[1,512]{1,0:T(1,128)S(1)}, f32[1,512]{1,0:T(1,128)S(1)}, u32[]{:S(2)}, u32[]{:S(2)}) collective-permute-start(f32[1,512]{1,0:T(1,128)S(1)} %get-tuple-element.25), channel_id=1, source_target_pairs={{0,6},{1,7},{4,2},{5,3},{8,0},{9,1},{12,4},{13,5},{14,8},{15,9},{1... | collective-permute-start | bytes 6152 | tf_op jit(solution)/shard_map/ppermute | solution.py:183
  70.3 0.0 collective-permute-start.8
  70.3 0.3 collective-permute-start.16
  70.6 0.6 collective-permute-start.9
  71.1 0.0 collective-permute-done.14
  71.2 1.5 %collective-permute-start.15 = (f32[1,512]{1,0:T(1,128)S(1)}, f32[1,512]{1,0:T(1,128)S(1)}, u32[]{:S(2)}, u32[]{:S(2)}) collective-permute-start(f32[1,512]{1,0:T(1,128)S(1)} %add_add_fusion), channel_id=1, source_target_pairs={{0,2},{1,3},{4,0},{5,1},{8,4},{9,5},{12,8},{13,9},{14,12},{15,13},... | collective-permute-start | bytes 6152 | tf_op jit(solution)/shard_map/ppermute | solution.py:183
  72.7 0.0 collective-permute-done.17
  72.7 0.0 collective-permute-done.8
  72.7 1.5 %collective-permute-done.16 = f32[1,512]{1,0:T(1,128)S(1)} collective-permute-done((f32[1,512]{1,0:T(1,128)S(1)}, f32[1,512]{1,0:T(1,128)S(1)}, u32[]{:S(2)}, u32[]{:S(2)}) %collective-permute-start.16) | collective-permute-done | bytes 2080 | tf_op jit(solution)/shard_map/ppermute | solution.py:232
  74.2 0.0 collective-permute-done.9
  74.2 0.6 collective-permute-done.15
  74.8 0.6 add_log-plus-one_fusion
  (3 shorter events, 0.0 us)
Async XLA Ops:
  0.0 28.2 %copy-start.2 = (s32[16]{0:T(128)S(1)}, s32[16]{0:T(128)}, u32[]{:S(2)}) copy-start(s32[16]{0:T(128)} %param.5) | copy-start | bytes 196
  0.0 26.3 %collective-permute-start.2 = (bf16[512,1024]{1,0:T(8,128)(2,1)}, bf16[512,1024]{1,0:T(8,128)(2,1)S(1)}, u32[]{:S(2)}, u32[]{:S(2)}) collective-permute-start(bf16[512,1024]{1,0:T(8,128)(2,1)} %mine.1), channel_id=1, source_target_pairs={{0,4},{1,5},{4,8},{5,9},{8,12},{9,13},{12,14},{13,15},{14,10},{15,... | collective-permute-start | bytes 3145736 | tf_op jit(solution)/shard_map/ppermute | solution.py:183
  3.0 25.1 %collective-permute-start.6 = (bf16[512,1024]{1,0:T(8,128)(2,1)}, bf16[512,1024]{1,0:T(8,128)(2,1)S(1)}, u32[]{:S(2)}, u32[]{:S(2)}) collective-permute-start(bf16[512,1024]{1,0:T(8,128)(2,1)} %mine.1), channel_id=1, source_target_pairs={{0,2},{1,3},{4,0},{5,1},{8,4},{9,5},{12,8},{13,9},{14,12},{15,13},... | collective-permute-start | bytes 3145736 | tf_op jit(solution)/shard_map/ppermute | solution.py:183
  3.0 50.7 %collective-permute-start = (bf16[512,1024]{1,0:T(8,128)(2,1)}, bf16[512,1024]{1,0:T(8,128)(2,1)S(1)}, u32[]{:S(2)}, u32[]{:S(2)}) collective-permute-start(bf16[512,1024]{1,0:T(8,128)(2,1)} %mine.1), channel_id=1, source_target_pairs={{0,1},{1,0},{2,3},{3,2},{4,5},{5,4},{6,7},{7,6},{8,9},{9,8},{10,11... | collective-permute-start | bytes 3145736 | tf_op jit(solution)/shard_map/ppermute | solution.py:186
  26.3 32.8 %collective-permute-start.3 = (bf16[512,1024]{1,0:T(8,128)(2,1)S(1)}, bf16[512,1024]{1,0:T(8,128)(2,1)S(1)}, u32[]{:S(2)}, u32[]{:S(2)}) collective-permute-start(bf16[512,1024]{1,0:T(8,128)(2,1)S(1)} %collective-permute-done.2.refs_2_), channel_id=1, source_target_pairs={{0,1},{1,0},{2,3},{3,2},{4,5},{5,4},{6,7},{7,6},{8,9},{9,8},{10,11... | collective-permute-start | bytes 3145736 | tf_op jit(solution)/shard_map/ppermute | solution.py:186
  26.3 37.3 %collective-permute-start.10 = (bf16[512,1024]{1,0:T(8,128)(2,1)S(1)}, bf16[512,1024]{1,0:T(8,128)(2,1)S(1)}, u32[]{:S(2)}, u32[]{:S(2)}) collective-permute-start(bf16[512,1024]{1,0:T(8,128)(2,1)S(1)} %collective-permute-done.2.refs_2_), channel_id=1, source_target_pairs={{0,4},{1,5},{4,8},{5,9},{8,12},{9,13},{12,14},{13,15},{14,10},{15,... | collective-permute-start | bytes 3145736 | tf_op jit(solution)/shard_map/ppermute | solution.py:183
  28.1 35.5 %collective-permute-start.12 = (bf16[512,1024]{1,0:T(8,128)(2,1)S(1)}, bf16[512,1024]{1,0:T(8,128)(2,1)S(1)}, u32[]{:S(2)}, u32[]{:S(2)}) collective-permute-start(bf16[512,1024]{1,0:T(8,128)(2,1)S(1)} %collective-permute-done.6.refs_8_), channel_id=1, source_target_pairs={{0,3},{1,2},{4,0},{5,1},{8,4},{9,5},{12,8},{13,9},{14,12},{15,13},... | collective-permute-start | bytes 3145736 | tf_op jit(solution)/shard_map/ppermute | solution.py:183
  28.2 0.8 %copy-start.1 = (s32[512,1]{0,1:T(1,128)S(1)}, s32[512,1]{0,1:T(1,128)}, u32[]{:S(2)}) copy-start(s32[512,1]{0,1:T(1,128)} %param.4) | copy-start | bytes 6148
  29.1 1.2 %collective-permute-start.1 = (s32[1,512]{1,0:T(1,128)S(1)}, s32[1,512]{1,0:T(1,128)S(1)}, u32[]{:S(2)}, u32[]{:S(2)}) collective-permute-start(s32[1,512]{1,0:T(1,128)S(1)} %bitcast_add_fusion.mine_code.refs_4_), channel_id=1, source_target_pairs={{0,1},{1,0},{2,3},{3,2},{4,5},{5,4},{6,7},{7,6},{8,9},{9,8},{10,11... | collective-permute-start | bytes 6152 | tf_op jit(solution)/shard_map/ppermute | solution.py:186
  30.3 21.7 %collective-permute-start.4 = (s32[1,512]{1,0:T(1,128)S(1)}, s32[1,512]{1,0:T(1,128)S(1)}, u32[]{:S(2)}, u32[]{:S(2)}) collective-permute-start(s32[1,512]{1,0:T(1,128)S(1)} %bitcast_add_fusion.mine_code.refs_4_), channel_id=1, source_target_pairs={{0,4},{1,5},{4,8},{5,9},{8,12},{9,13},{12,14},{13,15},{14,10},{15,... | collective-permute-start | bytes 6152 | tf_op jit(solution)/shard_map/ppermute | solution.py:183
  52.0 5.2 %collective-permute-start.7 = (s32[1,512]{1,0:T(1,128)S(1)}, s32[1,512]{1,0:T(1,128)S(1)}, u32[]{:S(2)}, u32[]{:S(2)}) collective-permute-start(s32[1,512]{1,0:T(1,128)S(1)} %bitcast_add_fusion.mine_code.refs_4_), channel_id=1, source_target_pairs={{0,2},{1,3},{4,0},{5,1},{8,4},{9,5},{12,8},{13,9},{14,12},{15,13},... | collective-permute-start | bytes 6152 | tf_op jit(solution)/shard_map/ppermute | solution.py:183
  53.7 3.8 %collective-permute-start.5 = (s32[1,512]{1,0:T(1,128)S(1)}, s32[1,512]{1,0:T(1,128)S(1)}, u32[]{:S(2)}, u32[]{:S(2)}) collective-permute-start(s32[1,512]{1,0:T(1,128)S(1)} %collective-permute-done.4.refs_6_.refs_3_), channel_id=1, source_target_pairs={{0,1},{1,0},{2,3},{3,2},{4,5},{5,4},{6,7},{7,6},{8,9},{9,8},{10,11... | collective-permute-start | bytes 6152 | tf_op jit(solution)/shard_map/ppermute | solution.py:186
  53.7 1.2 %copy-start = (bf16[512,1024]{1,0:T(8,128)(2,1)S(1)}, bf16[512,1024]{1,0:T(8,128)(2,1)}, u32[]{:S(2)}) copy-start(bf16[512,1024]{1,0:T(8,128)(2,1)} %mine.1) | copy-start | bytes 3145732
  57.2 6.4 %collective-permute-start.11 = (s32[1,512]{1,0:T(1,128)S(1)}, s32[1,512]{1,0:T(1,128)S(1)}, u32[]{:S(2)}, u32[]{:S(2)}) collective-permute-start(s32[1,512]{1,0:T(1,128)S(1)} %collective-permute-done.4.refs_6_.refs_3_), channel_id=1, source_target_pairs={{0,4},{1,5},{4,8},{5,9},{8,12},{9,13},{12,14},{13,15},{14,10},{15,... | collective-permute-start | bytes 6152 | tf_op jit(solution)/shard_map/ppermute | solution.py:183
  57.5 6.1 %collective-permute-start.13 = (s32[1,512]{1,0:T(1,128)S(1)}, s32[1,512]{1,0:T(1,128)S(1)}, u32[]{:S(2)}, u32[]{:S(2)}) collective-permute-start(s32[1,512]{1,0:T(1,128)S(1)} %collective-permute-done.7.refs_9_), channel_id=1, source_target_pairs={{0,3},{1,2},{4,0},{5,1},{8,4},{9,5},{12,8},{13,9},{14,12},{15,13},... | collective-permute-start | bytes 6152 | tf_op jit(solution)/shard_map/ppermute | solution.py:183
  67.3 3.8 %collective-permute-start.14 = (f32[1,512]{1,0:T(1,128)S(1)}, f32[1,512]{1,0:T(1,128)S(1)}, u32[]{:S(2)}, u32[]{:S(2)}) collective-permute-start(f32[1,512]{1,0:T(1,128)S(1)} %get-tuple-element.24), channel_id=1, source_target_pairs={{0,1},{1,0},{2,3},{3,2},{4,5},{5,4},{6,7},{7,6},{8,9},{9,8},{10,11... | collective-permute-start | bytes 6152 | tf_op jit(solution)/shard_map/ppermute | solution.py:186
  67.7 5.0 %collective-permute-start.17 = (f32[1,512]{1,0:T(1,128)S(1)}, f32[1,512]{1,0:T(1,128)S(1)}, u32[]{:S(2)}, u32[]{:S(2)}) collective-permute-start(f32[1,512]{1,0:T(1,128)S(1)} %get-tuple-element.25), channel_id=1, source_target_pairs={{0,6},{1,7},{4,2},{5,3},{8,0},{9,1},{12,4},{13,5},{14,8},{15,9},{1... | collective-permute-start | bytes 6152 | tf_op jit(solution)/shard_map/ppermute | solution.py:183
  70.3 2.4 %collective-permute-start.8 = (f32[1,512]{1,0:T(1,128)S(1)}, f32[1,512]{1,0:T(1,128)S(1)}, u32[]{:S(2)}, u32[]{:S(2)}) collective-permute-start(f32[1,512]{1,0:T(1,128)S(1)} %get-tuple-element.23), channel_id=1, source_target_pairs={{0,1},{1,0},{2,3},{3,2},{4,5},{5,4},{6,7},{7,6},{8,9},{9,8},{10,11... | collective-permute-start | bytes 6152 | tf_op jit(solution)/shard_map/ppermute | solution.py:186
  70.3 3.9 %collective-permute-start.16 = (f32[1,512]{1,0:T(1,128)S(1)}, f32[1,512]{1,0:T(1,128)S(1)}, u32[]{:S(2)}, u32[]{:S(2)}) collective-permute-start(f32[1,512]{1,0:T(1,128)S(1)} %get-tuple-element.22), channel_id=1, source_target_pairs={{0,8},{1,9},{4,12},{5,13},{8,14},{9,15},{12,10},{13,11},{14,7},{15... | collective-permute-start | bytes 6152 | tf_op jit(solution)/shard_map/ppermute | solution.py:232
  70.6 3.6 %collective-permute-start.9 = (f32[1,512]{1,0:T(1,128)S(1)}, f32[1,512]{1,0:T(1,128)S(1)}, u32[]{:S(2)}, u32[]{:S(2)}) collective-permute-start(f32[1,512]{1,0:T(1,128)S(1)} %get-tuple-element.18), channel_id=1, source_target_pairs={{0,4},{1,5},{4,8},{5,9},{8,12},{9,13},{12,14},{13,15},{14,10},{15,... | collective-permute-start | bytes 6152 | tf_op jit(solution)/shard_map/ppermute | solution.py:183
  71.2 3.6 %collective-permute-start.15 = (f32[1,512]{1,0:T(1,128)S(1)}, f32[1,512]{1,0:T(1,128)S(1)}, u32[]{:S(2)}, u32[]{:S(2)}) collective-permute-start(f32[1,512]{1,0:T(1,128)S(1)} %add_add_fusion), channel_id=1, source_target_pairs={{0,2},{1,3},{4,0},{5,1},{8,4},{9,5},{12,8},{13,9},{14,12},{15,13},... | collective-permute-start | bytes 6152 | tf_op jit(solution)/shard_map/ppermute | solution.py:183

commit v2 on v1

v2 whole, which is shorter than its diff:
```python
import functools

import jax
import jax.numpy as jnp
from jax import lax
from jax.experimental import pallas as pl
from jax.experimental.pallas import tpu as pltpu
from jax.sharding import PartitionSpec as P

STRIP = 256
META = 16


def unit_rows(values):
    values = values.astype(jnp.float32)
    width = values.shape[-1]
    scale = lax.rsqrt(jnp.mean(values * values, axis=-1, keepdims=True) + 1e-06) / jnp.sqrt(
        jnp.float32(width)
    )
    return (values * scale).astype(jnp.bfloat16)


def decode(code, clusters):
    own = code // 2
    near = code - 2 * own
    nearest = own + 2 * near - 1
    nearest = jnp.where(nearest < 0, nearest + clusters, nearest)
    nearest = jnp.where(nearest >= clusters, nearest - clusters, nearest)
    return own, nearest


def as_column(row):
    return jnp.transpose(jnp.broadcast_to(row, (128, row.shape[1])))


def terms(a_unit, b_unit, a_own, a_near, b_own, b_near):
    sim = lax.dot_general(
        a_unit, b_unit, (((1,), (1,)), ((), ())), preferred_element_type=jnp.float32
    )
    value = jnp.exp(16.0 * sim)
    wide = value.shape[1] // 128
    a_own, a_near = jnp.tile(a_own, (1, wide)), jnp.tile(a_near, (1, wide))
    near = jnp.where(a_near == b_own, value, 0.0) + jnp.where(a_own == b_near, value, 0.0)
    return jnp.where(a_own == b_own, value, 0.0) + 0.5 * near


def lanes_added(x):
    out = x[:, :128]
    for at in range(128, x.shape[1], 128):
        out = out + x[:, at : at + 128]
    return out


def as_row(x):
    return jnp.sum(jnp.transpose(x), axis=0, keepdims=True)


def codes_of(ref, clusters):
    rows = ref.shape[0] - META
    code = ref[rows:, :rows].astype(jnp.float32)[:1].astype(jnp.int32)
    return decode(code, clusters)


def pack_kernel(clusters, embed, owner, near, out, held, sems):
    rows = embed.shape[0]
    copies = []
    for i, at in enumerate(range(0, rows, STRIP // 2)):
        part = pl.ds(at, STRIP // 2)
        copies.append(pltpu.make_async_copy(embed.at[part], held.at[part], sems.at[i]))
        copies[-1].start()
    own = owner[...]
    near_own = jnp.zeros_like(own)
    for name in range(clusters):
        near_own = jnp.where(own == name, near[name], near_own)
    code = (2 * own + near_own).astype(jnp.float32)
    out[rows:, :] = jnp.zeros((META, out.shape[1]), jnp.bfloat16)
    out[rows:, :rows] = jnp.broadcast_to(code, (META, rows)).astype(jnp.bfloat16)
    for i, at in enumerate(range(0, rows, STRIP // 2)):
        copies[i].wait()
        out[at : at + STRIP // 2, :] = unit_rows(held[at : at + STRIP // 2, :])


def own_kernel(clusters, mine, other, sums):
    rows = mine.shape[0] - META
    a_own, a_near = [as_column(v) for v in codes_of(mine, clusters)]
    strips = []
    for at in range(0, rows, STRIP):
        total = jnp.zeros((STRIP, 128), jnp.float32)
        for same, block in ((True, mine), (False, other)):
            b_own, b_near = codes_of(block, clusters)
            value = terms(
                mine[at : at + STRIP, :],
                block[:rows, :],
                a_own[at : at + STRIP],
                a_near[at : at + STRIP],
                b_own,
                b_near,
            )
            if same:
                place = lax.broadcasted_iota(jnp.int32, value.shape, 0) + at
                value = jnp.where(
                    place == lax.broadcasted_iota(jnp.int32, value.shape, 1), 0.0, value
                )
            total = total + lanes_added(value)
        strips.append(as_row(total))
    sums[...] = jnp.concatenate(strips, axis=1)


def pair_kernel(clusters, blocks, *refs):
    a_blocks, b, a_sums, b_sums = refs[:blocks], refs[blocks], refs[-2], refs[-1]
    b_own, b_near = codes_of(b, clusters)
    rows = b.shape[0] - META
    b_total = jnp.zeros((8, rows), jnp.float32)
    for number, block in enumerate(a_blocks):
        a_own, a_near = [as_column(v) for v in codes_of(block, clusters)]
        for at in range(0, rows, STRIP):
            value = terms(
                block[at : at + STRIP, :],
                b[:rows, :],
                a_own[at : at + STRIP],
                a_near[at : at + STRIP],
                b_own,
                b_near,
            )
            a_sums[number : number + 1, at : at + STRIP] = as_row(lanes_added(value))
            b_total = b_total + jnp.sum(value.reshape(STRIP // 8, 8, rows), axis=0)
    b_sums[...] = jnp.sum(b_total, axis=0, keepdims=True)


def vmem(count):
    return [pl.BlockSpec(memory_space=pltpu.VMEM)] * count


def cost(tiles, rows, width):
    return pl.CostEstimate(
        flops=2 * tiles * rows * rows * width,
        bytes_accessed=4 * rows * width,
        transcendentals=tiles * rows * rows,
    )


def packed(clusters, embed, owner, near):
    rows, width = embed.shape
    return pl.pallas_call(
        functools.partial(pack_kernel, clusters),
        out_shape=jax.ShapeDtypeStruct((rows + META, width), jnp.bfloat16),
        in_specs=[
            pl.BlockSpec(memory_space=pl.ANY),
            pl.BlockSpec(memory_space=pltpu.VMEM),
            pl.BlockSpec(memory_space=pltpu.SMEM),
        ],
        out_specs=pl.BlockSpec(memory_space=pltpu.VMEM),
        scratch_shapes=[
            pltpu.VMEM((rows, width), jnp.bfloat16),
            pltpu.SemaphoreType.DMA((2 * rows // STRIP,)),
        ],
        compiler_params=pltpu.CompilerParams(vmem_limit_bytes=40 << 20),
        cost_estimate=cost(0, rows, width),
        name="packed",
    )(embed, owner, near)


def own_terms(clusters, mine, other):
    rows, width = mine.shape[0] - META, mine.shape[1]
    return pl.pallas_call(
        functools.partial(own_kernel, clusters),
        out_shape=jax.ShapeDtypeStruct((1, rows), jnp.float32),
        in_specs=vmem(2),
        out_specs=pl.BlockSpec(memory_space=pltpu.VMEM),
        compiler_params=pltpu.CompilerParams(vmem_limit_bytes=40 << 20),
        cost_estimate=cost(2, rows, width),
        name="own_terms",
    )(mine, other)


def pair_sums(clusters, a_blocks, b):
    rows, width = b.shape[0] - META, b.shape[1]
    blocks = len(a_blocks)
    a_sums, b_sums = pl.pallas_call(
        functools.partial(pair_kernel, clusters, blocks),
        out_shape=(
            jax.ShapeDtypeStruct((blocks, rows), jnp.float32),
            jax.ShapeDtypeStruct((1, rows), jnp.float32),
        ),
        in_specs=vmem(blocks + 1),
        out_specs=vmem(2),
        compiler_params=pltpu.CompilerParams(vmem_limit_bytes=40 << 20),
        cost_estimate=cost(blocks, rows, width),
        name="pair_sums",
    )(*a_blocks, b)
    return [a_sums[i : i + 1] for i in range(blocks)], b_sums


def per_device(embed, owner, near):
    rows = embed.shape[0]
    clusters = near.shape[0]
    chips = lax.axis_size("blk") // 2
    hops = chips // 4
    order = list(range(0, chips, 2)) + list(range(chips - 1, 0, -2))

    def along(block, distance, crossed=lambda place: 0):
        route = []
        for place in range(chips):
            there = (place + distance) % chips
            for core in range(2):
                route.append((2 * order[place] + core, 2 * order[there] + (core ^ crossed(there))))
        return lax.ppermute(block, "blk", route)

    def other_core(block):
        return lax.ppermute(block, "blk", [(i, i ^ 1) for i in range(2 * chips)])

    def late(place):
        return int(place >= chips // 2)

    block = packed(clusters, embed, owner.reshape(1, rows), near)
    behind, ahead = [block], [block]
    for hop in range(1, hops + 1):
        behind.append(along(behind[-1], 1))
        ahead.append(along(ahead[-1], -1, late if hop == hops else lambda place: 0))
    spare = [other_core(half) for half in behind[:hops]]

    total = own_terms(clusters, block, spare[0])
    inner, sums = [block, spare[0]], None
    for hop in range(1, hops + 1):
        outer = [behind[hop]] if hop == hops else [behind[hop], spare[hop]]
        a_sums, b_sums = pair_sums(clusters, inner + outer, ahead[hop])
        if sums is not None:
            a_sums[0], a_sums[1] = a_sums[0] + sums[0], a_sums[1] + sums[1]
        done = a_sums[0] + other_core(a_sums[1])
        total = total + (done if hop == 1 else along(done, 1 - hop))
        if hop < hops:
            total = total + along(b_sums, hop)
            inner, sums = outer, a_sums[2:]
            continue
        route = []
        for place in range(chips):
            there = (place + hop) % chips
            for core in range(2):
                route.append((2 * order[place] + core, 2 * order[there] + (core ^ late(place))))
        total = total + lax.ppermute(b_sums, "blk", route)
        total = total + along(a_sums[2], -hop)
    return jnp.log1p(total)[0]


def solution(mesh):
    return jax.shard_map(
        per_device,
        mesh=mesh,
        in_specs=(P(("groups", "blk"), None), P(("groups", "blk"), None), P("groups")),
        out_specs=P(("groups", "blk")),
        check_vma=False,
    )
```

time: 75.6 us -> 69.5 us (0.919)
  starting transfers between devices: 16.2 us -> 10.5 us
  local copies, waits for them, and re-layouts: 1.23 us -> 2.56 us
  other arithmetic: 1.46 us -> 0.61 us
    ppermute x11 -> x7, starting transfers between devices: 15.2 us -> 8.6 us  [along(): return lax.ppermute(block, 'blk', route)]
    ppermute x11 -> x7, waiting for transfers between devices: 43.7 us -> 45.9 us  [along(): return lax.ppermute(block, 'blk', route)]
    ppermute x1, waiting for transfers between devices: 1.48 us -> 0.01 us  [per_device(): total = total + lax.ppermute(b_sums, 'blk', route)]
    unnamed x6, local copies, waits for them, and re-layouts: 1.23 us -> 2.56 us
    ppermute x1, starting transfers between devices: 0.33 us -> 1.63 us  [per_device(): total = total + lax.ppermute(b_sums, 'blk', route)]
    ppermute x6 -> x4, waiting for transfers between devices: 0.89 us -> 0.01 us  [other_core(): return lax.ppermute(block, 'blk', [(i, i ^ 1) for i in range(2 * chips)])]
    reduce_sum x1 -> x0, other arithmetic: 0.84 us -> none  [per_device(): jnp.sum(jnp.where(owned[None, :] == names[:, None], near[:, None], 0), ax...]
    pallas_call x3 -> x4, Pallas kernels: 10.4 us -> 9.66 us  [the longest x2 6.8 us: pair_sums(): pl.pallas_call(functools.partial(pair_kernel, clusters, blocks), out_shap...]
  transfers between devices with their start and end apart: 18 -> 12, of which waited for: 5 -> 5; matrix products, arithmetic and copies ran while one was open for 1% -> 0% of each run, Pallas kernels for 9% -> 8%
where the time goes in v2:
time: 69.5 us; the launch traced here: 69.3 us
  waiting for transfers between devices  46 us (66%)
  starting transfers between devices  10.5 us (15%)
  Pallas kernels  9.66 us (14%)
  local copies, waits for them, and re-layouts  2.56 us (4%)
    ppermute x7, waiting for transfers between devices, along(): return lax.ppermute(block, 'blk', route)  45.9 us
    ppermute x7, starting transfers between devices, along(): return lax.ppermute(block, 'blk', route)  8.6 us
    pallas_call x2, Pallas kernels, pair_sums(): pl.pallas_call(functools.partial(pair_kernel, clusters, blocks), out_shap...  6.8 us
    unnamed x6, local copies, waits for them, and re-layouts  2.56 us
    ppermute x1, starting transfers between devices, per_device(): total = total + lax.ppermute(b_sums, 'blk', route)  1.63 us
    pallas_call x1, Pallas kernels, own_terms(): pl.pallas_call(functools.partial(own_kernel, clusters), out_shape=jax.Sha...  1.62 us
  transfers between devices with their start and end apart: 12, of which 5 were waited for; matrix products, arithmetic and copies ran while one was open for 0% of the time, Pallas kernels for 8%

profile of v2, /device:TPU:0, one launch (start us, length us, event | category | flops | bytes accessed | tf_op | source)
XLA Modules:
  0.0 69.3 jit_solution(11514130776698844936)
XLA Ops:
  0.0 0.0 copy-start
  0.0 1.2 %copy-done = bf16[512,1024]{1,0:T(8,128)(2,1)S(1)} copy-done((bf16[512,1024]{1,0:T(8,128)(2,1)S(1)}, bf16[512,1024]{1,0:T(8,128)(2,1)}, u32[]{:S(2)}) %copy-start) | copy-done | bytes 1048600
  1.2 0.0 copy-start.1
  1.2 0.7 copy-done.1
  1.9 0.0 copy-start.2
  1.9 0.7 copy-done.2
  2.6 1.2 %packed.1.mine.refs_0_ = bf16[528,1024]{1,0:T(8,128)(2,1)S(1)} custom-call(bf16[512,1024]{1,0:T(8,128)(2,1)S(1)} %copy-done, s32[1,512]{1,0:T(1,128)S(1)} %bitcast.2, s32[16]{0:T(128)S(1)} %copy-done.2), custom_call_target="tpu_custom_call" | custom-call | bytes 2097152 | tf_op jit(solution)/shard_map/packed/pallas_call | solution.py:144
  3.8 3.1 %collective-permute-start.1 = (bf16[528,1024]{1,0:T(8,128)(2,1)S(1)}, bf16[528,1024]{1,0:T(8,128)(2,1)S(1)}, u32[]{:S(2)}, u32[]{:S(2)}) collective-permute-start(bf16[528,1024]{1,0:T(8,128)(2,1)S(1)} %packed.1.mine.refs_0_), channel_id=1, source_target_pairs={{0,4},{1,5},{4,8},{5,9},{8,12},{9,13},{12,14},{13,15},{14,10},{15,... | collective-permute-start | bytes 3244040 | tf_op jit(solution)/shard_map/ppermute | solution.py:207
  6.9 0.0 collective-permute-start.3
  6.9 0.0 collective-permute-start
  6.9 23.8 %collective-permute-done.1.refs_2_.refs_0_ = bf16[528,1024]{1,0:T(8,128)(2,1)S(1)} collective-permute-done((bf16[528,1024]{1,0:T(8,128)(2,1)S(1)}, bf16[528,1024]{1,0:T(8,128)(2,1)S(1)}, u32[]{:S(2)}, u32[]{:S(2)}) %collective-permute-start.1) | collective-permute-done | bytes 1081376 | tf_op jit(solution)/shard_map/ppermute | solution.py:207
  30.7 0.0 collective-permute-start.2
  30.7 1.5 %collective-permute-done.3.refs_4_ = bf16[528,1024]{1,0:T(8,128)(2,1)S(1)} collective-permute-done((bf16[528,1024]{1,0:T(8,128)(2,1)S(1)}, bf16[528,1024]{1,0:T(8,128)(2,1)S(1)}, u32[]{:S(2)}, u32[]{:S(2)}) %collective-permute-start.3) | collective-permute-done | bytes 1081376 | tf_op jit(solution)/shard_map/ppermute | solution.py:207
  32.2 0.3 collective-permute-start.7
  32.5 1.7 %collective-permute-start.6 = (bf16[528,1024]{1,0:T(8,128)(2,1)S(1)}, bf16[528,1024]{1,0:T(8,128)(2,1)S(1)}, u32[]{:S(2)}, u32[]{:S(2)}) collective-permute-start(bf16[528,1024]{1,0:T(8,128)(2,1)S(1)} %collective-permute-done.1.refs_2_.refs_0_), channel_id=1, source_target_pairs={{0,4},{1,5},{4,8},{5,9},{8,12},{9,13},{12,14},{13,15},{14,10},{15,... | collective-permute-start | bytes 3244040 | tf_op jit(solution)/shard_map/ppermute | solution.py:207
  34.2 0.0 collective-permute-done.other.refs_1_
  34.2 0.0 collective-permute-done.2.refs_3_.refs_1_
  34.2 3.9 %pair_sums.2 = (f32[4,512]{1,0:T(4,128)S(1)}, f32[1,512]{1,0:T(1,128)S(1)}) custom-call(bf16[528,1024]{1,0:T(8,128)(2,1)S(1)} %packed.1.mine.refs_0_, bf16[528,1024]{1,0:T(8,128)(2,1)S(1)} %collective-permute-done.other.refs_1_, bf16[528,1024]{1,0:T(8,128)(2,1)S(1)} %collective-permute-done.1.refs_2_.refs_0_, ...), custom_call_target="tpu_custom_call" | custom-call | flops 2147483648 | bytes 2097152 | tf_op jit(solution)/shard_map/pair_sums/pallas_call | solution.py:179
  38.1 18.9 %collective-permute-done.7.refs_3_ = bf16[528,1024]{1,0:T(8,128)(2,1)S(1)} collective-permute-done((bf16[528,1024]{1,0:T(8,128)(2,1)S(1)}, bf16[528,1024]{1,0:T(8,128)(2,1)S(1)}, u32[]{:S(2)}, u32[]{:S(2)}) %collective-permute-start.7) | collective-permute-done | bytes 1081376 | tf_op jit(solution)/shard_map/ppermute | solution.py:207
  57.0 1.4 %collective-permute-done.6.refs_2_ = bf16[528,1024]{1,0:T(8,128)(2,1)S(1)} collective-permute-done((bf16[528,1024]{1,0:T(8,128)(2,1)S(1)}, bf16[528,1024]{1,0:T(8,128)(2,1)S(1)}, u32[]{:S(2)}, u32[]{:S(2)}) %collective-permute-start.6) | collective-permute-done | bytes 1081376 | tf_op jit(solution)/shard_map/ppermute | solution.py:207
  58.4 2.9 %pair_sums.3 = (f32[3,512]{1,0:T(4,128)S(1)}, f32[1,512]{1,0:T(1,128)S(1)}) custom-call(bf16[528,1024]{1,0:T(8,128)(2,1)S(1)} %collective-permute-done.1.refs_2_.refs_0_, bf16[528,1024]{1,0:T(8,128)(2,1)S(1)} %collective-permute-done.2.refs_3_.refs_1_, bf16[528,1024]{1,0:T(8,128)(2,1)S(1)} %collective-permute-done.6.refs_2_, ...), custom_call_target="tpu_custom_call" | custom-call | flops 1610612736 | bytes 2097152 | tf_op jit(solution)/shard_map/pair_sums/pallas_call | solution.py:179
  61.3 0.1 collective-permute-start.8
  61.4 1.6 %collective-permute-start.10 = (f32[1,512]{1,0:T(1,128)S(1)}, f32[1,512]{1,0:T(1,128)S(1)}, u32[]{:S(2)}, u32[]{:S(2)}) collective-permute-start(f32[1,512]{1,0:T(1,128)S(1)} %get-tuple-element.12), channel_id=1, source_target_pairs={{0,8},{1,9},{4,12},{5,13},{8,14},{9,15},{12,10},{13,11},{14,7},{15... | collective-permute-start | bytes 6152 | tf_op jit(solution)/shard_map/ppermute | solution.py:240
  63.0 0.2 collective-permute-start.4
  63.2 1.4 %collective-permute-start.11 = (f32[1,512]{1,0:T(1,128)S(1)}, f32[1,512]{1,0:T(1,128)S(1)}, u32[]{:S(2)}, u32[]{:S(2)}) collective-permute-start(f32[1,512]{1,0:T(1,128)S(1)} %get-tuple-element.15), channel_id=1, source_target_pairs={{0,6},{1,7},{4,2},{5,3},{8,0},{9,1},{12,4},{13,5},{14,8},{15,9},{1... | collective-permute-start | bytes 6152 | tf_op jit(solution)/shard_map/ppermute | solution.py:207
  64.6 0.5 collective-permute-start.5
  65.1 0.0 collective-permute-done.8
  65.1 1.6 %collective-permute-start.9 = (f32[1,512]{1,0:T(1,128)S(1)}, f32[1,512]{1,0:T(1,128)S(1)}, u32[]{:S(2)}, u32[]{:S(2)}) collective-permute-start(f32[1,512]{1,0:T(1,128)S(1)} %add_add_fusion), channel_id=1, source_target_pairs={{0,2},{1,3},{4,0},{5,1},{8,4},{9,5},{12,8},{13,9},{14,12},{15,13},... | collective-permute-start | bytes 6152 | tf_op jit(solution)/shard_map/ppermute | solution.py:207
  66.7 1.6 %own_terms.1 = f32[1,512]{1,0:T(1,128)S(1)} custom-call(bf16[528,1024]{1,0:T(8,128)(2,1)S(1)} %packed.1.mine.refs_0_, bf16[528,1024]{1,0:T(8,128)(2,1)S(1)} %collective-permute-done.other.refs_1_), custom_call_target="tpu_custom_call" | custom-call | flops 1073741824 | bytes 2097152 | tf_op jit(solution)/shard_map/own_terms/pallas_call | solution.py:165
  68.3 0.0 collective-permute-done.10
  68.3 0.0 collective-permute-done.4
  68.4 0.0 collective-permute-done.11
  68.4 0.0 collective-permute-done.5
  68.4 0.3 collective-permute-done.9
  68.7 0.6 add_log-plus-one_fusion
  (2 shorter events, 0.0 us)
Async XLA Ops:
  0.0 1.2 %copy-start = (bf16[512,1024]{1,0:T(8,128)(2,1)S(1)}, bf16[512,1024]{1,0:T(8,128)(2,1)}, u32[]{:S(2)}) copy-start(bf16[512,1024]{1,0:T(8,128)(2,1)} %embed.1) | copy-start | bytes 3145732
  1.2 0.7 copy-start.1
  1.9 0.7 copy-start.2
  3.8 26.9 %collective-permute-start.1 = (bf16[528,1024]{1,0:T(8,128)(2,1)S(1)}, bf16[528,1024]{1,0:T(8,128)(2,1)S(1)}, u32[]{:S(2)}, u32[]{:S(2)}) collective-permute-start(bf16[528,1024]{1,0:T(8,128)(2,1)S(1)} %packed.1.mine.refs_0_), channel_id=1, source_target_pairs={{0,4},{1,5},{4,8},{5,9},{8,12},{9,13},{12,14},{13,15},{14,10},{15,... | collective-permute-start | bytes 3244040 | tf_op jit(solution)/shard_map/ppermute | solution.py:207
  6.9 25.3 %collective-permute-start.3 = (bf16[528,1024]{1,0:T(8,128)(2,1)S(1)}, bf16[528,1024]{1,0:T(8,128)(2,1)S(1)}, u32[]{:S(2)}, u32[]{:S(2)}) collective-permute-start(bf16[528,1024]{1,0:T(8,128)(2,1)S(1)} %packed.1.mine.refs_0_), channel_id=1, source_target_pairs={{0,2},{1,3},{4,0},{5,1},{8,4},{9,5},{12,8},{13,9},{14,12},{15,13},... | collective-permute-start | bytes 3244040 | tf_op jit(solution)/shard_map/ppermute | solution.py:207
  6.9 27.3 %collective-permute-start = (bf16[528,1024]{1,0:T(8,128)(2,1)S(1)}, bf16[528,1024]{1,0:T(8,128)(2,1)S(1)}, u32[]{:S(2)}, u32[]{:S(2)}) collective-permute-start(bf16[528,1024]{1,0:T(8,128)(2,1)S(1)} %packed.1.mine.refs_0_), channel_id=1, source_target_pairs={{0,1},{1,0},{2,3},{3,2},{4,5},{5,4},{6,7},{7,6},{8,9},{9,8},{10,11... | collective-permute-start | bytes 3244040 | tf_op jit(solution)/shard_map/ppermute | solution.py:210
  30.7 3.5 %collective-permute-start.2 = (bf16[528,1024]{1,0:T(8,128)(2,1)S(1)}, bf16[528,1024]{1,0:T(8,128)(2,1)S(1)}, u32[]{:S(2)}, u32[]{:S(2)}) collective-permute-start(bf16[528,1024]{1,0:T(8,128)(2,1)S(1)} %collective-permute-done.1.refs_2_.refs_0_), channel_id=1, source_target_pairs={{0,1},{1,0},{2,3},{3,2},{4,5},{5,4},{6,7},{7,6},{8,9},{9,8},{10,11... | collective-permute-start | bytes 3244040 | tf_op jit(solution)/shard_map/ppermute | solution.py:210
  32.2 24.8 %collective-permute-start.7 = (bf16[528,1024]{1,0:T(8,128)(2,1)S(1)}, bf16[528,1024]{1,0:T(8,128)(2,1)S(1)}, u32[]{:S(2)}, u32[]{:S(2)}) collective-permute-start(bf16[528,1024]{1,0:T(8,128)(2,1)S(1)} %collective-permute-done.3.refs_4_), channel_id=1, source_target_pairs={{0,3},{1,2},{4,0},{5,1},{8,4},{9,5},{12,8},{13,9},{14,12},{15,13},... | collective-permute-start | bytes 3244040 | tf_op jit(solution)/shard_map/ppermute | solution.py:207
  32.5 25.8 %collective-permute-start.6 = (bf16[528,1024]{1,0:T(8,128)(2,1)S(1)}, bf16[528,1024]{1,0:T(8,128)(2,1)S(1)}, u32[]{:S(2)}, u32[]{:S(2)}) collective-permute-start(bf16[528,1024]{1,0:T(8,128)(2,1)S(1)} %collective-permute-done.1.refs_2_.refs_0_), channel_id=1, source_target_pairs={{0,4},{1,5},{4,8},{5,9},{8,12},{9,13},{12,14},{13,15},{14,10},{15,... | collective-permute-start | bytes 3244040 | tf_op jit(solution)/shard_map/ppermute | solution.py:207
  61.3 3.7 %collective-permute-start.8 = (f32[1,512]{1,0:T(1,128)S(1)}, f32[1,512]{1,0:T(1,128)S(1)}, u32[]{:S(2)}, u32[]{:S(2)}) collective-permute-start(f32[1,512]{1,0:T(1,128)S(1)} %get-tuple-element.14), channel_id=1, source_target_pairs={{0,1},{1,0},{2,3},{3,2},{4,5},{5,4},{6,7},{7,6},{8,9},{9,8},{10,11... | collective-permute-start | bytes 6152 | tf_op jit(solution)/shard_map/ppermute | solution.py:210
  61.4 6.9 %collective-permute-start.10 = (f32[1,512]{1,0:T(1,128)S(1)}, f32[1,512]{1,0:T(1,128)S(1)}, u32[]{:S(2)}, u32[]{:S(2)}) collective-permute-start(f32[1,512]{1,0:T(1,128)S(1)} %get-tuple-element.12), channel_id=1, source_target_pairs={{0,8},{1,9},{4,12},{5,13},{8,14},{9,15},{12,10},{13,11},{14,7},{15... | collective-permute-start | bytes 6152 | tf_op jit(solution)/shard_map/ppermute | solution.py:240
  63.0 5.3 %collective-permute-start.4 = (f32[1,512]{1,0:T(1,128)S(1)}, f32[1,512]{1,0:T(1,128)S(1)}, u32[]{:S(2)}, u32[]{:S(2)}) collective-permute-start(f32[1,512]{1,0:T(1,128)S(1)} %get-tuple-element.13), channel_id=1, source_target_pairs={{0,1},{1,0},{2,3},{3,2},{4,5},{5,4},{6,7},{7,6},{8,9},{9,8},{10,11... | collective-permute-start | bytes 6152 | tf_op jit(solution)/shard_map/ppermute | solution.py:210
  63.2 5.2 %collective-permute-start.11 = (f32[1,512]{1,0:T(1,128)S(1)}, f32[1,512]{1,0:T(1,128)S(1)}, u32[]{:S(2)}, u32[]{:S(2)}) collective-permute-start(f32[1,512]{1,0:T(1,128)S(1)} %get-tuple-element.15), channel_id=1, source_target_pairs={{0,6},{1,7},{4,2},{5,3},{8,0},{9,1},{12,4},{13,5},{14,8},{15,9},{1... | collective-permute-start | bytes 6152 | tf_op jit(solution)/shard_map/ppermute | solution.py:207
  64.6 3.7 %collective-permute-start.5 = (f32[1,512]{1,0:T(1,128)S(1)}, f32[1,512]{1,0:T(1,128)S(1)}, u32[]{:S(2)}, u32[]{:S(2)}) collective-permute-start(f32[1,512]{1,0:T(1,128)S(1)} %get-tuple-element.10), channel_id=1, source_target_pairs={{0,4},{1,5},{4,8},{5,9},{8,12},{9,13},{12,14},{13,15},{14,10},{15,... | collective-permute-start | bytes 6152 | tf_op jit(solution)/shard_map/ppermute | solution.py:207
  65.1 3.6 %collective-permute-start.9 = (f32[1,512]{1,0:T(1,128)S(1)}, f32[1,512]{1,0:T(1,128)S(1)}, u32[]{:S(2)}, u32[]{:S(2)}) collective-permute-start(f32[1,512]{1,0:T(1,128)S(1)} %add_add_fusion), channel_id=1, source_target_pairs={{0,2},{1,3},{4,0},{5,1},{8,4},{9,5},{12,8},{13,9},{14,12},{15,13},... | collective-permute-start | bytes 6152 | tf_op jit(solution)/shard_map/ppermute | solution.py:207

commit v3 on v1

v3 whole, which is shorter than its diff:
```python
import functools

import jax
import jax.numpy as jnp
from jax import lax
from jax.experimental import pallas as pl
from jax.experimental.pallas import tpu as pltpu
from jax.sharding import PartitionSpec as P

STRIP = 256


def unit_rows(values):
    values = values.astype(jnp.float32)
    width = values.shape[-1]
    scale = lax.rsqrt(jnp.mean(values * values, axis=-1, keepdims=True) + 1e-06) / jnp.sqrt(
        jnp.float32(width)
    )
    return (values * scale).astype(jnp.bfloat16)


def as_column(row):
    return jnp.transpose(jnp.broadcast_to(row, (128, row.shape[1])))


def nearest(own, near, clusters):
    step = jnp.zeros_like(own)
    for name in range(clusters):
        step = jnp.where(own == name, 2 * near[name] - 1, step)
    other = own + step
    other = jnp.where(other < 0, other + clusters, other)
    return jnp.where(other >= clusters, other - clusters, other)


def terms(a_unit, b_unit, a_own, a_near, b_own, b_near):
    sim = lax.dot_general(
        a_unit, b_unit, (((1,), (1,)), ((), ())), preferred_element_type=jnp.float32
    )
    wide = sim.shape[1] // 128
    a_own, a_near = jnp.tile(a_own, (1, wide)), jnp.tile(a_near, (1, wide))
    near = jnp.where(a_near == b_own, 0.5, 0.0) + jnp.where(a_own == b_near, 0.5, 0.0)
    return jnp.where(a_own == b_own, 1.0, near) * jnp.exp(16.0 * sim)


def lanes_added(x):
    out = x[:, :128]
    for at in range(128, x.shape[1], 128):
        out = out + x[:, at : at + 128]
    return out


def as_row(x):
    return jnp.sum(jnp.transpose(x), axis=0, keepdims=True)


def normalise(source, target):
    for at in range(0, source.shape[0], STRIP):
        target[at : at + STRIP, :] = unit_rows(source[at : at + STRIP, :])


def codes(names, half, near, clusters):
    own = names[half : half + 1, :]
    return own, nearest(own, near, clusters)


def own_kernel(clusters, near, mine, other, names, mine_unit, other_unit, sums):
    normalise(mine, mine_unit)
    normalise(other, other_unit)
    a_own, a_near = [as_column(row) for row in codes(names, 0, near, clusters)]
    halves = [(unit, *codes(names, i, near, clusters)) for i, unit in enumerate((mine_unit, other_unit))]
    for at in range(0, mine.shape[0], STRIP):
        here = slice(at, at + STRIP)
        total = jnp.zeros((STRIP, 128), jnp.float32)
        for unit, b_own, b_near in halves:
            value = terms(mine_unit[here, :], unit[...], a_own[here], a_near[here], b_own, b_near)
            if unit is mine_unit:
                place = lax.broadcasted_iota(jnp.int32, value.shape, 0) + at
                same = place == lax.broadcasted_iota(jnp.int32, value.shape, 1)
                value = jnp.where(same, 0.0, value)
            total = total + lanes_added(value)
        sums[:, here] = as_row(total)


def pair_kernel(clusters, ready, raw, near, *refs):
    blocks = ready + raw
    a_rows, refs = refs[:blocks], refs[blocks:]
    inner, outer, b_rows, b_names, a_from = refs[:5]
    a_units = refs[5:-3]
    a_sums, b_sums, b_unit = refs[-3:]
    normalise(b_rows, b_unit)
    b_own, b_near = codes(b_names, 0, near, clusters)
    rows = b_rows.shape[0]
    b_total = jnp.zeros((8, rows), jnp.float32)
    for block in range(blocks):
        names, half = (inner, block) if block < ready else (outer, block - ready)
        a_own, a_near = [as_column(row) for row in codes(names, half, near, clusters)]
        unit = a_rows[block]
        if block >= ready:
            unit = a_units[block - ready]
            normalise(a_rows[block], unit)
        for at in range(0, rows, STRIP):
            here = slice(at, at + STRIP)
            value = terms(unit[here, :], b_unit[...], a_own[here], a_near[here], b_own, b_near)
            added = as_row(lanes_added(value))
            if block < a_from.shape[0]:
                added = added + a_from[block : block + 1, here]
            a_sums[block : block + 1, here] = added
            b_total = b_total + jnp.sum(value.reshape(STRIP // 8, 8, rows), axis=0)
    b_sums[...] = jnp.sum(b_total, axis=0, keepdims=True)


def vmem(count):
    return [pl.BlockSpec(memory_space=pltpu.VMEM)] * count


SMEM = pl.BlockSpec(memory_space=pltpu.SMEM)
PARAMS = pltpu.CompilerParams(vmem_limit_bytes=40 << 20)


def cost(tiles, rows, width):
    return pl.CostEstimate(
        flops=2 * tiles * rows * rows * width,
        bytes_accessed=4 * rows * width,
        transcendentals=tiles * rows * rows,
    )


def own_terms(near, mine, other, names):
    rows, width = mine.shape
    unit = jax.ShapeDtypeStruct((rows, width), jnp.bfloat16)
    return pl.pallas_call(
        functools.partial(own_kernel, near.shape[0]),
        out_shape=(unit, unit, jax.ShapeDtypeStruct((1, rows), jnp.float32)),
        in_specs=[SMEM] + vmem(3),
        out_specs=vmem(3),
        compiler_params=PARAMS,
        cost_estimate=cost(2, rows, width),
        name="own_terms",
    )(near, mine, other, names)


def pair_sums(near, ready, raw, inner, outer, b_rows, b_names, a_from):
    rows, width = b_rows.shape
    blocks = len(ready) + len(raw)
    unit = jax.ShapeDtypeStruct((rows, width), jnp.bfloat16)
    outs = pl.pallas_call(
        functools.partial(pair_kernel, near.shape[0], len(ready), len(raw)),
        out_shape=(unit,) * len(raw)
        + (
            jax.ShapeDtypeStruct((blocks, rows), jnp.float32),
            jax.ShapeDtypeStruct((1, rows), jnp.float32),
        ),
        in_specs=[SMEM] + vmem(blocks + 5),
        out_specs=vmem(len(raw) + 2),
        scratch_shapes=[pltpu.VMEM((rows, width), jnp.bfloat16)],
        compiler_params=PARAMS,
        cost_estimate=cost(blocks, rows, width),
        name="pair_sums",
    )(near, *ready, *raw, inner, outer, b_rows, b_names, a_from)
    return outs[: len(raw)], outs[-2], outs[-1]


def per_device(embed, owner, near):
    rows = embed.shape[0]
    chips = lax.axis_size("blk") // 2
    hops = chips // 4
    order = list(range(0, chips, 2)) + list(range(chips - 1, 0, -2))

    def sent(block, distance, crossed=lambda place: 0):
        route = []
        for place in range(chips):
            there = order[(place + distance) % chips]
            for core in range(2):
                route.append((2 * order[place] + core, 2 * there + (core ^ crossed(place))))
        return lax.ppermute(block, "blk", route)

    def other_core(block):
        return sent(block, 0, lambda place: 1)

    def late(place):
        return int(place % chips >= chips // 2)

    name = owner.reshape(1, rows)
    names = jnp.concatenate([name, other_core(name)], axis=0)
    behind, ahead, behind_names, ahead_names = [embed], [embed], [names], [names]
    for hop in range(1, hops + 1):
        if hop == 2:
            behind[1], ahead[1], behind_names[1], ahead_names[1] = lax.optimization_barrier(
                (behind[1], ahead[1], behind_names[1], ahead_names[1])
            )
        crossed = (lambda place: late(place - 1)) if hop == hops else (lambda place: 0)
        behind.append(sent(behind[-1], 1))
        ahead.append(sent(ahead[-1], -1, crossed))
        behind_names.append(sent(behind_names[-1], 1))
        ahead_names.append(sent(ahead_names[-1], -1, crossed))
    spare = [other_core(half) for half in behind[:hops]]

    unit, spare_unit, sums = own_terms(near, embed, spare[0], names)
    units, total = [unit, spare_unit], None
    for hop in range(1, hops + 1):
        last = hop == hops
        raw = [behind[hop]] if last else [behind[hop], spare[hop]]
        block = ahead[hop]
        if last and total is not None:
            block, total = lax.optimization_barrier((block, total))
        units, a_sums, b_sums = pair_sums(
            near, units, raw, behind_names[hop - 1], behind_names[hop], block, ahead_names[hop], sums
        )
        done = a_sums[0:1] + other_core(a_sums[1:2])
        total = done if hop == 1 else total + sent(done, 1 - hop)
        total = total + sent(b_sums, hop, late if last else (lambda place: 0))
        if last:
            total = total + sent(a_sums[2:3], -hop)
        sums = a_sums[2:]
    return jnp.log1p(total)[0]


def solution(mesh):
    return jax.shard_map(
        per_device,
        mesh=mesh,
        in_specs=(P(("groups", "blk"), None), P(("groups", "blk"), None), P("groups")),
        out_specs=P(("groups", "blk")),
        check_vma=False,
    )
```

time: 75.6 us -> 66.2 us (0.88)
  waiting for transfers between devices: 46 us -> 35.5 us
  Pallas kernels: 10.4 us -> 11.5 us
    ppermute x18 -> x17, waiting for transfers between devices: 46 us -> 35.5 us  [sent(): return lax.ppermute(block, 'blk', route)]
    pallas_call x3, Pallas kernels: 10.4 us -> 11.5 us  [the longest x2 8.5 us: pair_sums(): pl.pallas_call(functools.partial(pair_kernel, near.shape[0], len(ready),...]
    reduce_sum x1 -> x0, other arithmetic: 0.84 us -> none  [per_device(): jnp.sum(jnp.where(owned[None, :] == names[:, None], near[:, None], 0), ax...]
    ppermute x18 -> x17, starting transfers between devices: 16.2 us -> 16.3 us  [sent(): return lax.ppermute(block, 'blk', route)]
  transfers between devices with their start and end apart: 18 -> 17, of which waited for: 5 -> 6; matrix products, arithmetic and copies ran while one was open for 1% -> 1% of each run, Pallas kernels for 9% -> 12%
where the time goes in v3:
time: 66.2 us; the launch traced here: 66 us
  waiting for transfers between devices  35.5 us (54%)
  starting transfers between devices  16.3 us (25%)
  Pallas kernels  11.5 us (17%)
  other arithmetic  1.29 us (2%)
  local copies, waits for them, and re-layouts  1.24 us (2%)
    ppermute x17, waiting for transfers between devices, sent(): return lax.ppermute(block, 'blk', route)  35.5 us
    ppermute x17, starting transfers between devices, sent(): return lax.ppermute(block, 'blk', route)  16.3 us
    pallas_call x2, Pallas kernels, pair_sums(): pl.pallas_call(functools.partial(pair_kernel, near.shape[0], len(ready),...  8.5 us
    pallas_call x1, Pallas kernels, own_terms(): pl.pallas_call(functools.partial(own_kernel, near.shape[0]), out_shape=(u...  3.05 us
  transfers between devices with their start and end apart: 17, of which 6 were waited for; matrix products, arithmetic and copies ran while one was open for 1% of the time, Pallas kernels for 12%

profile of v3, /device:TPU:0, one launch (start us, length us, event | category | flops | bytes accessed | tf_op | source)
XLA Modules:
  0.0 66.0 jit_solution(1830960481759527367)
XLA Ops:
  0.0 3.0 %collective-permute-start = (bf16[512,1024]{1,0:T(8,128)(2,1)}, bf16[512,1024]{1,0:T(8,128)(2,1)S(1)}, u32[]{:S(2)}, u32[]{:S(2)}) collective-permute-start(bf16[512,1024]{1,0:T(8,128)(2,1)} %mine.1), channel_id=1, source_target_pairs={{0,4},{1,5},{4,8},{5,9},{8,12},{9,13},{12,14},{13,15},{14,10},{15,... | collective-permute-start | bytes 3145736 | tf_op jit(solution)/shard_map/ppermute | solution.py:175
  3.0 0.0 collective-permute-start.1
  3.0 0.0 copy-start.1
  3.0 0.0 collective-permute-start.2
  3.0 0.5 collective-permute-start.6
  3.5 0.9 %collective-permute-done.2 = s32[1,512]{1,0:T(1,128)S(1)} collective-permute-done((s32[1,512]{1,0:T(1,128)}, s32[1,512]{1,0:T(1,128)S(1)}, u32[]{:S(2)}, u32[]{:S(2)}) %collective-permute-start.2) | collective-permute-done | bytes 2080 | tf_op jit(solution)/shard_map/ppermute | solution.py:175
  4.4 0.7 %pad_add_fusion.names.refs_4_ = s32[2,512]{1,0:T(2,128)S(1)} fusion(s32[1,512]{1,0:T(1,128)S(1)} %collective-permute-done.2, s32[1,512]{1,0:T(1,128)} %bitcast.3), kind=kLoop, calls=%fused_computation | loop fusion | flops 1024 | bytes 8192 | tf_op jit(solution)/shard_map/concatenate | solution.py:184
  5.1 2.0 %collective-permute-start.3 = (s32[2,512]{1,0:T(2,128)S(1)}, s32[2,512]{1,0:T(2,128)S(1)}, u32[]{:S(2)}, u32[]{:S(2)}) collective-permute-start(s32[2,512]{1,0:T(2,128)S(1)} %pad_add_fusion.names.refs_4_), channel_id=1, source_target_pairs={{0,4},{1,5},{4,8},{5,9},{8,12},{9,13},{12,14},{13,15},{14,10},{15,... | collective-permute-start | bytes 12296 | tf_op jit(solution)/shard_map/ppermute | solution.py:175
  7.1 0.0 collective-permute-start.4
  7.1 19.3 %collective-permute-done.3.refs_5_.refs_3_ = s32[2,512]{1,0:T(2,128)S(1)} collective-permute-done((s32[2,512]{1,0:T(2,128)S(1)}, s32[2,512]{1,0:T(2,128)S(1)}, u32[]{:S(2)}, u32[]{:S(2)}) %collective-permute-start.3) | collective-permute-done | bytes 4128 | tf_op jit(solution)/shard_map/ppermute | solution.py:175
  26.4 1.5 %collective-permute-done.4.refs_7_ = s32[2,512]{1,0:T(2,128)S(1)} collective-permute-done((s32[2,512]{1,0:T(2,128)S(1)}, s32[2,512]{1,0:T(2,128)S(1)}, u32[]{:S(2)}, u32[]{:S(2)}) %collective-permute-start.4) | collective-permute-done | bytes 4128 | tf_op jit(solution)/shard_map/ppermute | solution.py:175
  27.9 0.0 collective-permute-done.refs_2_
  27.9 0.0 collective-permute-done.1.refs_6_
  27.9 0.0 collective-permute-start.7
  28.0 0.4 collective-permute-start.5
  28.4 1.6 %collective-permute-start.10 = (bf16[512,1024]{1,0:T(8,128)(2,1)S(1)}, bf16[512,1024]{1,0:T(8,128)(2,1)S(1)}, u32[]{:S(2)}, u32[]{:S(2)}) collective-permute-start(bf16[512,1024]{1,0:T(8,128)(2,1)S(1)} %collective-permute-done.refs_2_), channel_id=1, source_target_pairs={{0,4},{1,5},{4,8},{5,9},{8,12},{9,13},{12,14},{13,15},{14,10},{15,... | collective-permute-start | bytes 3145736 | tf_op jit(solution)/shard_map/ppermute | solution.py:175
  30.0 0.0 collective-permute-done.6.other
  30.0 0.0 copy-done.1
  30.0 0.0 copy-start
  30.0 1.2 %copy-done = bf16[512,1024]{1,0:T(8,128)(2,1)S(1)} copy-done((bf16[512,1024]{1,0:T(8,128)(2,1)S(1)}, bf16[512,1024]{1,0:T(8,128)(2,1)}, u32[]{:S(2)}) %copy-start) | copy-done | bytes 1048600
  31.3 3.0 %own_terms.1 = (bf16[512,1024]{1,0:T(8,128)(2,1)S(1)}, bf16[512,1024]{1,0:T(8,128)(2,1)S(1)}, f32[1,512]{1,0:T(1,128)S(1)}) custom-call(s32[16]{0:T(128)S(1)} %copy-done.1, bf16[512,1024]{1,0:T(8,128)(2,1)S(1)} %copy-done, bf16[512,1024]{1,0:T(8,128)(2,1)S(1)} %collective-permute-done.6.other, s32[2,512]{1,0:T(2,128)S(1)} %pad_add_fusion.names.refs_4_), custom_call_target="tpu_custom_call" | custom-call | flops 1073741824 | bytes 2097152 | tf_op jit(solution)/shard_map/own_terms/pallas_call | solution.py:131
  34.3 0.0 collective-permute-done.7.refs_3_
  34.3 4.6 %pair_sums.2 = (bf16[512,1024]{1,0:T(8,128)(2,1)S(1)}, bf16[512,1024]{1,0:T(8,128)(2,1)S(1)}, f32[4,512]{1,0:T(4,128)S(1)}, f32[1,512]{1,0:T(1,128)S(1)}) custom-call(s32[16]{0:T(128)S(1)} %copy-done.1, bf16[512,1024]{1,0:T(8,128)(2,1)S(1)} %get-tuple-element.21.refs_0_, bf16[512,1024]{1,0:T(8,128)(2,1)S(1)} %get-tuple-element.22.refs_1_, ...), custom_call_target="tpu_custom_call" | custom-call | flops 2147483648 | bytes 2097152 | tf_op jit(solution)/shard_map/pair_sums/pallas_call | solution.py:146
  39.0 0.1 collective-permute-start.8
  39.1 1.6 %collective-permute-start.9 = (f32[1,512]{1,0:T(1,128)S(1)}, f32[1,512]{1,0:T(1,128)S(1)}, u32[]{:S(2)}, u32[]{:S(2)}) collective-permute-start(f32[1,512]{1,0:T(1,128)S(1)} %get-tuple-element.28), channel_id=1, source_target_pairs={{0,4},{1,5},{4,8},{5,9},{8,12},{9,13},{12,14},{13,15},{14,10},{15,... | collective-permute-start | bytes 6152 | tf_op jit(solution)/shard_map/ppermute | solution.py:175
  40.7 1.6 %collective-permute-start.11 = (s32[2,512]{1,0:T(2,128)S(1)}, s32[2,512]{1,0:T(2,128)S(1)}, u32[]{:S(2)}, u32[]{:S(2)}) collective-permute-start(s32[2,512]{1,0:T(2,128)S(1)} %collective-permute-done.3.refs_5_.refs_3_), channel_id=1, source_target_pairs={{0,4},{1,5},{4,8},{5,9},{8,12},{9,13},{12,14},{13,15},{14,10},{15,... | collective-permute-start | bytes 12296 | tf_op jit(solution)/shard_map/ppermute | solution.py:175
  42.3 0.0 collective-permute-done.8
  42.3 0.1 collective-permute-start.12
  42.3 11.3 %collective-permute-done.9 = f32[1,512]{1,0:T(1,128)S(1)} collective-permute-done((f32[1,512]{1,0:T(1,128)S(1)}, f32[1,512]{1,0:T(1,128)S(1)}, u32[]{:S(2)}, u32[]{:S(2)}) %collective-permute-start.9) | collective-permute-done | bytes 2080 | tf_op jit(solution)/shard_map/ppermute | solution.py:175
  53.6 0.0 collective-permute-done.5.refs_5_
  53.6 0.0 collective-permute-done.11.refs_4_
  53.7 0.0 collective-permute-done.12.refs_6_
  53.7 0.0 collective-permute-done.10.refs_2_
  53.7 3.9 %pair_sums.3 = (bf16[512,1024]{1,0:T(8,128)(2,1)}, f32[3,512]{1,0:T(4,128)S(1)}, f32[1,512]{1,0:T(1,128)S(1)}) custom-call(s32[16]{0:T(128)S(1)} %copy-done.1, bf16[512,1024]{1,0:T(8,128)(2,1)S(1)} %get-tuple-element.30.refs_0_, bf16[512,1024]{1,0:T(8,128)(2,1)S(1)} %get-tuple-element.31.refs_1_, bf16[512,1024]{1,0:T(8,128)(2,1)S(1)} %collective-permute-done.10.refs_2_, ...), custom_call_target="tpu_custom_call" | custom-call | flops 1610612736 | bytes 2097152 | tf_op jit(solution)/shard_map/pair_sums/pallas_call | solution.py:146
  57.5 0.0 collective-permute-start.13
  57.5 2.8 %collective-permute-start.15 = (f32[1,512]{1,0:T(1,128)S(1)}, f32[1,512]{1,0:T(1,128)S(1)}, u32[]{:S(2)}, u32[]{:S(2)}) collective-permute-start(f32[1,512]{1,0:T(1,128)S(1)} %get-tuple-element.34), channel_id=1, source_target_pairs={{0,8},{1,9},{4,12},{5,13},{8,14},{9,15},{12,10},{13,11},{14,7},{15... | collective-permute-start | bytes 6152 | tf_op jit(solution)/shard_map/ppermute | solution.py:175
  60.3 0.0 collective-permute-done.13
  60.4 0.6 collective-permute-start.14
  60.9 2.0 %collective-permute-start.16 = (f32[1,512]{1,0:T(1,128)S(1)}, f32[1,512]{1,0:T(1,128)S(1)}, u32[]{:S(2)}, u32[]{:S(2)}) collective-permute-start(f32[1,512]{1,0:T(1,128)S(1)} %get-tuple-element.36), channel_id=1, source_target_pairs={{0,6},{1,7},{4,2},{5,3},{8,0},{9,1},{12,4},{13,5},{14,8},{15,9},{1... | collective-permute-start | bytes 6152 | tf_op jit(solution)/shard_map/ppermute | solution.py:175
  62.9 0.0 collective-permute-done.15
  62.9 1.1 %collective-permute-done.14 = f32[1,512]{1,0:T(1,128)S(1)} collective-permute-done((f32[1,512]{1,0:T(1,128)S(1)}, f32[1,512]{1,0:T(1,128)S(1)}, u32[]{:S(2)}, u32[]{:S(2)}) %collective-permute-start.14) | collective-permute-done | bytes 2080 | tf_op jit(solution)/shard_map/ppermute | solution.py:175
  64.0 1.4 %collective-permute-done.16 = f32[1,512]{1,0:T(1,128)S(1)} collective-permute-done((f32[1,512]{1,0:T(1,128)S(1)}, f32[1,512]{1,0:T(1,128)S(1)}, u32[]{:S(2)}, u32[]{:S(2)}) %collective-permute-start.16) | collective-permute-done | bytes 2080 | tf_op jit(solution)/shard_map/ppermute | solution.py:175
  65.4 0.6 add_log-plus-one_fusion
  (5 shorter events, 0.0 us)
Async XLA Ops:
  0.0 27.9 %collective-permute-start = (bf16[512,1024]{1,0:T(8,128)(2,1)}, bf16[512,1024]{1,0:T(8,128)(2,1)S(1)}, u32[]{:S(2)}, u32[]{:S(2)}) collective-permute-start(bf16[512,1024]{1,0:T(8,128)(2,1)} %mine.1), channel_id=1, source_target_pairs={{0,4},{1,5},{4,8},{5,9},{8,12},{9,13},{12,14},{13,15},{14,10},{15,... | collective-permute-start | bytes 3145736 | tf_op jit(solution)/shard_map/ppermute | solution.py:175
  3.0 24.9 %collective-permute-start.1 = (bf16[512,1024]{1,0:T(8,128)(2,1)}, bf16[512,1024]{1,0:T(8,128)(2,1)S(1)}, u32[]{:S(2)}, u32[]{:S(2)}) collective-permute-start(bf16[512,1024]{1,0:T(8,128)(2,1)} %mine.1), channel_id=1, source_target_pairs={{0,2},{1,3},{4,0},{5,1},{8,4},{9,5},{12,8},{13,9},{14,12},{15,13},... | collective-permute-start | bytes 3145736 | tf_op jit(solution)/shard_map/ppermute | solution.py:175
  3.0 27.0 %copy-start.1 = (s32[16]{0:T(128)S(1)}, s32[16]{0:T(128)}, u32[]{:S(2)}) copy-start(s32[16]{0:T(128)} %near.5) | copy-start | bytes 196
  3.0 1.4 %collective-permute-start.2 = (s32[1,512]{1,0:T(1,128)}, s32[1,512]{1,0:T(1,128)S(1)}, u32[]{:S(2)}, u32[]{:S(2)}) collective-permute-start(s32[1,512]{1,0:T(1,128)} %bitcast.2), channel_id=1, source_target_pairs={{0,1},{1,0},{4,5},{5,4},{8,9},{9,8},{12,13},{13,12},{14,15},{15,14... | collective-permute-start | bytes 6152 | tf_op jit(solution)/shard_map/ppermute | solution.py:175
  3.0 27.0 %collective-permute-start.6 = (bf16[512,1024]{1,0:T(8,128)(2,1)}, bf16[512,1024]{1,0:T(8,128)(2,1)S(1)}, u32[]{:S(2)}, u32[]{:S(2)}) collective-permute-start(bf16[512,1024]{1,0:T(8,128)(2,1)} %mine.1), channel_id=1, source_target_pairs={{0,1},{1,0},{4,5},{5,4},{8,9},{9,8},{12,13},{13,12},{14,15},{15,14... | collective-permute-start | bytes 3145736 | tf_op jit(solution)/shard_map/ppermute | solution.py:175
  5.1 21.3 %collective-permute-start.3 = (s32[2,512]{1,0:T(2,128)S(1)}, s32[2,512]{1,0:T(2,128)S(1)}, u32[]{:S(2)}, u32[]{:S(2)}) collective-permute-start(s32[2,512]{1,0:T(2,128)S(1)} %pad_add_fusion.names.refs_4_), channel_id=1, source_target_pairs={{0,4},{1,5},{4,8},{5,9},{8,12},{9,13},{12,14},{13,15},{14,10},{15,... | collective-permute-start | bytes 12296 | tf_op jit(solution)/shard_map/ppermute | solution.py:175
  7.1 20.8 %collective-permute-start.4 = (s32[2,512]{1,0:T(2,128)S(1)}, s32[2,512]{1,0:T(2,128)S(1)}, u32[]{:S(2)}, u32[]{:S(2)}) collective-permute-start(s32[2,512]{1,0:T(2,128)S(1)} %pad_add_fusion.names.refs_4_), channel_id=1, source_target_pairs={{0,2},{1,3},{4,0},{5,1},{8,4},{9,5},{12,8},{13,9},{14,12},{15,13},... | collective-permute-start | bytes 12296 | tf_op jit(solution)/shard_map/ppermute | solution.py:175
  27.9 6.4 %collective-permute-start.7 = (bf16[512,1024]{1,0:T(8,128)(2,1)S(1)}, bf16[512,1024]{1,0:T(8,128)(2,1)S(1)}, u32[]{:S(2)}, u32[]{:S(2)}) collective-permute-start(bf16[512,1024]{1,0:T(8,128)(2,1)S(1)} %collective-permute-done.refs_2_), channel_id=1, source_target_pairs={{0,1},{1,0},{4,5},{5,4},{8,9},{9,8},{12,13},{13,12},{14,15},{15,14... | collective-permute-start | bytes 3145736 | tf_op jit(solution)/shard_map/ppermute | solution.py:175
  28.0 25.7 %collective-permute-start.5 = (bf16[512,1024]{1,0:T(8,128)(2,1)S(1)}, bf16[512,1024]{1,0:T(8,128)(2,1)S(1)}, u32[]{:S(2)}, u32[]{:S(2)}) collective-permute-start(bf16[512,1024]{1,0:T(8,128)(2,1)S(1)} %collective-permute-done.1.refs_6_), channel_id=1, source_target_pairs={{0,3},{1,2},{4,0},{5,1},{8,4},{9,5},{12,8},{13,9},{14,12},{15,13},... | collective-permute-start | bytes 3145736 | tf_op jit(solution)/shard_map/ppermute | solution.py:175
  28.4 25.3 %collective-permute-start.10 = (bf16[512,1024]{1,0:T(8,128)(2,1)S(1)}, bf16[512,1024]{1,0:T(8,128)(2,1)S(1)}, u32[]{:S(2)}, u32[]{:S(2)}) collective-permute-start(bf16[512,1024]{1,0:T(8,128)(2,1)S(1)} %collective-permute-done.refs_2_), channel_id=1, source_target_pairs={{0,4},{1,5},{4,8},{5,9},{8,12},{9,13},{12,14},{13,15},{14,10},{15,... | collective-permute-start | bytes 3145736 | tf_op jit(solution)/shard_map/ppermute | solution.py:175
  30.0 1.2 %copy-start = (bf16[512,1024]{1,0:T(8,128)(2,1)S(1)}, bf16[512,1024]{1,0:T(8,128)(2,1)}, u32[]{:S(2)}) copy-start(bf16[512,1024]{1,0:T(8,128)(2,1)} %mine.1) | copy-start | bytes 3145732
  39.0 3.3 %collective-permute-start.8 = (f32[1,512]{1,0:T(1,128)S(1)}, f32[1,512]{1,0:T(1,128)S(1)}, u32[]{:S(2)}, u32[]{:S(2)}) collective-permute-start(f32[1,512]{1,0:T(1,128)S(1)} %slice.19), channel_id=1, source_target_pairs={{0,1},{1,0},{4,5},{5,4},{8,9},{9,8},{12,13},{13,12},{14,15},{15,14... | collective-permute-start | bytes 6152 | tf_op jit(solution)/shard_map/ppermute | solution.py:175
  39.1 14.6 %collective-permute-start.9 = (f32[1,512]{1,0:T(1,128)S(1)}, f32[1,512]{1,0:T(1,128)S(1)}, u32[]{:S(2)}, u32[]{:S(2)}) collective-permute-start(f32[1,512]{1,0:T(1,128)S(1)} %get-tuple-element.28), channel_id=1, source_target_pairs={{0,4},{1,5},{4,8},{5,9},{8,12},{9,13},{12,14},{13,15},{14,10},{15,... | collective-permute-start | bytes 6152 | tf_op jit(solution)/shard_map/ppermute | solution.py:175
  40.7 13.0 %collective-permute-start.11 = (s32[2,512]{1,0:T(2,128)S(1)}, s32[2,512]{1,0:T(2,128)S(1)}, u32[]{:S(2)}, u32[]{:S(2)}) collective-permute-start(s32[2,512]{1,0:T(2,128)S(1)} %collective-permute-done.3.refs_5_.refs_3_), channel_id=1, source_target_pairs={{0,4},{1,5},{4,8},{5,9},{8,12},{9,13},{12,14},{13,15},{14,10},{15,... | collective-permute-start | bytes 12296 | tf_op jit(solution)/shard_map/ppermute | solution.py:175
  42.3 11.4 %collective-permute-start.12 = (s32[2,512]{1,0:T(2,128)S(1)}, s32[2,512]{1,0:T(2,128)S(1)}, u32[]{:S(2)}, u32[]{:S(2)}) collective-permute-start(s32[2,512]{1,0:T(2,128)S(1)} %collective-permute-done.4.refs_7_), channel_id=1, source_target_pairs={{0,3},{1,2},{4,0},{5,1},{8,4},{9,5},{12,8},{13,9},{14,12},{15,13},... | collective-permute-start | bytes 12296 | tf_op jit(solution)/shard_map/ppermute | solution.py:175
  57.5 2.8 %collective-permute-start.13 = (f32[1,512]{1,0:T(1,128)S(1)}, f32[1,512]{1,0:T(1,128)S(1)}, u32[]{:S(2)}, u32[]{:S(2)}) collective-permute-start(f32[1,512]{1,0:T(1,128)S(1)} %slice.22), channel_id=1, source_target_pairs={{0,1},{1,0},{4,5},{5,4},{8,9},{9,8},{12,13},{13,12},{14,15},{15,14... | collective-permute-start | bytes 6152 | tf_op jit(solution)/shard_map/ppermute | solution.py:175
  57.5 5.4 %collective-permute-start.15 = (f32[1,512]{1,0:T(1,128)S(1)}, f32[1,512]{1,0:T(1,128)S(1)}, u32[]{:S(2)}, u32[]{:S(2)}) collective-permute-start(f32[1,512]{1,0:T(1,128)S(1)} %get-tuple-element.34), channel_id=1, source_target_pairs={{0,8},{1,9},{4,12},{5,13},{8,14},{9,15},{12,10},{13,11},{14,7},{15... | collective-permute-start | bytes 6152 | tf_op jit(solution)/shard_map/ppermute | solution.py:175
  60.4 3.6 %collective-permute-start.14 = (f32[1,512]{1,0:T(1,128)S(1)}, f32[1,512]{1,0:T(1,128)S(1)}, u32[]{:S(2)}, u32[]{:S(2)}) collective-permute-start(f32[1,512]{1,0:T(1,128)S(1)} %get-tuple-element.35), channel_id=1, source_target_pairs={{0,2},{1,3},{4,0},{5,1},{8,4},{9,5},{12,8},{13,9},{14,12},{15,13},... | collective-permute-start | bytes 6152 | tf_op jit(solution)/shard_map/ppermute | solution.py:175
  60.9 4.5 %collective-permute-start.16 = (f32[1,512]{1,0:T(1,128)S(1)}, f32[1,512]{1,0:T(1,128)S(1)}, u32[]{:S(2)}, u32[]{:S(2)}) collective-permute-start(f32[1,512]{1,0:T(1,128)S(1)} %get-tuple-element.36), channel_id=1, source_target_pairs={{0,6},{1,7},{4,2},{5,3},{8,0},{9,1},{12,4},{13,5},{14,8},{15,9},{1... | collective-permute-start | bytes 6152 | tf_op jit(solution)/shard_map/ppermute | solution.py:175

commit v4 on v0

v4 whole, which is shorter than its diff:
```python
import functools

import jax
import jax.numpy as jnp
from jax import lax
from jax.experimental import pallas as pl
from jax.experimental.pallas import tpu as pltpu
from jax.sharding import PartitionSpec as P

STRIP = 256
SPLIT = 2
ROOM = 8


def unit_rows(values):
    values = values.astype(jnp.float32)
    width = values.shape[-1]
    scale = lax.rsqrt(jnp.mean(values * values, axis=-1, keepdims=True) + 1e-06) / jnp.sqrt(
        jnp.float32(width)
    )
    return (values * scale).astype(jnp.bfloat16)


def strips(rows):
    return [slice(at, min(at + STRIP, rows)) for at in range(0, rows, STRIP)]


def normalise(sources, target, raw=True):
    put = 0
    for source in sources:
        for here in strips(source.shape[0]):
            values = source[here, :]
            target[put + here.start : put + here.stop, :] = unit_rows(values) if raw else values
        put += source.shape[0]


def nearest(own, near, clusters):
    step = jnp.zeros_like(own)
    for name in range(clusters):
        step = jnp.where(own == name, 2 * near[name] - 1, step)
    other = own + step
    other = jnp.where(other < 0, other + clusters, other)
    return jnp.where(other >= clusters, other - clusters, other)


def as_column(row):
    return jnp.transpose(jnp.broadcast_to(row, (128, row.shape[1])))


def terms(a_unit, b_unit, a_own, a_near, b_own, b_near):
    sim = lax.dot_general(
        a_unit, b_unit, (((1,), (1,)), ((), ())), preferred_element_type=jnp.float32
    )
    wide = sim.shape[1] // 128
    a_own, a_near = jnp.tile(a_own, (1, wide)), jnp.tile(a_near, (1, wide))
    near = jnp.where(a_near == b_own, 0.5, 0.0) + jnp.where(a_own == b_near, 0.5, 0.0)
    return jnp.where(a_own == b_own, 1.0, near) * jnp.exp(16.0 * sim)


def lanes_added(x):
    out = x[:, :128]
    for at in range(128, x.shape[1], 128):
        out = out + x[:, at : at + 128]
    return out


def as_row(x):
    return jnp.sum(jnp.transpose(x), axis=0, keepdims=True)


def sums_kernel(clusters, blocks, lists, tasks, kept, near, *refs):
    units = []
    for pieces, *_ in blocks:
        units.append(refs[:pieces])
        refs = refs[pieces:]
    names, refs = refs[:lists], refs[lists:]
    before, sums, refs = (refs[0], refs[1], refs[2:]) if kept is None else (None, refs[0], refs[1:])
    kept = kept or ()
    given, scratch = refs[: len(kept)], list(refs[len(kept) :])
    codes = {}

    def code(block):
        if block not in codes:
            *_, at, row, place = blocks[block]
            own = names[at][row : row + 1, place : place + units[block].shape[0]]
            codes[block] = own, nearest(own, near, clusters)
        return codes[block]

    for block, (pieces, raw, *_) in enumerate(blocks):
        if raw or pieces > 1:
            target = given[kept.index(block)] if block in kept else scratch.pop(0)
            normalise(units[block], target, raw)
            units[block] = target
        else:
            (units[block],) = units[block]
    sums[...] = jnp.zeros_like(sums) if before is None else before[...]
    for task, (block, others) in enumerate(tasks):
        a_own, a_near = [as_column(row) for row in code(block)]
        place = blocks[block][-1]
        for here in strips(units[block].shape[0]):
            total = jnp.zeros((here.stop - here.start, 128), jnp.float32)
            for other in others:
                value = terms(
                    units[block][here, :], units[other][...], a_own[here], a_near[here], *code(other)
                )
                if other == block:
                    row = lax.broadcasted_iota(jnp.int32, value.shape, 0) + here.start
                    same = row == lax.broadcasted_iota(jnp.int32, value.shape, 1)
                    value = jnp.where(same, 0.0, value)
                total = total + lanes_added(value)
            sums[task : task + 1, place + here.start : place + here.stop] = as_row(total)


def row_sums(near, blocks, names, tasks, label, kept=(), before=None, room=0):
    blocks = [(block if isinstance(block, list) else [block], *rest) for block, *rest in blocks]
    width = blocks[0][0][0].shape[1]
    units = [
        jax.ShapeDtypeStruct((sum(piece.shape[0] for piece in block[0]), width), jnp.bfloat16)
        for block in blocks
    ]
    made = [i for i, block in enumerate(blocks) if block[1] or len(block[0]) > 1]
    scratch = [i for i in made if i not in kept]
    vmem = pl.BlockSpec(memory_space=pltpu.VMEM)
    operands = [piece for block in blocks for piece in block[0]] + names
    operands += [] if before is None else [before]
    sums, *given = pl.pallas_call(
        functools.partial(
            sums_kernel,
            near.shape[0],
            [(len(block[0]), *block[1:]) for block in blocks],
            len(names),
            tasks,
            kept if before is None else None,
        ),
        out_shape=[
            jax.ShapeDtypeStruct((max(len(tasks), room), names[0].shape[1]), jnp.float32),
            *[units[i] for i in kept],
        ],
        in_specs=[pl.BlockSpec(memory_space=pltpu.SMEM)] + [vmem] * len(operands),
        out_specs=[vmem] * (1 + len(kept)),
        scratch_shapes=[pltpu.VMEM(units[i].shape, jnp.bfloat16) for i in scratch],
        compiler_params=pltpu.CompilerParams(vmem_limit_bytes=40 << 20),
        cost_estimate=pl.CostEstimate(flops=0, bytes_accessed=0, transcendentals=0),
        name=label,
    )(near, *operands)
    return sums, given


def unit_block(rows):
    vmem = pl.BlockSpec(memory_space=pltpu.VMEM)
    return pl.pallas_call(
        lambda source, target: normalise([source], target),
        out_shape=jax.ShapeDtypeStruct(rows.shape, jnp.bfloat16),
        in_specs=[vmem],
        out_specs=vmem,
        compiler_params=pltpu.CompilerParams(vmem_limit_bytes=40 << 20),
        cost_estimate=pl.CostEstimate(flops=0, bytes_accessed=0, transcendentals=0),
        name="unit_rows",
    )(rows)


def per_device(embed, owner, near):
    rows = embed.shape[0]
    chips = lax.axis_size("blk") // 2
    hops = chips // 4
    order = list(range(0, chips, 2)) + list(range(chips - 1, 0, -2))

    def moved(block, target):
        route = []
        for place in range(chips):
            for core in range(2):
                there, to = target(place, core)
                route.append((2 * order[place] + core, 2 * order[there % chips] + to))
        return lax.ppermute(block, "blk", route)

    def other_core(block):
        return moved(block, lambda place, core: (place, 1 - core))

    def late(place):
        return int(place % chips >= chips // 2)

    def onward(distance):
        return lambda place, core: (place + distance * (1 - 2 * core), core)

    def first(half):
        def target(place, core):
            forward = core == late(place + hops) ^ half
            return (place + 1, 0) if forward else (place - 1, 1)

        return target

    def back(distance, half):
        def target(place, core):
            home = place - distance * (1 - 2 * core)
            return home, late(home + hops * (1 - 2 * core)) ^ half

        return target

    name = owner.reshape(1, rows)
    own_names = jnp.concatenate([name, other_core(name)], axis=0)
    swapped = lax.axis_index("blk") // 2 >= chips // 2
    sent_names = jnp.where(swapped, own_names[::-1], own_names)
    side_names = [own_names] + [moved(sent_names, onward(h)) for h in range(1, hops + 1)]
    side = [None, [moved(embed, first(half)) for half in range(2)]]
    total, own = row_sums(
        near,
        [(embed, True, 0, 0, 0), (other_core(embed), True, 0, 1, 0)],
        [own_names],
        ((0, (0, 1)),),
        "own_terms",
        (0,),
    )
    if hops > 1:
        side[1][0], total, side_names[1] = lax.optimization_barrier((side[1][0], total, side_names[1]))
    side[1][1] = unit_block(side[1][1])
    for hop in range(2, hops + 1):
        side.append([moved(half, onward(1)) for half in side[-1]])
    *ready, side_names = lax.optimization_barrier((*side[1], side_names))
    across = [None] + [
        [[other_core(part) for part in jnp.split(half, SPLIT)] for half in pair]
        for pair in [ready, *side[2:hops]]
    ]
    across_names = [other_core(pair) for pair in side_names]

    inner = None
    for hop in range(1, hops):
        blocks = [(half, i == 0, 0, i, 0) for i, half in enumerate(side[hop])]
        blocks += [(half, i == 0, 1, i, 0) for i, half in enumerate(across[hop])]
        if hop == 1:
            blocks += [(own[0], False, 2, 0, 0)]
            names = [side_names[1], across_names[1], own_names]
            tasks = ((0, (2, 3)), (1, (2, 3)), (4, (0, 1, 2, 3)))
        else:
            blocks += [(half, False, 2, i, 0) for i, half in enumerate(inner)]
            names = [side_names[hop], across_names[hop], across_names[hop - 1]]
            tasks = ((0, (2, 3, 4, 5)), (1, (2, 3, 4, 5)))
        sums, inner = row_sums(near, blocks, names, tasks, "pair_terms", (2, 3))
        for half in range(2):
            total = total + moved(sums[half : half + 1], back(hop, half))
        if hop == 1:
            total = total + sums[2:]
    facing, *inner = lax.optimization_barrier((side[hops][0], *inner))
    facing = [other_core(part) for part in jnp.split(facing, SPLIT)]
    names = [side_names[hops], across_names[hops], across_names[hops - 1]]
    others = [(unit, False, 2, i, 0) for i, unit in enumerate(inner)]
    task = ((0, (1, 2, 3)),)
    blocks = [(side[hops][0], True, 0, 0, 0), (facing, True, 1, 0, 0), *others]
    sums, (facing,) = row_sums(near, blocks, names, task, "end_terms", (1,), room=ROOM)
    total = total + moved(sums, back(hops, 0))[:1]
    others = [(facing, False, 1, 0, 0), *others]
    sums, _ = row_sums(near, [(side[hops][1], False, 0, 1, 0), *others], names, task, "end_terms")
    total = total + moved(sums, back(hops, 1))
    return jnp.log1p(total)[0]


def solution(mesh):
    return jax.shard_map(
        per_device,
        mesh=mesh,
        in_specs=(P(("groups", "blk"), None), P(("groups", "blk"), None), P("groups")),
        out_specs=P(("groups", "blk")),
        check_vma=False,
    )
```

time: 125 us -> 61.3 us (0.49)
  blocking collectives: 78.6 us -> 0 us
  Pallas kernels: 0 us -> 17.1 us
  starting transfers between devices: 5.2 us -> 22 us
  matrix products: 9.9 us -> 0 us
  waiting for transfers between devices: 10.1 us -> 19.2 us
  other arithmetic: 9.53 us -> 0.62 us
  local copies, waits for them, and re-layouts: 9.42 us -> 1.58 us
  between operations: 1.37 us -> 0.11 us
    all_to_all x2 -> x0, blocking collectives: 78.6 us -> none  [the longest x1 54.6 us: per_device(): lax.all_to_all(send_rows.reshape(blocks, cap, width), 'blk', split_axis=0...]
    ppermute x3 -> x20, starting transfers between devices: 1.71 us -> 22 us  [moved(): return lax.ppermute(block, 'blk', route)]
    pallas_call x0 -> x5, Pallas kernels: none -> 17.1 us  [the longest x4 16.8 us: row_sums(): pl.pallas_call(functools.partial(sums_kernel, near.shape[0], [(len(block[...]
    ppermute x3 -> x20, waiting for transfers between devices: 3.77 us -> 19.2 us  [moved(): return lax.ppermute(block, 'blk', route)]
    dot_general x2 -> x0, matrix products: 9.9 us -> none  [pair_terms(): lax.dot_general(a_rows, b_rows, (((1,), (1,)), ((), ())), preferred_eleme...]
    all_to_all x1 -> x0, waiting for transfers between devices: 6.36 us -> none  [per_device(): lax.all_to_all(scores.reshape(blocks, cap), 'blk', split_axis=0, concat_a...]
    scatter x1 -> x0, other arithmetic: 3.97 us -> none  [per_device(): send_rows = jnp.zeros((slots, width), jnp.bfloat16).at[position].set(unit)]
    scatter x1 -> x0, local copies, waits for them, and re-layouts: 3.77 us -> none  [per_device(): jnp.zeros((slots,), jnp.bfloat16).at[position]]
  transfers between devices with their start and end apart: 4 -> 20, of which waited for: 2 -> 5; matrix products, arithmetic and copies ran while one was open for 8% -> 1% of each run, Pallas kernels for 0% -> 28%
where the time goes in v4:
time: 61.3 us; the launch traced here: 60.6 us
  starting transfers between devices  22 us (36%)
  waiting for transfers between devices  19.2 us (31%)
  Pallas kernels  17.1 us (28%)
  local copies, waits for them, and re-layouts  1.58 us (3%)
  other arithmetic  0.62 us (1%)
    ppermute x20, starting transfers between devices, moved(): return lax.ppermute(block, 'blk', route)  22 us
    ppermute x20, waiting for transfers between devices, moved(): return lax.ppermute(block, 'blk', route)  19.2 us
    pallas_call x4, Pallas kernels, row_sums(): pl.pallas_call(functools.partial(sums_kernel, near.shape[0], [(len(block[...  16.8 us
    unnamed x6, local copies, waits for them, and re-layouts  1.24 us
  transfers between devices with their start and end apart: 20, of which 5 were waited for; matrix products, arithmetic and copies ran while one was open for 1% of the time, Pallas kernels for 28%

profile of v4, /device:TPU:0, one launch (start us, length us, event | category | flops | bytes accessed | tf_op | source)
XLA Modules:
  0.0 60.6 jit_solution(7996257166090053638)
XLA Ops:
  0.0 0.5 collective-permute-start.1
  0.5 2.6 %collective-permute-start = (bf16[512,1024]{1,0:T(8,128)(2,1)}, bf16[512,1024]{1,0:T(8,128)(2,1)S(1)}, u32[]{:S(2)}, u32[]{:S(2)}) collective-permute-start(bf16[512,1024]{1,0:T(8,128)(2,1)} %refs_0_.1), channel_id=1, source_target_pairs={{0,4},{1,3},{4,8},{5,1},{8,5},{9,12},{12,9},{13,14},{14,13},{15,10... | collective-permute-start | bytes 3145736 | tf_op jit(solution)/shard_map/ppermute | solution.py:174
  3.0 1.4 %collective-permute-start.4 = (bf16[512,1024]{1,0:T(8,128)(2,1)}, bf16[512,1024]{1,0:T(8,128)(2,1)S(1)}, u32[]{:S(2)}, u32[]{:S(2)}) collective-permute-start(bf16[512,1024]{1,0:T(8,128)(2,1)} %refs_0_.1), channel_id=1, source_target_pairs={{0,3},{1,4},{4,1},{5,8},{8,12},{9,5},{12,14},{13,9},{14,10},{15,13... | collective-permute-start | bytes 3145736 | tf_op jit(solution)/shard_map/ppermute | solution.py:174
  4.4 0.3 collective-permute-start.2
  4.7 0.0 copy-start.2
  4.7 1.0 %collective-permute-done.2 = s32[1,512]{1,0:T(1,128)S(1)} collective-permute-done((s32[1,512]{1,0:T(1,128)}, s32[1,512]{1,0:T(1,128)S(1)}, u32[]{:S(2)}, u32[]{:S(2)}) %collective-permute-start.2) | collective-permute-done | bytes 2080 | tf_op jit(solution)/shard_map/ppermute | solution.py:174
  5.8 0.0 copy-done.2
  5.8 0.1 rev.3
  5.9 0.0 copy-start.1
  5.9 0.6 %collective-permute-start.3 = (s32[2,512]{1,0:T(2,128)S(1)}, s32[2,512]{1,0:T(2,128)S(1)}, u32[]{:S(2)}, u32[]{:S(2)}) collective-permute-start(s32[2,512]{1,0:T(2,128)S(1)} %broadcast_select_fusion), channel_id=1, source_target_pairs={{0,4},{1,3},{4,8},{5,1},{8,12},{9,5},{12,14},{13,9},{14,10},{15,13... | collective-permute-start | bytes 12296 | tf_op jit(solution)/shard_map/ppermute | solution.py:174
  6.5 2.8 %collective-permute-start.5 = (s32[2,512]{1,0:T(2,128)S(1)}, s32[2,512]{1,0:T(2,128)S(1)}, u32[]{:S(2)}, u32[]{:S(2)}) collective-permute-start(s32[2,512]{1,0:T(2,128)S(1)} %broadcast_select_fusion), channel_id=1, source_target_pairs={{0,8},{1,7},{4,12},{5,3},{8,14},{9,1},{12,10},{13,5},{14,6},{15,9}... | collective-permute-start | bytes 12296 | tf_op jit(solution)/shard_map/ppermute | solution.py:174
  9.4 0.0 collective-permute-done.1.refs_1_
  9.4 0.0 copy-done.1
  9.4 0.0 copy-start
  9.4 1.2 %copy-done = bf16[512,1024]{1,0:T(8,128)(2,1)S(1)} copy-done((bf16[512,1024]{1,0:T(8,128)(2,1)S(1)}, bf16[512,1024]{1,0:T(8,128)(2,1)}, u32[]{:S(2)}) %copy-start) | copy-done | bytes 1048600
  10.6 2.7 %own_terms.1 = (f32[1,512]{1,0:T(1,128)S(1)}, bf16[512,1024]{1,0:T(8,128)(2,1)S(1)}) custom-call(s32[16]{0:T(128)S(1)} %copy-done.1, bf16[512,1024]{1,0:T(8,128)(2,1)S(1)} %copy-done, bf16[512,1024]{1,0:T(8,128)(2,1)S(1)} %collective-permute-done.1.refs_1_, s32[2,512]{1,0:T(2,128)S(1)} %pad_add_fusion.refs_2_.refs_9_), custom_call_target="tpu_custom_call" | custom-call | tf_op jit(solution)/shard_map/own_terms/pallas_call | solution.py:126
  13.3 12.6 %collective-permute-done.3.refs_7_ = s32[2,512]{1,0:T(2,128)S(1)} collective-permute-done((s32[2,512]{1,0:T(2,128)S(1)}, s32[2,512]{1,0:T(2,128)S(1)}, u32[]{:S(2)}, u32[]{:S(2)}) %collective-permute-start.3) | collective-permute-done | bytes 4128 | tf_op jit(solution)/shard_map/ppermute | solution.py:174
  25.9 0.0 collective-permute-done.refs_0_
  25.9 2.6 %collective-permute-start.13 = (bf16[512,1024]{1,0:T(8,128)(2,1)S(1)}, bf16[512,1024]{1,0:T(8,128)(2,1)S(1)}, u32[]{:S(2)}, u32[]{:S(2)}) collective-permute-start(bf16[512,1024]{1,0:T(8,128)(2,1)S(1)} %collective-permute-done.refs_0_), channel_id=1, source_target_pairs={{0,4},{1,3},{4,8},{5,1},{8,12},{9,5},{12,14},{13,9},{14,10},{15,13... | collective-permute-start | bytes 3145736 | tf_op jit(solution)/shard_map/ppermute | solution.py:174
  28.5 0.0 collective-permute-done.4.source
  28.5 0.3 unit_rows.1.refs_1_
  28.8 0.0 collective-permute-done.5.refs_5_.refs_4_
  28.9 0.1 fusion.4
  28.9 0.1 collective-permute-start.6
  29.0 0.5 collective-permute-start.7
  29.5 0.1 collective-permute-start.10
  29.6 0.1 fusion.3
  29.7 0.5 collective-permute-start.8
  30.2 1.5 %collective-permute-done.10.refs_8_.refs_7_.refs_6_ = s32[2,512]{1,0:T(2,128)S(1)} collective-permute-done((s32[2,512]{1,0:T(2,128)S(1)}, s32[2,512]{1,0:T(2,128)S(1)}, u32[]{:S(2)}, u32[]{:S(2)}) %collective-permute-start.10) | collective-permute-done | bytes 4128 | tf_op jit(solution)/shard_map/ppermute | solution.py:174
  31.7 0.1 collective-permute-start.9
  31.8 0.0 collective-permute-done.6.refs_2_
  31.8 2.4 %collective-permute-start.18 = (bf16[512,1024]{1,0:T(8,128)(2,1)S(1)}, bf16[512,1024]{1,0:T(8,128)(2,1)S(1)}, u32[]{:S(2)}, u32[]{:S(2)}) collective-permute-start(bf16[512,1024]{1,0:T(8,128)(2,1)S(1)} %unit_rows.1.refs_1_), channel_id=1, source_target_pairs={{0,4},{1,3},{4,8},{5,1},{8,12},{9,5},{12,14},{13,9},{14,10},{15,13... | collective-permute-start | bytes 3145736 | tf_op jit(solution)/shard_map/ppermute | solution.py:174
  34.2 0.0 collective-permute-done.7.refs_3_
  34.2 0.0 collective-permute-done.8.refs_4_
  34.2 0.0 collective-permute-done.9.refs_5_
  34.2 7.6 %pair_terms.1 = (f32[3,512]{1,0:T(4,128)S(1)}, bf16[512,1024]{1,0:T(8,128)(2,1)S(1)}, bf16[512,1024]{1,0:T(8,128)(2,1)S(1)}) custom-call(s32[16]{0:T(128)S(1)} %copy-done.1, bf16[512,1024]{1,0:T(8,128)(2,1)S(1)} %collective-permute-done.refs_0_, bf16[512,1024]{1,0:T(8,128)(2,1)S(1)} %unit_rows.1.refs_1_, ...), custom_call_target="tpu_custom_call" | custom-call | tf_op jit(solution)/shard_map/pair_terms/pallas_call | solution.py:126
  41.8 0.0 collective-permute-done.13.refs_0_
  41.8 0.1 fusion.2
  41.9 0.1 collective-permute-start.14
  42.0 0.5 collective-permute-start.15
  42.5 0.1 collective-permute-start.16
  42.6 2.1 %collective-permute-done.16.refs_6_.refs_5_ = s32[2,512]{1,0:T(2,128)S(1)} collective-permute-done((s32[2,512]{1,0:T(2,128)S(1)}, s32[2,512]{1,0:T(2,128)S(1)}, u32[]{:S(2)}, u32[]{:S(2)}) %collective-permute-start.16) | collective-permute-done | bytes 4128 | tf_op jit(solution)/shard_map/ppermute | solution.py:174
  44.6 0.0 collective-permute-done.14.refs_1_
  44.6 0.0 collective-permute-done.15.refs_2_
  44.6 3.7 %end_terms.2 = (f32[8,512]{1,0:T(8,128)S(1)}, bf16[512,1024]{1,0:T(8,128)(2,1)S(1)}) custom-call(s32[16]{0:T(128)S(1)} %copy-done.1, bf16[512,1024]{1,0:T(8,128)(2,1)S(1)} %collective-permute-done.13.refs_0_, bf16[256,1024]{1,0:T(8,128)(2,1)S(1)} %collective-permute-done.14.refs_1_, bf16[256,1024]{1,0:T(8,128)(2,1)S(1)} %collective-permute-done.15.refs_2_, ...), custom_call_target="tpu_custom_call" | custom-call | tf_op jit(solution)/shard_map/end_terms/pallas_call | solution.py:126
  48.4 2.7 %collective-permute-start.17 = (f32[8,512]{1,0:T(8,128)S(1)}, f32[8,512]{1,0:T(8,128)S(1)}, u32[]{:S(2)}, u32[]{:S(2)}) collective-permute-start(f32[8,512]{1,0:T(8,128)S(1)} %get-tuple-element.37), channel_id=1, source_target_pairs={{0,6},{1,8},{4,2},{5,12},{8,0},{9,14},{12,4},{13,10},{14,9},{15,7}... | collective-permute-start | bytes 49160 | tf_op jit(solution)/shard_map/ppermute | solution.py:174
  51.1 1.3 %collective-permute-start.11 = (f32[1,512]{1,0:T(1,128)S(1)}, f32[1,512]{1,0:T(1,128)S(1)}, u32[]{:S(2)}, u32[]{:S(2)}) collective-permute-start(f32[1,512]{1,0:T(1,128)S(1)} %get-tuple-element.45), channel_id=1, source_target_pairs={{0,2},{1,5},{4,0},{5,8},{8,4},{9,12},{12,9},{13,14},{14,13},{15,10... | collective-permute-start | bytes 6152 | tf_op jit(solution)/shard_map/ppermute | solution.py:174
  52.5 0.8 %collective-permute-start.12 = (f32[1,512]{1,0:T(1,128)S(1)}, f32[1,512]{1,0:T(1,128)S(1)}, u32[]{:S(2)}, u32[]{:S(2)}) collective-permute-start(f32[1,512]{1,0:T(1,128)S(1)} %get-tuple-element.46), channel_id=1, source_target_pairs={{0,3},{1,4},{4,1},{5,9},{8,5},{9,13},{12,8},{13,15},{14,12},{15,11... | collective-permute-start | bytes 6152 | tf_op jit(solution)/shard_map/ppermute | solution.py:174
  53.2 0.0 collective-permute-done.18.refs_0_
  53.3 2.8 %end_terms.3 = f32[1,512]{1,0:T(1,128)S(1)} custom-call(s32[16]{0:T(128)S(1)} %copy-done.1, bf16[512,1024]{1,0:T(8,128)(2,1)S(1)} %collective-permute-done.18.refs_0_, bf16[512,1024]{1,0:T(8,128)(2,1)S(1)} %get-tuple-element.38.refs_1_, bf16[512,1024]{1,0:T(8,128)(2,1)S(1)} %get-tuple-element.34.refs_3_.refs_2_, ...), custom_call_target="tpu_custom_call" | custom-call | tf_op jit(solution)/shard_map/end_terms/pallas_call | solution.py:126
  56.0 2.0 %collective-permute-start.19 = (f32[1,512]{1,0:T(1,128)S(1)}, f32[1,512]{1,0:T(1,128)S(1)}, u32[]{:S(2)}, u32[]{:S(2)}) collective-permute-start(f32[1,512]{1,0:T(1,128)S(1)} %end_terms.3), channel_id=1, source_target_pairs={{0,7},{1,9},{4,3},{5,13},{8,1},{9,15},{12,5},{13,11},{14,8},{15,6}... | collective-permute-start | bytes 6152 | tf_op jit(solution)/shard_map/ppermute | solution.py:174
  58.0 0.0 collective-permute-done.11
  58.0 0.0 collective-permute-done.12
  58.1 1.9 %collective-permute-done.19 = f32[1,512]{1,0:T(1,128)S(1)} collective-permute-done((f32[1,512]{1,0:T(1,128)S(1)}, f32[1,512]{1,0:T(1,128)S(1)}, u32[]{:S(2)}, u32[]{:S(2)}) %collective-permute-start.19) | collective-permute-done | bytes 2080 | tf_op jit(solution)/shard_map/ppermute | solution.py:174
  60.0 0.0 collective-permute-done.17
  60.0 0.6 fusion.1
  (3 shorter events, 0.0 us)
Async XLA Ops:
  0.0 9.4 %collective-permute-start.1 = (bf16[512,1024]{1,0:T(8,128)(2,1)}, bf16[512,1024]{1,0:T(8,128)(2,1)S(1)}, u32[]{:S(2)}, u32[]{:S(2)}) collective-permute-start(bf16[512,1024]{1,0:T(8,128)(2,1)} %refs_0_.1), channel_id=1, source_target_pairs={{0,1},{1,0},{4,5},{5,4},{8,9},{9,8},{12,13},{13,12},{14,15},{15,14... | collective-permute-start | bytes 3145736 | tf_op jit(solution)/shard_map/ppermute | solution.py:174
  0.5 25.4 %collective-permute-start = (bf16[512,1024]{1,0:T(8,128)(2,1)}, bf16[512,1024]{1,0:T(8,128)(2,1)S(1)}, u32[]{:S(2)}, u32[]{:S(2)}) collective-permute-start(bf16[512,1024]{1,0:T(8,128)(2,1)} %refs_0_.1), channel_id=1, source_target_pairs={{0,4},{1,3},{4,8},{5,1},{8,5},{9,12},{12,9},{13,14},{14,13},{15,10... | collective-permute-start | bytes 3145736 | tf_op jit(solution)/shard_map/ppermute | solution.py:174
  3.0 25.5 %collective-permute-start.4 = (bf16[512,1024]{1,0:T(8,128)(2,1)}, bf16[512,1024]{1,0:T(8,128)(2,1)S(1)}, u32[]{:S(2)}, u32[]{:S(2)}) collective-permute-start(bf16[512,1024]{1,0:T(8,128)(2,1)} %refs_0_.1), channel_id=1, source_target_pairs={{0,3},{1,4},{4,1},{5,8},{8,12},{9,5},{12,14},{13,9},{14,10},{15,13... | collective-permute-start | bytes 3145736 | tf_op jit(solution)/shard_map/ppermute | solution.py:174
  4.4 1.4 %collective-permute-start.2 = (s32[1,512]{1,0:T(1,128)}, s32[1,512]{1,0:T(1,128)S(1)}, u32[]{:S(2)}, u32[]{:S(2)}) collective-permute-start(s32[1,512]{1,0:T(1,128)} %bitcast.2), channel_id=1, source_target_pairs={{0,1},{1,0},{4,5},{5,4},{8,9},{9,8},{12,13},{13,12},{14,15},{15,14... | collective-permute-start | bytes 6152 | tf_op jit(solution)/shard_map/ppermute | solution.py:174
  4.7 1.0 %copy-start.2 = (s32[512,1]{0,1:T(1,128)S(1)}, s32[512,1]{0,1:T(1,128)}, u32[]{:S(2)}) copy-start(s32[512,1]{0,1:T(1,128)} %param.4) | copy-start | bytes 6148
  5.9 3.5 %copy-start.1 = (s32[16]{0:T(128)S(1)}, s32[16]{0:T(128)}, u32[]{:S(2)}) copy-start(s32[16]{0:T(128)} %near.7) | copy-start | bytes 196
  5.9 20.0 %collective-permute-start.3 = (s32[2,512]{1,0:T(2,128)S(1)}, s32[2,512]{1,0:T(2,128)S(1)}, u32[]{:S(2)}, u32[]{:S(2)}) collective-permute-start(s32[2,512]{1,0:T(2,128)S(1)} %broadcast_select_fusion), channel_id=1, source_target_pairs={{0,4},{1,3},{4,8},{5,1},{8,12},{9,5},{12,14},{13,9},{14,10},{15,13... | collective-permute-start | bytes 12296 | tf_op jit(solution)/shard_map/ppermute | solution.py:174
  6.5 22.3 %collective-permute-start.5 = (s32[2,512]{1,0:T(2,128)S(1)}, s32[2,512]{1,0:T(2,128)S(1)}, u32[]{:S(2)}, u32[]{:S(2)}) collective-permute-start(s32[2,512]{1,0:T(2,128)S(1)} %broadcast_select_fusion), channel_id=1, source_target_pairs={{0,8},{1,7},{4,12},{5,3},{8,14},{9,1},{12,10},{13,5},{14,6},{15,9}... | collective-permute-start | bytes 12296 | tf_op jit(solution)/shard_map/ppermute | solution.py:174
  9.4 1.2 %copy-start = (bf16[512,1024]{1,0:T(8,128)(2,1)S(1)}, bf16[512,1024]{1,0:T(8,128)(2,1)}, u32[]{:S(2)}) copy-start(bf16[512,1024]{1,0:T(8,128)(2,1)} %refs_0_.1) | copy-start | bytes 3145732
  25.9 15.9 %collective-permute-start.13 = (bf16[512,1024]{1,0:T(8,128)(2,1)S(1)}, bf16[512,1024]{1,0:T(8,128)(2,1)S(1)}, u32[]{:S(2)}, u32[]{:S(2)}) collective-permute-start(bf16[512,1024]{1,0:T(8,128)(2,1)S(1)} %collective-permute-done.refs_0_), channel_id=1, source_target_pairs={{0,4},{1,3},{4,8},{5,1},{8,12},{9,5},{12,14},{13,9},{14,10},{15,13... | collective-permute-start | bytes 3145736 | tf_op jit(solution)/shard_map/ppermute | solution.py:174
  28.9 2.9 %collective-permute-start.6 = (bf16[256,1024]{1,0:T(8,128)(2,1)S(1)}, bf16[256,1024]{1,0:T(8,128)(2,1)S(1)}, u32[]{:S(2)}, u32[]{:S(2)}) collective-permute-start(bf16[256,1024]{1,0:T(8,128)(2,1)S(1)} %get-tuple-element.44), channel_id=1, source_target_pairs={{0,1},{1,0},{4,5},{5,4},{8,9},{9,8},{12,13},{13,12},{14,15},{15,14... | collective-permute-start | bytes 1572872 | tf_op jit(solution)/shard_map/ppermute | solution.py:174
  29.0 5.2 %collective-permute-start.7 = (bf16[256,1024]{1,0:T(8,128)(2,1)S(1)}, bf16[256,1024]{1,0:T(8,128)(2,1)S(1)}, u32[]{:S(2)}, u32[]{:S(2)}) collective-permute-start(bf16[256,1024]{1,0:T(8,128)(2,1)S(1)} %get-tuple-element.43), channel_id=1, source_target_pairs={{0,1},{1,0},{4,5},{5,4},{8,9},{9,8},{12,13},{13,12},{14,15},{15,14... | collective-permute-start | bytes 1572872 | tf_op jit(solution)/shard_map/ppermute | solution.py:174
  29.5 2.2 %collective-permute-start.10 = (s32[2,512]{1,0:T(2,128)S(1)}, s32[2,512]{1,0:T(2,128)S(1)}, u32[]{:S(2)}, u32[]{:S(2)}) collective-permute-start(s32[2,512]{1,0:T(2,128)S(1)} %collective-permute-done.3.refs_7_), channel_id=1, source_target_pairs={{0,1},{1,0},{4,5},{5,4},{8,9},{9,8},{12,13},{13,12},{14,15},{15,14... | collective-permute-start | bytes 12296 | tf_op jit(solution)/shard_map/ppermute | solution.py:174
  29.7 4.6 %collective-permute-start.8 = (bf16[256,1024]{1,0:T(8,128)(2,1)S(1)}, bf16[256,1024]{1,0:T(8,128)(2,1)S(1)}, u32[]{:S(2)}, u32[]{:S(2)}) collective-permute-start(bf16[256,1024]{1,0:T(8,128)(2,1)S(1)} %get-tuple-element.42), channel_id=1, source_target_pairs={{0,1},{1,0},{4,5},{5,4},{8,9},{9,8},{12,13},{13,12},{14,15},{15,14... | collective-permute-start | bytes 1572872 | tf_op jit(solution)/shard_map/ppermute | solution.py:174
  31.7 2.6 %collective-permute-start.9 = (bf16[256,1024]{1,0:T(8,128)(2,1)S(1)}, bf16[256,1024]{1,0:T(8,128)(2,1)S(1)}, u32[]{:S(2)}, u32[]{:S(2)}) collective-permute-start(bf16[256,1024]{1,0:T(8,128)(2,1)S(1)} %get-tuple-element.41), channel_id=1, source_target_pairs={{0,1},{1,0},{4,5},{5,4},{8,9},{9,8},{12,13},{13,12},{14,15},{15,14... | collective-permute-start | bytes 1572872 | tf_op jit(solution)/shard_map/ppermute | solution.py:174
  31.8 21.4 %collective-permute-start.18 = (bf16[512,1024]{1,0:T(8,128)(2,1)S(1)}, bf16[512,1024]{1,0:T(8,128)(2,1)S(1)}, u32[]{:S(2)}, u32[]{:S(2)}) collective-permute-start(bf16[512,1024]{1,0:T(8,128)(2,1)S(1)} %unit_rows.1.refs_1_), channel_id=1, source_target_pairs={{0,4},{1,3},{4,8},{5,1},{8,12},{9,5},{12,14},{13,9},{14,10},{15,13... | collective-permute-start | bytes 3145736 | tf_op jit(solution)/shard_map/ppermute | solution.py:174
  41.9 2.7 %collective-permute-start.14 = (bf16[256,1024]{1,0:T(8,128)(2,1)S(1)}, bf16[256,1024]{1,0:T(8,128)(2,1)S(1)}, u32[]{:S(2)}, u32[]{:S(2)}) collective-permute-start(bf16[256,1024]{1,0:T(8,128)(2,1)S(1)} %get-tuple-element.40), channel_id=1, source_target_pairs={{0,1},{1,0},{4,5},{5,4},{8,9},{9,8},{12,13},{13,12},{14,15},{15,14... | collective-permute-start | bytes 1572872 | tf_op jit(solution)/shard_map/ppermute | solution.py:174
  42.0 2.7 %collective-permute-start.15 = (bf16[256,1024]{1,0:T(8,128)(2,1)S(1)}, bf16[256,1024]{1,0:T(8,128)(2,1)S(1)}, u32[]{:S(2)}, u32[]{:S(2)}) collective-permute-start(bf16[256,1024]{1,0:T(8,128)(2,1)S(1)} %get-tuple-element.39), channel_id=1, source_target_pairs={{0,1},{1,0},{4,5},{5,4},{8,9},{9,8},{12,13},{13,12},{14,15},{15,14... | collective-permute-start | bytes 1572872 | tf_op jit(solution)/shard_map/ppermute | solution.py:174
  42.5 2.2 %collective-permute-start.16 = (s32[2,512]{1,0:T(2,128)S(1)}, s32[2,512]{1,0:T(2,128)S(1)}, u32[]{:S(2)}, u32[]{:S(2)}) collective-permute-start(s32[2,512]{1,0:T(2,128)S(1)} %collective-permute-done.5.refs_5_.refs_4_), channel_id=1, source_target_pairs={{0,1},{1,0},{4,5},{5,4},{8,9},{9,8},{12,13},{13,12},{14,15},{15,14... | collective-permute-start | bytes 12296 | tf_op jit(solution)/shard_map/ppermute | solution.py:174
  48.4 11.6 %collective-permute-start.17 = (f32[8,512]{1,0:T(8,128)S(1)}, f32[8,512]{1,0:T(8,128)S(1)}, u32[]{:S(2)}, u32[]{:S(2)}) collective-permute-start(f32[8,512]{1,0:T(8,128)S(1)} %get-tuple-element.37), channel_id=1, source_target_pairs={{0,6},{1,8},{4,2},{5,12},{8,0},{9,14},{12,4},{13,10},{14,9},{15,7}... | collective-permute-start | bytes 49160 | tf_op jit(solution)/shard_map/ppermute | solution.py:174
  51.1 6.9 %collective-permute-start.11 = (f32[1,512]{1,0:T(1,128)S(1)}, f32[1,512]{1,0:T(1,128)S(1)}, u32[]{:S(2)}, u32[]{:S(2)}) collective-permute-start(f32[1,512]{1,0:T(1,128)S(1)} %get-tuple-element.45), channel_id=1, source_target_pairs={{0,2},{1,5},{4,0},{5,8},{8,4},{9,12},{12,9},{13,14},{14,13},{15,10... | collective-permute-start | bytes 6152 | tf_op jit(solution)/shard_map/ppermute | solution.py:174
  52.5 5.6 %collective-permute-start.12 = (f32[1,512]{1,0:T(1,128)S(1)}, f32[1,512]{1,0:T(1,128)S(1)}, u32[]{:S(2)}, u32[]{:S(2)}) collective-permute-start(f32[1,512]{1,0:T(1,128)S(1)} %get-tuple-element.46), channel_id=1, source_target_pairs={{0,3},{1,4},{4,1},{5,9},{8,5},{9,13},{12,8},{13,15},{14,12},{15,11... | collective-permute-start | bytes 6152 | tf_op jit(solution)/shard_map/ppermute | solution.py:174
  56.0 4.0 %collective-permute-start.19 = (f32[1,512]{1,0:T(1,128)S(1)}, f32[1,512]{1,0:T(1,128)S(1)}, u32[]{:S(2)}, u32[]{:S(2)}) collective-permute-start(f32[1,512]{1,0:T(1,128)S(1)} %end_terms.3), channel_id=1, source_target_pairs={{0,7},{1,9},{4,3},{5,13},{8,1},{9,15},{12,5},{13,11},{14,8},{15,6}... | collective-permute-start | bytes 6152 | tf_op jit(solution)/shard_map/ppermute | solution.py:174

commit v5 on v4

--- a/solution.py
+++ b/solution.py
@@ -176,51 +176,41 @@
     def other_core(block):
         return moved(block, lambda place, core: (place, 1 - core))
 
-    def late(place):
-        return int(place % chips >= chips // 2)
-
-    def onward(distance):
-        return lambda place, core: (place + distance * (1 - 2 * core), core)
-
-    def first(half):
-        def target(place, core):
-            forward = core == late(place + hops) ^ half
-            return (place + 1, 0) if forward else (place - 1, 1)
-
-        return target
+    def onward(place, core):
+        return place + 1 - 2 * core, core
+
+    def against(place, core):
+        return place - 1 + 2 * core, 1 - core
 
     def back(distance, half):
-        def target(place, core):
-            home = place - distance * (1 - 2 * core)
-            return home, late(home + hops * (1 - 2 * core)) ^ half
-
-        return target
+        return lambda place, core: (place - distance * (1 - 2 * core), core ^ half)
 
     name = owner.reshape(1, rows)
-    own_names = jnp.concatenate([name, other_core(name)], axis=0)
-    swapped = lax.axis_index("blk") // 2 >= chips // 2
-    sent_names = jnp.where(swapped, own_names[::-1], own_names)
-    side_names = [own_names] + [moved(sent_names, onward(h)) for h in range(1, hops + 1)]
-    side = [None, [moved(embed, first(half)) for half in range(2)]]
+    other_name, other = other_core(name), other_core(embed)
+    own_names = jnp.concatenate([name, other_name], axis=0)
+    side_names, across_names = [own_names], [jnp.concatenate([other_name, name], axis=0)]
+    for hop in range(1, hops + 1):
+        side_names.append(moved(across_names[-1], against))
+        across_names.append(other_core(side_names[-1]))
     total, own = row_sums(
         near,
-        [(embed, True, 0, 0, 0), (other_core(embed), True, 0, 1, 0)],
+        [(embed, True, 0, 0, 0), (other, True, 0, 1, 0)],
         [own_names],
         ((0, (0, 1)),),
         "own_terms",
         (0,),
     )
-    if hops > 1:
-        side[1][0], total, side_names[1] = lax.optimization_barrier((side[1][0], total, side_names[1]))
-    side[1][1] = unit_block(side[1][1])
+    first, second = moved(embed, onward), moved(other, onward)
+    first, total, side_names, across_names = lax.optimization_barrier(
+        (first, total, side_names, across_names)
+    )
+    side = [None, [first, unit_block(second)]]
     for hop in range(2, hops + 1):
-        side.append([moved(half, onward(1)) for half in side[-1]])
-    *ready, side_names = lax.optimization_barrier((*side[1], side_names))
+        side.append([moved(half, onward) for half in side[-1]])
     across = [None] + [
         [[other_core(part) for part in jnp.split(half, SPLIT)] for half in pair]
-        for pair in [ready, *side[2:hops]]
+        for pair in side[1:hops]
     ]
-    across_names = [other_core(pair) for pair in side_names]
 
     inner = None
     for hop in range(1, hops):

time: 61.3 us -> 57.7 us (0.941)
  waiting for transfers between devices: 19.2 us -> 15.4 us
  other arithmetic: 0.62 us -> 1.37 us
    ppermute x20, waiting for transfers between devices: 19.2 us -> 15.4 us  [moved(): return lax.ppermute(block, 'blk', route)]
    concatenate x1, other arithmetic: 0.01 us -> 0.77 us  [per_device(): jnp.concatenate([other_name, name], axis=0)]
    unnamed x6 -> x4, local copies, waits for them, and re-layouts: 1.24 us -> 1.23 us
  transfers between devices with their start and end apart: 20 -> 20, of which waited for: 5 -> 11; matrix products, arithmetic and copies ran while one was open for 1% -> 2% of each run, Pallas kernels for 28% -> 30%
where the time goes in v5:
time: 57.7 us; the launch traced here: 57.3 us
  starting transfers between devices  21.9 us (38%)
  Pallas kernels  17.1 us (30%)
  waiting for transfers between devices  15.4 us (27%)
  local copies, waits for them, and re-layouts  1.44 us (2%)
  other arithmetic  1.37 us (2%)
    ppermute x20, starting transfers between devices, moved(): return lax.ppermute(block, 'blk', route)  21.9 us
    pallas_call x4, Pallas kernels, row_sums(): pl.pallas_call(functools.partial(sums_kernel, near.shape[0], [(len(block[...  16.8 us
    ppermute x20, waiting for transfers between devices, moved(): return lax.ppermute(block, 'blk', route)  15.4 us
    unnamed x4, local copies, waits for them, and re-layouts  1.23 us
  transfers between devices with their start and end apart: 20, of which 11 were waited for; matrix products, arithmetic and copies ran while one was open for 2% of the time, Pallas kernels for 30%

profile of v5, /device:TPU:0, one launch (start us, length us, event | category | flops | bytes accessed | tf_op | source)
XLA Modules:
  0.0 57.3 jit_solution(700534198824083607)
XLA Ops:
  0.0 0.5 collective-permute-start.1
  0.5 2.6 %collective-permute-start = (bf16[512,1024]{1,0:T(8,128)(2,1)}, bf16[512,1024]{1,0:T(8,128)(2,1)S(1)}, u32[]{:S(2)}, u32[]{:S(2)}) collective-permute-start(bf16[512,1024]{1,0:T(8,128)(2,1)} %refs_0_.1), channel_id=1, source_target_pairs={{0,4},{1,3},{4,8},{5,1},{8,12},{9,5},{12,14},{13,9},{14,10},{15,13... | collective-permute-start | bytes 3145736 | tf_op jit(solution)/shard_map/ppermute | solution.py:174
  3.0 0.0 collective-permute-done.1.refs_1_
  3.0 2.9 %collective-permute-start.7 = (bf16[512,1024]{1,0:T(8,128)(2,1)S(1)}, bf16[512,1024]{1,0:T(8,128)(2,1)S(1)}, u32[]{:S(2)}, u32[]{:S(2)}) collective-permute-start(bf16[512,1024]{1,0:T(8,128)(2,1)S(1)} %collective-permute-done.1.refs_1_), channel_id=1, source_target_pairs={{0,4},{1,3},{4,8},{5,1},{8,12},{9,5},{12,14},{13,9},{14,10},{15,13... | collective-permute-start | bytes 3145736 | tf_op jit(solution)/shard_map/ppermute | solution.py:174
  5.9 0.0 collective-permute-start.2
  5.9 1.4 %collective-permute-done.2 = s32[1,512]{1,0:T(1,128)S(1)} collective-permute-done((s32[1,512]{1,0:T(1,128)}, s32[1,512]{1,0:T(1,128)S(1)}, u32[]{:S(2)}, u32[]{:S(2)}) %collective-permute-start.2) | collective-permute-done | bytes 2080 | tf_op jit(solution)/shard_map/ppermute | solution.py:174
  7.3 0.8 %pad_add_fusion.1 = (s32[2,512]{1,0:T(2,128)S(1)}, s32[2,512]{1,0:T(2,128)S(1)}) fusion(s32[1,512]{1,0:T(1,128)} %bitcast.3, s32[1,512]{1,0:T(1,128)S(1)} %collective-permute-done.2), kind=kLoop, calls=%fused_computation.1 | loop fusion | flops 2048 | bytes 12288 | tf_op jit(solution)/shard_map/concatenate | solution.py:191
  8.0 0.0 copy-start.1
  8.0 1.0 %collective-permute-start.3 = (s32[2,512]{1,0:T(2,128)S(1)}, s32[2,512]{1,0:T(2,128)S(1)}, u32[]{:S(2)}, u32[]{:S(2)}) collective-permute-start(s32[2,512]{1,0:T(2,128)S(1)} %get-tuple-element.45), channel_id=1, source_target_pairs={{0,3},{1,4},{4,1},{5,8},{8,5},{9,12},{12,9},{13,14},{14,13},{15,10... | collective-permute-start | bytes 12296 | tf_op jit(solution)/shard_map/ppermute | solution.py:174
  9.1 2.2 %collective-permute-done.3.refs_7_ = s32[2,512]{1,0:T(2,128)S(1)} collective-permute-done((s32[2,512]{1,0:T(2,128)S(1)}, s32[2,512]{1,0:T(2,128)S(1)}, u32[]{:S(2)}, u32[]{:S(2)}) %collective-permute-start.3) | collective-permute-done | bytes 4128 | tf_op jit(solution)/shard_map/ppermute | solution.py:174
  11.3 0.5 collective-permute-start.4
  11.7 0.8 %collective-permute-done.4.refs_8_.refs_7_.refs_6_ = s32[2,512]{1,0:T(2,128)S(1)} collective-permute-done((s32[2,512]{1,0:T(2,128)S(1)}, s32[2,512]{1,0:T(2,128)S(1)}, u32[]{:S(2)}, u32[]{:S(2)}) %collective-permute-start.4) | collective-permute-done | bytes 4128 | tf_op jit(solution)/shard_map/ppermute | solution.py:174
  12.5 1.2 %collective-permute-start.5 = (s32[2,512]{1,0:T(2,128)S(1)}, s32[2,512]{1,0:T(2,128)S(1)}, u32[]{:S(2)}, u32[]{:S(2)}) collective-permute-start(s32[2,512]{1,0:T(2,128)S(1)} %collective-permute-done.4.refs_8_.refs_7_.refs_6_), channel_id=1, source_target_pairs={{0,3},{1,4},{4,1},{5,8},{8,5},{9,12},{12,9},{13,14},{14,13},{15,10... | collective-permute-start | bytes 12296 | tf_op jit(solution)/shard_map/ppermute | solution.py:174
  13.7 2.0 %collective-permute-done.5.refs_5_.refs_4_ = s32[2,512]{1,0:T(2,128)S(1)} collective-permute-done((s32[2,512]{1,0:T(2,128)S(1)}, s32[2,512]{1,0:T(2,128)S(1)}, u32[]{:S(2)}, u32[]{:S(2)}) %collective-permute-start.5) | collective-permute-done | bytes 4128 | tf_op jit(solution)/shard_map/ppermute | solution.py:174
  15.7 0.6 %collective-permute-start.6 = (s32[2,512]{1,0:T(2,128)S(1)}, s32[2,512]{1,0:T(2,128)S(1)}, u32[]{:S(2)}, u32[]{:S(2)}) collective-permute-start(s32[2,512]{1,0:T(2,128)S(1)} %collective-permute-done.5.refs_5_.refs_4_), channel_id=1, source_target_pairs={{0,1},{1,0},{4,5},{5,4},{8,9},{9,8},{12,13},{13,12},{14,15},{15,14... | collective-permute-start | bytes 12296 | tf_op jit(solution)/shard_map/ppermute | solution.py:174
  16.3 0.0 copy-done.1
  16.3 0.0 copy-start
  16.3 1.2 %copy-done = bf16[512,1024]{1,0:T(8,128)(2,1)S(1)} copy-done((bf16[512,1024]{1,0:T(8,128)(2,1)S(1)}, bf16[512,1024]{1,0:T(8,128)(2,1)}, u32[]{:S(2)}) %copy-start) | copy-done | bytes 1048600
  17.5 2.7 %own_terms.1 = (f32[1,512]{1,0:T(1,128)S(1)}, bf16[512,1024]{1,0:T(8,128)(2,1)S(1)}) custom-call(s32[16]{0:T(128)S(1)} %copy-done.1, bf16[512,1024]{1,0:T(8,128)(2,1)S(1)} %copy-done, bf16[512,1024]{1,0:T(8,128)(2,1)S(1)} %collective-permute-done.1.refs_1_, s32[2,512]{1,0:T(2,128)S(1)} %get-tuple-element.46.refs_2_.refs_9_), custom_call_target="tpu_custom_call" | custom-call | tf_op jit(solution)/shard_map/own_terms/pallas_call | solution.py:126
  20.3 0.0 collective-permute-done.6.refs_6_.refs_5_
  20.3 0.0 collective-permute-done.refs_0_
  20.3 1.6 %collective-permute-start.14 = (bf16[512,1024]{1,0:T(8,128)(2,1)S(1)}, bf16[512,1024]{1,0:T(8,128)(2,1)S(1)}, u32[]{:S(2)}, u32[]{:S(2)}) collective-permute-start(bf16[512,1024]{1,0:T(8,128)(2,1)S(1)} %collective-permute-done.refs_0_), channel_id=1, source_target_pairs={{0,4},{1,3},{4,8},{5,1},{8,12},{9,5},{12,14},{13,9},{14,10},{15,13... | collective-permute-start | bytes 3145736 | tf_op jit(solution)/shard_map/ppermute | solution.py:174
  21.9 0.1 fusion.4
  22.0 0.1 collective-permute-start.8
  22.1 0.5 collective-permute-start.9
  22.6 4.7 %collective-permute-done.7.source = bf16[512,1024]{1,0:T(8,128)(2,1)S(1)} collective-permute-done((bf16[512,1024]{1,0:T(8,128)(2,1)S(1)}, bf16[512,1024]{1,0:T(8,128)(2,1)S(1)}, u32[]{:S(2)}, u32[]{:S(2)}) %collective-permute-start.7) | collective-permute-done | bytes 1048608 | tf_op jit(solution)/shard_map/ppermute | solution.py:174
  27.3 0.3 unit_rows.1.refs_1_
  27.6 0.1 fusion.3
  27.7 0.1 collective-permute-start.10
  27.8 0.5 collective-permute-start.11
  28.3 0.0 collective-permute-done.8.refs_2_
  28.3 2.1 %collective-permute-start.18 = (bf16[512,1024]{1,0:T(8,128)(2,1)S(1)}, bf16[512,1024]{1,0:T(8,128)(2,1)S(1)}, u32[]{:S(2)}, u32[]{:S(2)}) collective-permute-start(bf16[512,1024]{1,0:T(8,128)(2,1)S(1)} %unit_rows.1.refs_1_), channel_id=1, source_target_pairs={{0,4},{1,3},{4,8},{5,1},{8,12},{9,5},{12,14},{13,9},{14,10},{15,13... | collective-permute-start | bytes 3145736 | tf_op jit(solution)/shard_map/ppermute | solution.py:174
  30.4 0.0 collective-permute-done.9.refs_3_
  30.4 0.0 collective-permute-done.10.refs_4_
  30.4 0.1 collective-permute-done.11.refs_5_
  30.4 7.6 %pair_terms.1 = (f32[3,512]{1,0:T(4,128)S(1)}, bf16[512,1024]{1,0:T(8,128)(2,1)S(1)}, bf16[512,1024]{1,0:T(8,128)(2,1)S(1)}) custom-call(s32[16]{0:T(128)S(1)} %copy-done.1, bf16[512,1024]{1,0:T(8,128)(2,1)S(1)} %collective-permute-done.refs_0_, bf16[512,1024]{1,0:T(8,128)(2,1)S(1)} %unit_rows.1.refs_1_, ...), custom_call_target="tpu_custom_call" | custom-call | tf_op jit(solution)/shard_map/pair_terms/pallas_call | solution.py:126
  38.0 0.5 collective-permute-done.14.refs_0_
  38.5 0.1 fusion.2
  38.6 0.1 collective-permute-start.15
  38.7 0.5 collective-permute-start.16
  39.2 1.4 %collective-permute-done.15.refs_1_ = bf16[256,1024]{1,0:T(8,128)(2,1)S(1)} collective-permute-done((bf16[256,1024]{1,0:T(8,128)(2,1)S(1)}, bf16[256,1024]{1,0:T(8,128)(2,1)S(1)}, u32[]{:S(2)}, u32[]{:S(2)}) %collective-permute-start.15) | collective-permute-done | bytes 524320 | tf_op jit(solution)/shard_map/ppermute | solution.py:174
  40.6 0.7 %collective-permute-done.16.refs_2_ = bf16[256,1024]{1,0:T(8,128)(2,1)S(1)} collective-permute-done((bf16[256,1024]{1,0:T(8,128)(2,1)S(1)}, bf16[256,1024]{1,0:T(8,128)(2,1)S(1)}, u32[]{:S(2)}, u32[]{:S(2)}) %collective-permute-start.16) | collective-permute-done | bytes 524320 | tf_op jit(solution)/shard_map/ppermute | solution.py:174
  41.3 3.7 %end_terms.2 = (f32[8,512]{1,0:T(8,128)S(1)}, bf16[512,1024]{1,0:T(8,128)(2,1)S(1)}) custom-call(s32[16]{0:T(128)S(1)} %copy-done.1, bf16[512,1024]{1,0:T(8,128)(2,1)S(1)} %collective-permute-done.14.refs_0_, bf16[256,1024]{1,0:T(8,128)(2,1)S(1)} %collective-permute-done.15.refs_1_, bf16[256,1024]{1,0:T(8,128)(2,1)S(1)} %collective-permute-done.16.refs_2_, ...), custom_call_target="tpu_custom_call" | custom-call | tf_op jit(solution)/shard_map/end_terms/pallas_call | solution.py:126
  45.0 3.1 %collective-permute-start.17 = (f32[8,512]{1,0:T(8,128)S(1)}, f32[8,512]{1,0:T(8,128)S(1)}, u32[]{:S(2)}, u32[]{:S(2)}) collective-permute-start(f32[8,512]{1,0:T(8,128)S(1)} %get-tuple-element.35), channel_id=1, source_target_pairs={{0,6},{1,9},{4,2},{5,13},{8,0},{9,15},{12,4},{13,11},{14,8},{15,7}... | collective-permute-start | bytes 49160 | tf_op jit(solution)/shard_map/ppermute | solution.py:174
  48.1 1.6 %collective-permute-start.12 = (f32[1,512]{1,0:T(1,128)S(1)}, f32[1,512]{1,0:T(1,128)S(1)}, u32[]{:S(2)}, u32[]{:S(2)}) collective-permute-start(f32[1,512]{1,0:T(1,128)S(1)} %get-tuple-element.43), channel_id=1, source_target_pairs={{0,2},{1,5},{4,0},{5,9},{8,4},{9,13},{12,8},{13,15},{14,12},{15,11... | collective-permute-start | bytes 6152 | tf_op jit(solution)/shard_map/ppermute | solution.py:174
  49.7 0.0 collective-permute-start.13
  49.7 0.2 collective-permute-done.18.refs_0_
  49.9 2.8 %end_terms.3 = f32[1,512]{1,0:T(1,128)S(1)} custom-call(s32[16]{0:T(128)S(1)} %copy-done.1, bf16[512,1024]{1,0:T(8,128)(2,1)S(1)} %collective-permute-done.18.refs_0_, bf16[512,1024]{1,0:T(8,128)(2,1)S(1)} %get-tuple-element.36.refs_1_, bf16[512,1024]{1,0:T(8,128)(2,1)S(1)} %get-tuple-element.31.refs_3_.refs_2_, ...), custom_call_target="tpu_custom_call" | custom-call | tf_op jit(solution)/shard_map/end_terms/pallas_call | solution.py:126
  52.7 2.6 %collective-permute-start.19 = (f32[1,512]{1,0:T(1,128)S(1)}, f32[1,512]{1,0:T(1,128)S(1)}, u32[]{:S(2)}, u32[]{:S(2)}) collective-permute-start(f32[1,512]{1,0:T(1,128)S(1)} %end_terms.3), channel_id=1, source_target_pairs={{0,7},{1,8},{4,3},{5,12},{8,1},{9,14},{12,5},{13,10},{14,9},{15,6}... | collective-permute-start | bytes 6152 | tf_op jit(solution)/shard_map/ppermute | solution.py:174
  55.3 0.0 collective-permute-done.12
  55.3 0.0 collective-permute-done.13
  55.3 1.3 %collective-permute-done.19 = f32[1,512]{1,0:T(1,128)S(1)} collective-permute-done((f32[1,512]{1,0:T(1,128)S(1)}, f32[1,512]{1,0:T(1,128)S(1)}, u32[]{:S(2)}, u32[]{:S(2)}) %collective-permute-start.19) | collective-permute-done | bytes 2080 | tf_op jit(solution)/shard_map/ppermute | solution.py:174
  56.7 0.0 collective-permute-done.17
  56.7 0.6 %fusion.1 = f32[1,512]{1,0:T(1,128)} fusion(f32[1,512]{1,0:T(1,128)S(1)} %collective-permute-done.19, f32[8,512]{1,0:T(8,128)S(1)} %collective-permute-done.17, f32[3,512]{1,0:T(4,128)S(1)} %get-tuple-element.27, f32[1,512]{1,0:T(1,128)S(1)} %collective-permute-done.13, f32[1,512]{1,0:T(1,128)S(1)} %get-tuple-element.22, f32[1,512]{1,0:T(1,128)S(1)} %collective-permute-done.12), kind=kLoop, calls=%fused_computation.4 | loop fusion | flops 2560 | bytes 14336 | tf_op jit(solution)/shard_map/log1p | solution.py:243
  (1 shorter events, 0.0 us)
Async XLA Ops:
  0.0 3.0 %collective-permute-start.1 = (bf16[512,1024]{1,0:T(8,128)(2,1)}, bf16[512,1024]{1,0:T(8,128)(2,1)S(1)}, u32[]{:S(2)}, u32[]{:S(2)}) collective-permute-start(bf16[512,1024]{1,0:T(8,128)(2,1)} %refs_0_.1), channel_id=1, source_target_pairs={{0,1},{1,0},{4,5},{5,4},{8,9},{9,8},{12,13},{13,12},{14,15},{15,14... | collective-permute-start | bytes 3145736 | tf_op jit(solution)/shard_map/ppermute | solution.py:174
  0.5 19.8 %collective-permute-start = (bf16[512,1024]{1,0:T(8,128)(2,1)}, bf16[512,1024]{1,0:T(8,128)(2,1)S(1)}, u32[]{:S(2)}, u32[]{:S(2)}) collective-permute-start(bf16[512,1024]{1,0:T(8,128)(2,1)} %refs_0_.1), channel_id=1, source_target_pairs={{0,4},{1,3},{4,8},{5,1},{8,12},{9,5},{12,14},{13,9},{14,10},{15,13... | collective-permute-start | bytes 3145736 | tf_op jit(solution)/shard_map/ppermute | solution.py:174
  3.0 24.2 %collective-permute-start.7 = (bf16[512,1024]{1,0:T(8,128)(2,1)S(1)}, bf16[512,1024]{1,0:T(8,128)(2,1)S(1)}, u32[]{:S(2)}, u32[]{:S(2)}) collective-permute-start(bf16[512,1024]{1,0:T(8,128)(2,1)S(1)} %collective-permute-done.1.refs_1_), channel_id=1, source_target_pairs={{0,4},{1,3},{4,8},{5,1},{8,12},{9,5},{12,14},{13,9},{14,10},{15,13... | collective-permute-start | bytes 3145736 | tf_op jit(solution)/shard_map/ppermute | solution.py:174
  5.9 1.4 %collective-permute-start.2 = (s32[1,512]{1,0:T(1,128)}, s32[1,512]{1,0:T(1,128)S(1)}, u32[]{:S(2)}, u32[]{:S(2)}) collective-permute-start(s32[1,512]{1,0:T(1,128)} %bitcast.2), channel_id=1, source_target_pairs={{0,1},{1,0},{4,5},{5,4},{8,9},{9,8},{12,13},{13,12},{14,15},{15,14... | collective-permute-start | bytes 6152 | tf_op jit(solution)/shard_map/ppermute | solution.py:174
  8.0 8.3 %copy-start.1 = (s32[16]{0:T(128)S(1)}, s32[16]{0:T(128)}, u32[]{:S(2)}) copy-start(s32[16]{0:T(128)} %near.7) | copy-start | bytes 196
  8.0 3.2 %collective-permute-start.3 = (s32[2,512]{1,0:T(2,128)S(1)}, s32[2,512]{1,0:T(2,128)S(1)}, u32[]{:S(2)}, u32[]{:S(2)}) collective-permute-start(s32[2,512]{1,0:T(2,128)S(1)} %get-tuple-element.45), channel_id=1, source_target_pairs={{0,3},{1,4},{4,1},{5,8},{8,5},{9,12},{12,9},{13,14},{14,13},{15,10... | collective-permute-start | bytes 12296 | tf_op jit(solution)/shard_map/ppermute | solution.py:174
  11.3 1.3 %collective-permute-start.4 = (s32[2,512]{1,0:T(2,128)S(1)}, s32[2,512]{1,0:T(2,128)S(1)}, u32[]{:S(2)}, u32[]{:S(2)}) collective-permute-start(s32[2,512]{1,0:T(2,128)S(1)} %collective-permute-done.3.refs_7_), channel_id=1, source_target_pairs={{0,1},{1,0},{4,5},{5,4},{8,9},{9,8},{12,13},{13,12},{14,15},{15,14... | collective-permute-start | bytes 12296 | tf_op jit(solution)/shard_map/ppermute | solution.py:174
  12.5 3.1 %collective-permute-start.5 = (s32[2,512]{1,0:T(2,128)S(1)}, s32[2,512]{1,0:T(2,128)S(1)}, u32[]{:S(2)}, u32[]{:S(2)}) collective-permute-start(s32[2,512]{1,0:T(2,128)S(1)} %collective-permute-done.4.refs_8_.refs_7_.refs_6_), channel_id=1, source_target_pairs={{0,3},{1,4},{4,1},{5,8},{8,5},{9,12},{12,9},{13,14},{14,13},{15,10... | collective-permute-start | bytes 12296 | tf_op jit(solution)/shard_map/ppermute | solution.py:174
  15.7 4.6 %collective-permute-start.6 = (s32[2,512]{1,0:T(2,128)S(1)}, s32[2,512]{1,0:T(2,128)S(1)}, u32[]{:S(2)}, u32[]{:S(2)}) collective-permute-start(s32[2,512]{1,0:T(2,128)S(1)} %collective-permute-done.5.refs_5_.refs_4_), channel_id=1, source_target_pairs={{0,1},{1,0},{4,5},{5,4},{8,9},{9,8},{12,13},{13,12},{14,15},{15,14... | collective-permute-start | bytes 12296 | tf_op jit(solution)/shard_map/ppermute | solution.py:174
  16.3 1.2 %copy-start = (bf16[512,1024]{1,0:T(8,128)(2,1)S(1)}, bf16[512,1024]{1,0:T(8,128)(2,1)}, u32[]{:S(2)}) copy-start(bf16[512,1024]{1,0:T(8,128)(2,1)} %refs_0_.1) | copy-start | bytes 3145732
  20.3 18.2 %collective-permute-start.14 = (bf16[512,1024]{1,0:T(8,128)(2,1)S(1)}, bf16[512,1024]{1,0:T(8,128)(2,1)S(1)}, u32[]{:S(2)}, u32[]{:S(2)}) collective-permute-start(bf16[512,1024]{1,0:T(8,128)(2,1)S(1)} %collective-permute-done.refs_0_), channel_id=1, source_target_pairs={{0,4},{1,3},{4,8},{5,1},{8,12},{9,5},{12,14},{13,9},{14,10},{15,13... | collective-permute-start | bytes 3145736 | tf_op jit(solution)/shard_map/ppermute | solution.py:174
  22.0 6.3 %collective-permute-start.8 = (bf16[256,1024]{1,0:T(8,128)(2,1)S(1)}, bf16[256,1024]{1,0:T(8,128)(2,1)S(1)}, u32[]{:S(2)}, u32[]{:S(2)}) collective-permute-start(bf16[256,1024]{1,0:T(8,128)(2,1)S(1)} %get-tuple-element.42), channel_id=1, source_target_pairs={{0,1},{1,0},{4,5},{5,4},{8,9},{9,8},{12,13},{13,12},{14,15},{15,14... | collective-permute-start | bytes 1572872 | tf_op jit(solution)/shard_map/ppermute | solution.py:174
  22.1 8.3 %collective-permute-start.9 = (bf16[256,1024]{1,0:T(8,128)(2,1)S(1)}, bf16[256,1024]{1,0:T(8,128)(2,1)S(1)}, u32[]{:S(2)}, u32[]{:S(2)}) collective-permute-start(bf16[256,1024]{1,0:T(8,128)(2,1)S(1)} %get-tuple-element.41), channel_id=1, source_target_pairs={{0,1},{1,0},{4,5},{5,4},{8,9},{9,8},{12,13},{13,12},{14,15},{15,14... | collective-permute-start | bytes 1572872 | tf_op jit(solution)/shard_map/ppermute | solution.py:174
  27.7 2.7 %collective-permute-start.10 = (bf16[256,1024]{1,0:T(8,128)(2,1)S(1)}, bf16[256,1024]{1,0:T(8,128)(2,1)S(1)}, u32[]{:S(2)}, u32[]{:S(2)}) collective-permute-start(bf16[256,1024]{1,0:T(8,128)(2,1)S(1)} %get-tuple-element.40), channel_id=1, source_target_pairs={{0,1},{1,0},{4,5},{5,4},{8,9},{9,8},{12,13},{13,12},{14,15},{15,14... | collective-permute-start | bytes 1572872 | tf_op jit(solution)/shard_map/ppermute | solution.py:174
  27.8 2.6 %collective-permute-start.11 = (bf16[256,1024]{1,0:T(8,128)(2,1)S(1)}, bf16[256,1024]{1,0:T(8,128)(2,1)S(1)}, u32[]{:S(2)}, u32[]{:S(2)}) collective-permute-start(bf16[256,1024]{1,0:T(8,128)(2,1)S(1)} %get-tuple-element.39), channel_id=1, source_target_pairs={{0,1},{1,0},{4,5},{5,4},{8,9},{9,8},{12,13},{13,12},{14,15},{15,14... | collective-permute-start | bytes 1572872 | tf_op jit(solution)/shard_map/ppermute | solution.py:174
  28.3 21.7 %collective-permute-start.18 = (bf16[512,1024]{1,0:T(8,128)(2,1)S(1)}, bf16[512,1024]{1,0:T(8,128)(2,1)S(1)}, u32[]{:S(2)}, u32[]{:S(2)}) collective-permute-start(bf16[512,1024]{1,0:T(8,128)(2,1)S(1)} %unit_rows.1.refs_1_), channel_id=1, source_target_pairs={{0,4},{1,3},{4,8},{5,1},{8,12},{9,5},{12,14},{13,9},{14,10},{15,13... | collective-permute-start | bytes 3145736 | tf_op jit(solution)/shard_map/ppermute | solution.py:174
  38.6 2.0 %collective-permute-start.15 = (bf16[256,1024]{1,0:T(8,128)(2,1)S(1)}, bf16[256,1024]{1,0:T(8,128)(2,1)S(1)}, u32[]{:S(2)}, u32[]{:S(2)}) collective-permute-start(bf16[256,1024]{1,0:T(8,128)(2,1)S(1)} %get-tuple-element.38), channel_id=1, source_target_pairs={{0,1},{1,0},{4,5},{5,4},{8,9},{9,8},{12,13},{13,12},{14,15},{15,14... | collective-permute-start | bytes 1572872 | tf_op jit(solution)/shard_map/ppermute | solution.py:174
  38.7 2.6 %collective-permute-start.16 = (bf16[256,1024]{1,0:T(8,128)(2,1)S(1)}, bf16[256,1024]{1,0:T(8,128)(2,1)S(1)}, u32[]{:S(2)}, u32[]{:S(2)}) collective-permute-start(bf16[256,1024]{1,0:T(8,128)(2,1)S(1)} %get-tuple-element.37), channel_id=1, source_target_pairs={{0,1},{1,0},{4,5},{5,4},{8,9},{9,8},{12,13},{13,12},{14,15},{15,14... | collective-permute-start | bytes 1572872 | tf_op jit(solution)/shard_map/ppermute | solution.py:174
  45.0 11.6 %collective-permute-start.17 = (f32[8,512]{1,0:T(8,128)S(1)}, f32[8,512]{1,0:T(8,128)S(1)}, u32[]{:S(2)}, u32[]{:S(2)}) collective-permute-start(f32[8,512]{1,0:T(8,128)S(1)} %get-tuple-element.35), channel_id=1, source_target_pairs={{0,6},{1,9},{4,2},{5,13},{8,0},{9,15},{12,4},{13,11},{14,8},{15,7}... | collective-permute-start | bytes 49160 | tf_op jit(solution)/shard_map/ppermute | solution.py:174
  48.1 7.2 %collective-permute-start.12 = (f32[1,512]{1,0:T(1,128)S(1)}, f32[1,512]{1,0:T(1,128)S(1)}, u32[]{:S(2)}, u32[]{:S(2)}) collective-permute-start(f32[1,512]{1,0:T(1,128)S(1)} %get-tuple-element.43), channel_id=1, source_target_pairs={{0,2},{1,5},{4,0},{5,9},{8,4},{9,13},{12,8},{13,15},{14,12},{15,11... | collective-permute-start | bytes 6152 | tf_op jit(solution)/shard_map/ppermute | solution.py:174
  49.7 5.6 %collective-permute-start.13 = (f32[1,512]{1,0:T(1,128)S(1)}, f32[1,512]{1,0:T(1,128)S(1)}, u32[]{:S(2)}, u32[]{:S(2)}) collective-permute-start(f32[1,512]{1,0:T(1,128)S(1)} %get-tuple-element.44), channel_id=1, source_target_pairs={{0,3},{1,4},{4,1},{5,8},{8,5},{9,12},{12,9},{13,14},{14,13},{15,10... | collective-permute-start | bytes 6152 | tf_op jit(solution)/shard_map/ppermute | solution.py:174
  52.7 4.0 %collective-permute-start.19 = (f32[1,512]{1,0:T(1,128)S(1)}, f32[1,512]{1,0:T(1,128)S(1)}, u32[]{:S(2)}, u32[]{:S(2)}) collective-permute-start(f32[1,512]{1,0:T(1,128)S(1)} %end_terms.3), channel_id=1, source_target_pairs={{0,7},{1,8},{4,3},{5,12},{8,1},{9,14},{12,5},{13,10},{14,9},{15,6}... | collective-permute-start | bytes 6152 | tf_op jit(solution)/shard_map/ppermute | solution.py:174

commit v6 on v5

--- a/solution.py
+++ b/solution.py
@@ -10,6 +10,7 @@
 STRIP = 256
 SPLIT = 2
 ROOM = 8
+END_ROOM = 4
 
 
 def unit_rows(values):
@@ -68,14 +69,13 @@
     return jnp.sum(jnp.transpose(x), axis=0, keepdims=True)
 
 
-def sums_kernel(clusters, blocks, lists, tasks, kept, near, *refs):
+def sums_kernel(clusters, blocks, lists, tasks, kept, added, near, *refs):
     units = []
     for pieces, *_ in blocks:
         units.append(refs[:pieces])
         refs = refs[pieces:]
     names, refs = refs[:lists], refs[lists:]
-    before, sums, refs = (refs[0], refs[1], refs[2:]) if kept is None else (None, refs[0], refs[1:])
-    kept = kept or ()
+    before, sums, refs = refs[:added], refs[added], refs[added + 1 :]
     given, scratch = refs[: len(kept)], list(refs[len(kept) :])
     codes = {}
 
@@ -93,8 +93,8 @@
             units[block] = target
         else:
             (units[block],) = units[block]
-    sums[...] = jnp.zeros_like(sums) if before is None else before[...]
-    for task, (block, others) in enumerate(tasks):
+    sums[...] = before[0][...] if added else jnp.zeros_like(sums)
+    for task, block, others in tasks:
         a_own, a_near = [as_column(row) for row in code(block)]
         place = blocks[block][-1]
         for here in strips(units[block].shape[0]):
@@ -108,10 +108,10 @@
                     same = row == lax.broadcasted_iota(jnp.int32, value.shape, 1)
                     value = jnp.where(same, 0.0, value)
                 total = total + lanes_added(value)
-            sums[task : task + 1, place + here.start : place + here.stop] = as_row(total)
-
-
-def row_sums(near, blocks, names, tasks, label, kept=(), before=None, room=0):
+            sums[task : task + 1, place + here.start : place + here.stop] += as_row(total)
+
+
+def row_sums(near, blocks, names, tasks, label, kept=(), before=None, room=1):
     blocks = [(block if isinstance(block, list) else [block], *rest) for block, *rest in blocks]
     width = blocks[0][0][0].shape[1]
     units = [
@@ -130,10 +130,11 @@
             [(len(block[0]), *block[1:]) for block in blocks],
             len(names),
             tasks,
-            kept if before is None else None,
+            kept,
+            int(before is not None),
         ),
         out_shape=[
-            jax.ShapeDtypeStruct((max(len(tasks), room), names[0].shape[1]), jnp.float32),
+            jax.ShapeDtypeStruct((room, names[0].shape[1]), jnp.float32),
             *[units[i] for i in kept],
         ],
         in_specs=[pl.BlockSpec(memory_space=pltpu.SMEM)] + [vmem] * len(operands),
@@ -182,8 +183,11 @@
     def against(place, core):
         return place - 1 + 2 * core, 1 - core
 
-    def back(distance, half):
+    def back(distance, half=0):
         return lambda place, core: (place - distance * (1 - 2 * core), core ^ half)
+
+    def split_swap(half):
+        return [other_core(part) for part in jnp.split(half, SPLIT)]
 
     name = owner.reshape(1, rows)
     other_name, other = other_core(name), other_core(embed)
@@ -196,7 +200,7 @@
         near,
         [(embed, True, 0, 0, 0), (other, True, 0, 1, 0)],
         [own_names],
-        ((0, (0, 1)),),
+        ((0, 0, (0, 1)),),
         "own_terms",
         (0,),
     )
@@ -204,41 +208,66 @@
     first, total, side_names, across_names = lax.optimization_barrier(
         (first, total, side_names, across_names)
     )
+    swapped = [None, [split_swap(first)]]
+    blocks = [(first, True, 0, 0, 0), (swapped[1][0], True, 1, 0, 0), (own[0], False, 2, 0, 0)]
+    sums, units = row_sums(
+        near,
+        blocks,
+        [side_names[1], across_names[1], own_names],
+        ((0, 0, (1,)), (2, 2, (0, 1))),
+        "first_terms",
+        (0, 1),
+        room=3,
+    )
+    second, sums = lax.optimization_barrier((second, sums))
     side = [None, [first, unit_block(second)]]
     for hop in range(2, hops + 1):
-        side.append([moved(half, onward) for half in side[-1]])
-    across = [None] + [
-        [[other_core(part) for part in jnp.split(half, SPLIT)] for half in pair]
-        for pair in side[1:hops]
-    ]
-
-    inner = None
+        halves = side[-1]
+        side.append([moved(half, onward) for half in halves])
+    across = [None, [swapped[1][0], split_swap(side[1][1])]]
+    across += [[split_swap(half) for half in pair] for pair in side[2:hops]]
+
+    inner, theirs = None, 0.0
     for hop in range(1, hops):
-        blocks = [(half, i == 0, 0, i, 0) for i, half in enumerate(side[hop])]
-        blocks += [(half, i == 0, 1, i, 0) for i, half in enumerate(across[hop])]
+        blocks = [(side[hop][0], True, 0, 0, 0), (across[hop][0], True, 1, 0, 0)]
         if hop == 1:
-            blocks += [(own[0], False, 2, 0, 0)]
-            names = [side_names[1], across_names[1], own_names]
-            tasks = ((0, (2, 3)), (1, (2, 3)), (4, (0, 1, 2, 3)))
+            extra, names = [(own[0], False, 2, 0, 0)], [side_names[1], across_names[1], own_names]
+            late = ((0, 0, (3,)), (1, 2, (1, 3)), (2, 4, (2, 3)))
         else:
-            blocks += [(half, False, 2, i, 0) for i, half in enumerate(inner)]
+            extra = [(unit, False, 2, i, 0) for i, unit in enumerate(inner)]
             names = [side_names[hop], across_names[hop], across_names[hop - 1]]
-            tasks = ((0, (2, 3, 4, 5)), (1, (2, 3, 4, 5)))
-        sums, inner = row_sums(near, blocks, names, tasks, "pair_terms", (2, 3))
-        for half in range(2):
-            total = total + moved(sums[half : half + 1], back(hop, half))
+            early = ((0, 0, (1, 2, 3)),)
+            late = ((0, 0, (3,)), (1, 2, (1, 3, 4, 5)))
+        if hop > 1:
+            sums, units = row_sums(
+                near, [*blocks, *extra], names, early, "first_terms", (0, 1), room=3
+            )
+        blocks = [(unit, False, i, 0, 0) for i, unit in enumerate(units)]
+        blocks += [(side[hop][1], False, 0, 1, 0), (across[hop][1], False, 1, 1, 0), *extra]
+        sums, (unit,) = row_sums(near, blocks, names, late, "pair_terms", (3,), before=sums, room=3)
+        inner = [units[1], unit]
+        returned = moved(sums[:2], back(hop))
         if hop == 1:
-            total = total + sums[2:]
-    facing, *inner = lax.optimization_barrier((side[hops][0], *inner))
-    facing = [other_core(part) for part in jnp.split(facing, SPLIT)]
+            total = total + sums[2:3]
+        if hop < hops - 1:
+            total, theirs = total + returned[:1], theirs + returned[1:]
+    facing, returned, *inner = lax.optimization_barrier((side[hops][0], returned, *inner))
+    facing = split_swap(facing)
+    total = total + returned[:1] + other_core(theirs + returned[1:])
     names = [side_names[hops], across_names[hops], across_names[hops - 1]]
-    others = [(unit, False, 2, i, 0) for i, unit in enumerate(inner)]
-    task = ((0, (1, 2, 3)),)
-    blocks = [(side[hops][0], True, 0, 0, 0), (facing, True, 1, 0, 0), *others]
-    sums, (facing,) = row_sums(near, blocks, names, task, "end_terms", (1,), room=ROOM)
-    total = total + moved(sums, back(hops, 0))[:1]
-    others = [(facing, False, 1, 0, 0), *others]
-    sums, _ = row_sums(near, [(side[hops][1], False, 0, 1, 0), *others], names, task, "end_terms")
+    blocks = [(side[hops][0], True, 0, 0, 0)]
+    blocks += [(unit, False, 2, i, 0) for i, unit in enumerate(inner)]
+    tasks = ((0, 0, (2,)), (1, 1, (0,)), (2, 2, (0,)))
+    sums, (unit,) = row_sums(near, blocks, names, tasks, "end_terms", (0,), room=ROOM)
+    for half in range(2):
+        total = total + moved(sums, back(1 - hops, 1 - half))[1 + half : 2 + half]
+    blocks = [(unit, False, 0, 0, 0), (facing, True, 1, 0, 0)]
+    sums, (facing,) = row_sums(
+        near, blocks, names, ((0, 0, (1,)),), "end_terms", (1,), before=sums[:END_ROOM], room=END_ROOM
+    )
+    total = total + moved(sums, back(hops))[:1]
+    blocks = [(side[hops][1], False, 0, 1, 0), (facing, False, 1, 0, 0), (inner[1], False, 2, 1, 0)]
+    sums, _ = row_sums(near, blocks, names, ((0, 0, (1, 2)),), "end_terms")
     total = total + moved(sums, back(hops, 1))
     return jnp.log1p(total)[0]
 

time: 57.7 us -> 56.8 us (0.984)
  waiting for transfers between devices: 15.4 us -> 10.7 us
  starting transfers between devices: 21.9 us -> 24.1 us
  Pallas kernels: 17.1 us -> 18.8 us
    ppermute x20 -> x22, waiting for transfers between devices: 15.4 us -> 10.7 us  [moved(): return lax.ppermute(block, 'blk', route)]
    ppermute x20 -> x22, starting transfers between devices: 21.9 us -> 24.1 us  [moved(): return lax.ppermute(block, 'blk', route)]
    pallas_call x4 -> x6, Pallas kernels: 16.8 us -> 18.5 us  [row_sums(): pl.pallas_call(functools.partial(sums_kernel, near.shape[0], [(len(block[...]
  transfers between devices with their start and end apart: 20 -> 22, of which waited for: 11 -> 10; matrix products, arithmetic and copies ran while one was open for 2% -> 2% of each run, Pallas kernels for 30% -> 33%
where the time goes in v6:
time: 56.8 us; the launch traced here: 56.6 us
  starting transfers between devices  24.1 us (42%)
  Pallas kernels  18.8 us (33%)
  waiting for transfers between devices  10.7 us (19%)
  local copies, waits for them, and re-layouts  1.45 us (3%)
  other arithmetic  1.37 us (2%)
    ppermute x22, starting transfers between devices, moved(): return lax.ppermute(block, 'blk', route)  24.1 us
    pallas_call x6, Pallas kernels, row_sums(): pl.pallas_call(functools.partial(sums_kernel, near.shape[0], [(len(block[...  18.5 us
    ppermute x22, waiting for transfers between devices, moved(): return lax.ppermute(block, 'blk', route)  10.7 us
    unnamed x4, local copies, waits for them, and re-layouts  1.23 us
  transfers between devices with their start and end apart: 22, of which 10 were waited for; matrix products, arithmetic and copies ran while one was open for 2% of the time, Pallas kernels for 33%

profile of v6, /device:TPU:0, one launch (start us, length us, event | category | flops | bytes accessed | tf_op | source)
XLA Modules:
  0.0 56.6 jit_solution(9727921945246717598)
XLA Ops:
  0.0 0.5 collective-permute-start.1
  0.5 2.6 %collective-permute-start = (bf16[512,1024]{1,0:T(8,128)(2,1)}, bf16[512,1024]{1,0:T(8,128)(2,1)S(1)}, u32[]{:S(2)}, u32[]{:S(2)}) collective-permute-start(bf16[512,1024]{1,0:T(8,128)(2,1)} %refs_0_.1), channel_id=1, source_target_pairs={{0,4},{1,3},{4,8},{5,1},{8,12},{9,5},{12,14},{13,9},{14,10},{15,13... | collective-permute-start | bytes 3145736 | tf_op jit(solution)/shard_map/ppermute | solution.py:175
  3.0 0.0 collective-permute-done.1.refs_1_
  3.0 2.9 %collective-permute-start.9 = (bf16[512,1024]{1,0:T(8,128)(2,1)S(1)}, bf16[512,1024]{1,0:T(8,128)(2,1)S(1)}, u32[]{:S(2)}, u32[]{:S(2)}) collective-permute-start(bf16[512,1024]{1,0:T(8,128)(2,1)S(1)} %collective-permute-done.1.refs_1_), channel_id=1, source_target_pairs={{0,4},{1,3},{4,8},{5,1},{8,12},{9,5},{12,14},{13,9},{14,10},{15,13... | collective-permute-start | bytes 3145736 | tf_op jit(solution)/shard_map/ppermute | solution.py:175
  5.9 0.0 collective-permute-start.2
  5.9 1.4 %collective-permute-done.2 = s32[1,512]{1,0:T(1,128)S(1)} collective-permute-done((s32[1,512]{1,0:T(1,128)}, s32[1,512]{1,0:T(1,128)S(1)}, u32[]{:S(2)}, u32[]{:S(2)}) %collective-permute-start.2) | collective-permute-done | bytes 2080 | tf_op jit(solution)/shard_map/ppermute | solution.py:175
  7.3 0.8 %pad_add_fusion.1 = (s32[2,512]{1,0:T(2,128)S(1)}, s32[2,512]{1,0:T(2,128)S(1)}) fusion(s32[1,512]{1,0:T(1,128)} %bitcast.3, s32[1,512]{1,0:T(1,128)S(1)} %collective-permute-done.2), kind=kLoop, calls=%fused_computation.1 | loop fusion | flops 2048 | bytes 12288 | tf_op jit(solution)/shard_map/concatenate | solution.py:195
  8.0 0.0 copy-start.1
  8.0 1.0 %collective-permute-start.3 = (s32[2,512]{1,0:T(2,128)S(1)}, s32[2,512]{1,0:T(2,128)S(1)}, u32[]{:S(2)}, u32[]{:S(2)}) collective-permute-start(s32[2,512]{1,0:T(2,128)S(1)} %get-tuple-element.57), channel_id=1, source_target_pairs={{0,3},{1,4},{4,1},{5,8},{8,5},{9,12},{12,9},{13,14},{14,13},{15,10... | collective-permute-start | bytes 12296 | tf_op jit(solution)/shard_map/ppermute | solution.py:175
  9.1 2.2 %collective-permute-done.3.refs_4_.refs_6_ = s32[2,512]{1,0:T(2,128)S(1)} collective-permute-done((s32[2,512]{1,0:T(2,128)S(1)}, s32[2,512]{1,0:T(2,128)S(1)}, u32[]{:S(2)}, u32[]{:S(2)}) %collective-permute-start.3) | collective-permute-done | bytes 4128 | tf_op jit(solution)/shard_map/ppermute | solution.py:175
  11.3 0.5 collective-permute-start.4
  11.7 0.8 %collective-permute-done.4.refs_5_.refs_7_ = s32[2,512]{1,0:T(2,128)S(1)} collective-permute-done((s32[2,512]{1,0:T(2,128)S(1)}, s32[2,512]{1,0:T(2,128)S(1)}, u32[]{:S(2)}, u32[]{:S(2)}) %collective-permute-start.4) | collective-permute-done | bytes 4128 | tf_op jit(solution)/shard_map/ppermute | solution.py:175
  12.5 1.2 %collective-permute-start.5 = (s32[2,512]{1,0:T(2,128)S(1)}, s32[2,512]{1,0:T(2,128)S(1)}, u32[]{:S(2)}, u32[]{:S(2)}) collective-permute-start(s32[2,512]{1,0:T(2,128)S(1)} %collective-permute-done.4.refs_5_.refs_7_), channel_id=1, source_target_pairs={{0,3},{1,4},{4,1},{5,8},{8,5},{9,12},{12,9},{13,14},{14,13},{15,10... | collective-permute-start | bytes 12296 | tf_op jit(solution)/shard_map/ppermute | solution.py:175
  13.7 2.0 %collective-permute-done.5.refs_3_ = s32[2,512]{1,0:T(2,128)S(1)} collective-permute-done((s32[2,512]{1,0:T(2,128)S(1)}, s32[2,512]{1,0:T(2,128)S(1)}, u32[]{:S(2)}, u32[]{:S(2)}) %collective-permute-start.5) | collective-permute-done | bytes 4128 | tf_op jit(solution)/shard_map/ppermute | solution.py:175
  15.7 0.6 %collective-permute-start.6 = (s32[2,512]{1,0:T(2,128)S(1)}, s32[2,512]{1,0:T(2,128)S(1)}, u32[]{:S(2)}, u32[]{:S(2)}) collective-permute-start(s32[2,512]{1,0:T(2,128)S(1)} %collective-permute-done.5.refs_3_), channel_id=1, source_target_pairs={{0,1},{1,0},{4,5},{5,4},{8,9},{9,8},{12,13},{13,12},{14,15},{15,14... | collective-permute-start | bytes 12296 | tf_op jit(solution)/shard_map/ppermute | solution.py:175
  16.3 0.0 copy-done.1
  16.3 0.0 copy-start
  16.3 1.2 %copy-done = bf16[512,1024]{1,0:T(8,128)(2,1)S(1)} copy-done((bf16[512,1024]{1,0:T(8,128)(2,1)S(1)}, bf16[512,1024]{1,0:T(8,128)(2,1)}, u32[]{:S(2)}) %copy-start) | copy-done | bytes 1048600
  17.5 2.7 %own_terms.1 = (f32[1,512]{1,0:T(1,128)S(1)}, bf16[512,1024]{1,0:T(8,128)(2,1)S(1)}) custom-call(s32[16]{0:T(128)S(1)} %copy-done.1, bf16[512,1024]{1,0:T(8,128)(2,1)S(1)} %copy-done, bf16[512,1024]{1,0:T(8,128)(2,1)S(1)} %collective-permute-done.1.refs_1_, s32[2,512]{1,0:T(2,128)S(1)} %get-tuple-element.58.refs_2_.refs_6_.refs_8_), custom_call_target="tpu_custom_call" | custom-call | tf_op jit(solution)/shard_map/own_terms/pallas_call | solution.py:126
  20.3 0.0 collective-permute-done.6.refs_4_
  20.3 0.0 collective-permute-done.refs_0_
  20.3 0.1 fusion.4
  20.4 0.1 collective-permute-start.8
  20.4 0.5 collective-permute-start.7
  20.9 1.6 %collective-permute-start.12 = (bf16[512,1024]{1,0:T(8,128)(2,1)S(1)}, bf16[512,1024]{1,0:T(8,128)(2,1)S(1)}, u32[]{:S(2)}, u32[]{:S(2)}) collective-permute-start(bf16[512,1024]{1,0:T(8,128)(2,1)S(1)} %collective-permute-done.refs_0_), channel_id=1, source_target_pairs={{0,4},{1,3},{4,8},{5,1},{8,12},{9,5},{12,14},{13,9},{14,10},{15,13... | collective-permute-start | bytes 3145736 | tf_op jit(solution)/shard_map/ppermute | solution.py:175
  22.5 0.0 collective-permute-done.8.refs_2_
  22.5 0.6 %collective-permute-done.7.refs_1_ = bf16[256,1024]{1,0:T(8,128)(2,1)S(1)} collective-permute-done((bf16[256,1024]{1,0:T(8,128)(2,1)S(1)}, bf16[256,1024]{1,0:T(8,128)(2,1)S(1)}, u32[]{:S(2)}, u32[]{:S(2)}) %collective-permute-start.7) | collective-permute-done | bytes 524320 | tf_op jit(solution)/shard_map/ppermute | solution.py:175
  23.1 3.9 %first_terms.1 = (f32[3,512]{1,0:T(4,128)S(1)}, bf16[512,1024]{1,0:T(8,128)(2,1)S(1)}, bf16[512,1024]{1,0:T(8,128)(2,1)S(1)}) custom-call(s32[16]{0:T(128)S(1)} %copy-done.1, bf16[512,1024]{1,0:T(8,128)(2,1)S(1)} %collective-permute-done.refs_0_, bf16[256,1024]{1,0:T(8,128)(2,1)S(1)} %collective-permute-done.7.refs_1_, ...), custom_call_target="tpu_custom_call" | custom-call | tf_op jit(solution)/shard_map/first_terms/pallas_call | solution.py:126
  27.0 0.3 collective-permute-done.9.source
  27.3 0.3 unit_rows.1.refs_2_
  27.6 0.1 fusion.3
  27.7 0.1 collective-permute-start.11
  27.8 0.5 collective-permute-start.10
  28.3 2.1 %collective-permute-start.20 = (bf16[512,1024]{1,0:T(8,128)(2,1)S(1)}, bf16[512,1024]{1,0:T(8,128)(2,1)S(1)}, u32[]{:S(2)}, u32[]{:S(2)}) collective-permute-start(bf16[512,1024]{1,0:T(8,128)(2,1)S(1)} %unit_rows.1.refs_2_), channel_id=1, source_target_pairs={{0,4},{1,3},{4,8},{5,1},{8,12},{9,5},{12,14},{13,9},{14,10},{15,13... | collective-permute-start | bytes 3145736 | tf_op jit(solution)/shard_map/ppermute | solution.py:175
  30.4 0.0 collective-permute-done.11.refs_4_
  30.4 0.1 collective-permute-done.10.refs_3_
  30.4 4.6 %pair_terms.1 = (f32[3,512]{1,0:T(4,128)S(1)}, bf16[512,1024]{1,0:T(8,128)(2,1)S(1)}) custom-call(s32[16]{0:T(128)S(1)} %copy-done.1, bf16[512,1024]{1,0:T(8,128)(2,1)S(1)} %get-tuple-element.34.refs_0_, bf16[512,1024]{1,0:T(8,128)(2,1)S(1)} %get-tuple-element.42.refs_1_, bf16[512,1024]{1,0:T(8,128)(2,1)S(1)} %unit_rows.1.refs_2_, ...), custom_call_target="tpu_custom_call" | custom-call | tf_op jit(solution)/shard_map/pair_terms/pallas_call | solution.py:126
  35.0 2.3 %collective-permute-start.13 = (f32[2,512]{1,0:T(2,128)S(1)}, f32[2,512]{1,0:T(2,128)S(1)}, u32[]{:S(2)}, u32[]{:S(2)}) collective-permute-start(f32[2,512]{1,0:T(2,128)S(1)} %slice.25), channel_id=1, source_target_pairs={{0,2},{1,5},{4,0},{5,9},{8,4},{9,13},{12,8},{13,15},{14,12},{15,11... | collective-permute-start | bytes 12296 | tf_op jit(solution)/shard_map/ppermute | solution.py:175
  37.3 1.3 %collective-permute-done.12.refs_0_ = bf16[512,1024]{1,0:T(8,128)(2,1)S(1)} collective-permute-done((bf16[512,1024]{1,0:T(8,128)(2,1)S(1)}, bf16[512,1024]{1,0:T(8,128)(2,1)S(1)}, u32[]{:S(2)}, u32[]{:S(2)}) %collective-permute-start.12) | collective-permute-done | bytes 1048608 | tf_op jit(solution)/shard_map/ppermute | solution.py:175
  38.6 0.5 collective-permute-done.13
  39.0 0.1 fusion.2
  39.1 0.1 collective-permute-start.18
  39.2 0.5 collective-permute-start.17
  39.7 3.3 %end_terms.3 = (f32[8,512]{1,0:T(8,128)S(1)}, bf16[512,1024]{1,0:T(8,128)(2,1)S(1)}) custom-call(s32[16]{0:T(128)S(1)} %copy-done.1, bf16[512,1024]{1,0:T(8,128)(2,1)S(1)} %collective-permute-done.12.refs_0_, bf16[512,1024]{1,0:T(8,128)(2,1)S(1)} %get-tuple-element.42.refs_1_, bf16[512,1024]{1,0:T(8,128)(2,1)S(1)} %get-tuple-element.43.refs_2_, ...), custom_call_target="tpu_custom_call" | custom-call | tf_op jit(solution)/shard_map/end_terms/pallas_call | solution.py:126
  43.0 2.1 %collective-permute-start.16 = (f32[8,512]{1,0:T(8,128)S(1)}, f32[8,512]{1,0:T(8,128)S(1)}, u32[]{:S(2)}, u32[]{:S(2)}) collective-permute-start(f32[8,512]{1,0:T(8,128)S(1)} %get-tuple-element.46), channel_id=1, source_target_pairs={{0,4},{1,3},{4,8},{5,1},{8,12},{9,5},{12,14},{13,9},{14,10},{15,13... | collective-permute-start | bytes 49160 | tf_op jit(solution)/shard_map/ppermute | solution.py:175
  45.1 0.0 collective-permute-start.15
  45.1 0.0 collective-permute-done.18.refs_2_
  45.1 0.0 collective-permute-done.17.refs_1_
  45.1 1.8 %end_terms.4 = (f32[4,512]{1,0:T(4,128)S(1)}, bf16[512,1024]{1,0:T(8,128)(2,1)S(1)}) custom-call(s32[16]{0:T(128)S(1)} %copy-done.1, bf16[512,1024]{1,0:T(8,128)(2,1)S(1)} %get-tuple-element.47.refs_0_, bf16[256,1024]{1,0:T(8,128)(2,1)S(1)} %collective-permute-done.17.refs_1_, bf16[256,1024]{1,0:T(8,128)(2,1)S(1)} %collective-permute-done.18.refs_2_, ...), custom_call_target="tpu_custom_call" | custom-call | tf_op jit(solution)/shard_map/end_terms/pallas_call | solution.py:126
  47.0 2.4 %collective-permute-start.19 = (f32[4,512]{1,0:T(4,128)S(1)}, f32[4,512]{1,0:T(4,128)S(1)}, u32[]{:S(2)}, u32[]{:S(2)}) collective-permute-start(f32[4,512]{1,0:T(4,128)S(1)} %get-tuple-element.49), channel_id=1, source_target_pairs={{0,6},{1,9},{4,2},{5,13},{8,0},{9,15},{12,4},{13,11},{14,8},{15,7}... | collective-permute-start | bytes 24584 | tf_op jit(solution)/shard_map/ppermute | solution.py:175
  49.4 0.5 collective-permute-start.14
  49.9 0.0 collective-permute-done.20.refs_0_
  49.9 2.2 %end_terms.5 = f32[1,512]{1,0:T(1,128)S(1)} custom-call(s32[16]{0:T(128)S(1)} %copy-done.1, bf16[512,1024]{1,0:T(8,128)(2,1)S(1)} %collective-permute-done.20.refs_0_, bf16[512,1024]{1,0:T(8,128)(2,1)S(1)} %get-tuple-element.50.refs_1_, bf16[512,1024]{1,0:T(8,128)(2,1)S(1)} %get-tuple-element.43.refs_2_, s32[2,512]{1,0:T(2,128)S(1)} %collective-permute-done.5.refs_3_, ...), custom_call_target="tpu_custom_call" | custom-call | tf_op jit(solution)/shard_map/end_terms/pallas_call | solution.py:126
  52.0 2.3 %collective-permute-start.21 = (f32[1,512]{1,0:T(1,128)S(1)}, f32[1,512]{1,0:T(1,128)S(1)}, u32[]{:S(2)}, u32[]{:S(2)}) collective-permute-start(f32[1,512]{1,0:T(1,128)S(1)} %end_terms.5), channel_id=1, source_target_pairs={{0,7},{1,8},{4,3},{5,12},{8,1},{9,14},{12,5},{13,10},{14,9},{15,6}... | collective-permute-start | bytes 6152 | tf_op jit(solution)/shard_map/ppermute | solution.py:175
  54.3 0.0 collective-permute-done.14
  54.3 0.0 collective-permute-done.16
  54.3 0.0 collective-permute-done.15
  54.3 1.7 %collective-permute-done.21 = f32[1,512]{1,0:T(1,128)S(1)} collective-permute-done((f32[1,512]{1,0:T(1,128)S(1)}, f32[1,512]{1,0:T(1,128)S(1)}, u32[]{:S(2)}, u32[]{:S(2)}) %collective-permute-start.21) | collective-permute-done | bytes 2080 | tf_op jit(solution)/shard_map/ppermute | solution.py:175
  56.0 0.0 collective-permute-done.19
  56.0 0.6 %fusion.1 = f32[1,512]{1,0:T(1,128)} fusion(f32[1,512]{1,0:T(1,128)S(1)} %collective-permute-done.21, f32[4,512]{1,0:T(4,128)S(1)} %collective-permute-done.19, f32[8,512]{1,0:T(8,128)S(1)} %collective-permute-done.16, f32[8,512]{1,0:T(8,128)S(1)} %collective-permute-done.15, f32[1,512]{1,0:T(1,128)S(1)} %collective-permute-done.14, ...), kind=kLoop, calls=%fused_computation.6 | loop fusion | flops 3584 | bytes 18432 | tf_op jit(solution)/shard_map/log1p | solution.py:272
  (3 shorter events, 0.0 us)
Async XLA Ops:
  0.0 3.0 %collective-permute-start.1 = (bf16[512,1024]{1,0:T(8,128)(2,1)}, bf16[512,1024]{1,0:T(8,128)(2,1)S(1)}, u32[]{:S(2)}, u32[]{:S(2)}) collective-permute-start(bf16[512,1024]{1,0:T(8,128)(2,1)} %refs_0_.1), channel_id=1, source_target_pairs={{0,1},{1,0},{4,5},{5,4},{8,9},{9,8},{12,13},{13,12},{14,15},{15,14... | collective-permute-start | bytes 3145736 | tf_op jit(solution)/shard_map/ppermute | solution.py:175
  0.5 19.8 %collective-permute-start = (bf16[512,1024]{1,0:T(8,128)(2,1)}, bf16[512,1024]{1,0:T(8,128)(2,1)S(1)}, u32[]{:S(2)}, u32[]{:S(2)}) collective-permute-start(bf16[512,1024]{1,0:T(8,128)(2,1)} %refs_0_.1), channel_id=1, source_target_pairs={{0,4},{1,3},{4,8},{5,1},{8,12},{9,5},{12,14},{13,9},{14,10},{15,13... | collective-permute-start | bytes 3145736 | tf_op jit(solution)/shard_map/ppermute | solution.py:175
  3.0 24.2 %collective-permute-start.9 = (bf16[512,1024]{1,0:T(8,128)(2,1)S(1)}, bf16[512,1024]{1,0:T(8,128)(2,1)S(1)}, u32[]{:S(2)}, u32[]{:S(2)}) collective-permute-start(bf16[512,1024]{1,0:T(8,128)(2,1)S(1)} %collective-permute-done.1.refs_1_), channel_id=1, source_target_pairs={{0,4},{1,3},{4,8},{5,1},{8,12},{9,5},{12,14},{13,9},{14,10},{15,13... | collective-permute-start | bytes 3145736 | tf_op jit(solution)/shard_map/ppermute | solution.py:175
  5.9 1.4 %collective-permute-start.2 = (s32[1,512]{1,0:T(1,128)}, s32[1,512]{1,0:T(1,128)S(1)}, u32[]{:S(2)}, u32[]{:S(2)}) collective-permute-start(s32[1,512]{1,0:T(1,128)} %bitcast.2), channel_id=1, source_target_pairs={{0,1},{1,0},{4,5},{5,4},{8,9},{9,8},{12,13},{13,12},{14,15},{15,14... | collective-permute-start | bytes 6152 | tf_op jit(solution)/shard_map/ppermute | solution.py:175
  8.0 8.3 %copy-start.1 = (s32[16]{0:T(128)S(1)}, s32[16]{0:T(128)}, u32[]{:S(2)}) copy-start(s32[16]{0:T(128)} %near.11) | copy-start | bytes 196
  8.0 3.2 %collective-permute-start.3 = (s32[2,512]{1,0:T(2,128)S(1)}, s32[2,512]{1,0:T(2,128)S(1)}, u32[]{:S(2)}, u32[]{:S(2)}) collective-permute-start(s32[2,512]{1,0:T(2,128)S(1)} %get-tuple-element.57), channel_id=1, source_target_pairs={{0,3},{1,4},{4,1},{5,8},{8,5},{9,12},{12,9},{13,14},{14,13},{15,10... | collective-permute-start | bytes 12296 | tf_op jit(solution)/shard_map/ppermute | solution.py:175
  11.3 1.3 %collective-permute-start.4 = (s32[2,512]{1,0:T(2,128)S(1)}, s32[2,512]{1,0:T(2,128)S(1)}, u32[]{:S(2)}, u32[]{:S(2)}) collective-permute-start(s32[2,512]{1,0:T(2,128)S(1)} %collective-permute-done.3.refs_4_.refs_6_), channel_id=1, source_target_pairs={{0,1},{1,0},{4,5},{5,4},{8,9},{9,8},{12,13},{13,12},{14,15},{15,14... | collective-permute-start | bytes 12296 | tf_op jit(solution)/shard_map/ppermute | solution.py:175
  12.5 3.1 %collective-permute-start.5 = (s32[2,512]{1,0:T(2,128)S(1)}, s32[2,512]{1,0:T(2,128)S(1)}, u32[]{:S(2)}, u32[]{:S(2)}) collective-permute-start(s32[2,512]{1,0:T(2,128)S(1)} %collective-permute-done.4.refs_5_.refs_7_), channel_id=1, source_target_pairs={{0,3},{1,4},{4,1},{5,8},{8,5},{9,12},{12,9},{13,14},{14,13},{15,10... | collective-permute-start | bytes 12296 | tf_op jit(solution)/shard_map/ppermute | solution.py:175
  15.7 4.6 %collective-permute-start.6 = (s32[2,512]{1,0:T(2,128)S(1)}, s32[2,512]{1,0:T(2,128)S(1)}, u32[]{:S(2)}, u32[]{:S(2)}) collective-permute-start(s32[2,512]{1,0:T(2,128)S(1)} %collective-permute-done.5.refs_3_), channel_id=1, source_target_pairs={{0,1},{1,0},{4,5},{5,4},{8,9},{9,8},{12,13},{13,12},{14,15},{15,14... | collective-permute-start | bytes 12296 | tf_op jit(solution)/shard_map/ppermute | solution.py:175
  16.3 1.2 %copy-start = (bf16[512,1024]{1,0:T(8,128)(2,1)S(1)}, bf16[512,1024]{1,0:T(8,128)(2,1)}, u32[]{:S(2)}) copy-start(bf16[512,1024]{1,0:T(8,128)(2,1)} %refs_0_.1) | copy-start | bytes 3145732
  20.4 2.2 %collective-permute-start.8 = (bf16[256,1024]{1,0:T(8,128)(2,1)S(1)}, bf16[256,1024]{1,0:T(8,128)(2,1)S(1)}, u32[]{:S(2)}, u32[]{:S(2)}) collective-permute-start(bf16[256,1024]{1,0:T(8,128)(2,1)S(1)} %get-tuple-element.55), channel_id=1, source_target_pairs={{0,1},{1,0},{4,5},{5,4},{8,9},{9,8},{12,13},{13,12},{14,15},{15,14... | collective-permute-start | bytes 1572872 | tf_op jit(solution)/shard_map/ppermute | solution.py:175
  20.4 2.6 %collective-permute-start.7 = (bf16[256,1024]{1,0:T(8,128)(2,1)S(1)}, bf16[256,1024]{1,0:T(8,128)(2,1)S(1)}, u32[]{:S(2)}, u32[]{:S(2)}) collective-permute-start(bf16[256,1024]{1,0:T(8,128)(2,1)S(1)} %get-tuple-element.56), channel_id=1, source_target_pairs={{0,1},{1,0},{4,5},{5,4},{8,9},{9,8},{12,13},{13,12},{14,15},{15,14... | collective-permute-start | bytes 1572872 | tf_op jit(solution)/shard_map/ppermute | solution.py:175
  20.9 17.6 %collective-permute-start.12 = (bf16[512,1024]{1,0:T(8,128)(2,1)S(1)}, bf16[512,1024]{1,0:T(8,128)(2,1)S(1)}, u32[]{:S(2)}, u32[]{:S(2)}) collective-permute-start(bf16[512,1024]{1,0:T(8,128)(2,1)S(1)} %collective-permute-done.refs_0_), channel_id=1, source_target_pairs={{0,4},{1,3},{4,8},{5,1},{8,12},{9,5},{12,14},{13,9},{14,10},{15,13... | collective-permute-start | bytes 3145736 | tf_op jit(solution)/shard_map/ppermute | solution.py:175
  27.7 2.7 %collective-permute-start.11 = (bf16[256,1024]{1,0:T(8,128)(2,1)S(1)}, bf16[256,1024]{1,0:T(8,128)(2,1)S(1)}, u32[]{:S(2)}, u32[]{:S(2)}) collective-permute-start(bf16[256,1024]{1,0:T(8,128)(2,1)S(1)} %get-tuple-element.53), channel_id=1, source_target_pairs={{0,1},{1,0},{4,5},{5,4},{8,9},{9,8},{12,13},{13,12},{14,15},{15,14... | collective-permute-start | bytes 1572872 | tf_op jit(solution)/shard_map/ppermute | solution.py:175
  27.8 2.6 %collective-permute-start.10 = (bf16[256,1024]{1,0:T(8,128)(2,1)S(1)}, bf16[256,1024]{1,0:T(8,128)(2,1)S(1)}, u32[]{:S(2)}, u32[]{:S(2)}) collective-permute-start(bf16[256,1024]{1,0:T(8,128)(2,1)S(1)} %get-tuple-element.54), channel_id=1, source_target_pairs={{0,1},{1,0},{4,5},{5,4},{8,9},{9,8},{12,13},{13,12},{14,15},{15,14... | collective-permute-start | bytes 1572872 | tf_op jit(solution)/shard_map/ppermute | solution.py:175
  28.3 21.6 %collective-permute-start.20 = (bf16[512,1024]{1,0:T(8,128)(2,1)S(1)}, bf16[512,1024]{1,0:T(8,128)(2,1)S(1)}, u32[]{:S(2)}, u32[]{:S(2)}) collective-permute-start(bf16[512,1024]{1,0:T(8,128)(2,1)S(1)} %unit_rows.1.refs_2_), channel_id=1, source_target_pairs={{0,4},{1,3},{4,8},{5,1},{8,12},{9,5},{12,14},{13,9},{14,10},{15,13... | collective-permute-start | bytes 3145736 | tf_op jit(solution)/shard_map/ppermute | solution.py:175
  35.0 4.0 %collective-permute-start.13 = (f32[2,512]{1,0:T(2,128)S(1)}, f32[2,512]{1,0:T(2,128)S(1)}, u32[]{:S(2)}, u32[]{:S(2)}) collective-permute-start(f32[2,512]{1,0:T(2,128)S(1)} %slice.25), channel_id=1, source_target_pairs={{0,2},{1,5},{4,0},{5,9},{8,4},{9,13},{12,8},{13,15},{14,12},{15,11... | collective-permute-start | bytes 12296 | tf_op jit(solution)/shard_map/ppermute | solution.py:175
  39.1 6.0 %collective-permute-start.18 = (bf16[256,1024]{1,0:T(8,128)(2,1)S(1)}, bf16[256,1024]{1,0:T(8,128)(2,1)S(1)}, u32[]{:S(2)}, u32[]{:S(2)}) collective-permute-start(bf16[256,1024]{1,0:T(8,128)(2,1)S(1)} %get-tuple-element.51), channel_id=1, source_target_pairs={{0,1},{1,0},{4,5},{5,4},{8,9},{9,8},{12,13},{13,12},{14,15},{15,14... | collective-permute-start | bytes 1572872 | tf_op jit(solution)/shard_map/ppermute | solution.py:175
  39.2 5.9 %collective-permute-start.17 = (bf16[256,1024]{1,0:T(8,128)(2,1)S(1)}, bf16[256,1024]{1,0:T(8,128)(2,1)S(1)}, u32[]{:S(2)}, u32[]{:S(2)}) collective-permute-start(bf16[256,1024]{1,0:T(8,128)(2,1)S(1)} %get-tuple-element.52), channel_id=1, source_target_pairs={{0,1},{1,0},{4,5},{5,4},{8,9},{9,8},{12,13},{13,12},{14,15},{15,14... | collective-permute-start | bytes 1572872 | tf_op jit(solution)/shard_map/ppermute | solution.py:175
  43.0 11.3 %collective-permute-start.16 = (f32[8,512]{1,0:T(8,128)S(1)}, f32[8,512]{1,0:T(8,128)S(1)}, u32[]{:S(2)}, u32[]{:S(2)}) collective-permute-start(f32[8,512]{1,0:T(8,128)S(1)} %get-tuple-element.46), channel_id=1, source_target_pairs={{0,4},{1,3},{4,8},{5,1},{8,12},{9,5},{12,14},{13,9},{14,10},{15,13... | collective-permute-start | bytes 49160 | tf_op jit(solution)/shard_map/ppermute | solution.py:175
  45.1 9.2 %collective-permute-start.15 = (f32[8,512]{1,0:T(8,128)S(1)}, f32[8,512]{1,0:T(8,128)S(1)}, u32[]{:S(2)}, u32[]{:S(2)}) collective-permute-start(f32[8,512]{1,0:T(8,128)S(1)} %get-tuple-element.46), channel_id=1, source_target_pairs={{0,5},{1,2},{4,9},{5,0},{8,13},{9,4},{12,15},{13,8},{14,11},{15,12... | collective-permute-start | bytes 49160 | tf_op jit(solution)/shard_map/ppermute | solution.py:175
  47.0 9.0 %collective-permute-start.19 = (f32[4,512]{1,0:T(4,128)S(1)}, f32[4,512]{1,0:T(4,128)S(1)}, u32[]{:S(2)}, u32[]{:S(2)}) collective-permute-start(f32[4,512]{1,0:T(4,128)S(1)} %get-tuple-element.49), channel_id=1, source_target_pairs={{0,6},{1,9},{4,2},{5,13},{8,0},{9,15},{12,4},{13,11},{14,8},{15,7}... | collective-permute-start | bytes 24584 | tf_op jit(solution)/shard_map/ppermute | solution.py:175
  49.4 4.9 %collective-permute-start.14 = (f32[1,512]{1,0:T(1,128)S(1)}, f32[1,512]{1,0:T(1,128)S(1)}, u32[]{:S(2)}, u32[]{:S(2)}) collective-permute-start(f32[1,512]{1,0:T(1,128)S(1)} %slice.27), channel_id=1, source_target_pairs={{0,1},{1,0},{4,5},{5,4},{8,9},{9,8},{12,13},{13,12},{14,15},{15,14... | collective-permute-start | bytes 6152 | tf_op jit(solution)/shard_map/ppermute | solution.py:175
  52.0 4.0 %collective-permute-start.21 = (f32[1,512]{1,0:T(1,128)S(1)}, f32[1,512]{1,0:T(1,128)S(1)}, u32[]{:S(2)}, u32[]{:S(2)}) collective-permute-start(f32[1,512]{1,0:T(1,128)S(1)} %end_terms.5), channel_id=1, source_target_pairs={{0,7},{1,8},{4,3},{5,12},{8,1},{9,14},{12,5},{13,10},{14,9},{15,6}... | collective-permute-start | bytes 6152 | tf_op jit(solution)/shard_map/ppermute | solution.py:175

commit v7 on v6

--- a/solution.py
+++ b/solution.py
@@ -69,7 +69,7 @@
     return jnp.sum(jnp.transpose(x), axis=0, keepdims=True)
 
 
-def sums_kernel(clusters, blocks, lists, tasks, kept, added, near, *refs):
+def sums_kernel(blocks, lists, tasks, kept, added, *refs):
     units = []
     for pieces, *_ in blocks:
         units.append(refs[:pieces])
@@ -82,8 +82,8 @@
     def code(block):
         if block not in codes:
             *_, at, row, place = blocks[block]
-            own = names[at][row : row + 1, place : place + units[block].shape[0]]
-            codes[block] = own, nearest(own, near, clusters)
+            here = slice(place, place + units[block].shape[0])
+            codes[block] = names[at][row : row + 1, here], names[at][row + 2 : row + 3, here]
         return codes[block]
 
     for block, (pieces, raw, *_) in enumerate(blocks):
@@ -111,7 +111,7 @@
             sums[task : task + 1, place + here.start : place + here.stop] += as_row(total)
 
 
-def row_sums(near, blocks, names, tasks, label, kept=(), before=None, room=1):
+def row_sums(blocks, names, tasks, label, kept=(), before=None, room=1):
     blocks = [(block if isinstance(block, list) else [block], *rest) for block, *rest in blocks]
     width = blocks[0][0][0].shape[1]
     units = [
@@ -126,7 +126,6 @@
     sums, *given = pl.pallas_call(
         functools.partial(
             sums_kernel,
-            near.shape[0],
             [(len(block[0]), *block[1:]) for block in blocks],
             len(names),
             tasks,
@@ -137,14 +136,36 @@
             jax.ShapeDtypeStruct((room, names[0].shape[1]), jnp.float32),
             *[units[i] for i in kept],
         ],
-        in_specs=[pl.BlockSpec(memory_space=pltpu.SMEM)] + [vmem] * len(operands),
+        in_specs=[vmem] * len(operands),
         out_specs=[vmem] * (1 + len(kept)),
         scratch_shapes=[pltpu.VMEM(units[i].shape, jnp.bfloat16) for i in scratch],
         compiler_params=pltpu.CompilerParams(vmem_limit_bytes=40 << 20),
         cost_estimate=pl.CostEstimate(flops=0, bytes_accessed=0, transcendentals=0),
         name=label,
-    )(near, *operands)
+    )(*operands)
     return sums, given
+
+
+def names_kernel(clusters, near, name, other, mine, swapped):
+    both = [ref[...] for ref in (name, other)]
+    both += [nearest(own, near, clusters) for own in both]
+    for at, row in enumerate(both):
+        mine[at : at + 1, :] = row
+        swapped[at ^ 1 : (at ^ 1) + 1, :] = row
+
+
+def name_tables(near, name, other):
+    table = jax.ShapeDtypeStruct((4, name.shape[1]), jnp.int32)
+    vmem = pl.BlockSpec(memory_space=pltpu.VMEM)
+    return pl.pallas_call(
+        functools.partial(names_kernel, near.shape[0]),
+        out_shape=(table, table),
+        in_specs=[pl.BlockSpec(memory_space=pltpu.SMEM), vmem, vmem],
+        out_specs=(vmem, vmem),
+        compiler_params=pltpu.CompilerParams(vmem_limit_bytes=40 << 20),
+        cost_estimate=pl.CostEstimate(flops=0, bytes_accessed=0, transcendentals=0),
+        name="name_tables",
+    )(near, name, other)
 
 
 def unit_block(rows):
@@ -191,13 +212,12 @@
 
     name = owner.reshape(1, rows)
     other_name, other = other_core(name), other_core(embed)
-    own_names = jnp.concatenate([name, other_name], axis=0)
-    side_names, across_names = [own_names], [jnp.concatenate([other_name, name], axis=0)]
+    own_names, swapped_names = name_tables(near, name, other_name)
+    side_names, across_names = [own_names], [swapped_names]
     for hop in range(1, hops + 1):
         side_names.append(moved(across_names[-1], against))
         across_names.append(other_core(side_names[-1]))
     total, own = row_sums(
-        near,
         [(embed, True, 0, 0, 0), (other, True, 0, 1, 0)],
         [own_names],
         ((0, 0, (0, 1)),),
@@ -211,7 +231,6 @@
     swapped = [None, [split_swap(first)]]
     blocks = [(first, True, 0, 0, 0), (swapped[1][0], True, 1, 0, 0), (own[0], False, 2, 0, 0)]
     sums, units = row_sums(
-        near,
         blocks,
         [side_names[1], across_names[1], own_names],
         ((0, 0, (1,)), (2, 2, (0, 1))),
@@ -240,11 +259,11 @@
             late = ((0, 0, (3,)), (1, 2, (1, 3, 4, 5)))
         if hop > 1:
             sums, units = row_sums(
-                near, [*blocks, *extra], names, early, "first_terms", (0, 1), room=3
+                [*blocks, *extra], names, early, "first_terms", (0, 1), room=3
             )
         blocks = [(unit, False, i, 0, 0) for i, unit in enumerate(units)]
         blocks += [(side[hop][1], False, 0, 1, 0), (across[hop][1], False, 1, 1, 0), *extra]
-        sums, (unit,) = row_sums(near, blocks, names, late, "pair_terms", (3,), before=sums, room=3)
+        sums, (unit,) = row_sums(blocks, names, late, "pair_terms", (3,), before=sums, room=3)
         inner = [units[1], unit]
         returned = moved(sums[:2], back(hop))
         if hop == 1:
@@ -258,16 +277,16 @@
     blocks = [(side[hops][0], True, 0, 0, 0)]
     blocks += [(unit, False, 2, i, 0) for i, unit in enumerate(inner)]
     tasks = ((0, 0, (2,)), (1, 1, (0,)), (2, 2, (0,)))
-    sums, (unit,) = row_sums(near, blocks, names, tasks, "end_terms", (0,), room=ROOM)
+    sums, (unit,) = row_sums(blocks, names, tasks, "end_terms", (0,), room=ROOM)
     for half in range(2):
         total = total + moved(sums, back(1 - hops, 1 - half))[1 + half : 2 + half]
     blocks = [(unit, False, 0, 0, 0), (facing, True, 1, 0, 0)]
     sums, (facing,) = row_sums(
-        near, blocks, names, ((0, 0, (1,)),), "end_terms", (1,), before=sums[:END_ROOM], room=END_ROOM
+        blocks, names, ((0, 0, (1,)),), "end_terms", (1,), before=sums[:END_ROOM], room=END_ROOM
     )
     total = total + moved(sums, back(hops))[:1]
     blocks = [(side[hops][1], False, 0, 1, 0), (facing, False, 1, 0, 0), (inner[1], False, 2, 1, 0)]
-    sums, _ = row_sums(near, blocks, names, ((0, 0, (1, 2)),), "end_terms")
+    sums, _ = row_sums(blocks, names, ((0, 0, (1, 2)),), "end_terms")
     total = total + moved(sums, back(hops, 1))
     return jnp.log1p(total)[0]
 

time: 56.8 us -> 56.6 us (level)
  Pallas kernels: 18.8 us -> 16.1 us
  waiting for transfers between devices: 10.7 us -> 13.2 us
  other arithmetic: 1.37 us -> 0.6 us
  local copies, waits for them, and re-layouts: 1.45 us -> 2.13 us
    pallas_call x6 -> x7, Pallas kernels: 18.5 us -> 15.8 us  [the longest x6 15.2 us: row_sums(): pl.pallas_call(functools.partial(sums_kernel, [(len(block[0]), *block[1:]...]
    ppermute x22, waiting for transfers between devices: 10.7 us -> 13.2 us  [moved(): return lax.ppermute(block, 'blk', route)]
    concatenate x1 -> x0, other arithmetic: 0.77 us -> none  [per_device(): jnp.concatenate([other_name, name], axis=0)]
    unnamed x4 -> x6, local copies, waits for them, and re-layouts: 1.23 us -> 1.91 us
  transfers between devices with their start and end apart: 22 -> 22, of which waited for: 10 -> 10; matrix products, arithmetic and copies ran while one was open for 2% -> 0% of each run, Pallas kernels for 33% -> 29%
where the time goes in v7:
time: 56.6 us; the launch traced here: 56.2 us
  starting transfers between devices  24.1 us (43%)
  Pallas kernels  16.1 us (28%)
  waiting for transfers between devices  13.2 us (23%)
  local copies, waits for them, and re-layouts  2.13 us (4%)
  other arithmetic  0.6 us (1%)
    ppermute x22, starting transfers between devices, moved(): return lax.ppermute(block, 'blk', route)  24.1 us
    pallas_call x6, Pallas kernels, row_sums(): pl.pallas_call(functools.partial(sums_kernel, [(len(block[0]), *block[1:]...  15.2 us
    ppermute x22, waiting for transfers between devices, moved(): return lax.ppermute(block, 'blk', route)  13.2 us
    unnamed x6, local copies, waits for them, and re-layouts  1.91 us
  transfers between devices with their start and end apart: 22, of which 10 were waited for; matrix products, arithmetic and copies ran while one was open for 0% of the time, Pallas kernels for 29%

profile of v7, /device:TPU:0, one launch (start us, length us, event | category | flops | bytes accessed | tf_op | source)
XLA Modules:
  0.0 56.2 jit_solution(28880521116704141)
XLA Ops:
  0.0 0.0 copy-start.2
  0.0 0.5 collective-permute-start.1
  0.5 2.6 %collective-permute-start = (bf16[512,1024]{1,0:T(8,128)(2,1)}, bf16[512,1024]{1,0:T(8,128)(2,1)S(1)}, u32[]{:S(2)}, u32[]{:S(2)}) collective-permute-start(bf16[512,1024]{1,0:T(8,128)(2,1)} %refs_0_.1), channel_id=1, source_target_pairs={{0,4},{1,3},{4,8},{5,1},{8,12},{9,5},{12,14},{13,9},{14,10},{15,13... | collective-permute-start | bytes 3145736 | tf_op jit(solution)/shard_map/ppermute | solution.py:196
  3.1 0.0 collective-permute-done.1.refs_1_
  3.1 2.8 %collective-permute-start.9 = (bf16[512,1024]{1,0:T(8,128)(2,1)S(1)}, bf16[512,1024]{1,0:T(8,128)(2,1)S(1)}, u32[]{:S(2)}, u32[]{:S(2)}) collective-permute-start(bf16[512,1024]{1,0:T(8,128)(2,1)S(1)} %collective-permute-done.1.refs_1_), channel_id=1, source_target_pairs={{0,4},{1,3},{4,8},{5,1},{8,12},{9,5},{12,14},{13,9},{14,10},{15,13... | collective-permute-start | bytes 3145736 | tf_op jit(solution)/shard_map/ppermute | solution.py:196
  5.9 0.0 collective-permute-start.2
  5.9 1.4 %collective-permute-done.2.other = s32[1,512]{1,0:T(1,128)S(1)} collective-permute-done((s32[1,512]{1,0:T(1,128)}, s32[1,512]{1,0:T(1,128)S(1)}, u32[]{:S(2)}, u32[]{:S(2)}) %collective-permute-start.2) | collective-permute-done | bytes 2080 | tf_op jit(solution)/shard_map/ppermute | solution.py:196
  7.3 0.0 copy-done.2
  7.3 0.0 copy-start.1
  7.3 0.7 %copy-done.1 = s32[512,1]{0,1:T(1,128)S(1)} copy-done((s32[512,1]{0,1:T(1,128)S(1)}, s32[512,1]{0,1:T(1,128)}, u32[]{:S(2)}) %copy-start.1) | copy-done | bytes 2072
  8.0 0.6 name_tables.1
  8.5 1.0 %collective-permute-start.3 = (s32[4,512]{1,0:T(4,128)S(1)}, s32[4,512]{1,0:T(4,128)S(1)}, u32[]{:S(2)}, u32[]{:S(2)}) collective-permute-start(s32[4,512]{1,0:T(4,128)S(1)} %get-tuple-element.32), channel_id=1, source_target_pairs={{0,3},{1,4},{4,1},{5,8},{8,5},{9,12},{12,9},{13,14},{14,13},{15,10... | collective-permute-start | bytes 24584 | tf_op jit(solution)/shard_map/ppermute | solution.py:196
  9.6 2.2 %collective-permute-done.3.refs_4_.refs_6_ = s32[4,512]{1,0:T(4,128)S(1)} collective-permute-done((s32[4,512]{1,0:T(4,128)S(1)}, s32[4,512]{1,0:T(4,128)S(1)}, u32[]{:S(2)}, u32[]{:S(2)}) %collective-permute-start.3) | collective-permute-done | bytes 8224 | tf_op jit(solution)/shard_map/ppermute | solution.py:196
  11.8 0.5 collective-permute-start.4
  12.3 0.8 %collective-permute-done.4.refs_5_.refs_7_ = s32[4,512]{1,0:T(4,128)S(1)} collective-permute-done((s32[4,512]{1,0:T(4,128)S(1)}, s32[4,512]{1,0:T(4,128)S(1)}, u32[]{:S(2)}, u32[]{:S(2)}) %collective-permute-start.4) | collective-permute-done | bytes 8224 | tf_op jit(solution)/shard_map/ppermute | solution.py:196
  13.1 1.1 %collective-permute-start.5 = (s32[4,512]{1,0:T(4,128)S(1)}, s32[4,512]{1,0:T(4,128)S(1)}, u32[]{:S(2)}, u32[]{:S(2)}) collective-permute-start(s32[4,512]{1,0:T(4,128)S(1)} %collective-permute-done.4.refs_5_.refs_7_), channel_id=1, source_target_pairs={{0,3},{1,4},{4,1},{5,8},{8,5},{9,12},{12,9},{13,14},{14,13},{15,10... | collective-permute-start | bytes 24584 | tf_op jit(solution)/shard_map/ppermute | solution.py:196
  14.3 2.1 %collective-permute-done.5.refs_3_ = s32[4,512]{1,0:T(4,128)S(1)} collective-permute-done((s32[4,512]{1,0:T(4,128)S(1)}, s32[4,512]{1,0:T(4,128)S(1)}, u32[]{:S(2)}, u32[]{:S(2)}) %collective-permute-start.5) | collective-permute-done | bytes 8224 | tf_op jit(solution)/shard_map/ppermute | solution.py:196
  16.3 0.6 %collective-permute-start.6 = (s32[4,512]{1,0:T(4,128)S(1)}, s32[4,512]{1,0:T(4,128)S(1)}, u32[]{:S(2)}, u32[]{:S(2)}) collective-permute-start(s32[4,512]{1,0:T(4,128)S(1)} %collective-permute-done.5.refs_3_), channel_id=1, source_target_pairs={{0,1},{1,0},{4,5},{5,4},{8,9},{9,8},{12,13},{13,12},{14,15},{15,14... | collective-permute-start | bytes 24584 | tf_op jit(solution)/shard_map/ppermute | solution.py:196
  17.0 0.0 copy-start
  17.0 1.2 %copy-done = bf16[512,1024]{1,0:T(8,128)(2,1)S(1)} copy-done((bf16[512,1024]{1,0:T(8,128)(2,1)S(1)}, bf16[512,1024]{1,0:T(8,128)(2,1)}, u32[]{:S(2)}) %copy-start) | copy-done | bytes 1048600
  18.2 2.2 %own_terms.1 = (f32[1,512]{1,0:T(1,128)S(1)}, bf16[512,1024]{1,0:T(8,128)(2,1)S(1)}) custom-call(bf16[512,1024]{1,0:T(8,128)(2,1)S(1)} %copy-done, bf16[512,1024]{1,0:T(8,128)(2,1)S(1)} %collective-permute-done.1.refs_1_, s32[4,512]{1,0:T(4,128)S(1)} %get-tuple-element.30.refs_2_.refs_6_.refs_8_), custom_call_target="tpu_custom_call" | custom-call | tf_op jit(solution)/shard_map/own_terms/pallas_call | solution.py:126
  20.4 0.0 collective-permute-done.6.refs_4_
  20.4 0.0 collective-permute-done.refs_0_
  20.4 0.1 fusion.4
  20.5 0.1 collective-permute-start.8
  20.6 0.5 collective-permute-start.7
  21.1 1.6 %collective-permute-start.12 = (bf16[512,1024]{1,0:T(8,128)(2,1)S(1)}, bf16[512,1024]{1,0:T(8,128)(2,1)S(1)}, u32[]{:S(2)}, u32[]{:S(2)}) collective-permute-start(bf16[512,1024]{1,0:T(8,128)(2,1)S(1)} %collective-permute-done.refs_0_), channel_id=1, source_target_pairs={{0,4},{1,3},{4,8},{5,1},{8,12},{9,5},{12,14},{13,9},{14,10},{15,13... | collective-permute-start | bytes 3145736 | tf_op jit(solution)/shard_map/ppermute | solution.py:196
  22.6 0.0 collective-permute-done.8.refs_2_
  22.6 0.6 %collective-permute-done.7.refs_1_ = bf16[256,1024]{1,0:T(8,128)(2,1)S(1)} collective-permute-done((bf16[256,1024]{1,0:T(8,128)(2,1)S(1)}, bf16[256,1024]{1,0:T(8,128)(2,1)S(1)}, u32[]{:S(2)}, u32[]{:S(2)}) %collective-permute-start.7) | collective-permute-done | bytes 524320 | tf_op jit(solution)/shard_map/ppermute | solution.py:196
  23.2 3.2 %first_terms.1 = (f32[3,512]{1,0:T(4,128)S(1)}, bf16[512,1024]{1,0:T(8,128)(2,1)S(1)}, bf16[512,1024]{1,0:T(8,128)(2,1)S(1)}) custom-call(bf16[512,1024]{1,0:T(8,128)(2,1)S(1)} %collective-permute-done.refs_0_, bf16[256,1024]{1,0:T(8,128)(2,1)S(1)} %collective-permute-done.7.refs_1_, bf16[256,1024]{1,0:T(8,128)(2,1)S(1)} %collective-permute-done.8.refs_2_, ...), custom_call_target="tpu_custom_call" | custom-call | tf_op jit(solution)/shard_map/first_terms/pallas_call | solution.py:126
  26.4 1.0 %collective-permute-done.9.source = bf16[512,1024]{1,0:T(8,128)(2,1)S(1)} collective-permute-done((bf16[512,1024]{1,0:T(8,128)(2,1)S(1)}, bf16[512,1024]{1,0:T(8,128)(2,1)S(1)}, u32[]{:S(2)}, u32[]{:S(2)}) %collective-permute-start.9) | collective-permute-done | bytes 1048608 | tf_op jit(solution)/shard_map/ppermute | solution.py:196
  27.4 0.3 unit_rows.1.refs_2_
  27.8 0.1 fusion.3
  27.8 0.1 collective-permute-start.11
  27.9 0.5 collective-permute-start.10
  28.4 2.1 %collective-permute-start.20 = (bf16[512,1024]{1,0:T(8,128)(2,1)S(1)}, bf16[512,1024]{1,0:T(8,128)(2,1)S(1)}, u32[]{:S(2)}, u32[]{:S(2)}) collective-permute-start(bf16[512,1024]{1,0:T(8,128)(2,1)S(1)} %unit_rows.1.refs_2_), channel_id=1, source_target_pairs={{0,4},{1,3},{4,8},{5,1},{8,12},{9,5},{12,14},{13,9},{14,10},{15,13... | collective-permute-start | bytes 3145736 | tf_op jit(solution)/shard_map/ppermute | solution.py:196
  30.5 0.0 collective-permute-done.11.refs_4_
  30.5 0.1 collective-permute-done.10.refs_3_
  30.6 4.1 %pair_terms.1 = (f32[3,512]{1,0:T(4,128)S(1)}, bf16[512,1024]{1,0:T(8,128)(2,1)S(1)}) custom-call(bf16[512,1024]{1,0:T(8,128)(2,1)S(1)} %get-tuple-element.38.refs_0_, bf16[512,1024]{1,0:T(8,128)(2,1)S(1)} %get-tuple-element.46.refs_1_, bf16[512,1024]{1,0:T(8,128)(2,1)S(1)} %unit_rows.1.refs_2_, bf16[256,1024]{1,0:T(8,128)(2,1)S(1)} %collective-permute-done.10.refs_3_, ...), custom_call_target="tpu_custom_call" | custom-call | tf_op jit(solution)/shard_map/pair_terms/pallas_call | solution.py:126
  34.7 2.3 %collective-permute-start.13 = (f32[2,512]{1,0:T(2,128)S(1)}, f32[2,512]{1,0:T(2,128)S(1)}, u32[]{:S(2)}, u32[]{:S(2)}) collective-permute-start(f32[2,512]{1,0:T(2,128)S(1)} %slice.25), channel_id=1, source_target_pairs={{0,2},{1,5},{4,0},{5,9},{8,4},{9,13},{12,8},{13,15},{14,12},{15,11... | collective-permute-start | bytes 12296 | tf_op jit(solution)/shard_map/ppermute | solution.py:196
  37.0 1.7 %collective-permute-done.12.refs_0_ = bf16[512,1024]{1,0:T(8,128)(2,1)S(1)} collective-permute-done((bf16[512,1024]{1,0:T(8,128)(2,1)S(1)}, bf16[512,1024]{1,0:T(8,128)(2,1)S(1)}, u32[]{:S(2)}, u32[]{:S(2)}) %collective-permute-start.12) | collective-permute-done | bytes 1048608 | tf_op jit(solution)/shard_map/ppermute | solution.py:196
  38.7 0.0 collective-permute-done.13
  38.7 0.1 fusion.2
  38.8 0.1 collective-permute-start.18
  38.9 0.5 collective-permute-start.17
  39.4 2.8 %end_terms.3 = (f32[8,512]{1,0:T(8,128)S(1)}, bf16[512,1024]{1,0:T(8,128)(2,1)S(1)}) custom-call(bf16[512,1024]{1,0:T(8,128)(2,1)S(1)} %collective-permute-done.12.refs_0_, bf16[512,1024]{1,0:T(8,128)(2,1)S(1)} %get-tuple-element.46.refs_1_, bf16[512,1024]{1,0:T(8,128)(2,1)S(1)} %get-tuple-element.47.refs_2_, s32[4,512]{1,0:T(4,128)S(1)} %collective-permute-done.5.refs_3_, ...), custom_call_target="tpu_custom_call" | custom-call | tf_op jit(solution)/shard_map/end_terms/pallas_call | solution.py:126
  42.2 2.1 %collective-permute-start.16 = (f32[8,512]{1,0:T(8,128)S(1)}, f32[8,512]{1,0:T(8,128)S(1)}, u32[]{:S(2)}, u32[]{:S(2)}) collective-permute-start(f32[8,512]{1,0:T(8,128)S(1)} %get-tuple-element.50), channel_id=1, source_target_pairs={{0,4},{1,3},{4,8},{5,1},{8,12},{9,5},{12,14},{13,9},{14,10},{15,13... | collective-permute-start | bytes 49160 | tf_op jit(solution)/shard_map/ppermute | solution.py:196
  44.3 0.0 collective-permute-start.15
  44.3 0.0 collective-permute-done.18.refs_2_
  44.3 0.0 collective-permute-done.17.refs_1_
  44.3 1.3 %end_terms.4 = (f32[4,512]{1,0:T(4,128)S(1)}, bf16[512,1024]{1,0:T(8,128)(2,1)S(1)}) custom-call(bf16[512,1024]{1,0:T(8,128)(2,1)S(1)} %get-tuple-element.51.refs_0_, bf16[256,1024]{1,0:T(8,128)(2,1)S(1)} %collective-permute-done.17.refs_1_, bf16[256,1024]{1,0:T(8,128)(2,1)S(1)} %collective-permute-done.18.refs_2_, ...), custom_call_target="tpu_custom_call" | custom-call | tf_op jit(solution)/shard_map/end_terms/pallas_call | solution.py:126
  45.6 2.4 %collective-permute-start.19 = (f32[4,512]{1,0:T(4,128)S(1)}, f32[4,512]{1,0:T(4,128)S(1)}, u32[]{:S(2)}, u32[]{:S(2)}) collective-permute-start(f32[4,512]{1,0:T(4,128)S(1)} %get-tuple-element.53), channel_id=1, source_target_pairs={{0,6},{1,9},{4,2},{5,13},{8,0},{9,15},{12,4},{13,11},{14,8},{15,7}... | collective-permute-start | bytes 24584 | tf_op jit(solution)/shard_map/ppermute | solution.py:196
  48.0 0.5 collective-permute-start.14
  48.5 1.5 %collective-permute-done.20.refs_0_ = bf16[512,1024]{1,0:T(8,128)(2,1)S(1)} collective-permute-done((bf16[512,1024]{1,0:T(8,128)(2,1)S(1)}, bf16[512,1024]{1,0:T(8,128)(2,1)S(1)}, u32[]{:S(2)}, u32[]{:S(2)}) %collective-permute-start.20) | collective-permute-done | bytes 1048608 | tf_op jit(solution)/shard_map/ppermute | solution.py:196
  50.0 1.6 %end_terms.5 = f32[1,512]{1,0:T(1,128)S(1)} custom-call(bf16[512,1024]{1,0:T(8,128)(2,1)S(1)} %collective-permute-done.20.refs_0_, bf16[512,1024]{1,0:T(8,128)(2,1)S(1)} %get-tuple-element.54.refs_1_, bf16[512,1024]{1,0:T(8,128)(2,1)S(1)} %get-tuple-element.47.refs_2_, s32[4,512]{1,0:T(4,128)S(1)} %collective-permute-done.5.refs_3_, ...), custom_call_target="tpu_custom_call" | custom-call | tf_op jit(solution)/shard_map/end_terms/pallas_call | solution.py:126
  51.7 2.2 %collective-permute-start.21 = (f32[1,512]{1,0:T(1,128)S(1)}, f32[1,512]{1,0:T(1,128)S(1)}, u32[]{:S(2)}, u32[]{:S(2)}) collective-permute-start(f32[1,512]{1,0:T(1,128)S(1)} %end_terms.5), channel_id=1, source_target_pairs={{0,7},{1,8},{4,3},{5,12},{8,1},{9,14},{12,5},{13,10},{14,9},{15,6}... | collective-permute-start | bytes 6152 | tf_op jit(solution)/shard_map/ppermute | solution.py:196
  53.9 0.0 collective-permute-done.14
  53.9 0.0 collective-permute-done.16
  53.9 0.0 collective-permute-done.15
  53.9 1.7 %collective-permute-done.21 = f32[1,512]{1,0:T(1,128)S(1)} collective-permute-done((f32[1,512]{1,0:T(1,128)S(1)}, f32[1,512]{1,0:T(1,128)S(1)}, u32[]{:S(2)}, u32[]{:S(2)}) %collective-permute-start.21) | collective-permute-done | bytes 2080 | tf_op jit(solution)/shard_map/ppermute | solution.py:196
  55.6 0.0 collective-permute-done.19
  55.6 0.6 %fusion.1 = f32[1,512]{1,0:T(1,128)} fusion(f32[1,512]{1,0:T(1,128)S(1)} %collective-permute-done.21, f32[4,512]{1,0:T(4,128)S(1)} %collective-permute-done.19, f32[8,512]{1,0:T(8,128)S(1)} %collective-permute-done.16, f32[8,512]{1,0:T(8,128)S(1)} %collective-permute-done.15, f32[1,512]{1,0:T(1,128)S(1)} %collective-permute-done.14, ...), kind=kLoop, calls=%fused_computation.4 | loop fusion | flops 3584 | bytes 18432 | tf_op jit(solution)/shard_map/log1p | solution.py:291
  (3 shorter events, 0.0 us)
Async XLA Ops:
  0.0 7.3 %copy-start.2 = (s32[16]{0:T(128)S(1)}, s32[16]{0:T(128)}, u32[]{:S(2)}) copy-start(s32[16]{0:T(128)} %near.1) | copy-start | bytes 196
  0.0 3.1 %collective-permute-start.1 = (bf16[512,1024]{1,0:T(8,128)(2,1)}, bf16[512,1024]{1,0:T(8,128)(2,1)S(1)}, u32[]{:S(2)}, u32[]{:S(2)}) collective-permute-start(bf16[512,1024]{1,0:T(8,128)(2,1)} %refs_0_.1), channel_id=1, source_target_pairs={{0,1},{1,0},{4,5},{5,4},{8,9},{9,8},{12,13},{13,12},{14,15},{15,14... | collective-permute-start | bytes 3145736 | tf_op jit(solution)/shard_map/ppermute | solution.py:196
  0.5 19.9 %collective-permute-start = (bf16[512,1024]{1,0:T(8,128)(2,1)}, bf16[512,1024]{1,0:T(8,128)(2,1)S(1)}, u32[]{:S(2)}, u32[]{:S(2)}) collective-permute-start(bf16[512,1024]{1,0:T(8,128)(2,1)} %refs_0_.1), channel_id=1, source_target_pairs={{0,4},{1,3},{4,8},{5,1},{8,12},{9,5},{12,14},{13,9},{14,10},{15,13... | collective-permute-start | bytes 3145736 | tf_op jit(solution)/shard_map/ppermute | solution.py:196
  3.1 24.3 %collective-permute-start.9 = (bf16[512,1024]{1,0:T(8,128)(2,1)S(1)}, bf16[512,1024]{1,0:T(8,128)(2,1)S(1)}, u32[]{:S(2)}, u32[]{:S(2)}) collective-permute-start(bf16[512,1024]{1,0:T(8,128)(2,1)S(1)} %collective-permute-done.1.refs_1_), channel_id=1, source_target_pairs={{0,4},{1,3},{4,8},{5,1},{8,12},{9,5},{12,14},{13,9},{14,10},{15,13... | collective-permute-start | bytes 3145736 | tf_op jit(solution)/shard_map/ppermute | solution.py:196
  5.9 1.4 %collective-permute-start.2 = (s32[1,512]{1,0:T(1,128)}, s32[1,512]{1,0:T(1,128)S(1)}, u32[]{:S(2)}, u32[]{:S(2)}) collective-permute-start(s32[1,512]{1,0:T(1,128)} %bitcast.2), channel_id=1, source_target_pairs={{0,1},{1,0},{4,5},{5,4},{8,9},{9,8},{12,13},{13,12},{14,15},{15,14... | collective-permute-start | bytes 6152 | tf_op jit(solution)/shard_map/ppermute | solution.py:196
  7.3 0.7 %copy-start.1 = (s32[512,1]{0,1:T(1,128)S(1)}, s32[512,1]{0,1:T(1,128)}, u32[]{:S(2)}) copy-start(s32[512,1]{0,1:T(1,128)} %param.4) | copy-start | bytes 6148
  8.5 3.3 %collective-permute-start.3 = (s32[4,512]{1,0:T(4,128)S(1)}, s32[4,512]{1,0:T(4,128)S(1)}, u32[]{:S(2)}, u32[]{:S(2)}) collective-permute-start(s32[4,512]{1,0:T(4,128)S(1)} %get-tuple-element.32), channel_id=1, source_target_pairs={{0,3},{1,4},{4,1},{5,8},{8,5},{9,12},{12,9},{13,14},{14,13},{15,10... | collective-permute-start | bytes 24584 | tf_op jit(solution)/shard_map/ppermute | solution.py:196
  11.8 1.3 %collective-permute-start.4 = (s32[4,512]{1,0:T(4,128)S(1)}, s32[4,512]{1,0:T(4,128)S(1)}, u32[]{:S(2)}, u32[]{:S(2)}) collective-permute-start(s32[4,512]{1,0:T(4,128)S(1)} %collective-permute-done.3.refs_4_.refs_6_), channel_id=1, source_target_pairs={{0,1},{1,0},{4,5},{5,4},{8,9},{9,8},{12,13},{13,12},{14,15},{15,14... | collective-permute-start | bytes 24584 | tf_op jit(solution)/shard_map/ppermute | solution.py:196
  13.1 3.2 %collective-permute-start.5 = (s32[4,512]{1,0:T(4,128)S(1)}, s32[4,512]{1,0:T(4,128)S(1)}, u32[]{:S(2)}, u32[]{:S(2)}) collective-permute-start(s32[4,512]{1,0:T(4,128)S(1)} %collective-permute-done.4.refs_5_.refs_7_), channel_id=1, source_target_pairs={{0,3},{1,4},{4,1},{5,8},{8,5},{9,12},{12,9},{13,14},{14,13},{15,10... | collective-permute-start | bytes 24584 | tf_op jit(solution)/shard_map/ppermute | solution.py:196
  16.3 4.0 %collective-permute-start.6 = (s32[4,512]{1,0:T(4,128)S(1)}, s32[4,512]{1,0:T(4,128)S(1)}, u32[]{:S(2)}, u32[]{:S(2)}) collective-permute-start(s32[4,512]{1,0:T(4,128)S(1)} %collective-permute-done.5.refs_3_), channel_id=1, source_target_pairs={{0,1},{1,0},{4,5},{5,4},{8,9},{9,8},{12,13},{13,12},{14,15},{15,14... | collective-permute-start | bytes 24584 | tf_op jit(solution)/shard_map/ppermute | solution.py:196
  17.0 1.2 %copy-start = (bf16[512,1024]{1,0:T(8,128)(2,1)S(1)}, bf16[512,1024]{1,0:T(8,128)(2,1)}, u32[]{:S(2)}) copy-start(bf16[512,1024]{1,0:T(8,128)(2,1)} %refs_0_.1) | copy-start | bytes 3145732
  20.5 2.2 %collective-permute-start.8 = (bf16[256,1024]{1,0:T(8,128)(2,1)S(1)}, bf16[256,1024]{1,0:T(8,128)(2,1)S(1)}, u32[]{:S(2)}, u32[]{:S(2)}) collective-permute-start(bf16[256,1024]{1,0:T(8,128)(2,1)S(1)} %get-tuple-element.59), channel_id=1, source_target_pairs={{0,1},{1,0},{4,5},{5,4},{8,9},{9,8},{12,13},{13,12},{14,15},{15,14... | collective-permute-start | bytes 1572872 | tf_op jit(solution)/shard_map/ppermute | solution.py:196
  20.6 2.6 %collective-permute-start.7 = (bf16[256,1024]{1,0:T(8,128)(2,1)S(1)}, bf16[256,1024]{1,0:T(8,128)(2,1)S(1)}, u32[]{:S(2)}, u32[]{:S(2)}) collective-permute-start(bf16[256,1024]{1,0:T(8,128)(2,1)S(1)} %get-tuple-element.60), channel_id=1, source_target_pairs={{0,1},{1,0},{4,5},{5,4},{8,9},{9,8},{12,13},{13,12},{14,15},{15,14... | collective-permute-start | bytes 1572872 | tf_op jit(solution)/shard_map/ppermute | solution.py:196
  21.1 17.6 %collective-permute-start.12 = (bf16[512,1024]{1,0:T(8,128)(2,1)S(1)}, bf16[512,1024]{1,0:T(8,128)(2,1)S(1)}, u32[]{:S(2)}, u32[]{:S(2)}) collective-permute-start(bf16[512,1024]{1,0:T(8,128)(2,1)S(1)} %collective-permute-done.refs_0_), channel_id=1, source_target_pairs={{0,4},{1,3},{4,8},{5,1},{8,12},{9,5},{12,14},{13,9},{14,10},{15,13... | collective-permute-start | bytes 3145736 | tf_op jit(solution)/shard_map/ppermute | solution.py:196
  27.8 2.7 %collective-permute-start.11 = (bf16[256,1024]{1,0:T(8,128)(2,1)S(1)}, bf16[256,1024]{1,0:T(8,128)(2,1)S(1)}, u32[]{:S(2)}, u32[]{:S(2)}) collective-permute-start(bf16[256,1024]{1,0:T(8,128)(2,1)S(1)} %get-tuple-element.57), channel_id=1, source_target_pairs={{0,1},{1,0},{4,5},{5,4},{8,9},{9,8},{12,13},{13,12},{14,15},{15,14... | collective-permute-start | bytes 1572872 | tf_op jit(solution)/shard_map/ppermute | solution.py:196
  27.9 2.6 %collective-permute-start.10 = (bf16[256,1024]{1,0:T(8,128)(2,1)S(1)}, bf16[256,1024]{1,0:T(8,128)(2,1)S(1)}, u32[]{:S(2)}, u32[]{:S(2)}) collective-permute-start(bf16[256,1024]{1,0:T(8,128)(2,1)S(1)} %get-tuple-element.58), channel_id=1, source_target_pairs={{0,1},{1,0},{4,5},{5,4},{8,9},{9,8},{12,13},{13,12},{14,15},{15,14... | collective-permute-start | bytes 1572872 | tf_op jit(solution)/shard_map/ppermute | solution.py:196
  28.4 21.6 %collective-permute-start.20 = (bf16[512,1024]{1,0:T(8,128)(2,1)S(1)}, bf16[512,1024]{1,0:T(8,128)(2,1)S(1)}, u32[]{:S(2)}, u32[]{:S(2)}) collective-permute-start(bf16[512,1024]{1,0:T(8,128)(2,1)S(1)} %unit_rows.1.refs_2_), channel_id=1, source_target_pairs={{0,4},{1,3},{4,8},{5,1},{8,12},{9,5},{12,14},{13,9},{14,10},{15,13... | collective-permute-start | bytes 3145736 | tf_op jit(solution)/shard_map/ppermute | solution.py:196
  34.7 4.0 %collective-permute-start.13 = (f32[2,512]{1,0:T(2,128)S(1)}, f32[2,512]{1,0:T(2,128)S(1)}, u32[]{:S(2)}, u32[]{:S(2)}) collective-permute-start(f32[2,512]{1,0:T(2,128)S(1)} %slice.25), channel_id=1, source_target_pairs={{0,2},{1,5},{4,0},{5,9},{8,4},{9,13},{12,8},{13,15},{14,12},{15,11... | collective-permute-start | bytes 12296 | tf_op jit(solution)/shard_map/ppermute | solution.py:196
  38.8 5.5 %collective-permute-start.18 = (bf16[256,1024]{1,0:T(8,128)(2,1)S(1)}, bf16[256,1024]{1,0:T(8,128)(2,1)S(1)}, u32[]{:S(2)}, u32[]{:S(2)}) collective-permute-start(bf16[256,1024]{1,0:T(8,128)(2,1)S(1)} %get-tuple-element.55), channel_id=1, source_target_pairs={{0,1},{1,0},{4,5},{5,4},{8,9},{9,8},{12,13},{13,12},{14,15},{15,14... | collective-permute-start | bytes 1572872 | tf_op jit(solution)/shard_map/ppermute | solution.py:196
  38.9 5.5 %collective-permute-start.17 = (bf16[256,1024]{1,0:T(8,128)(2,1)S(1)}, bf16[256,1024]{1,0:T(8,128)(2,1)S(1)}, u32[]{:S(2)}, u32[]{:S(2)}) collective-permute-start(bf16[256,1024]{1,0:T(8,128)(2,1)S(1)} %get-tuple-element.56), channel_id=1, source_target_pairs={{0,1},{1,0},{4,5},{5,4},{8,9},{9,8},{12,13},{13,12},{14,15},{15,14... | collective-permute-start | bytes 1572872 | tf_op jit(solution)/shard_map/ppermute | solution.py:196
  42.2 11.7 %collective-permute-start.16 = (f32[8,512]{1,0:T(8,128)S(1)}, f32[8,512]{1,0:T(8,128)S(1)}, u32[]{:S(2)}, u32[]{:S(2)}) collective-permute-start(f32[8,512]{1,0:T(8,128)S(1)} %get-tuple-element.50), channel_id=1, source_target_pairs={{0,4},{1,3},{4,8},{5,1},{8,12},{9,5},{12,14},{13,9},{14,10},{15,13... | collective-permute-start | bytes 49160 | tf_op jit(solution)/shard_map/ppermute | solution.py:196
  44.3 9.6 %collective-permute-start.15 = (f32[8,512]{1,0:T(8,128)S(1)}, f32[8,512]{1,0:T(8,128)S(1)}, u32[]{:S(2)}, u32[]{:S(2)}) collective-permute-start(f32[8,512]{1,0:T(8,128)S(1)} %get-tuple-element.50), channel_id=1, source_target_pairs={{0,5},{1,2},{4,9},{5,0},{8,13},{9,4},{12,15},{13,8},{14,11},{15,12... | collective-permute-start | bytes 49160 | tf_op jit(solution)/shard_map/ppermute | solution.py:196
  45.6 10.0 %collective-permute-start.19 = (f32[4,512]{1,0:T(4,128)S(1)}, f32[4,512]{1,0:T(4,128)S(1)}, u32[]{:S(2)}, u32[]{:S(2)}) collective-permute-start(f32[4,512]{1,0:T(4,128)S(1)} %get-tuple-element.53), channel_id=1, source_target_pairs={{0,6},{1,9},{4,2},{5,13},{8,0},{9,15},{12,4},{13,11},{14,8},{15,7}... | collective-permute-start | bytes 24584 | tf_op jit(solution)/shard_map/ppermute | solution.py:196
  48.0 5.9 %collective-permute-start.14 = (f32[1,512]{1,0:T(1,128)S(1)}, f32[1,512]{1,0:T(1,128)S(1)}, u32[]{:S(2)}, u32[]{:S(2)}) collective-permute-start(f32[1,512]{1,0:T(1,128)S(1)} %slice.27), channel_id=1, source_target_pairs={{0,1},{1,0},{4,5},{5,4},{8,9},{9,8},{12,13},{13,12},{14,15},{15,14... | collective-permute-start | bytes 6152 | tf_op jit(solution)/shard_map/ppermute | solution.py:196
  51.7 4.0 %collective-permute-start.21 = (f32[1,512]{1,0:T(1,128)S(1)}, f32[1,512]{1,0:T(1,128)S(1)}, u32[]{:S(2)}, u32[]{:S(2)}) collective-permute-start(f32[1,512]{1,0:T(1,128)S(1)} %end_terms.5), channel_id=1, source_target_pairs={{0,7},{1,8},{4,3},{5,12},{8,1},{9,14},{12,5},{13,10},{14,9},{15,6}... | collective-permute-start | bytes 6152 | tf_op jit(solution)/shard_map/ppermute | solution.py:196

commit v8 on v7

--- a/solution.py
+++ b/solution.py
@@ -9,8 +9,7 @@
 
 STRIP = 256
 SPLIT = 2
-ROOM = 8
-END_ROOM = 4
+END_ROOM = 2
 
 
 def unit_rows(values):
@@ -277,9 +276,9 @@
     blocks = [(side[hops][0], True, 0, 0, 0)]
     blocks += [(unit, False, 2, i, 0) for i, unit in enumerate(inner)]
     tasks = ((0, 0, (2,)), (1, 1, (0,)), (2, 2, (0,)))
-    sums, (unit,) = row_sums(blocks, names, tasks, "end_terms", (0,), room=ROOM)
+    sums, (unit,) = row_sums(blocks, names, tasks, "end_terms", (0,), room=3)
     for half in range(2):
-        total = total + moved(sums, back(1 - hops, 1 - half))[1 + half : 2 + half]
+        total = total + moved(sums[1:], back(1 - hops, 1 - half))[half : half + 1]
     blocks = [(unit, False, 0, 0, 0), (facing, True, 1, 0, 0)]
     sums, (facing,) = row_sums(
         blocks, names, ((0, 0, (1,)),), "end_terms", (1,), before=sums[:END_ROOM], room=END_ROOM

time: 56.6 us -> 56.5 us (level)
  no operation moved by 1% of the time
where the time goes in v8:
time: 56.5 us; the launch traced here: 56.2 us
  starting transfers between devices  24.1 us (43%)
  Pallas kernels  16.1 us (28%)
  waiting for transfers between devices  13.1 us (23%)
  local copies, waits for them, and re-layouts  2.14 us (4%)
  other arithmetic  0.6 us (1%)
    ppermute x22, starting transfers between devices, moved(): return lax.ppermute(block, 'blk', route)  24.1 us
    pallas_call x6, Pallas kernels, row_sums(): pl.pallas_call(functools.partial(sums_kernel, [(len(block[0]), *block[1:]...  15.2 us
    ppermute x22, waiting for transfers between devices, moved(): return lax.ppermute(block, 'blk', route)  13.1 us
    unnamed x6, local copies, waits for them, and re-layouts  1.91 us
  transfers between devices with their start and end apart: 22, of which 10 were waited for; matrix products, arithmetic and copies ran while one was open for 0% of the time, Pallas kernels for 29%

profile of v8, /device:TPU:0, one launch (start us, length us, event | category | flops | bytes accessed | tf_op | source)
XLA Modules:
  0.0 56.2 jit_solution(1187156036100268641)
XLA Ops:
  0.0 0.0 copy-start.2
  0.0 0.5 collective-permute-start.1
  0.5 2.6 %collective-permute-start = (bf16[512,1024]{1,0:T(8,128)(2,1)}, bf16[512,1024]{1,0:T(8,128)(2,1)S(1)}, u32[]{:S(2)}, u32[]{:S(2)}) collective-permute-start(bf16[512,1024]{1,0:T(8,128)(2,1)} %refs_0_.1), channel_id=1, source_target_pairs={{0,4},{1,3},{4,8},{5,1},{8,12},{9,5},{12,14},{13,9},{14,10},{15,13... | collective-permute-start | bytes 3145736 | tf_op jit(solution)/shard_map/ppermute | solution.py:195
  3.1 0.0 collective-permute-done.1.refs_1_
  3.1 2.8 %collective-permute-start.9 = (bf16[512,1024]{1,0:T(8,128)(2,1)S(1)}, bf16[512,1024]{1,0:T(8,128)(2,1)S(1)}, u32[]{:S(2)}, u32[]{:S(2)}) collective-permute-start(bf16[512,1024]{1,0:T(8,128)(2,1)S(1)} %collective-permute-done.1.refs_1_), channel_id=1, source_target_pairs={{0,4},{1,3},{4,8},{5,1},{8,12},{9,5},{12,14},{13,9},{14,10},{15,13... | collective-permute-start | bytes 3145736 | tf_op jit(solution)/shard_map/ppermute | solution.py:195
  5.9 0.0 collective-permute-start.2
  5.9 1.4 %collective-permute-done.2.other = s32[1,512]{1,0:T(1,128)S(1)} collective-permute-done((s32[1,512]{1,0:T(1,128)}, s32[1,512]{1,0:T(1,128)S(1)}, u32[]{:S(2)}, u32[]{:S(2)}) %collective-permute-start.2) | collective-permute-done | bytes 2080 | tf_op jit(solution)/shard_map/ppermute | solution.py:195
  7.3 0.0 copy-done.2
  7.3 0.0 copy-start.1
  7.3 0.7 %copy-done.1 = s32[512,1]{0,1:T(1,128)S(1)} copy-done((s32[512,1]{0,1:T(1,128)S(1)}, s32[512,1]{0,1:T(1,128)}, u32[]{:S(2)}) %copy-start.1) | copy-done | bytes 2072
  8.0 0.6 name_tables.1
  8.5 1.0 %collective-permute-start.3 = (s32[4,512]{1,0:T(4,128)S(1)}, s32[4,512]{1,0:T(4,128)S(1)}, u32[]{:S(2)}, u32[]{:S(2)}) collective-permute-start(s32[4,512]{1,0:T(4,128)S(1)} %get-tuple-element.32), channel_id=1, source_target_pairs={{0,3},{1,4},{4,1},{5,8},{8,5},{9,12},{12,9},{13,14},{14,13},{15,10... | collective-permute-start | bytes 24584 | tf_op jit(solution)/shard_map/ppermute | solution.py:195
  9.6 2.2 %collective-permute-done.3.refs_4_.refs_6_ = s32[4,512]{1,0:T(4,128)S(1)} collective-permute-done((s32[4,512]{1,0:T(4,128)S(1)}, s32[4,512]{1,0:T(4,128)S(1)}, u32[]{:S(2)}, u32[]{:S(2)}) %collective-permute-start.3) | collective-permute-done | bytes 8224 | tf_op jit(solution)/shard_map/ppermute | solution.py:195
  11.8 0.5 collective-permute-start.4
  12.3 0.8 %collective-permute-done.4.refs_5_.refs_7_ = s32[4,512]{1,0:T(4,128)S(1)} collective-permute-done((s32[4,512]{1,0:T(4,128)S(1)}, s32[4,512]{1,0:T(4,128)S(1)}, u32[]{:S(2)}, u32[]{:S(2)}) %collective-permute-start.4) | collective-permute-done | bytes 8224 | tf_op jit(solution)/shard_map/ppermute | solution.py:195
  13.1 1.1 %collective-permute-start.5 = (s32[4,512]{1,0:T(4,128)S(1)}, s32[4,512]{1,0:T(4,128)S(1)}, u32[]{:S(2)}, u32[]{:S(2)}) collective-permute-start(s32[4,512]{1,0:T(4,128)S(1)} %collective-permute-done.4.refs_5_.refs_7_), channel_id=1, source_target_pairs={{0,3},{1,4},{4,1},{5,8},{8,5},{9,12},{12,9},{13,14},{14,13},{15,10... | collective-permute-start | bytes 24584 | tf_op jit(solution)/shard_map/ppermute | solution.py:195
  14.3 2.1 %collective-permute-done.5.refs_3_ = s32[4,512]{1,0:T(4,128)S(1)} collective-permute-done((s32[4,512]{1,0:T(4,128)S(1)}, s32[4,512]{1,0:T(4,128)S(1)}, u32[]{:S(2)}, u32[]{:S(2)}) %collective-permute-start.5) | collective-permute-done | bytes 8224 | tf_op jit(solution)/shard_map/ppermute | solution.py:195
  16.3 0.6 %collective-permute-start.6 = (s32[4,512]{1,0:T(4,128)S(1)}, s32[4,512]{1,0:T(4,128)S(1)}, u32[]{:S(2)}, u32[]{:S(2)}) collective-permute-start(s32[4,512]{1,0:T(4,128)S(1)} %collective-permute-done.5.refs_3_), channel_id=1, source_target_pairs={{0,1},{1,0},{4,5},{5,4},{8,9},{9,8},{12,13},{13,12},{14,15},{15,14... | collective-permute-start | bytes 24584 | tf_op jit(solution)/shard_map/ppermute | solution.py:195
  17.0 0.0 copy-start
  17.0 1.2 %copy-done = bf16[512,1024]{1,0:T(8,128)(2,1)S(1)} copy-done((bf16[512,1024]{1,0:T(8,128)(2,1)S(1)}, bf16[512,1024]{1,0:T(8,128)(2,1)}, u32[]{:S(2)}) %copy-start) | copy-done | bytes 1048600
  18.2 2.2 %own_terms.1 = (f32[1,512]{1,0:T(1,128)S(1)}, bf16[512,1024]{1,0:T(8,128)(2,1)S(1)}) custom-call(bf16[512,1024]{1,0:T(8,128)(2,1)S(1)} %copy-done, bf16[512,1024]{1,0:T(8,128)(2,1)S(1)} %collective-permute-done.1.refs_1_, s32[4,512]{1,0:T(4,128)S(1)} %get-tuple-element.30.refs_2_.refs_6_.refs_8_), custom_call_target="tpu_custom_call" | custom-call | tf_op jit(solution)/shard_map/own_terms/pallas_call | solution.py:125
  20.4 0.0 collective-permute-done.6.refs_4_
  20.4 0.0 collective-permute-done.refs_0_
  20.4 0.1 fusion.4
  20.5 0.1 collective-permute-start.8
  20.6 0.5 collective-permute-start.7
  21.1 1.6 %collective-permute-start.12 = (bf16[512,1024]{1,0:T(8,128)(2,1)S(1)}, bf16[512,1024]{1,0:T(8,128)(2,1)S(1)}, u32[]{:S(2)}, u32[]{:S(2)}) collective-permute-start(bf16[512,1024]{1,0:T(8,128)(2,1)S(1)} %collective-permute-done.refs_0_), channel_id=1, source_target_pairs={{0,4},{1,3},{4,8},{5,1},{8,12},{9,5},{12,14},{13,9},{14,10},{15,13... | collective-permute-start | bytes 3145736 | tf_op jit(solution)/shard_map/ppermute | solution.py:195
  22.6 0.0 collective-permute-done.8.refs_2_
  22.6 0.6 %collective-permute-done.7.refs_1_ = bf16[256,1024]{1,0:T(8,128)(2,1)S(1)} collective-permute-done((bf16[256,1024]{1,0:T(8,128)(2,1)S(1)}, bf16[256,1024]{1,0:T(8,128)(2,1)S(1)}, u32[]{:S(2)}, u32[]{:S(2)}) %collective-permute-start.7) | collective-permute-done | bytes 524320 | tf_op jit(solution)/shard_map/ppermute | solution.py:195
  23.2 3.2 %first_terms.1 = (f32[3,512]{1,0:T(4,128)S(1)}, bf16[512,1024]{1,0:T(8,128)(2,1)S(1)}, bf16[512,1024]{1,0:T(8,128)(2,1)S(1)}) custom-call(bf16[512,1024]{1,0:T(8,128)(2,1)S(1)} %collective-permute-done.refs_0_, bf16[256,1024]{1,0:T(8,128)(2,1)S(1)} %collective-permute-done.7.refs_1_, bf16[256,1024]{1,0:T(8,128)(2,1)S(1)} %collective-permute-done.8.refs_2_, ...), custom_call_target="tpu_custom_call" | custom-call | tf_op jit(solution)/shard_map/first_terms/pallas_call | solution.py:125
  26.4 1.0 %collective-permute-done.9.source = bf16[512,1024]{1,0:T(8,128)(2,1)S(1)} collective-permute-done((bf16[512,1024]{1,0:T(8,128)(2,1)S(1)}, bf16[512,1024]{1,0:T(8,128)(2,1)S(1)}, u32[]{:S(2)}, u32[]{:S(2)}) %collective-permute-start.9) | collective-permute-done | bytes 1048608 | tf_op jit(solution)/shard_map/ppermute | solution.py:195
  27.4 0.3 unit_rows.1.refs_2_
  27.8 0.1 fusion.3
  27.8 0.1 collective-permute-start.11
  27.9 0.5 collective-permute-start.10
  28.4 2.1 %collective-permute-start.20 = (bf16[512,1024]{1,0:T(8,128)(2,1)S(1)}, bf16[512,1024]{1,0:T(8,128)(2,1)S(1)}, u32[]{:S(2)}, u32[]{:S(2)}) collective-permute-start(bf16[512,1024]{1,0:T(8,128)(2,1)S(1)} %unit_rows.1.refs_2_), channel_id=1, source_target_pairs={{0,4},{1,3},{4,8},{5,1},{8,12},{9,5},{12,14},{13,9},{14,10},{15,13... | collective-permute-start | bytes 3145736 | tf_op jit(solution)/shard_map/ppermute | solution.py:195
  30.5 0.0 collective-permute-done.11.refs_4_
  30.5 0.1 collective-permute-done.10.refs_3_
  30.6 4.1 %pair_terms.1 = (f32[3,512]{1,0:T(4,128)S(1)}, bf16[512,1024]{1,0:T(8,128)(2,1)S(1)}) custom-call(bf16[512,1024]{1,0:T(8,128)(2,1)S(1)} %get-tuple-element.38.refs_0_, bf16[512,1024]{1,0:T(8,128)(2,1)S(1)} %get-tuple-element.46.refs_1_, bf16[512,1024]{1,0:T(8,128)(2,1)S(1)} %unit_rows.1.refs_2_, bf16[256,1024]{1,0:T(8,128)(2,1)S(1)} %collective-permute-done.10.refs_3_, ...), custom_call_target="tpu_custom_call" | custom-call | tf_op jit(solution)/shard_map/pair_terms/pallas_call | solution.py:125
  34.7 2.3 %collective-permute-start.13 = (f32[2,512]{1,0:T(2,128)S(1)}, f32[2,512]{1,0:T(2,128)S(1)}, u32[]{:S(2)}, u32[]{:S(2)}) collective-permute-start(f32[2,512]{1,0:T(2,128)S(1)} %slice.29), channel_id=1, source_target_pairs={{0,2},{1,5},{4,0},{5,9},{8,4},{9,13},{12,8},{13,15},{14,12},{15,11... | collective-permute-start | bytes 12296 | tf_op jit(solution)/shard_map/ppermute | solution.py:195
  37.0 1.7 %collective-permute-done.12.refs_0_ = bf16[512,1024]{1,0:T(8,128)(2,1)S(1)} collective-permute-done((bf16[512,1024]{1,0:T(8,128)(2,1)S(1)}, bf16[512,1024]{1,0:T(8,128)(2,1)S(1)}, u32[]{:S(2)}, u32[]{:S(2)}) %collective-permute-start.12) | collective-permute-done | bytes 1048608 | tf_op jit(solution)/shard_map/ppermute | solution.py:195
  38.7 0.0 collective-permute-done.13
  38.7 0.1 fusion.2
  38.8 0.1 collective-permute-start.18
  38.9 0.5 collective-permute-start.17
  39.4 2.8 %end_terms.3 = (f32[3,512]{1,0:T(4,128)S(1)}, bf16[512,1024]{1,0:T(8,128)(2,1)S(1)}) custom-call(bf16[512,1024]{1,0:T(8,128)(2,1)S(1)} %collective-permute-done.12.refs_0_, bf16[512,1024]{1,0:T(8,128)(2,1)S(1)} %get-tuple-element.46.refs_1_, bf16[512,1024]{1,0:T(8,128)(2,1)S(1)} %get-tuple-element.47.refs_2_, s32[4,512]{1,0:T(4,128)S(1)} %collective-permute-done.5.refs_3_, ...), custom_call_target="tpu_custom_call" | custom-call | tf_op jit(solution)/shard_map/end_terms/pallas_call | solution.py:125
  42.2 2.1 %collective-permute-start.16 = (f32[2,512]{1,0:T(2,128)S(1)}, f32[2,512]{1,0:T(2,128)S(1)}, u32[]{:S(2)}, u32[]{:S(2)}) collective-permute-start(f32[2,512]{1,0:T(2,128)S(1)} %get-tuple-element.61), channel_id=1, source_target_pairs={{0,4},{1,3},{4,8},{5,1},{8,12},{9,5},{12,14},{13,9},{14,10},{15,13... | collective-permute-start | bytes 12296 | tf_op jit(solution)/shard_map/ppermute | solution.py:195
  44.3 0.0 collective-permute-start.15
  44.3 0.0 collective-permute-done.18.refs_2_
  44.3 0.0 collective-permute-done.17.refs_1_
  44.3 1.3 %end_terms.4 = (f32[2,512]{1,0:T(2,128)S(1)}, bf16[512,1024]{1,0:T(8,128)(2,1)S(1)}) custom-call(bf16[512,1024]{1,0:T(8,128)(2,1)S(1)} %get-tuple-element.51.refs_0_, bf16[256,1024]{1,0:T(8,128)(2,1)S(1)} %collective-permute-done.17.refs_1_, bf16[256,1024]{1,0:T(8,128)(2,1)S(1)} %collective-permute-done.18.refs_2_, ...), custom_call_target="tpu_custom_call" | custom-call | tf_op jit(solution)/shard_map/end_terms/pallas_call | solution.py:125
  45.6 2.5 %collective-permute-start.19 = (f32[2,512]{1,0:T(2,128)S(1)}, f32[2,512]{1,0:T(2,128)S(1)}, u32[]{:S(2)}, u32[]{:S(2)}) collective-permute-start(f32[2,512]{1,0:T(2,128)S(1)} %get-tuple-element.53), channel_id=1, source_target_pairs={{0,6},{1,9},{4,2},{5,13},{8,0},{9,15},{12,4},{13,11},{14,8},{15,7}... | collective-permute-start | bytes 12296 | tf_op jit(solution)/shard_map/ppermute | solution.py:195
  48.0 0.5 collective-permute-start.14
  48.5 1.5 %collective-permute-done.20.refs_0_ = bf16[512,1024]{1,0:T(8,128)(2,1)S(1)} collective-permute-done((bf16[512,1024]{1,0:T(8,128)(2,1)S(1)}, bf16[512,1024]{1,0:T(8,128)(2,1)S(1)}, u32[]{:S(2)}, u32[]{:S(2)}) %collective-permute-start.20) | collective-permute-done | bytes 1048608 | tf_op jit(solution)/shard_map/ppermute | solution.py:195
  50.0 1.6 %end_terms.5 = f32[1,512]{1,0:T(1,128)S(1)} custom-call(bf16[512,1024]{1,0:T(8,128)(2,1)S(1)} %collective-permute-done.20.refs_0_, bf16[512,1024]{1,0:T(8,128)(2,1)S(1)} %get-tuple-element.54.refs_1_, bf16[512,1024]{1,0:T(8,128)(2,1)S(1)} %get-tuple-element.47.refs_2_, s32[4,512]{1,0:T(4,128)S(1)} %collective-permute-done.5.refs_3_, ...), custom_call_target="tpu_custom_call" | custom-call | tf_op jit(solution)/shard_map/end_terms/pallas_call | solution.py:125
  51.6 2.3 %collective-permute-start.21 = (f32[1,512]{1,0:T(1,128)S(1)}, f32[1,512]{1,0:T(1,128)S(1)}, u32[]{:S(2)}, u32[]{:S(2)}) collective-permute-start(f32[1,512]{1,0:T(1,128)S(1)} %end_terms.5), channel_id=1, source_target_pairs={{0,7},{1,8},{4,3},{5,12},{8,1},{9,14},{12,5},{13,10},{14,9},{15,6}... | collective-permute-start | bytes 6152 | tf_op jit(solution)/shard_map/ppermute | solution.py:195
  53.9 0.0 collective-permute-done.14
  53.9 0.0 collective-permute-done.16
  53.9 0.0 collective-permute-done.15
  53.9 1.7 %collective-permute-done.21 = f32[1,512]{1,0:T(1,128)S(1)} collective-permute-done((f32[1,512]{1,0:T(1,128)S(1)}, f32[1,512]{1,0:T(1,128)S(1)}, u32[]{:S(2)}, u32[]{:S(2)}) %collective-permute-start.21) | collective-permute-done | bytes 2080 | tf_op jit(solution)/shard_map/ppermute | solution.py:195
  55.6 0.0 collective-permute-done.19
  55.6 0.6 %fusion.1 = f32[1,512]{1,0:T(1,128)} fusion(f32[1,512]{1,0:T(1,128)S(1)} %collective-permute-done.21, f32[2,512]{1,0:T(2,128)S(1)} %collective-permute-done.19, f32[2,512]{1,0:T(2,128)S(1)} %collective-permute-done.16, f32[2,512]{1,0:T(2,128)S(1)} %collective-permute-done.15, f32[1,512]{1,0:T(1,128)S(1)} %collective-permute-done.14, ...), kind=kLoop, calls=%fused_computation.4 | loop fusion | flops 3584 | bytes 18432 | tf_op jit(solution)/shard_map/log1p | solution.py:290
  (3 shorter events, 0.0 us)
Async XLA Ops:
  0.0 7.3 %copy-start.2 = (s32[16]{0:T(128)S(1)}, s32[16]{0:T(128)}, u32[]{:S(2)}) copy-start(s32[16]{0:T(128)} %near.1) | copy-start | bytes 196
  0.0 3.1 %collective-permute-start.1 = (bf16[512,1024]{1,0:T(8,128)(2,1)}, bf16[512,1024]{1,0:T(8,128)(2,1)S(1)}, u32[]{:S(2)}, u32[]{:S(2)}) collective-permute-start(bf16[512,1024]{1,0:T(8,128)(2,1)} %refs_0_.1), channel_id=1, source_target_pairs={{0,1},{1,0},{4,5},{5,4},{8,9},{9,8},{12,13},{13,12},{14,15},{15,14... | collective-permute-start | bytes 3145736 | tf_op jit(solution)/shard_map/ppermute | solution.py:195
  0.5 19.9 %collective-permute-start = (bf16[512,1024]{1,0:T(8,128)(2,1)}, bf16[512,1024]{1,0:T(8,128)(2,1)S(1)}, u32[]{:S(2)}, u32[]{:S(2)}) collective-permute-start(bf16[512,1024]{1,0:T(8,128)(2,1)} %refs_0_.1), channel_id=1, source_target_pairs={{0,4},{1,3},{4,8},{5,1},{8,12},{9,5},{12,14},{13,9},{14,10},{15,13... | collective-permute-start | bytes 3145736 | tf_op jit(solution)/shard_map/ppermute | solution.py:195
  3.1 24.3 %collective-permute-start.9 = (bf16[512,1024]{1,0:T(8,128)(2,1)S(1)}, bf16[512,1024]{1,0:T(8,128)(2,1)S(1)}, u32[]{:S(2)}, u32[]{:S(2)}) collective-permute-start(bf16[512,1024]{1,0:T(8,128)(2,1)S(1)} %collective-permute-done.1.refs_1_), channel_id=1, source_target_pairs={{0,4},{1,3},{4,8},{5,1},{8,12},{9,5},{12,14},{13,9},{14,10},{15,13... | collective-permute-start | bytes 3145736 | tf_op jit(solution)/shard_map/ppermute | solution.py:195
  5.9 1.4 %collective-permute-start.2 = (s32[1,512]{1,0:T(1,128)}, s32[1,512]{1,0:T(1,128)S(1)}, u32[]{:S(2)}, u32[]{:S(2)}) collective-permute-start(s32[1,512]{1,0:T(1,128)} %bitcast.2), channel_id=1, source_target_pairs={{0,1},{1,0},{4,5},{5,4},{8,9},{9,8},{12,13},{13,12},{14,15},{15,14... | collective-permute-start | bytes 6152 | tf_op jit(solution)/shard_map/ppermute | solution.py:195
  7.3 0.7 %copy-start.1 = (s32[512,1]{0,1:T(1,128)S(1)}, s32[512,1]{0,1:T(1,128)}, u32[]{:S(2)}) copy-start(s32[512,1]{0,1:T(1,128)} %param.4) | copy-start | bytes 6148
  8.5 3.3 %collective-permute-start.3 = (s32[4,512]{1,0:T(4,128)S(1)}, s32[4,512]{1,0:T(4,128)S(1)}, u32[]{:S(2)}, u32[]{:S(2)}) collective-permute-start(s32[4,512]{1,0:T(4,128)S(1)} %get-tuple-element.32), channel_id=1, source_target_pairs={{0,3},{1,4},{4,1},{5,8},{8,5},{9,12},{12,9},{13,14},{14,13},{15,10... | collective-permute-start | bytes 24584 | tf_op jit(solution)/shard_map/ppermute | solution.py:195
  11.8 1.3 %collective-permute-start.4 = (s32[4,512]{1,0:T(4,128)S(1)}, s32[4,512]{1,0:T(4,128)S(1)}, u32[]{:S(2)}, u32[]{:S(2)}) collective-permute-start(s32[4,512]{1,0:T(4,128)S(1)} %collective-permute-done.3.refs_4_.refs_6_), channel_id=1, source_target_pairs={{0,1},{1,0},{4,5},{5,4},{8,9},{9,8},{12,13},{13,12},{14,15},{15,14... | collective-permute-start | bytes 24584 | tf_op jit(solution)/shard_map/ppermute | solution.py:195
  13.1 3.2 %collective-permute-start.5 = (s32[4,512]{1,0:T(4,128)S(1)}, s32[4,512]{1,0:T(4,128)S(1)}, u32[]{:S(2)}, u32[]{:S(2)}) collective-permute-start(s32[4,512]{1,0:T(4,128)S(1)} %collective-permute-done.4.refs_5_.refs_7_), channel_id=1, source_target_pairs={{0,3},{1,4},{4,1},{5,8},{8,5},{9,12},{12,9},{13,14},{14,13},{15,10... | collective-permute-start | bytes 24584 | tf_op jit(solution)/shard_map/ppermute | solution.py:195
  16.3 4.0 %collective-permute-start.6 = (s32[4,512]{1,0:T(4,128)S(1)}, s32[4,512]{1,0:T(4,128)S(1)}, u32[]{:S(2)}, u32[]{:S(2)}) collective-permute-start(s32[4,512]{1,0:T(4,128)S(1)} %collective-permute-done.5.refs_3_), channel_id=1, source_target_pairs={{0,1},{1,0},{4,5},{5,4},{8,9},{9,8},{12,13},{13,12},{14,15},{15,14... | collective-permute-start | bytes 24584 | tf_op jit(solution)/shard_map/ppermute | solution.py:195
  17.0 1.2 %copy-start = (bf16[512,1024]{1,0:T(8,128)(2,1)S(1)}, bf16[512,1024]{1,0:T(8,128)(2,1)}, u32[]{:S(2)}) copy-start(bf16[512,1024]{1,0:T(8,128)(2,1)} %refs_0_.1) | copy-start | bytes 3145732
  20.5 2.2 %collective-permute-start.8 = (bf16[256,1024]{1,0:T(8,128)(2,1)S(1)}, bf16[256,1024]{1,0:T(8,128)(2,1)S(1)}, u32[]{:S(2)}, u32[]{:S(2)}) collective-permute-start(bf16[256,1024]{1,0:T(8,128)(2,1)S(1)} %get-tuple-element.59), channel_id=1, source_target_pairs={{0,1},{1,0},{4,5},{5,4},{8,9},{9,8},{12,13},{13,12},{14,15},{15,14... | collective-permute-start | bytes 1572872 | tf_op jit(solution)/shard_map/ppermute | solution.py:195
  20.6 2.6 %collective-permute-start.7 = (bf16[256,1024]{1,0:T(8,128)(2,1)S(1)}, bf16[256,1024]{1,0:T(8,128)(2,1)S(1)}, u32[]{:S(2)}, u32[]{:S(2)}) collective-permute-start(bf16[256,1024]{1,0:T(8,128)(2,1)S(1)} %get-tuple-element.60), channel_id=1, source_target_pairs={{0,1},{1,0},{4,5},{5,4},{8,9},{9,8},{12,13},{13,12},{14,15},{15,14... | collective-permute-start | bytes 1572872 | tf_op jit(solution)/shard_map/ppermute | solution.py:195
  21.1 17.6 %collective-permute-start.12 = (bf16[512,1024]{1,0:T(8,128)(2,1)S(1)}, bf16[512,1024]{1,0:T(8,128)(2,1)S(1)}, u32[]{:S(2)}, u32[]{:S(2)}) collective-permute-start(bf16[512,1024]{1,0:T(8,128)(2,1)S(1)} %collective-permute-done.refs_0_), channel_id=1, source_target_pairs={{0,4},{1,3},{4,8},{5,1},{8,12},{9,5},{12,14},{13,9},{14,10},{15,13... | collective-permute-start | bytes 3145736 | tf_op jit(solution)/shard_map/ppermute | solution.py:195
  27.8 2.7 %collective-permute-start.11 = (bf16[256,1024]{1,0:T(8,128)(2,1)S(1)}, bf16[256,1024]{1,0:T(8,128)(2,1)S(1)}, u32[]{:S(2)}, u32[]{:S(2)}) collective-permute-start(bf16[256,1024]{1,0:T(8,128)(2,1)S(1)} %get-tuple-element.57), channel_id=1, source_target_pairs={{0,1},{1,0},{4,5},{5,4},{8,9},{9,8},{12,13},{13,12},{14,15},{15,14... | collective-permute-start | bytes 1572872 | tf_op jit(solution)/shard_map/ppermute | solution.py:195
  27.9 2.6 %collective-permute-start.10 = (bf16[256,1024]{1,0:T(8,128)(2,1)S(1)}, bf16[256,1024]{1,0:T(8,128)(2,1)S(1)}, u32[]{:S(2)}, u32[]{:S(2)}) collective-permute-start(bf16[256,1024]{1,0:T(8,128)(2,1)S(1)} %get-tuple-element.58), channel_id=1, source_target_pairs={{0,1},{1,0},{4,5},{5,4},{8,9},{9,8},{12,13},{13,12},{14,15},{15,14... | collective-permute-start | bytes 1572872 | tf_op jit(solution)/shard_map/ppermute | solution.py:195
  28.4 21.6 %collective-permute-start.20 = (bf16[512,1024]{1,0:T(8,128)(2,1)S(1)}, bf16[512,1024]{1,0:T(8,128)(2,1)S(1)}, u32[]{:S(2)}, u32[]{:S(2)}) collective-permute-start(bf16[512,1024]{1,0:T(8,128)(2,1)S(1)} %unit_rows.1.refs_2_), channel_id=1, source_target_pairs={{0,4},{1,3},{4,8},{5,1},{8,12},{9,5},{12,14},{13,9},{14,10},{15,13... | collective-permute-start | bytes 3145736 | tf_op jit(solution)/shard_map/ppermute | solution.py:195
  34.7 4.0 %collective-permute-start.13 = (f32[2,512]{1,0:T(2,128)S(1)}, f32[2,512]{1,0:T(2,128)S(1)}, u32[]{:S(2)}, u32[]{:S(2)}) collective-permute-start(f32[2,512]{1,0:T(2,128)S(1)} %slice.29), channel_id=1, source_target_pairs={{0,2},{1,5},{4,0},{5,9},{8,4},{9,13},{12,8},{13,15},{14,12},{15,11... | collective-permute-start | bytes 12296 | tf_op jit(solution)/shard_map/ppermute | solution.py:195
  38.8 5.5 %collective-permute-start.18 = (bf16[256,1024]{1,0:T(8,128)(2,1)S(1)}, bf16[256,1024]{1,0:T(8,128)(2,1)S(1)}, u32[]{:S(2)}, u32[]{:S(2)}) collective-permute-start(bf16[256,1024]{1,0:T(8,128)(2,1)S(1)} %get-tuple-element.55), channel_id=1, source_target_pairs={{0,1},{1,0},{4,5},{5,4},{8,9},{9,8},{12,13},{13,12},{14,15},{15,14... | collective-permute-start | bytes 1572872 | tf_op jit(solution)/shard_map/ppermute | solution.py:195
  38.9 5.4 %collective-permute-start.17 = (bf16[256,1024]{1,0:T(8,128)(2,1)S(1)}, bf16[256,1024]{1,0:T(8,128)(2,1)S(1)}, u32[]{:S(2)}, u32[]{:S(2)}) collective-permute-start(bf16[256,1024]{1,0:T(8,128)(2,1)S(1)} %get-tuple-element.56), channel_id=1, source_target_pairs={{0,1},{1,0},{4,5},{5,4},{8,9},{9,8},{12,13},{13,12},{14,15},{15,14... | collective-permute-start | bytes 1572872 | tf_op jit(solution)/shard_map/ppermute | solution.py:195
  42.2 11.7 %collective-permute-start.16 = (f32[2,512]{1,0:T(2,128)S(1)}, f32[2,512]{1,0:T(2,128)S(1)}, u32[]{:S(2)}, u32[]{:S(2)}) collective-permute-start(f32[2,512]{1,0:T(2,128)S(1)} %get-tuple-element.61), channel_id=1, source_target_pairs={{0,4},{1,3},{4,8},{5,1},{8,12},{9,5},{12,14},{13,9},{14,10},{15,13... | collective-permute-start | bytes 12296 | tf_op jit(solution)/shard_map/ppermute | solution.py:195
  44.3 9.6 %collective-permute-start.15 = (f32[2,512]{1,0:T(2,128)S(1)}, f32[2,512]{1,0:T(2,128)S(1)}, u32[]{:S(2)}, u32[]{:S(2)}) collective-permute-start(f32[2,512]{1,0:T(2,128)S(1)} %get-tuple-element.61), channel_id=1, source_target_pairs={{0,5},{1,2},{4,9},{5,0},{8,13},{9,4},{12,15},{13,8},{14,11},{15,12... | collective-permute-start | bytes 12296 | tf_op jit(solution)/shard_map/ppermute | solution.py:195
  45.6 10.0 %collective-permute-start.19 = (f32[2,512]{1,0:T(2,128)S(1)}, f32[2,512]{1,0:T(2,128)S(1)}, u32[]{:S(2)}, u32[]{:S(2)}) collective-permute-start(f32[2,512]{1,0:T(2,128)S(1)} %get-tuple-element.53), channel_id=1, source_target_pairs={{0,6},{1,9},{4,2},{5,13},{8,0},{9,15},{12,4},{13,11},{14,8},{15,7}... | collective-permute-start | bytes 12296 | tf_op jit(solution)/shard_map/ppermute | solution.py:195
  48.0 5.9 %collective-permute-start.14 = (f32[1,512]{1,0:T(1,128)S(1)}, f32[1,512]{1,0:T(1,128)S(1)}, u32[]{:S(2)}, u32[]{:S(2)}) collective-permute-start(f32[1,512]{1,0:T(1,128)S(1)} %slice.31), channel_id=1, source_target_pairs={{0,1},{1,0},{4,5},{5,4},{8,9},{9,8},{12,13},{13,12},{14,15},{15,14... | collective-permute-start | bytes 6152 | tf_op jit(solution)/shard_map/ppermute | solution.py:195
  51.6 4.0 %collective-permute-start.21 = (f32[1,512]{1,0:T(1,128)S(1)}, f32[1,512]{1,0:T(1,128)S(1)}, u32[]{:S(2)}, u32[]{:S(2)}) collective-permute-start(f32[1,512]{1,0:T(1,128)S(1)} %end_terms.5), channel_id=1, source_target_pairs={{0,7},{1,8},{4,3},{5,12},{8,1},{9,14},{12,5},{13,10},{14,9},{15,6}... | collective-permute-start | bytes 6152 | tf_op jit(solution)/shard_map/ppermute | solution.py:195

commit v9 on v8

--- a/solution.py
+++ b/solution.py
@@ -96,17 +96,26 @@
     for task, block, others in tasks:
         a_own, a_near = [as_column(row) for row in code(block)]
         place = blocks[block][-1]
-        for here in strips(units[block].shape[0]):
-            total = jnp.zeros((here.stop - here.start, 128), jnp.float32)
-            for other in others:
-                value = terms(
-                    units[block][here, :], units[other][...], a_own[here], a_near[here], *code(other)
-                )
-                if other == block:
-                    row = lax.broadcasted_iota(jnp.int32, value.shape, 0) + here.start
-                    same = row == lax.broadcasted_iota(jnp.int32, value.shape, 1)
-                    value = jnp.where(same, 0.0, value)
-                total = total + lanes_added(value)
+        here_all = strips(units[block].shape[0])
+        totals = [jnp.zeros((here.stop - here.start, 128), jnp.float32) for here in here_all]
+        for other in others:
+            b_own, b_near = code(other)
+            for there in strips(units[other].shape[0]):
+                for at, here in enumerate(here_all):
+                    value = terms(
+                        units[block][here, :],
+                        units[other][there, :],
+                        a_own[here],
+                        a_near[here],
+                        b_own[:, there],
+                        b_near[:, there],
+                    )
+                    if other == block and here == there:
+                        row = lax.broadcasted_iota(jnp.int32, value.shape, 0)
+                        same = row == lax.broadcasted_iota(jnp.int32, value.shape, 1)
+                        value = jnp.where(same, 0.0, value)
+                    totals[at] = totals[at] + lanes_added(value)
+        for here, total in zip(here_all, totals):
             sums[task : task + 1, place + here.start : place + here.stop] += as_row(total)
 
 

time: 56.5 us -> 56.4 us (level)
  Pallas kernels: 16.1 us -> 15.3 us
  waiting for transfers between devices: 13.1 us -> 13.7 us
    pallas_call x6, Pallas kernels: 15.2 us -> 14.4 us  [row_sums(): pl.pallas_call(functools.partial(sums_kernel, [(len(block[0]), *block[1:]...]
    ppermute x22, waiting for transfers between devices: 13.1 us -> 13.7 us  [moved(): return lax.ppermute(block, 'blk', route)]
  transfers between devices with their start and end apart: 22 -> 22, of which waited for: 10 -> 10; matrix products, arithmetic and copies ran while one was open for 0% -> 0% of each run, Pallas kernels for 29% -> 27%
where the time goes in v9:
time: 56.4 us; the launch traced here: 56 us
  starting transfers between devices  24.1 us (43%)
  Pallas kernels  15.3 us (27%)
  waiting for transfers between devices  13.7 us (24%)
  local copies, waits for them, and re-layouts  2.14 us (4%)
  other arithmetic  0.6 us (1%)
    ppermute x22, starting transfers between devices, moved(): return lax.ppermute(block, 'blk', route)  24.1 us
    pallas_call x6, Pallas kernels, row_sums(): pl.pallas_call(functools.partial(sums_kernel, [(len(block[0]), *block[1:]...  14.4 us
    ppermute x22, waiting for transfers between devices, moved(): return lax.ppermute(block, 'blk', route)  13.7 us
    unnamed x6, local copies, waits for them, and re-layouts  1.91 us
  transfers between devices with their start and end apart: 22, of which 10 were waited for; matrix products, arithmetic and copies ran while one was open for 0% of the time, Pallas kernels for 27%

profile of v9, /device:TPU:0, one launch (start us, length us, event | category | flops | bytes accessed | tf_op | source)
XLA Modules:
  0.0 56.0 jit_solution(4065910098489496929)
XLA Ops:
  0.0 0.0 copy-start.2
  0.0 0.5 collective-permute-start.1
  0.5 2.6 %collective-permute-start = (bf16[512,1024]{1,0:T(8,128)(2,1)}, bf16[512,1024]{1,0:T(8,128)(2,1)S(1)}, u32[]{:S(2)}, u32[]{:S(2)}) collective-permute-start(bf16[512,1024]{1,0:T(8,128)(2,1)} %refs_0_.1), channel_id=1, source_target_pairs={{0,4},{1,3},{4,8},{5,1},{8,12},{9,5},{12,14},{13,9},{14,10},{15,13... | collective-permute-start | bytes 3145736 | tf_op jit(solution)/shard_map/ppermute | solution.py:204
  3.1 0.0 collective-permute-done.1.refs_1_
  3.1 2.8 %collective-permute-start.9 = (bf16[512,1024]{1,0:T(8,128)(2,1)S(1)}, bf16[512,1024]{1,0:T(8,128)(2,1)S(1)}, u32[]{:S(2)}, u32[]{:S(2)}) collective-permute-start(bf16[512,1024]{1,0:T(8,128)(2,1)S(1)} %collective-permute-done.1.refs_1_), channel_id=1, source_target_pairs={{0,4},{1,3},{4,8},{5,1},{8,12},{9,5},{12,14},{13,9},{14,10},{15,13... | collective-permute-start | bytes 3145736 | tf_op jit(solution)/shard_map/ppermute | solution.py:204
  5.9 0.0 collective-permute-start.2
  5.9 1.4 %collective-permute-done.2.other = s32[1,512]{1,0:T(1,128)S(1)} collective-permute-done((s32[1,512]{1,0:T(1,128)}, s32[1,512]{1,0:T(1,128)S(1)}, u32[]{:S(2)}, u32[]{:S(2)}) %collective-permute-start.2) | collective-permute-done | bytes 2080 | tf_op jit(solution)/shard_map/ppermute | solution.py:204
  7.3 0.0 copy-done.2
  7.3 0.0 copy-start.1
  7.3 0.7 %copy-done.1 = s32[512,1]{0,1:T(1,128)S(1)} copy-done((s32[512,1]{0,1:T(1,128)S(1)}, s32[512,1]{0,1:T(1,128)}, u32[]{:S(2)}) %copy-start.1) | copy-done | bytes 2072
  8.0 0.6 %name_tables.1 = (s32[4,512]{1,0:T(4,128)S(1)}, s32[4,512]{1,0:T(4,128)S(1)}) custom-call(s32[16]{0:T(128)S(1)} %copy-done.2, s32[1,512]{1,0:T(1,128)S(1)} %bitcast.3, s32[1,512]{1,0:T(1,128)S(1)} %collective-permute-done.2.other), custom_call_target="tpu_custom_call" | custom-call | tf_op jit(solution)/shard_map/name_tables/pallas_call | solution.py:168
  8.5 1.0 %collective-permute-start.3 = (s32[4,512]{1,0:T(4,128)S(1)}, s32[4,512]{1,0:T(4,128)S(1)}, u32[]{:S(2)}, u32[]{:S(2)}) collective-permute-start(s32[4,512]{1,0:T(4,128)S(1)} %get-tuple-element.32), channel_id=1, source_target_pairs={{0,3},{1,4},{4,1},{5,8},{8,5},{9,12},{12,9},{13,14},{14,13},{15,10... | collective-permute-start | bytes 24584 | tf_op jit(solution)/shard_map/ppermute | solution.py:204
  9.6 2.2 %collective-permute-done.3.refs_4_.refs_6_ = s32[4,512]{1,0:T(4,128)S(1)} collective-permute-done((s32[4,512]{1,0:T(4,128)S(1)}, s32[4,512]{1,0:T(4,128)S(1)}, u32[]{:S(2)}, u32[]{:S(2)}) %collective-permute-start.3) | collective-permute-done | bytes 8224 | tf_op jit(solution)/shard_map/ppermute | solution.py:204
  11.8 0.5 collective-permute-start.4
  12.3 0.8 %collective-permute-done.4.refs_5_.refs_7_ = s32[4,512]{1,0:T(4,128)S(1)} collective-permute-done((s32[4,512]{1,0:T(4,128)S(1)}, s32[4,512]{1,0:T(4,128)S(1)}, u32[]{:S(2)}, u32[]{:S(2)}) %collective-permute-start.4) | collective-permute-done | bytes 8224 | tf_op jit(solution)/shard_map/ppermute | solution.py:204
  13.1 1.1 %collective-permute-start.5 = (s32[4,512]{1,0:T(4,128)S(1)}, s32[4,512]{1,0:T(4,128)S(1)}, u32[]{:S(2)}, u32[]{:S(2)}) collective-permute-start(s32[4,512]{1,0:T(4,128)S(1)} %collective-permute-done.4.refs_5_.refs_7_), channel_id=1, source_target_pairs={{0,3},{1,4},{4,1},{5,8},{8,5},{9,12},{12,9},{13,14},{14,13},{15,10... | collective-permute-start | bytes 24584 | tf_op jit(solution)/shard_map/ppermute | solution.py:204
  14.3 2.1 %collective-permute-done.5.refs_3_ = s32[4,512]{1,0:T(4,128)S(1)} collective-permute-done((s32[4,512]{1,0:T(4,128)S(1)}, s32[4,512]{1,0:T(4,128)S(1)}, u32[]{:S(2)}, u32[]{:S(2)}) %collective-permute-start.5) | collective-permute-done | bytes 8224 | tf_op jit(solution)/shard_map/ppermute | solution.py:204
  16.3 0.6 %collective-permute-start.6 = (s32[4,512]{1,0:T(4,128)S(1)}, s32[4,512]{1,0:T(4,128)S(1)}, u32[]{:S(2)}, u32[]{:S(2)}) collective-permute-start(s32[4,512]{1,0:T(4,128)S(1)} %collective-permute-done.5.refs_3_), channel_id=1, source_target_pairs={{0,1},{1,0},{4,5},{5,4},{8,9},{9,8},{12,13},{13,12},{14,15},{15,14... | collective-permute-start | bytes 24584 | tf_op jit(solution)/shard_map/ppermute | solution.py:204
  17.0 0.0 copy-start
  17.0 1.2 %copy-done = bf16[512,1024]{1,0:T(8,128)(2,1)S(1)} copy-done((bf16[512,1024]{1,0:T(8,128)(2,1)S(1)}, bf16[512,1024]{1,0:T(8,128)(2,1)}, u32[]{:S(2)}) %copy-start) | copy-done | bytes 1048600
  18.2 2.0 %own_terms.1 = (f32[1,512]{1,0:T(1,128)S(1)}, bf16[512,1024]{1,0:T(8,128)(2,1)S(1)}) custom-call(bf16[512,1024]{1,0:T(8,128)(2,1)S(1)} %copy-done, bf16[512,1024]{1,0:T(8,128)(2,1)S(1)} %collective-permute-done.1.refs_1_, s32[4,512]{1,0:T(4,128)S(1)} %get-tuple-element.30.refs_2_.refs_6_.refs_8_), custom_call_target="tpu_custom_call" | custom-call | tf_op jit(solution)/shard_map/own_terms/pallas_call | solution.py:134
  20.2 0.0 collective-permute-done.6.refs_4_
  20.2 0.0 collective-permute-done.refs_0_
  20.2 0.1 fusion.4
  20.3 0.1 collective-permute-start.8
  20.4 0.5 collective-permute-start.7
  20.9 1.6 %collective-permute-start.12 = (bf16[512,1024]{1,0:T(8,128)(2,1)S(1)}, bf16[512,1024]{1,0:T(8,128)(2,1)S(1)}, u32[]{:S(2)}, u32[]{:S(2)}) collective-permute-start(bf16[512,1024]{1,0:T(8,128)(2,1)S(1)} %collective-permute-done.refs_0_), channel_id=1, source_target_pairs={{0,4},{1,3},{4,8},{5,1},{8,12},{9,5},{12,14},{13,9},{14,10},{15,13... | collective-permute-start | bytes 3145736 | tf_op jit(solution)/shard_map/ppermute | solution.py:204
  22.4 0.0 collective-permute-done.8.refs_2_
  22.5 0.6 %collective-permute-done.7.refs_1_ = bf16[256,1024]{1,0:T(8,128)(2,1)S(1)} collective-permute-done((bf16[256,1024]{1,0:T(8,128)(2,1)S(1)}, bf16[256,1024]{1,0:T(8,128)(2,1)S(1)}, u32[]{:S(2)}, u32[]{:S(2)}) %collective-permute-start.7) | collective-permute-done | bytes 524320 | tf_op jit(solution)/shard_map/ppermute | solution.py:204
  23.0 3.1 %first_terms.1 = (f32[3,512]{1,0:T(4,128)S(1)}, bf16[512,1024]{1,0:T(8,128)(2,1)S(1)}, bf16[512,1024]{1,0:T(8,128)(2,1)S(1)}) custom-call(bf16[512,1024]{1,0:T(8,128)(2,1)S(1)} %collective-permute-done.refs_0_, bf16[256,1024]{1,0:T(8,128)(2,1)S(1)} %collective-permute-done.7.refs_1_, bf16[256,1024]{1,0:T(8,128)(2,1)S(1)} %collective-permute-done.8.refs_2_, ...), custom_call_target="tpu_custom_call" | custom-call | tf_op jit(solution)/shard_map/first_terms/pallas_call | solution.py:134
  26.2 1.3 %collective-permute-done.9.source = bf16[512,1024]{1,0:T(8,128)(2,1)S(1)} collective-permute-done((bf16[512,1024]{1,0:T(8,128)(2,1)S(1)}, bf16[512,1024]{1,0:T(8,128)(2,1)S(1)}, u32[]{:S(2)}, u32[]{:S(2)}) %collective-permute-start.9) | collective-permute-done | bytes 1048608 | tf_op jit(solution)/shard_map/ppermute | solution.py:204
  27.4 0.3 unit_rows.1.refs_2_
  27.8 0.1 fusion.3
  27.8 0.1 collective-permute-start.11
  27.9 0.5 collective-permute-start.10
  28.4 2.1 %collective-permute-start.20 = (bf16[512,1024]{1,0:T(8,128)(2,1)S(1)}, bf16[512,1024]{1,0:T(8,128)(2,1)S(1)}, u32[]{:S(2)}, u32[]{:S(2)}) collective-permute-start(bf16[512,1024]{1,0:T(8,128)(2,1)S(1)} %unit_rows.1.refs_2_), channel_id=1, source_target_pairs={{0,4},{1,3},{4,8},{5,1},{8,12},{9,5},{12,14},{13,9},{14,10},{15,13... | collective-permute-start | bytes 3145736 | tf_op jit(solution)/shard_map/ppermute | solution.py:204
  30.5 0.0 collective-permute-done.11.refs_4_
  30.5 0.1 collective-permute-done.10.refs_3_
  30.6 4.0 %pair_terms.1 = (f32[3,512]{1,0:T(4,128)S(1)}, bf16[512,1024]{1,0:T(8,128)(2,1)S(1)}) custom-call(bf16[512,1024]{1,0:T(8,128)(2,1)S(1)} %get-tuple-element.38.refs_0_, bf16[512,1024]{1,0:T(8,128)(2,1)S(1)} %get-tuple-element.46.refs_1_, bf16[512,1024]{1,0:T(8,128)(2,1)S(1)} %unit_rows.1.refs_2_, bf16[256,1024]{1,0:T(8,128)(2,1)S(1)} %collective-permute-done.10.refs_3_, ...), custom_call_target="tpu_custom_call" | custom-call | tf_op jit(solution)/shard_map/pair_terms/pallas_call | solution.py:134
  34.6 2.3 %collective-permute-start.13 = (f32[2,512]{1,0:T(2,128)S(1)}, f32[2,512]{1,0:T(2,128)S(1)}, u32[]{:S(2)}, u32[]{:S(2)}) collective-permute-start(f32[2,512]{1,0:T(2,128)S(1)} %slice.29), channel_id=1, source_target_pairs={{0,2},{1,5},{4,0},{5,9},{8,4},{9,13},{12,8},{13,15},{14,12},{15,11... | collective-permute-start | bytes 12296 | tf_op jit(solution)/shard_map/ppermute | solution.py:204
  36.8 1.9 %collective-permute-done.12.refs_0_ = bf16[512,1024]{1,0:T(8,128)(2,1)S(1)} collective-permute-done((bf16[512,1024]{1,0:T(8,128)(2,1)S(1)}, bf16[512,1024]{1,0:T(8,128)(2,1)S(1)}, u32[]{:S(2)}, u32[]{:S(2)}) %collective-permute-start.12) | collective-permute-done | bytes 1048608 | tf_op jit(solution)/shard_map/ppermute | solution.py:204
  38.7 0.0 collective-permute-done.13
  38.7 0.1 fusion.2
  38.8 0.1 collective-permute-start.18
  38.9 0.5 collective-permute-start.17
  39.4 2.7 %end_terms.3 = (f32[3,512]{1,0:T(4,128)S(1)}, bf16[512,1024]{1,0:T(8,128)(2,1)S(1)}) custom-call(bf16[512,1024]{1,0:T(8,128)(2,1)S(1)} %collective-permute-done.12.refs_0_, bf16[512,1024]{1,0:T(8,128)(2,1)S(1)} %get-tuple-element.46.refs_1_, bf16[512,1024]{1,0:T(8,128)(2,1)S(1)} %get-tuple-element.47.refs_2_, s32[4,512]{1,0:T(4,128)S(1)} %collective-permute-done.5.refs_3_, ...), custom_call_target="tpu_custom_call" | custom-call | tf_op jit(solution)/shard_map/end_terms/pallas_call | solution.py:134
  42.1 2.1 %collective-permute-start.16 = (f32[2,512]{1,0:T(2,128)S(1)}, f32[2,512]{1,0:T(2,128)S(1)}, u32[]{:S(2)}, u32[]{:S(2)}) collective-permute-start(f32[2,512]{1,0:T(2,128)S(1)} %get-tuple-element.61), channel_id=1, source_target_pairs={{0,4},{1,3},{4,8},{5,1},{8,12},{9,5},{12,14},{13,9},{14,10},{15,13... | collective-permute-start | bytes 12296 | tf_op jit(solution)/shard_map/ppermute | solution.py:204
  44.2 0.0 collective-permute-start.15
  44.2 0.0 collective-permute-done.18.refs_2_
  44.2 0.0 collective-permute-done.17.refs_1_
  44.2 1.1 %end_terms.4 = (f32[2,512]{1,0:T(2,128)S(1)}, bf16[512,1024]{1,0:T(8,128)(2,1)S(1)}) custom-call(bf16[512,1024]{1,0:T(8,128)(2,1)S(1)} %get-tuple-element.51.refs_0_, bf16[256,1024]{1,0:T(8,128)(2,1)S(1)} %collective-permute-done.17.refs_1_, bf16[256,1024]{1,0:T(8,128)(2,1)S(1)} %collective-permute-done.18.refs_2_, ...), custom_call_target="tpu_custom_call" | custom-call | tf_op jit(solution)/shard_map/end_terms/pallas_call | solution.py:134
  45.3 2.4 %collective-permute-start.19 = (f32[2,512]{1,0:T(2,128)S(1)}, f32[2,512]{1,0:T(2,128)S(1)}, u32[]{:S(2)}, u32[]{:S(2)}) collective-permute-start(f32[2,512]{1,0:T(2,128)S(1)} %get-tuple-element.53), channel_id=1, source_target_pairs={{0,6},{1,9},{4,2},{5,13},{8,0},{9,15},{12,4},{13,11},{14,8},{15,7}... | collective-permute-start | bytes 12296 | tf_op jit(solution)/shard_map/ppermute | solution.py:204
  47.7 0.5 collective-permute-start.14
  48.2 1.8 %collective-permute-done.20.refs_0_ = bf16[512,1024]{1,0:T(8,128)(2,1)S(1)} collective-permute-done((bf16[512,1024]{1,0:T(8,128)(2,1)S(1)}, bf16[512,1024]{1,0:T(8,128)(2,1)S(1)}, u32[]{:S(2)}, u32[]{:S(2)}) %collective-permute-start.20) | collective-permute-done | bytes 1048608 | tf_op jit(solution)/shard_map/ppermute | solution.py:204
  50.0 1.5 %end_terms.5 = f32[1,512]{1,0:T(1,128)S(1)} custom-call(bf16[512,1024]{1,0:T(8,128)(2,1)S(1)} %collective-permute-done.20.refs_0_, bf16[512,1024]{1,0:T(8,128)(2,1)S(1)} %get-tuple-element.54.refs_1_, bf16[512,1024]{1,0:T(8,128)(2,1)S(1)} %get-tuple-element.47.refs_2_, s32[4,512]{1,0:T(4,128)S(1)} %collective-permute-done.5.refs_3_, ...), custom_call_target="tpu_custom_call" | custom-call | tf_op jit(solution)/shard_map/end_terms/pallas_call | solution.py:134
  51.5 2.3 %collective-permute-start.21 = (f32[1,512]{1,0:T(1,128)S(1)}, f32[1,512]{1,0:T(1,128)S(1)}, u32[]{:S(2)}, u32[]{:S(2)}) collective-permute-start(f32[1,512]{1,0:T(1,128)S(1)} %end_terms.5), channel_id=1, source_target_pairs={{0,7},{1,8},{4,3},{5,12},{8,1},{9,14},{12,5},{13,10},{14,9},{15,6}... | collective-permute-start | bytes 6152 | tf_op jit(solution)/shard_map/ppermute | solution.py:204
  53.8 0.0 collective-permute-done.14
  53.8 0.0 collective-permute-done.16
  53.8 0.0 collective-permute-done.15
  53.8 1.7 %collective-permute-done.21 = f32[1,512]{1,0:T(1,128)S(1)} collective-permute-done((f32[1,512]{1,0:T(1,128)S(1)}, f32[1,512]{1,0:T(1,128)S(1)}, u32[]{:S(2)}, u32[]{:S(2)}) %collective-permute-start.21) | collective-permute-done | bytes 2080 | tf_op jit(solution)/shard_map/ppermute | solution.py:204
  55.4 0.0 collective-permute-done.19
  55.4 0.6 %fusion.1 = f32[1,512]{1,0:T(1,128)} fusion(f32[1,512]{1,0:T(1,128)S(1)} %collective-permute-done.21, f32[2,512]{1,0:T(2,128)S(1)} %collective-permute-done.19, f32[2,512]{1,0:T(2,128)S(1)} %collective-permute-done.16, f32[2,512]{1,0:T(2,128)S(1)} %collective-permute-done.15, f32[1,512]{1,0:T(1,128)S(1)} %collective-permute-done.14, ...), kind=kLoop, calls=%fused_computation.4 | loop fusion | flops 3584 | bytes 18432 | tf_op jit(solution)/shard_map/log1p | solution.py:299
  (3 shorter events, 0.0 us)
Async XLA Ops:
  0.0 7.3 %copy-start.2 = (s32[16]{0:T(128)S(1)}, s32[16]{0:T(128)}, u32[]{:S(2)}) copy-start(s32[16]{0:T(128)} %near.1) | copy-start | bytes 196
  0.0 3.1 %collective-permute-start.1 = (bf16[512,1024]{1,0:T(8,128)(2,1)}, bf16[512,1024]{1,0:T(8,128)(2,1)S(1)}, u32[]{:S(2)}, u32[]{:S(2)}) collective-permute-start(bf16[512,1024]{1,0:T(8,128)(2,1)} %refs_0_.1), channel_id=1, source_target_pairs={{0,1},{1,0},{4,5},{5,4},{8,9},{9,8},{12,13},{13,12},{14,15},{15,14... | collective-permute-start | bytes 3145736 | tf_op jit(solution)/shard_map/ppermute | solution.py:204
  0.5 19.8 %collective-permute-start = (bf16[512,1024]{1,0:T(8,128)(2,1)}, bf16[512,1024]{1,0:T(8,128)(2,1)S(1)}, u32[]{:S(2)}, u32[]{:S(2)}) collective-permute-start(bf16[512,1024]{1,0:T(8,128)(2,1)} %refs_0_.1), channel_id=1, source_target_pairs={{0,4},{1,3},{4,8},{5,1},{8,12},{9,5},{12,14},{13,9},{14,10},{15,13... | collective-permute-start | bytes 3145736 | tf_op jit(solution)/shard_map/ppermute | solution.py:204
  3.1 24.3 %collective-permute-start.9 = (bf16[512,1024]{1,0:T(8,128)(2,1)S(1)}, bf16[512,1024]{1,0:T(8,128)(2,1)S(1)}, u32[]{:S(2)}, u32[]{:S(2)}) collective-permute-start(bf16[512,1024]{1,0:T(8,128)(2,1)S(1)} %collective-permute-done.1.refs_1_), channel_id=1, source_target_pairs={{0,4},{1,3},{4,8},{5,1},{8,12},{9,5},{12,14},{13,9},{14,10},{15,13... | collective-permute-start | bytes 3145736 | tf_op jit(solution)/shard_map/ppermute | solution.py:204
  5.9 1.4 %collective-permute-start.2 = (s32[1,512]{1,0:T(1,128)}, s32[1,512]{1,0:T(1,128)S(1)}, u32[]{:S(2)}, u32[]{:S(2)}) collective-permute-start(s32[1,512]{1,0:T(1,128)} %bitcast.2), channel_id=1, source_target_pairs={{0,1},{1,0},{4,5},{5,4},{8,9},{9,8},{12,13},{13,12},{14,15},{15,14... | collective-permute-start | bytes 6152 | tf_op jit(solution)/shard_map/ppermute | solution.py:204
  7.3 0.7 %copy-start.1 = (s32[512,1]{0,1:T(1,128)S(1)}, s32[512,1]{0,1:T(1,128)}, u32[]{:S(2)}) copy-start(s32[512,1]{0,1:T(1,128)} %param.4) | copy-start | bytes 6148
  8.5 3.3 %collective-permute-start.3 = (s32[4,512]{1,0:T(4,128)S(1)}, s32[4,512]{1,0:T(4,128)S(1)}, u32[]{:S(2)}, u32[]{:S(2)}) collective-permute-start(s32[4,512]{1,0:T(4,128)S(1)} %get-tuple-element.32), channel_id=1, source_target_pairs={{0,3},{1,4},{4,1},{5,8},{8,5},{9,12},{12,9},{13,14},{14,13},{15,10... | collective-permute-start | bytes 24584 | tf_op jit(solution)/shard_map/ppermute | solution.py:204
  11.8 1.3 %collective-permute-start.4 = (s32[4,512]{1,0:T(4,128)S(1)}, s32[4,512]{1,0:T(4,128)S(1)}, u32[]{:S(2)}, u32[]{:S(2)}) collective-permute-start(s32[4,512]{1,0:T(4,128)S(1)} %collective-permute-done.3.refs_4_.refs_6_), channel_id=1, source_target_pairs={{0,1},{1,0},{4,5},{5,4},{8,9},{9,8},{12,13},{13,12},{14,15},{15,14... | collective-permute-start | bytes 24584 | tf_op jit(solution)/shard_map/ppermute | solution.py:204
  13.1 3.2 %collective-permute-start.5 = (s32[4,512]{1,0:T(4,128)S(1)}, s32[4,512]{1,0:T(4,128)S(1)}, u32[]{:S(2)}, u32[]{:S(2)}) collective-permute-start(s32[4,512]{1,0:T(4,128)S(1)} %collective-permute-done.4.refs_5_.refs_7_), channel_id=1, source_target_pairs={{0,3},{1,4},{4,1},{5,8},{8,5},{9,12},{12,9},{13,14},{14,13},{15,10... | collective-permute-start | bytes 24584 | tf_op jit(solution)/shard_map/ppermute | solution.py:204
  16.3 3.9 %collective-permute-start.6 = (s32[4,512]{1,0:T(4,128)S(1)}, s32[4,512]{1,0:T(4,128)S(1)}, u32[]{:S(2)}, u32[]{:S(2)}) collective-permute-start(s32[4,512]{1,0:T(4,128)S(1)} %collective-permute-done.5.refs_3_), channel_id=1, source_target_pairs={{0,1},{1,0},{4,5},{5,4},{8,9},{9,8},{12,13},{13,12},{14,15},{15,14... | collective-permute-start | bytes 24584 | tf_op jit(solution)/shard_map/ppermute | solution.py:204
  17.0 1.2 %copy-start = (bf16[512,1024]{1,0:T(8,128)(2,1)S(1)}, bf16[512,1024]{1,0:T(8,128)(2,1)}, u32[]{:S(2)}) copy-start(bf16[512,1024]{1,0:T(8,128)(2,1)} %refs_0_.1) | copy-start | bytes 3145732
  20.3 2.2 %collective-permute-start.8 = (bf16[256,1024]{1,0:T(8,128)(2,1)S(1)}, bf16[256,1024]{1,0:T(8,128)(2,1)S(1)}, u32[]{:S(2)}, u32[]{:S(2)}) collective-permute-start(bf16[256,1024]{1,0:T(8,128)(2,1)S(1)} %get-tuple-element.59), channel_id=1, source_target_pairs={{0,1},{1,0},{4,5},{5,4},{8,9},{9,8},{12,13},{13,12},{14,15},{15,14... | collective-permute-start | bytes 1572872 | tf_op jit(solution)/shard_map/ppermute | solution.py:204
  20.4 2.6 %collective-permute-start.7 = (bf16[256,1024]{1,0:T(8,128)(2,1)S(1)}, bf16[256,1024]{1,0:T(8,128)(2,1)S(1)}, u32[]{:S(2)}, u32[]{:S(2)}) collective-permute-start(bf16[256,1024]{1,0:T(8,128)(2,1)S(1)} %get-tuple-element.60), channel_id=1, source_target_pairs={{0,1},{1,0},{4,5},{5,4},{8,9},{9,8},{12,13},{13,12},{14,15},{15,14... | collective-permute-start | bytes 1572872 | tf_op jit(solution)/shard_map/ppermute | solution.py:204
  20.9 17.8 %collective-permute-start.12 = (bf16[512,1024]{1,0:T(8,128)(2,1)S(1)}, bf16[512,1024]{1,0:T(8,128)(2,1)S(1)}, u32[]{:S(2)}, u32[]{:S(2)}) collective-permute-start(bf16[512,1024]{1,0:T(8,128)(2,1)S(1)} %collective-permute-done.refs_0_), channel_id=1, source_target_pairs={{0,4},{1,3},{4,8},{5,1},{8,12},{9,5},{12,14},{13,9},{14,10},{15,13... | collective-permute-start | bytes 3145736 | tf_op jit(solution)/shard_map/ppermute | solution.py:204
  27.8 2.7 %collective-permute-start.11 = (bf16[256,1024]{1,0:T(8,128)(2,1)S(1)}, bf16[256,1024]{1,0:T(8,128)(2,1)S(1)}, u32[]{:S(2)}, u32[]{:S(2)}) collective-permute-start(bf16[256,1024]{1,0:T(8,128)(2,1)S(1)} %get-tuple-element.57), channel_id=1, source_target_pairs={{0,1},{1,0},{4,5},{5,4},{8,9},{9,8},{12,13},{13,12},{14,15},{15,14... | collective-permute-start | bytes 1572872 | tf_op jit(solution)/shard_map/ppermute | solution.py:204
  27.9 2.6 %collective-permute-start.10 = (bf16[256,1024]{1,0:T(8,128)(2,1)S(1)}, bf16[256,1024]{1,0:T(8,128)(2,1)S(1)}, u32[]{:S(2)}, u32[]{:S(2)}) collective-permute-start(bf16[256,1024]{1,0:T(8,128)(2,1)S(1)} %get-tuple-element.58), channel_id=1, source_target_pairs={{0,1},{1,0},{4,5},{5,4},{8,9},{9,8},{12,13},{13,12},{14,15},{15,14... | collective-permute-start | bytes 1572872 | tf_op jit(solution)/shard_map/ppermute | solution.py:204
  28.4 21.6 %collective-permute-start.20 = (bf16[512,1024]{1,0:T(8,128)(2,1)S(1)}, bf16[512,1024]{1,0:T(8,128)(2,1)S(1)}, u32[]{:S(2)}, u32[]{:S(2)}) collective-permute-start(bf16[512,1024]{1,0:T(8,128)(2,1)S(1)} %unit_rows.1.refs_2_), channel_id=1, source_target_pairs={{0,4},{1,3},{4,8},{5,1},{8,12},{9,5},{12,14},{13,9},{14,10},{15,13... | collective-permute-start | bytes 3145736 | tf_op jit(solution)/shard_map/ppermute | solution.py:204
  34.6 4.1 %collective-permute-start.13 = (f32[2,512]{1,0:T(2,128)S(1)}, f32[2,512]{1,0:T(2,128)S(1)}, u32[]{:S(2)}, u32[]{:S(2)}) collective-permute-start(f32[2,512]{1,0:T(2,128)S(1)} %slice.29), channel_id=1, source_target_pairs={{0,2},{1,5},{4,0},{5,9},{8,4},{9,13},{12,8},{13,15},{14,12},{15,11... | collective-permute-start | bytes 12296 | tf_op jit(solution)/shard_map/ppermute | solution.py:204
  38.8 5.4 %collective-permute-start.18 = (bf16[256,1024]{1,0:T(8,128)(2,1)S(1)}, bf16[256,1024]{1,0:T(8,128)(2,1)S(1)}, u32[]{:S(2)}, u32[]{:S(2)}) collective-permute-start(bf16[256,1024]{1,0:T(8,128)(2,1)S(1)} %get-tuple-element.55), channel_id=1, source_target_pairs={{0,1},{1,0},{4,5},{5,4},{8,9},{9,8},{12,13},{13,12},{14,15},{15,14... | collective-permute-start | bytes 1572872 | tf_op jit(solution)/shard_map/ppermute | solution.py:204
  38.9 5.4 %collective-permute-start.17 = (bf16[256,1024]{1,0:T(8,128)(2,1)S(1)}, bf16[256,1024]{1,0:T(8,128)(2,1)S(1)}, u32[]{:S(2)}, u32[]{:S(2)}) collective-permute-start(bf16[256,1024]{1,0:T(8,128)(2,1)S(1)} %get-tuple-element.56), channel_id=1, source_target_pairs={{0,1},{1,0},{4,5},{5,4},{8,9},{9,8},{12,13},{13,12},{14,15},{15,14... | collective-permute-start | bytes 1572872 | tf_op jit(solution)/shard_map/ppermute | solution.py:204
  42.1 11.7 %collective-permute-start.16 = (f32[2,512]{1,0:T(2,128)S(1)}, f32[2,512]{1,0:T(2,128)S(1)}, u32[]{:S(2)}, u32[]{:S(2)}) collective-permute-start(f32[2,512]{1,0:T(2,128)S(1)} %get-tuple-element.61), channel_id=1, source_target_pairs={{0,4},{1,3},{4,8},{5,1},{8,12},{9,5},{12,14},{13,9},{14,10},{15,13... | collective-permute-start | bytes 12296 | tf_op jit(solution)/shard_map/ppermute | solution.py:204
  44.2 9.6 %collective-permute-start.15 = (f32[2,512]{1,0:T(2,128)S(1)}, f32[2,512]{1,0:T(2,128)S(1)}, u32[]{:S(2)}, u32[]{:S(2)}) collective-permute-start(f32[2,512]{1,0:T(2,128)S(1)} %get-tuple-element.61), channel_id=1, source_target_pairs={{0,5},{1,2},{4,9},{5,0},{8,13},{9,4},{12,15},{13,8},{14,11},{15,12... | collective-permute-start | bytes 12296 | tf_op jit(solution)/shard_map/ppermute | solution.py:204
  45.3 10.1 %collective-permute-start.19 = (f32[2,512]{1,0:T(2,128)S(1)}, f32[2,512]{1,0:T(2,128)S(1)}, u32[]{:S(2)}, u32[]{:S(2)}) collective-permute-start(f32[2,512]{1,0:T(2,128)S(1)} %get-tuple-element.53), channel_id=1, source_target_pairs={{0,6},{1,9},{4,2},{5,13},{8,0},{9,15},{12,4},{13,11},{14,8},{15,7}... | collective-permute-start | bytes 12296 | tf_op jit(solution)/shard_map/ppermute | solution.py:204
  47.7 6.0 %collective-permute-start.14 = (f32[1,512]{1,0:T(1,128)S(1)}, f32[1,512]{1,0:T(1,128)S(1)}, u32[]{:S(2)}, u32[]{:S(2)}) collective-permute-start(f32[1,512]{1,0:T(1,128)S(1)} %slice.31), channel_id=1, source_target_pairs={{0,1},{1,0},{4,5},{5,4},{8,9},{9,8},{12,13},{13,12},{14,15},{15,14... | collective-permute-start | bytes 6152 | tf_op jit(solution)/shard_map/ppermute | solution.py:204
  51.5 4.0 %collective-permute-start.21 = (f32[1,512]{1,0:T(1,128)S(1)}, f32[1,512]{1,0:T(1,128)S(1)}, u32[]{:S(2)}, u32[]{:S(2)}) collective-permute-start(f32[1,512]{1,0:T(1,128)S(1)} %end_terms.5), channel_id=1, source_target_pairs={{0,7},{1,8},{4,3},{5,12},{8,1},{9,14},{12,5},{13,10},{14,9},{15,6}... | collective-permute-start | bytes 6152 | tf_op jit(solution)/shard_map/ppermute | solution.py:204

commit v10 on v9

--- a/solution.py
+++ b/solution.py
@@ -47,14 +47,22 @@
     return jnp.transpose(jnp.broadcast_to(row, (128, row.shape[1])))
 
 
-def terms(a_unit, b_unit, a_own, a_near, b_own, b_near):
+def weights(a_own, a_near, b_own, b_near):
+    wide = b_own.shape[1] // 128
+    a_own, a_near = jnp.tile(a_own, (1, wide)), jnp.tile(a_near, (1, wide))
+    near = jnp.where(a_near == b_own, 0.5, 0.0) + jnp.where(a_own == b_near, 0.5, 0.0)
+    return jnp.where(a_own == b_own, 1.0, near)
+
+
+def exponentials(a_unit, b_unit):
     sim = lax.dot_general(
         a_unit, b_unit, (((1,), (1,)), ((), ())), preferred_element_type=jnp.float32
     )
-    wide = sim.shape[1] // 128
-    a_own, a_near = jnp.tile(a_own, (1, wide)), jnp.tile(a_near, (1, wide))
-    near = jnp.where(a_near == b_own, 0.5, 0.0) + jnp.where(a_own == b_near, 0.5, 0.0)
-    return jnp.where(a_own == b_own, 1.0, near) * jnp.exp(16.0 * sim)
+    return jnp.exp(16.0 * sim)
+
+
+def terms(a_unit, b_unit, a_own, a_near, b_own, b_near):
+    return weights(a_own, a_near, b_own, b_near) * exponentials(a_unit, b_unit)
 
 
 def lanes_added(x):
@@ -187,6 +195,45 @@
         cost_estimate=pl.CostEstimate(flops=0, bytes_accessed=0, transcendentals=0),
         name="unit_rows",
     )(rows)
+
+
+def weights_kernel(a_names, *refs):
+    b_names, result = refs[:-1], refs[-1]
+    a_own, a_near = [as_column(a_names[row : row + 1, :]) for row in (1, 3)]
+    rows = a_names.shape[1]
+    for at, names in enumerate(b_names):
+        there = slice(at * rows, (at + 1) * rows)
+        for here in strips(rows):
+            value = weights(a_own[here], a_near[here], names[at : at + 1, :], names[at + 2 : at + 3, :])
+            result[here, there] = value.astype(jnp.bfloat16)
+
+
+def last_kernel(a, *refs):
+    others, weight, sums = refs[:-2], refs[-2], refs[-1]
+    rows = a.shape[0]
+    totals = [jnp.zeros((here.stop - here.start, 128), jnp.float32) for here in strips(rows)]
+    for number, other in enumerate(others):
+        for there in strips(rows):
+            column = slice(number * rows + there.start, number * rows + there.stop)
+            for at, here in enumerate(strips(rows)):
+                value = exponentials(a[here, :], other[there, :])
+                value = weight[here, column].astype(jnp.float32) * value
+                totals[at] = totals[at] + lanes_added(value)
+    for here, total in zip(strips(rows), totals):
+        sums[:, here] = as_row(total)
+
+
+def in_vmem(kernel, shape, dtype, label, *operands):
+    vmem = pl.BlockSpec(memory_space=pltpu.VMEM)
+    return pl.pallas_call(
+        kernel,
+        out_shape=jax.ShapeDtypeStruct(shape, dtype),
+        in_specs=[vmem] * len(operands),
+        out_specs=vmem,
+        compiler_params=pltpu.CompilerParams(vmem_limit_bytes=40 << 20),
+        cost_estimate=pl.CostEstimate(flops=0, bytes_accessed=0, transcendentals=0),
+        name=label,
+    )(*operands)
 
 
 def per_device(embed, owner, near):
@@ -293,8 +340,10 @@
         blocks, names, ((0, 0, (1,)),), "end_terms", (1,), before=sums[:END_ROOM], room=END_ROOM
     )
     total = total + moved(sums, back(hops))[:1]
-    blocks = [(side[hops][1], False, 0, 1, 0), (facing, False, 1, 0, 0), (inner[1], False, 2, 1, 0)]
-    sums, _ = row_sums(blocks, names, ((0, 0, (1, 2)),), "end_terms")
+    weight = in_vmem(weights_kernel, (rows, 2 * rows), jnp.bfloat16, "end_weights", *names)
+    sums = in_vmem(
+        last_kernel, (1, rows), jnp.float32, "last_terms", side[hops][1], facing, inner[1], weight
+    )
     total = total + moved(sums, back(hops, 1))
     return jnp.log1p(total)[0]
 

time: 56.4 us -> 56.3 us (level)
  starting transfers between devices: 24.1 us -> 22.9 us
  waiting for transfers between devices: 13.7 us -> 14.3 us
  Pallas kernels: 15.3 us -> 15.9 us
    pallas_call x0 -> x2, Pallas kernels: none -> 2.06 us  [in_vmem(): pl.pallas_call(kernel, out_shape=jax.ShapeDtypeStruct(shape, dtype), in_s...]
    pallas_call x6 -> x5, Pallas kernels: 14.4 us -> 13 us  [row_sums(): pl.pallas_call(functools.partial(sums_kernel, [(len(block[0]), *block[1:]...]
    ppermute x22, starting transfers between devices: 24.1 us -> 22.9 us  [moved(): return lax.ppermute(block, 'blk', route)]
    ppermute x22, waiting for transfers between devices: 13.7 us -> 14.3 us  [moved(): return lax.ppermute(block, 'blk', route)]
  transfers between devices with their start and end apart: 22 -> 22, of which waited for: 10 -> 10; matrix products, arithmetic and copies ran while one was open for 0% -> 0% of each run, Pallas kernels for 27% -> 28%
where the time goes in v10:
time: 56.3 us; the launch traced here: 56 us
  starting transfers between devices  22.9 us (41%)
  Pallas kernels  15.9 us (28%)
  waiting for transfers between devices  14.3 us (25%)
  local copies, waits for them, and re-layouts  2.14 us (4%)
  other arithmetic  0.6 us (1%)
    ppermute x22, starting transfers between devices, moved(): return lax.ppermute(block, 'blk', route)  22.9 us
    ppermute x22, waiting for transfers between devices, moved(): return lax.ppermute(block, 'blk', route)  14.3 us
    pallas_call x5, Pallas kernels, row_sums(): pl.pallas_call(functools.partial(sums_kernel, [(len(block[0]), *block[1:]...  13 us
    pallas_call x2, Pallas kernels, in_vmem(): pl.pallas_call(kernel, out_shape=jax.ShapeDtypeStruct(shape, dtype), in_s...  2.06 us
    unnamed x6, local copies, waits for them, and re-layouts  1.91 us
  transfers between devices with their start and end apart: 22, of which 10 were waited for; matrix products, arithmetic and copies ran while one was open for 0% of the time, Pallas kernels for 28%

profile of v10, /device:TPU:0, one launch (start us, length us, event | category | flops | bytes accessed | tf_op | source)
XLA Modules:
  0.0 56.0 jit_solution(4600080712787611059)
XLA Ops:
  0.0 0.0 copy-start.2
  0.0 0.5 collective-permute-start.1
  0.5 2.6 %collective-permute-start = (bf16[512,1024]{1,0:T(8,128)(2,1)}, bf16[512,1024]{1,0:T(8,128)(2,1)S(1)}, u32[]{:S(2)}, u32[]{:S(2)}) collective-permute-start(bf16[512,1024]{1,0:T(8,128)(2,1)} %refs_0_.1), channel_id=1, source_target_pairs={{0,4},{1,3},{4,8},{5,1},{8,12},{9,5},{12,14},{13,9},{14,10},{15,13... | collective-permute-start | bytes 3145736 | tf_op jit(solution)/shard_map/ppermute | solution.py:251
  3.1 0.0 collective-permute-done.1.refs_1_
  3.1 2.8 %collective-permute-start.9 = (bf16[512,1024]{1,0:T(8,128)(2,1)S(1)}, bf16[512,1024]{1,0:T(8,128)(2,1)S(1)}, u32[]{:S(2)}, u32[]{:S(2)}) collective-permute-start(bf16[512,1024]{1,0:T(8,128)(2,1)S(1)} %collective-permute-done.1.refs_1_), channel_id=1, source_target_pairs={{0,4},{1,3},{4,8},{5,1},{8,12},{9,5},{12,14},{13,9},{14,10},{15,13... | collective-permute-start | bytes 3145736 | tf_op jit(solution)/shard_map/ppermute | solution.py:251
  5.9 0.0 collective-permute-start.2
  5.9 1.4 %collective-permute-done.2.other = s32[1,512]{1,0:T(1,128)S(1)} collective-permute-done((s32[1,512]{1,0:T(1,128)}, s32[1,512]{1,0:T(1,128)S(1)}, u32[]{:S(2)}, u32[]{:S(2)}) %collective-permute-start.2) | collective-permute-done | bytes 2080 | tf_op jit(solution)/shard_map/ppermute | solution.py:251
  7.3 0.0 copy-done.2
  7.3 0.0 copy-start.1
  7.3 0.7 %copy-done.1 = s32[512,1]{0,1:T(1,128)S(1)} copy-done((s32[512,1]{0,1:T(1,128)S(1)}, s32[512,1]{0,1:T(1,128)}, u32[]{:S(2)}) %copy-start.1) | copy-done | bytes 2072
  8.0 0.6 %name_tables.1 = (s32[4,512]{1,0:T(4,128)S(1)}, s32[4,512]{1,0:T(4,128)S(1)}) custom-call(s32[16]{0:T(128)S(1)} %copy-done.2, s32[1,512]{1,0:T(1,128)S(1)} %bitcast.3, s32[1,512]{1,0:T(1,128)S(1)} %collective-permute-done.2.other), custom_call_target="tpu_custom_call" | custom-call | tf_op jit(solution)/shard_map/name_tables/pallas_call | solution.py:176
  8.5 1.0 %collective-permute-start.3 = (s32[4,512]{1,0:T(4,128)S(1)}, s32[4,512]{1,0:T(4,128)S(1)}, u32[]{:S(2)}, u32[]{:S(2)}) collective-permute-start(s32[4,512]{1,0:T(4,128)S(1)} %get-tuple-element.32), channel_id=1, source_target_pairs={{0,3},{1,4},{4,1},{5,8},{8,5},{9,12},{12,9},{13,14},{14,13},{15,10... | collective-permute-start | bytes 24584 | tf_op jit(solution)/shard_map/ppermute | solution.py:251
  9.6 2.2 %collective-permute-done.3.refs_4_.refs_6_ = s32[4,512]{1,0:T(4,128)S(1)} collective-permute-done((s32[4,512]{1,0:T(4,128)S(1)}, s32[4,512]{1,0:T(4,128)S(1)}, u32[]{:S(2)}, u32[]{:S(2)}) %collective-permute-start.3) | collective-permute-done | bytes 8224 | tf_op jit(solution)/shard_map/ppermute | solution.py:251
  11.8 0.5 collective-permute-start.4
  12.3 0.8 %collective-permute-done.4.refs_5_.refs_7_.refs_1_ = s32[4,512]{1,0:T(4,128)S(1)} collective-permute-done((s32[4,512]{1,0:T(4,128)S(1)}, s32[4,512]{1,0:T(4,128)S(1)}, u32[]{:S(2)}, u32[]{:S(2)}) %collective-permute-start.4) | collective-permute-done | bytes 8224 | tf_op jit(solution)/shard_map/ppermute | solution.py:251
  13.1 1.1 %collective-permute-start.5 = (s32[4,512]{1,0:T(4,128)S(1)}, s32[4,512]{1,0:T(4,128)S(1)}, u32[]{:S(2)}, u32[]{:S(2)}) collective-permute-start(s32[4,512]{1,0:T(4,128)S(1)} %collective-permute-done.4.refs_5_.refs_7_.refs_1_), channel_id=1, source_target_pairs={{0,3},{1,4},{4,1},{5,8},{8,5},{9,12},{12,9},{13,14},{14,13},{15,10... | collective-permute-start | bytes 24584 | tf_op jit(solution)/shard_map/ppermute | solution.py:251
  14.3 2.1 %collective-permute-done.5.refs_3_.a_names = s32[4,512]{1,0:T(4,128)S(1)} collective-permute-done((s32[4,512]{1,0:T(4,128)S(1)}, s32[4,512]{1,0:T(4,128)S(1)}, u32[]{:S(2)}, u32[]{:S(2)}) %collective-permute-start.5) | collective-permute-done | bytes 8224 | tf_op jit(solution)/shard_map/ppermute | solution.py:251
  16.3 0.6 %collective-permute-start.6 = (s32[4,512]{1,0:T(4,128)S(1)}, s32[4,512]{1,0:T(4,128)S(1)}, u32[]{:S(2)}, u32[]{:S(2)}) collective-permute-start(s32[4,512]{1,0:T(4,128)S(1)} %collective-permute-done.5.refs_3_.a_names), channel_id=1, source_target_pairs={{0,1},{1,0},{4,5},{5,4},{8,9},{9,8},{12,13},{13,12},{14,15},{15,14... | collective-permute-start | bytes 24584 | tf_op jit(solution)/shard_map/ppermute | solution.py:251
  17.0 0.0 copy-start
  17.0 1.2 %copy-done = bf16[512,1024]{1,0:T(8,128)(2,1)S(1)} copy-done((bf16[512,1024]{1,0:T(8,128)(2,1)S(1)}, bf16[512,1024]{1,0:T(8,128)(2,1)}, u32[]{:S(2)}) %copy-start) | copy-done | bytes 1048600
  18.2 2.0 %own_terms.1 = (f32[1,512]{1,0:T(1,128)S(1)}, bf16[512,1024]{1,0:T(8,128)(2,1)S(1)}) custom-call(bf16[512,1024]{1,0:T(8,128)(2,1)S(1)} %copy-done, bf16[512,1024]{1,0:T(8,128)(2,1)S(1)} %collective-permute-done.1.refs_1_, s32[4,512]{1,0:T(4,128)S(1)} %get-tuple-element.30.refs_2_.refs_6_.refs_8_), custom_call_target="tpu_custom_call" | custom-call | tf_op jit(solution)/shard_map/own_terms/pallas_call | solution.py:142
  20.2 0.0 collective-permute-done.6.refs_4_.refs_0_
  20.2 0.0 collective-permute-done.refs_0_
  20.2 0.1 fusion.4
  20.3 0.1 collective-permute-start.7
  20.4 0.5 collective-permute-start.8
  20.9 1.6 %collective-permute-start.12 = (bf16[512,1024]{1,0:T(8,128)(2,1)S(1)}, bf16[512,1024]{1,0:T(8,128)(2,1)S(1)}, u32[]{:S(2)}, u32[]{:S(2)}) collective-permute-start(bf16[512,1024]{1,0:T(8,128)(2,1)S(1)} %collective-permute-done.refs_0_), channel_id=1, source_target_pairs={{0,4},{1,3},{4,8},{5,1},{8,12},{9,5},{12,14},{13,9},{14,10},{15,13... | collective-permute-start | bytes 3145736 | tf_op jit(solution)/shard_map/ppermute | solution.py:251
  22.4 0.0 collective-permute-done.7.refs_1_
  22.5 0.6 %collective-permute-done.8.refs_2_ = bf16[256,1024]{1,0:T(8,128)(2,1)S(1)} collective-permute-done((bf16[256,1024]{1,0:T(8,128)(2,1)S(1)}, bf16[256,1024]{1,0:T(8,128)(2,1)S(1)}, u32[]{:S(2)}, u32[]{:S(2)}) %collective-permute-start.8) | collective-permute-done | bytes 524320 | tf_op jit(solution)/shard_map/ppermute | solution.py:251
  23.0 3.2 %first_terms.1 = (f32[3,512]{1,0:T(4,128)S(1)}, bf16[512,1024]{1,0:T(8,128)(2,1)S(1)}, bf16[512,1024]{1,0:T(8,128)(2,1)S(1)}) custom-call(bf16[512,1024]{1,0:T(8,128)(2,1)S(1)} %collective-permute-done.refs_0_, bf16[256,1024]{1,0:T(8,128)(2,1)S(1)} %collective-permute-done.7.refs_1_, bf16[256,1024]{1,0:T(8,128)(2,1)S(1)} %collective-permute-done.8.refs_2_, ...), custom_call_target="tpu_custom_call" | custom-call | tf_op jit(solution)/shard_map/first_terms/pallas_call | solution.py:142
  26.2 1.2 %collective-permute-done.9.source = bf16[512,1024]{1,0:T(8,128)(2,1)S(1)} collective-permute-done((bf16[512,1024]{1,0:T(8,128)(2,1)S(1)}, bf16[512,1024]{1,0:T(8,128)(2,1)S(1)}, u32[]{:S(2)}, u32[]{:S(2)}) %collective-permute-start.9) | collective-permute-done | bytes 1048608 | tf_op jit(solution)/shard_map/ppermute | solution.py:251
  27.4 0.3 unit_rows.1.refs_2_
  27.8 0.1 fusion.3
  27.8 0.1 collective-permute-start.10
  27.9 0.5 collective-permute-start.11
  28.4 2.1 %collective-permute-start.20 = (bf16[512,1024]{1,0:T(8,128)(2,1)S(1)}, bf16[512,1024]{1,0:T(8,128)(2,1)S(1)}, u32[]{:S(2)}, u32[]{:S(2)}) collective-permute-start(bf16[512,1024]{1,0:T(8,128)(2,1)S(1)} %unit_rows.1.refs_2_), channel_id=1, source_target_pairs={{0,4},{1,3},{4,8},{5,1},{8,12},{9,5},{12,14},{13,9},{14,10},{15,13... | collective-permute-start | bytes 3145736 | tf_op jit(solution)/shard_map/ppermute | solution.py:251
  30.5 0.0 collective-permute-done.10.refs_3_
  30.5 0.1 collective-permute-done.11.refs_4_
  30.6 4.0 %pair_terms.1 = (f32[3,512]{1,0:T(4,128)S(1)}, bf16[512,1024]{1,0:T(8,128)(2,1)S(1)}) custom-call(bf16[512,1024]{1,0:T(8,128)(2,1)S(1)} %get-tuple-element.38.refs_0_, bf16[512,1024]{1,0:T(8,128)(2,1)S(1)} %get-tuple-element.46.refs_1_, bf16[512,1024]{1,0:T(8,128)(2,1)S(1)} %unit_rows.1.refs_2_, bf16[256,1024]{1,0:T(8,128)(2,1)S(1)} %collective-permute-done.10.refs_3_, ...), custom_call_target="tpu_custom_call" | custom-call | tf_op jit(solution)/shard_map/pair_terms/pallas_call | solution.py:142
  34.6 2.2 %collective-permute-start.13 = (f32[2,512]{1,0:T(2,128)S(1)}, f32[2,512]{1,0:T(2,128)S(1)}, u32[]{:S(2)}, u32[]{:S(2)}) collective-permute-start(f32[2,512]{1,0:T(2,128)S(1)} %slice.29), channel_id=1, source_target_pairs={{0,2},{1,5},{4,0},{5,9},{8,4},{9,13},{12,8},{13,15},{14,12},{15,11... | collective-permute-start | bytes 12296 | tf_op jit(solution)/shard_map/ppermute | solution.py:251
  36.9 1.8 %collective-permute-done.12.refs_0_ = bf16[512,1024]{1,0:T(8,128)(2,1)S(1)} collective-permute-done((bf16[512,1024]{1,0:T(8,128)(2,1)S(1)}, bf16[512,1024]{1,0:T(8,128)(2,1)S(1)}, u32[]{:S(2)}, u32[]{:S(2)}) %collective-permute-start.12) | collective-permute-done | bytes 1048608 | tf_op jit(solution)/shard_map/ppermute | solution.py:251
  38.7 0.0 collective-permute-done.13
  38.7 0.1 fusion.2
  38.8 0.1 collective-permute-start.17
  38.9 0.5 collective-permute-start.18
  39.4 2.7 %end_terms.2 = (f32[3,512]{1,0:T(4,128)S(1)}, bf16[512,1024]{1,0:T(8,128)(2,1)S(1)}) custom-call(bf16[512,1024]{1,0:T(8,128)(2,1)S(1)} %collective-permute-done.12.refs_0_, bf16[512,1024]{1,0:T(8,128)(2,1)S(1)} %get-tuple-element.46.refs_1_, bf16[512,1024]{1,0:T(8,128)(2,1)S(1)} %get-tuple-element.47.refs_2_.refs_1_, ...), custom_call_target="tpu_custom_call" | custom-call | tf_op jit(solution)/shard_map/end_terms/pallas_call | solution.py:142
  42.1 1.8 %collective-permute-start.15 = (f32[2,512]{1,0:T(2,128)S(1)}, f32[2,512]{1,0:T(2,128)S(1)}, u32[]{:S(2)}, u32[]{:S(2)}) collective-permute-start(f32[2,512]{1,0:T(2,128)S(1)} %get-tuple-element.61), channel_id=1, source_target_pairs={{0,5},{1,2},{4,9},{5,0},{8,13},{9,4},{12,15},{13,8},{14,11},{15,12... | collective-permute-start | bytes 12296 | tf_op jit(solution)/shard_map/ppermute | solution.py:251
  43.9 1.6 %collective-permute-start.16 = (f32[2,512]{1,0:T(2,128)S(1)}, f32[2,512]{1,0:T(2,128)S(1)}, u32[]{:S(2)}, u32[]{:S(2)}) collective-permute-start(f32[2,512]{1,0:T(2,128)S(1)} %get-tuple-element.61), channel_id=1, source_target_pairs={{0,4},{1,3},{4,8},{5,1},{8,12},{9,5},{12,14},{13,9},{14,10},{15,13... | collective-permute-start | bytes 12296 | tf_op jit(solution)/shard_map/ppermute | solution.py:251
  45.5 0.0 collective-permute-done.17.refs_1_
  45.5 0.0 collective-permute-done.18.refs_2_
  45.5 1.1 %end_terms.3 = (f32[2,512]{1,0:T(2,128)S(1)}, bf16[512,1024]{1,0:T(8,128)(2,1)S(1)}) custom-call(bf16[512,1024]{1,0:T(8,128)(2,1)S(1)} %get-tuple-element.51.refs_0_, bf16[256,1024]{1,0:T(8,128)(2,1)S(1)} %collective-permute-done.17.refs_1_, bf16[256,1024]{1,0:T(8,128)(2,1)S(1)} %collective-permute-done.18.refs_2_, ...), custom_call_target="tpu_custom_call" | custom-call | tf_op jit(solution)/shard_map/end_terms/pallas_call | solution.py:142
  46.6 0.3 collective-permute-start.19
  46.8 0.6 %end_weights.1.refs_2_ = bf16[512,1024]{1,0:T(8,128)(2,1)S(1)} custom-call(s32[4,512]{1,0:T(4,128)S(1)} %collective-permute-done.5.refs_3_.a_names, s32[4,512]{1,0:T(4,128)S(1)} %collective-permute-done.6.refs_4_.refs_0_, s32[4,512]{1,0:T(4,128)S(1)} %collective-permute-done.4.refs_5_.refs_7_.refs_1_), custom_call_target="tpu_custom_call" | custom-call | tf_op jit(solution)/shard_map/end_weights/pallas_call | solution.py:228
  47.4 0.1 collective-permute-start.14
  47.5 2.4 %collective-permute-done.20.a = bf16[512,1024]{1,0:T(8,128)(2,1)S(1)} collective-permute-done((bf16[512,1024]{1,0:T(8,128)(2,1)S(1)}, bf16[512,1024]{1,0:T(8,128)(2,1)S(1)}, u32[]{:S(2)}, u32[]{:S(2)}) %collective-permute-start.20) | collective-permute-done | bytes 1048608 | tf_op jit(solution)/shard_map/ppermute | solution.py:251
  49.9 1.5 %last_terms.1 = f32[1,512]{1,0:T(1,128)S(1)} custom-call(bf16[512,1024]{1,0:T(8,128)(2,1)S(1)} %collective-permute-done.20.a, bf16[512,1024]{1,0:T(8,128)(2,1)S(1)} %get-tuple-element.54.refs_0_, bf16[512,1024]{1,0:T(8,128)(2,1)S(1)} %get-tuple-element.47.refs_2_.refs_1_, bf16[512,1024]{1,0:T(8,128)(2,1)S(1)} %end_weights.1.refs_2_), custom_call_target="tpu_custom_call" | custom-call | tf_op jit(solution)/shard_map/last_terms/pallas_call | solution.py:228
  51.4 2.3 %collective-permute-start.21 = (f32[1,512]{1,0:T(1,128)S(1)}, f32[1,512]{1,0:T(1,128)S(1)}, u32[]{:S(2)}, u32[]{:S(2)}) collective-permute-start(f32[1,512]{1,0:T(1,128)S(1)} %last_terms.1), channel_id=1, source_target_pairs={{0,7},{1,8},{4,3},{5,12},{8,1},{9,14},{12,5},{13,10},{14,9},{15,6}... | collective-permute-start | bytes 6152 | tf_op jit(solution)/shard_map/ppermute | solution.py:251
  53.7 0.0 collective-permute-done.14
  53.7 0.0 collective-permute-done.15
  53.8 0.0 collective-permute-done.16
  53.8 1.6 %collective-permute-done.21 = f32[1,512]{1,0:T(1,128)S(1)} collective-permute-done((f32[1,512]{1,0:T(1,128)S(1)}, f32[1,512]{1,0:T(1,128)S(1)}, u32[]{:S(2)}, u32[]{:S(2)}) %collective-permute-start.21) | collective-permute-done | bytes 2080 | tf_op jit(solution)/shard_map/ppermute | solution.py:251
  55.4 0.0 collective-permute-done.19
  55.4 0.6 %fusion.1 = f32[1,512]{1,0:T(1,128)} fusion(f32[1,512]{1,0:T(1,128)S(1)} %collective-permute-done.21, f32[2,512]{1,0:T(2,128)S(1)} %collective-permute-done.19, f32[2,512]{1,0:T(2,128)S(1)} %collective-permute-done.16, f32[2,512]{1,0:T(2,128)S(1)} %collective-permute-done.15, f32[1,512]{1,0:T(1,128)S(1)} %collective-permute-done.14, ...), kind=kLoop, calls=%fused_computation.4 | loop fusion | flops 3584 | bytes 18432 | tf_op jit(solution)/shard_map/log1p | solution.py:348
  (3 shorter events, 0.0 us)
Async XLA Ops:
  0.0 7.3 %copy-start.2 = (s32[16]{0:T(128)S(1)}, s32[16]{0:T(128)}, u32[]{:S(2)}) copy-start(s32[16]{0:T(128)} %near.1) | copy-start | bytes 196
  0.0 3.1 %collective-permute-start.1 = (bf16[512,1024]{1,0:T(8,128)(2,1)}, bf16[512,1024]{1,0:T(8,128)(2,1)S(1)}, u32[]{:S(2)}, u32[]{:S(2)}) collective-permute-start(bf16[512,1024]{1,0:T(8,128)(2,1)} %refs_0_.1), channel_id=1, source_target_pairs={{0,1},{1,0},{4,5},{5,4},{8,9},{9,8},{12,13},{13,12},{14,15},{15,14... | collective-permute-start | bytes 3145736 | tf_op jit(solution)/shard_map/ppermute | solution.py:251
  0.5 19.8 %collective-permute-start = (bf16[512,1024]{1,0:T(8,128)(2,1)}, bf16[512,1024]{1,0:T(8,128)(2,1)S(1)}, u32[]{:S(2)}, u32[]{:S(2)}) collective-permute-start(bf16[512,1024]{1,0:T(8,128)(2,1)} %refs_0_.1), channel_id=1, source_target_pairs={{0,4},{1,3},{4,8},{5,1},{8,12},{9,5},{12,14},{13,9},{14,10},{15,13... | collective-permute-start | bytes 3145736 | tf_op jit(solution)/shard_map/ppermute | solution.py:251
  3.1 24.3 %collective-permute-start.9 = (bf16[512,1024]{1,0:T(8,128)(2,1)S(1)}, bf16[512,1024]{1,0:T(8,128)(2,1)S(1)}, u32[]{:S(2)}, u32[]{:S(2)}) collective-permute-start(bf16[512,1024]{1,0:T(8,128)(2,1)S(1)} %collective-permute-done.1.refs_1_), channel_id=1, source_target_pairs={{0,4},{1,3},{4,8},{5,1},{8,12},{9,5},{12,14},{13,9},{14,10},{15,13... | collective-permute-start | bytes 3145736 | tf_op jit(solution)/shard_map/ppermute | solution.py:251
  5.9 1.4 %collective-permute-start.2 = (s32[1,512]{1,0:T(1,128)}, s32[1,512]{1,0:T(1,128)S(1)}, u32[]{:S(2)}, u32[]{:S(2)}) collective-permute-start(s32[1,512]{1,0:T(1,128)} %bitcast.2), channel_id=1, source_target_pairs={{0,1},{1,0},{4,5},{5,4},{8,9},{9,8},{12,13},{13,12},{14,15},{15,14... | collective-permute-start | bytes 6152 | tf_op jit(solution)/shard_map/ppermute | solution.py:251
  7.3 0.7 %copy-start.1 = (s32[512,1]{0,1:T(1,128)S(1)}, s32[512,1]{0,1:T(1,128)}, u32[]{:S(2)}) copy-start(s32[512,1]{0,1:T(1,128)} %param.4) | copy-start | bytes 6148
  8.5 3.3 %collective-permute-start.3 = (s32[4,512]{1,0:T(4,128)S(1)}, s32[4,512]{1,0:T(4,128)S(1)}, u32[]{:S(2)}, u32[]{:S(2)}) collective-permute-start(s32[4,512]{1,0:T(4,128)S(1)} %get-tuple-element.32), channel_id=1, source_target_pairs={{0,3},{1,4},{4,1},{5,8},{8,5},{9,12},{12,9},{13,14},{14,13},{15,10... | collective-permute-start | bytes 24584 | tf_op jit(solution)/shard_map/ppermute | solution.py:251
  11.8 1.3 %collective-permute-start.4 = (s32[4,512]{1,0:T(4,128)S(1)}, s32[4,512]{1,0:T(4,128)S(1)}, u32[]{:S(2)}, u32[]{:S(2)}) collective-permute-start(s32[4,512]{1,0:T(4,128)S(1)} %collective-permute-done.3.refs_4_.refs_6_), channel_id=1, source_target_pairs={{0,1},{1,0},{4,5},{5,4},{8,9},{9,8},{12,13},{13,12},{14,15},{15,14... | collective-permute-start | bytes 24584 | tf_op jit(solution)/shard_map/ppermute | solution.py:251
  13.1 3.2 %collective-permute-start.5 = (s32[4,512]{1,0:T(4,128)S(1)}, s32[4,512]{1,0:T(4,128)S(1)}, u32[]{:S(2)}, u32[]{:S(2)}) collective-permute-start(s32[4,512]{1,0:T(4,128)S(1)} %collective-permute-done.4.refs_5_.refs_7_.refs_1_), channel_id=1, source_target_pairs={{0,3},{1,4},{4,1},{5,8},{8,5},{9,12},{12,9},{13,14},{14,13},{15,10... | collective-permute-start | bytes 24584 | tf_op jit(solution)/shard_map/ppermute | solution.py:251
  16.3 3.9 %collective-permute-start.6 = (s32[4,512]{1,0:T(4,128)S(1)}, s32[4,512]{1,0:T(4,128)S(1)}, u32[]{:S(2)}, u32[]{:S(2)}) collective-permute-start(s32[4,512]{1,0:T(4,128)S(1)} %collective-permute-done.5.refs_3_.a_names), channel_id=1, source_target_pairs={{0,1},{1,0},{4,5},{5,4},{8,9},{9,8},{12,13},{13,12},{14,15},{15,14... | collective-permute-start | bytes 24584 | tf_op jit(solution)/shard_map/ppermute | solution.py:251
  17.0 1.2 %copy-start = (bf16[512,1024]{1,0:T(8,128)(2,1)S(1)}, bf16[512,1024]{1,0:T(8,128)(2,1)}, u32[]{:S(2)}) copy-start(bf16[512,1024]{1,0:T(8,128)(2,1)} %refs_0_.1) | copy-start | bytes 3145732
  20.3 2.2 %collective-permute-start.7 = (bf16[256,1024]{1,0:T(8,128)(2,1)S(1)}, bf16[256,1024]{1,0:T(8,128)(2,1)S(1)}, u32[]{:S(2)}, u32[]{:S(2)}) collective-permute-start(bf16[256,1024]{1,0:T(8,128)(2,1)S(1)} %get-tuple-element.60), channel_id=1, source_target_pairs={{0,1},{1,0},{4,5},{5,4},{8,9},{9,8},{12,13},{13,12},{14,15},{15,14... | collective-permute-start | bytes 1572872 | tf_op jit(solution)/shard_map/ppermute | solution.py:251
  20.4 2.6 %collective-permute-start.8 = (bf16[256,1024]{1,0:T(8,128)(2,1)S(1)}, bf16[256,1024]{1,0:T(8,128)(2,1)S(1)}, u32[]{:S(2)}, u32[]{:S(2)}) collective-permute-start(bf16[256,1024]{1,0:T(8,128)(2,1)S(1)} %get-tuple-element.59), channel_id=1, source_target_pairs={{0,1},{1,0},{4,5},{5,4},{8,9},{9,8},{12,13},{13,12},{14,15},{15,14... | collective-permute-start | bytes 1572872 | tf_op jit(solution)/shard_map/ppermute | solution.py:251
  20.9 17.8 %collective-permute-start.12 = (bf16[512,1024]{1,0:T(8,128)(2,1)S(1)}, bf16[512,1024]{1,0:T(8,128)(2,1)S(1)}, u32[]{:S(2)}, u32[]{:S(2)}) collective-permute-start(bf16[512,1024]{1,0:T(8,128)(2,1)S(1)} %collective-permute-done.refs_0_), channel_id=1, source_target_pairs={{0,4},{1,3},{4,8},{5,1},{8,12},{9,5},{12,14},{13,9},{14,10},{15,13... | collective-permute-start | bytes 3145736 | tf_op jit(solution)/shard_map/ppermute | solution.py:251
  27.8 2.7 %collective-permute-start.10 = (bf16[256,1024]{1,0:T(8,128)(2,1)S(1)}, bf16[256,1024]{1,0:T(8,128)(2,1)S(1)}, u32[]{:S(2)}, u32[]{:S(2)}) collective-permute-start(bf16[256,1024]{1,0:T(8,128)(2,1)S(1)} %get-tuple-element.58), channel_id=1, source_target_pairs={{0,1},{1,0},{4,5},{5,4},{8,9},{9,8},{12,13},{13,12},{14,15},{15,14... | collective-permute-start | bytes 1572872 | tf_op jit(solution)/shard_map/ppermute | solution.py:251
  27.9 2.6 %collective-permute-start.11 = (bf16[256,1024]{1,0:T(8,128)(2,1)S(1)}, bf16[256,1024]{1,0:T(8,128)(2,1)S(1)}, u32[]{:S(2)}, u32[]{:S(2)}) collective-permute-start(bf16[256,1024]{1,0:T(8,128)(2,1)S(1)} %get-tuple-element.57), channel_id=1, source_target_pairs={{0,1},{1,0},{4,5},{5,4},{8,9},{9,8},{12,13},{13,12},{14,15},{15,14... | collective-permute-start | bytes 1572872 | tf_op jit(solution)/shard_map/ppermute | solution.py:251
  28.4 21.5 %collective-permute-start.20 = (bf16[512,1024]{1,0:T(8,128)(2,1)S(1)}, bf16[512,1024]{1,0:T(8,128)(2,1)S(1)}, u32[]{:S(2)}, u32[]{:S(2)}) collective-permute-start(bf16[512,1024]{1,0:T(8,128)(2,1)S(1)} %unit_rows.1.refs_2_), channel_id=1, source_target_pairs={{0,4},{1,3},{4,8},{5,1},{8,12},{9,5},{12,14},{13,9},{14,10},{15,13... | collective-permute-start | bytes 3145736 | tf_op jit(solution)/shard_map/ppermute | solution.py:251
  34.6 4.1 %collective-permute-start.13 = (f32[2,512]{1,0:T(2,128)S(1)}, f32[2,512]{1,0:T(2,128)S(1)}, u32[]{:S(2)}, u32[]{:S(2)}) collective-permute-start(f32[2,512]{1,0:T(2,128)S(1)} %slice.29), channel_id=1, source_target_pairs={{0,2},{1,5},{4,0},{5,9},{8,4},{9,13},{12,8},{13,15},{14,12},{15,11... | collective-permute-start | bytes 12296 | tf_op jit(solution)/shard_map/ppermute | solution.py:251
  38.8 6.7 %collective-permute-start.17 = (bf16[256,1024]{1,0:T(8,128)(2,1)S(1)}, bf16[256,1024]{1,0:T(8,128)(2,1)S(1)}, u32[]{:S(2)}, u32[]{:S(2)}) collective-permute-start(bf16[256,1024]{1,0:T(8,128)(2,1)S(1)} %get-tuple-element.56), channel_id=1, source_target_pairs={{0,1},{1,0},{4,5},{5,4},{8,9},{9,8},{12,13},{13,12},{14,15},{15,14... | collective-permute-start | bytes 1572872 | tf_op jit(solution)/shard_map/ppermute | solution.py:251
  38.9 6.6 %collective-permute-start.18 = (bf16[256,1024]{1,0:T(8,128)(2,1)S(1)}, bf16[256,1024]{1,0:T(8,128)(2,1)S(1)}, u32[]{:S(2)}, u32[]{:S(2)}) collective-permute-start(bf16[256,1024]{1,0:T(8,128)(2,1)S(1)} %get-tuple-element.55), channel_id=1, source_target_pairs={{0,1},{1,0},{4,5},{5,4},{8,9},{9,8},{12,13},{13,12},{14,15},{15,14... | collective-permute-start | bytes 1572872 | tf_op jit(solution)/shard_map/ppermute | solution.py:251
  42.1 11.7 %collective-permute-start.15 = (f32[2,512]{1,0:T(2,128)S(1)}, f32[2,512]{1,0:T(2,128)S(1)}, u32[]{:S(2)}, u32[]{:S(2)}) collective-permute-start(f32[2,512]{1,0:T(2,128)S(1)} %get-tuple-element.61), channel_id=1, source_target_pairs={{0,5},{1,2},{4,9},{5,0},{8,13},{9,4},{12,15},{13,8},{14,11},{15,12... | collective-permute-start | bytes 12296 | tf_op jit(solution)/shard_map/ppermute | solution.py:251
  43.9 9.9 %collective-permute-start.16 = (f32[2,512]{1,0:T(2,128)S(1)}, f32[2,512]{1,0:T(2,128)S(1)}, u32[]{:S(2)}, u32[]{:S(2)}) collective-permute-start(f32[2,512]{1,0:T(2,128)S(1)} %get-tuple-element.61), channel_id=1, source_target_pairs={{0,4},{1,3},{4,8},{5,1},{8,12},{9,5},{12,14},{13,9},{14,10},{15,13... | collective-permute-start | bytes 12296 | tf_op jit(solution)/shard_map/ppermute | solution.py:251
  46.6 8.8 %collective-permute-start.19 = (f32[2,512]{1,0:T(2,128)S(1)}, f32[2,512]{1,0:T(2,128)S(1)}, u32[]{:S(2)}, u32[]{:S(2)}) collective-permute-start(f32[2,512]{1,0:T(2,128)S(1)} %get-tuple-element.53), channel_id=1, source_target_pairs={{0,6},{1,9},{4,2},{5,13},{8,0},{9,15},{12,4},{13,11},{14,8},{15,7}... | collective-permute-start | bytes 12296 | tf_op jit(solution)/shard_map/ppermute | solution.py:251
  47.4 6.3 %collective-permute-start.14 = (f32[1,512]{1,0:T(1,128)S(1)}, f32[1,512]{1,0:T(1,128)S(1)}, u32[]{:S(2)}, u32[]{:S(2)}) collective-permute-start(f32[1,512]{1,0:T(1,128)S(1)} %slice.31), channel_id=1, source_target_pairs={{0,1},{1,0},{4,5},{5,4},{8,9},{9,8},{12,13},{13,12},{14,15},{15,14... | collective-permute-start | bytes 6152 | tf_op jit(solution)/shard_map/ppermute | solution.py:251
  51.4 4.0 %collective-permute-start.21 = (f32[1,512]{1,0:T(1,128)S(1)}, f32[1,512]{1,0:T(1,128)S(1)}, u32[]{:S(2)}, u32[]{:S(2)}) collective-permute-start(f32[1,512]{1,0:T(1,128)S(1)} %last_terms.1), channel_id=1, source_target_pairs={{0,7},{1,8},{4,3},{5,12},{8,1},{9,14},{12,5},{13,10},{14,9},{15,6}... | collective-permute-start | bytes 6152 | tf_op jit(solution)/shard_map/ppermute | solution.py:251

commit v11 on v10

--- a/solution.py
+++ b/solution.py
@@ -7,7 +7,7 @@
 from jax.experimental.pallas import tpu as pltpu
 from jax.sharding import PartitionSpec as P
 
-STRIP = 256
+STRIP = 512
 SPLIT = 2
 END_ROOM = 2
 

time: 56.3 us -> 56.4 us (level)
  no operation moved by 1% of the time
where the time goes in v11:
time: 56.4 us; the launch traced here: 56 us
  starting transfers between devices  22.9 us (41%)
  Pallas kernels  15.5 us (27%)
  waiting for transfers between devices  14.8 us (26%)
  local copies, waits for them, and re-layouts  2.14 us (4%)
  other arithmetic  0.6 us (1%)
    ppermute x22, starting transfers between devices, moved(): return lax.ppermute(block, 'blk', route)  22.9 us
    ppermute x22, waiting for transfers between devices, moved(): return lax.ppermute(block, 'blk', route)  14.8 us
    pallas_call x5, Pallas kernels, row_sums(): pl.pallas_call(functools.partial(sums_kernel, [(len(block[0]), *block[1:]...  12.5 us
    pallas_call x2, Pallas kernels, in_vmem(): pl.pallas_call(kernel, out_shape=jax.ShapeDtypeStruct(shape, dtype), in_s...  2.07 us
    unnamed x6, local copies, waits for them, and re-layouts  1.91 us
  transfers between devices with their start and end apart: 22, of which 10 were waited for; matrix products, arithmetic and copies ran while one was open for 0% of the time, Pallas kernels for 28%

profile of v11, /device:TPU:0, one launch (start us, length us, event | category | flops | bytes accessed | tf_op | source)
XLA Modules:
  0.0 56.0 jit_solution(14274006780103348278)
XLA Ops:
  0.0 0.0 copy-start.2
  0.0 0.5 collective-permute-start.1
  0.5 2.6 %collective-permute-start = (bf16[512,1024]{1,0:T(8,128)(2,1)}, bf16[512,1024]{1,0:T(8,128)(2,1)S(1)}, u32[]{:S(2)}, u32[]{:S(2)}) collective-permute-start(bf16[512,1024]{1,0:T(8,128)(2,1)} %refs_0_.1), channel_id=1, source_target_pairs={{0,4},{1,3},{4,8},{5,1},{8,12},{9,5},{12,14},{13,9},{14,10},{15,13... | collective-permute-start | bytes 3145736 | tf_op jit(solution)/shard_map/ppermute | solution.py:251
  3.1 0.0 collective-permute-done.1.refs_1_
  3.1 2.8 %collective-permute-start.9 = (bf16[512,1024]{1,0:T(8,128)(2,1)S(1)}, bf16[512,1024]{1,0:T(8,128)(2,1)S(1)}, u32[]{:S(2)}, u32[]{:S(2)}) collective-permute-start(bf16[512,1024]{1,0:T(8,128)(2,1)S(1)} %collective-permute-done.1.refs_1_), channel_id=1, source_target_pairs={{0,4},{1,3},{4,8},{5,1},{8,12},{9,5},{12,14},{13,9},{14,10},{15,13... | collective-permute-start | bytes 3145736 | tf_op jit(solution)/shard_map/ppermute | solution.py:251
  5.9 0.0 collective-permute-start.2
  5.9 1.4 %collective-permute-done.2.other = s32[1,512]{1,0:T(1,128)S(1)} collective-permute-done((s32[1,512]{1,0:T(1,128)}, s32[1,512]{1,0:T(1,128)S(1)}, u32[]{:S(2)}, u32[]{:S(2)}) %collective-permute-start.2) | collective-permute-done | bytes 2080 | tf_op jit(solution)/shard_map/ppermute | solution.py:251
  7.3 0.0 copy-done.2
  7.3 0.0 copy-start.1
  7.3 0.7 %copy-done.1 = s32[512,1]{0,1:T(1,128)S(1)} copy-done((s32[512,1]{0,1:T(1,128)S(1)}, s32[512,1]{0,1:T(1,128)}, u32[]{:S(2)}) %copy-start.1) | copy-done | bytes 2072
  8.0 0.6 %name_tables.1 = (s32[4,512]{1,0:T(4,128)S(1)}, s32[4,512]{1,0:T(4,128)S(1)}) custom-call(s32[16]{0:T(128)S(1)} %copy-done.2, s32[1,512]{1,0:T(1,128)S(1)} %bitcast.3, s32[1,512]{1,0:T(1,128)S(1)} %collective-permute-done.2.other), custom_call_target="tpu_custom_call" | custom-call | tf_op jit(solution)/shard_map/name_tables/pallas_call | solution.py:176
  8.5 1.0 %collective-permute-start.3 = (s32[4,512]{1,0:T(4,128)S(1)}, s32[4,512]{1,0:T(4,128)S(1)}, u32[]{:S(2)}, u32[]{:S(2)}) collective-permute-start(s32[4,512]{1,0:T(4,128)S(1)} %get-tuple-element.32), channel_id=1, source_target_pairs={{0,3},{1,4},{4,1},{5,8},{8,5},{9,12},{12,9},{13,14},{14,13},{15,10... | collective-permute-start | bytes 24584 | tf_op jit(solution)/shard_map/ppermute | solution.py:251
  9.6 2.2 %collective-permute-done.3.refs_4_.refs_6_ = s32[4,512]{1,0:T(4,128)S(1)} collective-permute-done((s32[4,512]{1,0:T(4,128)S(1)}, s32[4,512]{1,0:T(4,128)S(1)}, u32[]{:S(2)}, u32[]{:S(2)}) %collective-permute-start.3) | collective-permute-done | bytes 8224 | tf_op jit(solution)/shard_map/ppermute | solution.py:251
  11.8 0.5 collective-permute-start.4
  12.3 0.8 %collective-permute-done.4.refs_5_.refs_7_.refs_1_ = s32[4,512]{1,0:T(4,128)S(1)} collective-permute-done((s32[4,512]{1,0:T(4,128)S(1)}, s32[4,512]{1,0:T(4,128)S(1)}, u32[]{:S(2)}, u32[]{:S(2)}) %collective-permute-start.4) | collective-permute-done | bytes 8224 | tf_op jit(solution)/shard_map/ppermute | solution.py:251
  13.1 1.1 %collective-permute-start.5 = (s32[4,512]{1,0:T(4,128)S(1)}, s32[4,512]{1,0:T(4,128)S(1)}, u32[]{:S(2)}, u32[]{:S(2)}) collective-permute-start(s32[4,512]{1,0:T(4,128)S(1)} %collective-permute-done.4.refs_5_.refs_7_.refs_1_), channel_id=1, source_target_pairs={{0,3},{1,4},{4,1},{5,8},{8,5},{9,12},{12,9},{13,14},{14,13},{15,10... | collective-permute-start | bytes 24584 | tf_op jit(solution)/shard_map/ppermute | solution.py:251
  14.3 2.1 %collective-permute-done.5.refs_3_.a_names = s32[4,512]{1,0:T(4,128)S(1)} collective-permute-done((s32[4,512]{1,0:T(4,128)S(1)}, s32[4,512]{1,0:T(4,128)S(1)}, u32[]{:S(2)}, u32[]{:S(2)}) %collective-permute-start.5) | collective-permute-done | bytes 8224 | tf_op jit(solution)/shard_map/ppermute | solution.py:251
  16.3 0.6 %collective-permute-start.6 = (s32[4,512]{1,0:T(4,128)S(1)}, s32[4,512]{1,0:T(4,128)S(1)}, u32[]{:S(2)}, u32[]{:S(2)}) collective-permute-start(s32[4,512]{1,0:T(4,128)S(1)} %collective-permute-done.5.refs_3_.a_names), channel_id=1, source_target_pairs={{0,1},{1,0},{4,5},{5,4},{8,9},{9,8},{12,13},{13,12},{14,15},{15,14... | collective-permute-start | bytes 24584 | tf_op jit(solution)/shard_map/ppermute | solution.py:251
  17.0 0.0 copy-start
  17.0 1.2 %copy-done = bf16[512,1024]{1,0:T(8,128)(2,1)S(1)} copy-done((bf16[512,1024]{1,0:T(8,128)(2,1)S(1)}, bf16[512,1024]{1,0:T(8,128)(2,1)}, u32[]{:S(2)}) %copy-start) | copy-done | bytes 1048600
  18.2 2.0 %own_terms.1 = (f32[1,512]{1,0:T(1,128)S(1)}, bf16[512,1024]{1,0:T(8,128)(2,1)S(1)}) custom-call(bf16[512,1024]{1,0:T(8,128)(2,1)S(1)} %copy-done, bf16[512,1024]{1,0:T(8,128)(2,1)S(1)} %collective-permute-done.1.refs_1_, s32[4,512]{1,0:T(4,128)S(1)} %get-tuple-element.30.refs_2_.refs_6_.refs_8_), custom_call_target="tpu_custom_call" | custom-call | tf_op jit(solution)/shard_map/own_terms/pallas_call | solution.py:142
  20.2 0.0 collective-permute-done.6.refs_4_.refs_0_
  20.2 0.0 collective-permute-done.refs_0_
  20.2 0.1 fusion.4
  20.3 0.1 collective-permute-start.7
  20.4 0.5 collective-permute-start.8
  20.9 1.6 %collective-permute-start.12 = (bf16[512,1024]{1,0:T(8,128)(2,1)S(1)}, bf16[512,1024]{1,0:T(8,128)(2,1)S(1)}, u32[]{:S(2)}, u32[]{:S(2)}) collective-permute-start(bf16[512,1024]{1,0:T(8,128)(2,1)S(1)} %collective-permute-done.refs_0_), channel_id=1, source_target_pairs={{0,4},{1,3},{4,8},{5,1},{8,12},{9,5},{12,14},{13,9},{14,10},{15,13... | collective-permute-start | bytes 3145736 | tf_op jit(solution)/shard_map/ppermute | solution.py:251
  22.5 0.0 collective-permute-done.7.refs_1_
  22.5 0.6 %collective-permute-done.8.refs_2_ = bf16[256,1024]{1,0:T(8,128)(2,1)S(1)} collective-permute-done((bf16[256,1024]{1,0:T(8,128)(2,1)S(1)}, bf16[256,1024]{1,0:T(8,128)(2,1)S(1)}, u32[]{:S(2)}, u32[]{:S(2)}) %collective-permute-start.8) | collective-permute-done | bytes 524320 | tf_op jit(solution)/shard_map/ppermute | solution.py:251
  23.0 2.9 %first_terms.1 = (f32[3,512]{1,0:T(4,128)S(1)}, bf16[512,1024]{1,0:T(8,128)(2,1)S(1)}, bf16[512,1024]{1,0:T(8,128)(2,1)S(1)}) custom-call(bf16[512,1024]{1,0:T(8,128)(2,1)S(1)} %collective-permute-done.refs_0_, bf16[256,1024]{1,0:T(8,128)(2,1)S(1)} %collective-permute-done.7.refs_1_, bf16[256,1024]{1,0:T(8,128)(2,1)S(1)} %collective-permute-done.8.refs_2_, ...), custom_call_target="tpu_custom_call" | custom-call | tf_op jit(solution)/shard_map/first_terms/pallas_call | solution.py:142
  26.0 1.5 %collective-permute-done.9.source = bf16[512,1024]{1,0:T(8,128)(2,1)S(1)} collective-permute-done((bf16[512,1024]{1,0:T(8,128)(2,1)S(1)}, bf16[512,1024]{1,0:T(8,128)(2,1)S(1)}, u32[]{:S(2)}, u32[]{:S(2)}) %collective-permute-start.9) | collective-permute-done | bytes 1048608 | tf_op jit(solution)/shard_map/ppermute | solution.py:251
  27.4 0.3 unit_rows.1.refs_2_
  27.8 0.1 fusion.3
  27.8 0.1 collective-permute-start.10
  27.9 0.5 collective-permute-start.11
  28.4 2.1 %collective-permute-start.20 = (bf16[512,1024]{1,0:T(8,128)(2,1)S(1)}, bf16[512,1024]{1,0:T(8,128)(2,1)S(1)}, u32[]{:S(2)}, u32[]{:S(2)}) collective-permute-start(bf16[512,1024]{1,0:T(8,128)(2,1)S(1)} %unit_rows.1.refs_2_), channel_id=1, source_target_pairs={{0,4},{1,3},{4,8},{5,1},{8,12},{9,5},{12,14},{13,9},{14,10},{15,13... | collective-permute-start | bytes 3145736 | tf_op jit(solution)/shard_map/ppermute | solution.py:251
  30.5 0.0 collective-permute-done.10.refs_3_
  30.5 0.1 collective-permute-done.11.refs_4_
  30.6 3.7 %pair_terms.1 = (f32[3,512]{1,0:T(4,128)S(1)}, bf16[512,1024]{1,0:T(8,128)(2,1)S(1)}) custom-call(bf16[512,1024]{1,0:T(8,128)(2,1)S(1)} %get-tuple-element.38.refs_0_, bf16[512,1024]{1,0:T(8,128)(2,1)S(1)} %get-tuple-element.46.refs_1_, bf16[512,1024]{1,0:T(8,128)(2,1)S(1)} %unit_rows.1.refs_2_, bf16[256,1024]{1,0:T(8,128)(2,1)S(1)} %collective-permute-done.10.refs_3_, ...), custom_call_target="tpu_custom_call" | custom-call | tf_op jit(solution)/shard_map/pair_terms/pallas_call | solution.py:142
  34.2 2.2 %collective-permute-start.13 = (f32[2,512]{1,0:T(2,128)S(1)}, f32[2,512]{1,0:T(2,128)S(1)}, u32[]{:S(2)}, u32[]{:S(2)}) collective-permute-start(f32[2,512]{1,0:T(2,128)S(1)} %slice.29), channel_id=1, source_target_pairs={{0,2},{1,5},{4,0},{5,9},{8,4},{9,13},{12,8},{13,15},{14,12},{15,11... | collective-permute-start | bytes 12296 | tf_op jit(solution)/shard_map/ppermute | solution.py:251
  36.5 2.2 %collective-permute-done.12.refs_0_ = bf16[512,1024]{1,0:T(8,128)(2,1)S(1)} collective-permute-done((bf16[512,1024]{1,0:T(8,128)(2,1)S(1)}, bf16[512,1024]{1,0:T(8,128)(2,1)S(1)}, u32[]{:S(2)}, u32[]{:S(2)}) %collective-permute-start.12) | collective-permute-done | bytes 1048608 | tf_op jit(solution)/shard_map/ppermute | solution.py:251
  38.7 0.0 collective-permute-done.13
  38.7 0.1 fusion.2
  38.8 0.1 collective-permute-start.17
  38.9 0.5 collective-permute-start.18
  39.4 2.6 %end_terms.2 = (f32[3,512]{1,0:T(4,128)S(1)}, bf16[512,1024]{1,0:T(8,128)(2,1)S(1)}) custom-call(bf16[512,1024]{1,0:T(8,128)(2,1)S(1)} %collective-permute-done.12.refs_0_, bf16[512,1024]{1,0:T(8,128)(2,1)S(1)} %get-tuple-element.46.refs_1_, bf16[512,1024]{1,0:T(8,128)(2,1)S(1)} %get-tuple-element.47.refs_2_.refs_1_, ...), custom_call_target="tpu_custom_call" | custom-call | tf_op jit(solution)/shard_map/end_terms/pallas_call | solution.py:142
  42.0 1.8 %collective-permute-start.15 = (f32[2,512]{1,0:T(2,128)S(1)}, f32[2,512]{1,0:T(2,128)S(1)}, u32[]{:S(2)}, u32[]{:S(2)}) collective-permute-start(f32[2,512]{1,0:T(2,128)S(1)} %get-tuple-element.61), channel_id=1, source_target_pairs={{0,5},{1,2},{4,9},{5,0},{8,13},{9,4},{12,15},{13,8},{14,11},{15,12... | collective-permute-start | bytes 12296 | tf_op jit(solution)/shard_map/ppermute | solution.py:251
  43.8 1.6 %collective-permute-start.16 = (f32[2,512]{1,0:T(2,128)S(1)}, f32[2,512]{1,0:T(2,128)S(1)}, u32[]{:S(2)}, u32[]{:S(2)}) collective-permute-start(f32[2,512]{1,0:T(2,128)S(1)} %get-tuple-element.61), channel_id=1, source_target_pairs={{0,4},{1,3},{4,8},{5,1},{8,12},{9,5},{12,14},{13,9},{14,10},{15,13... | collective-permute-start | bytes 12296 | tf_op jit(solution)/shard_map/ppermute | solution.py:251
  45.4 0.0 collective-permute-done.17.refs_1_
  45.4 0.0 collective-permute-done.18.refs_2_
  45.4 1.3 %end_terms.3 = (f32[2,512]{1,0:T(2,128)S(1)}, bf16[512,1024]{1,0:T(8,128)(2,1)S(1)}) custom-call(bf16[512,1024]{1,0:T(8,128)(2,1)S(1)} %get-tuple-element.51.refs_0_, bf16[256,1024]{1,0:T(8,128)(2,1)S(1)} %collective-permute-done.17.refs_1_, bf16[256,1024]{1,0:T(8,128)(2,1)S(1)} %collective-permute-done.18.refs_2_, ...), custom_call_target="tpu_custom_call" | custom-call | tf_op jit(solution)/shard_map/end_terms/pallas_call | solution.py:142
  46.7 0.3 collective-permute-start.19
  47.0 0.6 %end_weights.1.refs_2_ = bf16[512,1024]{1,0:T(8,128)(2,1)S(1)} custom-call(s32[4,512]{1,0:T(4,128)S(1)} %collective-permute-done.5.refs_3_.a_names, s32[4,512]{1,0:T(4,128)S(1)} %collective-permute-done.6.refs_4_.refs_0_, s32[4,512]{1,0:T(4,128)S(1)} %collective-permute-done.4.refs_5_.refs_7_.refs_1_), custom_call_target="tpu_custom_call" | custom-call | tf_op jit(solution)/shard_map/end_weights/pallas_call | solution.py:228
  47.6 0.1 collective-permute-start.14
  47.7 2.3 %collective-permute-done.20.a = bf16[512,1024]{1,0:T(8,128)(2,1)S(1)} collective-permute-done((bf16[512,1024]{1,0:T(8,128)(2,1)S(1)}, bf16[512,1024]{1,0:T(8,128)(2,1)S(1)}, u32[]{:S(2)}, u32[]{:S(2)}) %collective-permute-start.20) | collective-permute-done | bytes 1048608 | tf_op jit(solution)/shard_map/ppermute | solution.py:251
  49.9 1.5 %last_terms.1 = f32[1,512]{1,0:T(1,128)S(1)} custom-call(bf16[512,1024]{1,0:T(8,128)(2,1)S(1)} %collective-permute-done.20.a, bf16[512,1024]{1,0:T(8,128)(2,1)S(1)} %get-tuple-element.54.refs_0_, bf16[512,1024]{1,0:T(8,128)(2,1)S(1)} %get-tuple-element.47.refs_2_.refs_1_, bf16[512,1024]{1,0:T(8,128)(2,1)S(1)} %end_weights.1.refs_2_), custom_call_target="tpu_custom_call" | custom-call | tf_op jit(solution)/shard_map/last_terms/pallas_call | solution.py:228
  51.4 2.4 %collective-permute-start.21 = (f32[1,512]{1,0:T(1,128)S(1)}, f32[1,512]{1,0:T(1,128)S(1)}, u32[]{:S(2)}, u32[]{:S(2)}) collective-permute-start(f32[1,512]{1,0:T(1,128)S(1)} %last_terms.1), channel_id=1, source_target_pairs={{0,7},{1,8},{4,3},{5,12},{8,1},{9,14},{12,5},{13,10},{14,9},{15,6}... | collective-permute-start | bytes 6152 | tf_op jit(solution)/shard_map/ppermute | solution.py:251
  53.8 0.0 collective-permute-done.14
  53.8 0.0 collective-permute-done.15
  53.8 0.0 collective-permute-done.16
  53.8 1.6 %collective-permute-done.21 = f32[1,512]{1,0:T(1,128)S(1)} collective-permute-done((f32[1,512]{1,0:T(1,128)S(1)}, f32[1,512]{1,0:T(1,128)S(1)}, u32[]{:S(2)}, u32[]{:S(2)}) %collective-permute-start.21) | collective-permute-done | bytes 2080 | tf_op jit(solution)/shard_map/ppermute | solution.py:251
  55.4 0.0 collective-permute-done.19
  55.4 0.6 %fusion.1 = f32[1,512]{1,0:T(1,128)} fusion(f32[1,512]{1,0:T(1,128)S(1)} %collective-permute-done.21, f32[2,512]{1,0:T(2,128)S(1)} %collective-permute-done.19, f32[2,512]{1,0:T(2,128)S(1)} %collective-permute-done.16, f32[2,512]{1,0:T(2,128)S(1)} %collective-permute-done.15, f32[1,512]{1,0:T(1,128)S(1)} %collective-permute-done.14, ...), kind=kLoop, calls=%fused_computation.4 | loop fusion | flops 3584 | bytes 18432 | tf_op jit(solution)/shard_map/log1p | solution.py:348
  (3 shorter events, 0.0 us)
Async XLA Ops:
  0.0 7.3 %copy-start.2 = (s32[16]{0:T(128)S(1)}, s32[16]{0:T(128)}, u32[]{:S(2)}) copy-start(s32[16]{0:T(128)} %near.1) | copy-start | bytes 196
  0.0 3.1 %collective-permute-start.1 = (bf16[512,1024]{1,0:T(8,128)(2,1)}, bf16[512,1024]{1,0:T(8,128)(2,1)S(1)}, u32[]{:S(2)}, u32[]{:S(2)}) collective-permute-start(bf16[512,1024]{1,0:T(8,128)(2,1)} %refs_0_.1), channel_id=1, source_target_pairs={{0,1},{1,0},{4,5},{5,4},{8,9},{9,8},{12,13},{13,12},{14,15},{15,14... | collective-permute-start | bytes 3145736 | tf_op jit(solution)/shard_map/ppermute | solution.py:251
  0.5 19.8 %collective-permute-start = (bf16[512,1024]{1,0:T(8,128)(2,1)}, bf16[512,1024]{1,0:T(8,128)(2,1)S(1)}, u32[]{:S(2)}, u32[]{:S(2)}) collective-permute-start(bf16[512,1024]{1,0:T(8,128)(2,1)} %refs_0_.1), channel_id=1, source_target_pairs={{0,4},{1,3},{4,8},{5,1},{8,12},{9,5},{12,14},{13,9},{14,10},{15,13... | collective-permute-start | bytes 3145736 | tf_op jit(solution)/shard_map/ppermute | solution.py:251
  3.1 24.3 %collective-permute-start.9 = (bf16[512,1024]{1,0:T(8,128)(2,1)S(1)}, bf16[512,1024]{1,0:T(8,128)(2,1)S(1)}, u32[]{:S(2)}, u32[]{:S(2)}) collective-permute-start(bf16[512,1024]{1,0:T(8,128)(2,1)S(1)} %collective-permute-done.1.refs_1_), channel_id=1, source_target_pairs={{0,4},{1,3},{4,8},{5,1},{8,12},{9,5},{12,14},{13,9},{14,10},{15,13... | collective-permute-start | bytes 3145736 | tf_op jit(solution)/shard_map/ppermute | solution.py:251
  5.9 1.4 %collective-permute-start.2 = (s32[1,512]{1,0:T(1,128)}, s32[1,512]{1,0:T(1,128)S(1)}, u32[]{:S(2)}, u32[]{:S(2)}) collective-permute-start(s32[1,512]{1,0:T(1,128)} %bitcast.2), channel_id=1, source_target_pairs={{0,1},{1,0},{4,5},{5,4},{8,9},{9,8},{12,13},{13,12},{14,15},{15,14... | collective-permute-start | bytes 6152 | tf_op jit(solution)/shard_map/ppermute | solution.py:251
  7.3 0.7 %copy-start.1 = (s32[512,1]{0,1:T(1,128)S(1)}, s32[512,1]{0,1:T(1,128)}, u32[]{:S(2)}) copy-start(s32[512,1]{0,1:T(1,128)} %param.4) | copy-start | bytes 6148
  8.5 3.3 %collective-permute-start.3 = (s32[4,512]{1,0:T(4,128)S(1)}, s32[4,512]{1,0:T(4,128)S(1)}, u32[]{:S(2)}, u32[]{:S(2)}) collective-permute-start(s32[4,512]{1,0:T(4,128)S(1)} %get-tuple-element.32), channel_id=1, source_target_pairs={{0,3},{1,4},{4,1},{5,8},{8,5},{9,12},{12,9},{13,14},{14,13},{15,10... | collective-permute-start | bytes 24584 | tf_op jit(solution)/shard_map/ppermute | solution.py:251
  11.8 1.3 %collective-permute-start.4 = (s32[4,512]{1,0:T(4,128)S(1)}, s32[4,512]{1,0:T(4,128)S(1)}, u32[]{:S(2)}, u32[]{:S(2)}) collective-permute-start(s32[4,512]{1,0:T(4,128)S(1)} %collective-permute-done.3.refs_4_.refs_6_), channel_id=1, source_target_pairs={{0,1},{1,0},{4,5},{5,4},{8,9},{9,8},{12,13},{13,12},{14,15},{15,14... | collective-permute-start | bytes 24584 | tf_op jit(solution)/shard_map/ppermute | solution.py:251
  13.1 3.2 %collective-permute-start.5 = (s32[4,512]{1,0:T(4,128)S(1)}, s32[4,512]{1,0:T(4,128)S(1)}, u32[]{:S(2)}, u32[]{:S(2)}) collective-permute-start(s32[4,512]{1,0:T(4,128)S(1)} %collective-permute-done.4.refs_5_.refs_7_.refs_1_), channel_id=1, source_target_pairs={{0,3},{1,4},{4,1},{5,8},{8,5},{9,12},{12,9},{13,14},{14,13},{15,10... | collective-permute-start | bytes 24584 | tf_op jit(solution)/shard_map/ppermute | solution.py:251
  16.3 3.9 %collective-permute-start.6 = (s32[4,512]{1,0:T(4,128)S(1)}, s32[4,512]{1,0:T(4,128)S(1)}, u32[]{:S(2)}, u32[]{:S(2)}) collective-permute-start(s32[4,512]{1,0:T(4,128)S(1)} %collective-permute-done.5.refs_3_.a_names), channel_id=1, source_target_pairs={{0,1},{1,0},{4,5},{5,4},{8,9},{9,8},{12,13},{13,12},{14,15},{15,14... | collective-permute-start | bytes 24584 | tf_op jit(solution)/shard_map/ppermute | solution.py:251
  17.0 1.2 %copy-start = (bf16[512,1024]{1,0:T(8,128)(2,1)S(1)}, bf16[512,1024]{1,0:T(8,128)(2,1)}, u32[]{:S(2)}) copy-start(bf16[512,1024]{1,0:T(8,128)(2,1)} %refs_0_.1) | copy-start | bytes 3145732
  20.3 2.1 %collective-permute-start.7 = (bf16[256,1024]{1,0:T(8,128)(2,1)S(1)}, bf16[256,1024]{1,0:T(8,128)(2,1)S(1)}, u32[]{:S(2)}, u32[]{:S(2)}) collective-permute-start(bf16[256,1024]{1,0:T(8,128)(2,1)S(1)} %get-tuple-element.60), channel_id=1, source_target_pairs={{0,1},{1,0},{4,5},{5,4},{8,9},{9,8},{12,13},{13,12},{14,15},{15,14... | collective-permute-start | bytes 1572872 | tf_op jit(solution)/shard_map/ppermute | solution.py:251
  20.4 2.6 %collective-permute-start.8 = (bf16[256,1024]{1,0:T(8,128)(2,1)S(1)}, bf16[256,1024]{1,0:T(8,128)(2,1)S(1)}, u32[]{:S(2)}, u32[]{:S(2)}) collective-permute-start(bf16[256,1024]{1,0:T(8,128)(2,1)S(1)} %get-tuple-element.59), channel_id=1, source_target_pairs={{0,1},{1,0},{4,5},{5,4},{8,9},{9,8},{12,13},{13,12},{14,15},{15,14... | collective-permute-start | bytes 1572872 | tf_op jit(solution)/shard_map/ppermute | solution.py:251
  20.9 17.8 %collective-permute-start.12 = (bf16[512,1024]{1,0:T(8,128)(2,1)S(1)}, bf16[512,1024]{1,0:T(8,128)(2,1)S(1)}, u32[]{:S(2)}, u32[]{:S(2)}) collective-permute-start(bf16[512,1024]{1,0:T(8,128)(2,1)S(1)} %collective-permute-done.refs_0_), channel_id=1, source_target_pairs={{0,4},{1,3},{4,8},{5,1},{8,12},{9,5},{12,14},{13,9},{14,10},{15,13... | collective-permute-start | bytes 3145736 | tf_op jit(solution)/shard_map/ppermute | solution.py:251
  27.8 2.7 %collective-permute-start.10 = (bf16[256,1024]{1,0:T(8,128)(2,1)S(1)}, bf16[256,1024]{1,0:T(8,128)(2,1)S(1)}, u32[]{:S(2)}, u32[]{:S(2)}) collective-permute-start(bf16[256,1024]{1,0:T(8,128)(2,1)S(1)} %get-tuple-element.58), channel_id=1, source_target_pairs={{0,1},{1,0},{4,5},{5,4},{8,9},{9,8},{12,13},{13,12},{14,15},{15,14... | collective-permute-start | bytes 1572872 | tf_op jit(solution)/shard_map/ppermute | solution.py:251
  27.9 2.6 %collective-permute-start.11 = (bf16[256,1024]{1,0:T(8,128)(2,1)S(1)}, bf16[256,1024]{1,0:T(8,128)(2,1)S(1)}, u32[]{:S(2)}, u32[]{:S(2)}) collective-permute-start(bf16[256,1024]{1,0:T(8,128)(2,1)S(1)} %get-tuple-element.57), channel_id=1, source_target_pairs={{0,1},{1,0},{4,5},{5,4},{8,9},{9,8},{12,13},{13,12},{14,15},{15,14... | collective-permute-start | bytes 1572872 | tf_op jit(solution)/shard_map/ppermute | solution.py:251
  28.4 21.5 %collective-permute-start.20 = (bf16[512,1024]{1,0:T(8,128)(2,1)S(1)}, bf16[512,1024]{1,0:T(8,128)(2,1)S(1)}, u32[]{:S(2)}, u32[]{:S(2)}) collective-permute-start(bf16[512,1024]{1,0:T(8,128)(2,1)S(1)} %unit_rows.1.refs_2_), channel_id=1, source_target_pairs={{0,4},{1,3},{4,8},{5,1},{8,12},{9,5},{12,14},{13,9},{14,10},{15,13... | collective-permute-start | bytes 3145736 | tf_op jit(solution)/shard_map/ppermute | solution.py:251
  34.2 4.5 %collective-permute-start.13 = (f32[2,512]{1,0:T(2,128)S(1)}, f32[2,512]{1,0:T(2,128)S(1)}, u32[]{:S(2)}, u32[]{:S(2)}) collective-permute-start(f32[2,512]{1,0:T(2,128)S(1)} %slice.29), channel_id=1, source_target_pairs={{0,2},{1,5},{4,0},{5,9},{8,4},{9,13},{12,8},{13,15},{14,12},{15,11... | collective-permute-start | bytes 12296 | tf_op jit(solution)/shard_map/ppermute | solution.py:251
  38.8 6.6 %collective-permute-start.17 = (bf16[256,1024]{1,0:T(8,128)(2,1)S(1)}, bf16[256,1024]{1,0:T(8,128)(2,1)S(1)}, u32[]{:S(2)}, u32[]{:S(2)}) collective-permute-start(bf16[256,1024]{1,0:T(8,128)(2,1)S(1)} %get-tuple-element.56), channel_id=1, source_target_pairs={{0,1},{1,0},{4,5},{5,4},{8,9},{9,8},{12,13},{13,12},{14,15},{15,14... | collective-permute-start | bytes 1572872 | tf_op jit(solution)/shard_map/ppermute | solution.py:251
  38.9 6.5 %collective-permute-start.18 = (bf16[256,1024]{1,0:T(8,128)(2,1)S(1)}, bf16[256,1024]{1,0:T(8,128)(2,1)S(1)}, u32[]{:S(2)}, u32[]{:S(2)}) collective-permute-start(bf16[256,1024]{1,0:T(8,128)(2,1)S(1)} %get-tuple-element.55), channel_id=1, source_target_pairs={{0,1},{1,0},{4,5},{5,4},{8,9},{9,8},{12,13},{13,12},{14,15},{15,14... | collective-permute-start | bytes 1572872 | tf_op jit(solution)/shard_map/ppermute | solution.py:251
  42.0 11.8 %collective-permute-start.15 = (f32[2,512]{1,0:T(2,128)S(1)}, f32[2,512]{1,0:T(2,128)S(1)}, u32[]{:S(2)}, u32[]{:S(2)}) collective-permute-start(f32[2,512]{1,0:T(2,128)S(1)} %get-tuple-element.61), channel_id=1, source_target_pairs={{0,5},{1,2},{4,9},{5,0},{8,13},{9,4},{12,15},{13,8},{14,11},{15,12... | collective-permute-start | bytes 12296 | tf_op jit(solution)/shard_map/ppermute | solution.py:251
  43.8 10.0 %collective-permute-start.16 = (f32[2,512]{1,0:T(2,128)S(1)}, f32[2,512]{1,0:T(2,128)S(1)}, u32[]{:S(2)}, u32[]{:S(2)}) collective-permute-start(f32[2,512]{1,0:T(2,128)S(1)} %get-tuple-element.61), channel_id=1, source_target_pairs={{0,4},{1,3},{4,8},{5,1},{8,12},{9,5},{12,14},{13,9},{14,10},{15,13... | collective-permute-start | bytes 12296 | tf_op jit(solution)/shard_map/ppermute | solution.py:251
  46.7 8.7 %collective-permute-start.19 = (f32[2,512]{1,0:T(2,128)S(1)}, f32[2,512]{1,0:T(2,128)S(1)}, u32[]{:S(2)}, u32[]{:S(2)}) collective-permute-start(f32[2,512]{1,0:T(2,128)S(1)} %get-tuple-element.53), channel_id=1, source_target_pairs={{0,6},{1,9},{4,2},{5,13},{8,0},{9,15},{12,4},{13,11},{14,8},{15,7}... | collective-permute-start | bytes 12296 | tf_op jit(solution)/shard_map/ppermute | solution.py:251
  47.6 6.2 %collective-permute-start.14 = (f32[1,512]{1,0:T(1,128)S(1)}, f32[1,512]{1,0:T(1,128)S(1)}, u32[]{:S(2)}, u32[]{:S(2)}) collective-permute-start(f32[1,512]{1,0:T(1,128)S(1)} %slice.31), channel_id=1, source_target_pairs={{0,1},{1,0},{4,5},{5,4},{8,9},{9,8},{12,13},{13,12},{14,15},{15,14... | collective-permute-start | bytes 6152 | tf_op jit(solution)/shard_map/ppermute | solution.py:251
  51.4 4.0 %collective-permute-start.21 = (f32[1,512]{1,0:T(1,128)S(1)}, f32[1,512]{1,0:T(1,128)S(1)}, u32[]{:S(2)}, u32[]{:S(2)}) collective-permute-start(f32[1,512]{1,0:T(1,128)S(1)} %last_terms.1), channel_id=1, source_target_pairs={{0,7},{1,8},{4,3},{5,12},{8,1},{9,14},{12,5},{13,10},{14,9},{15,6}... | collective-permute-start | bytes 6152 | tf_op jit(solution)/shard_map/ppermute | solution.py:251
